TPU v7x, 32 devices: a whole 2x2x4 slice. The times are simulated.
32 devices in a mesh: grid: 8 (over z, core), occ: 4 (over y, x).
Axes of the slice: x: 2, y: 2, z: 4, core: 2. Of those that a mesh axis runs over, the one named last changes fastest.
Arguments:
- orbital_values: bfloat16 [2048, 16000], P('grid', 'occ'), may hold values from -6 to 6
- occupied: bfloat16 [16000, 512], P('occ', 'grid'), may hold values from -0.046875 to 0.046875
- trial: bfloat16 [16000, 512], P('occ', 'grid'), may hold values from -0.046875 to 0.046875
- point_weights: float32 [2048], P('grid'), may hold values from 0.1 to 1
- batch_sizes: int32 [64], P('grid'), may hold values from 1 to 32, 1024 in all
- significant: int32 [64, 128], P('grid', 'occ'), may hold values 0 or 1
Outputs:
- exchange: float32 [16000, 512], P('occ', 'grid')
Inputs may be any that keep to these rules, and one draw needn't show every extreme that they name: `batch_sizes`: batch sizes sum to 1024 and the largest is exactly 32.
All inputs are finite; a program needn't handle non-finite values. No bound on the sum of `batch_sizes` or of `significant` on one device may be relied on, other than what follows from the above.
Results may differ from a plain program's by a relative error of at most 0.0027.
Values may be sent and summed in bfloat16 or wider, within the bound.
No kernel may reach another device: no remote copies, remote signals or barrier semaphores. Data moves between devices by JAX's collectives and lax.ppermute only.
A program may use at most 64 MiB of HBM per device.

v0:
```python
import math

import jax
import jax.numpy as jnp
from jax import lax
from jax.experimental import pallas as pl
from jax.experimental.pallas import tpu as pltpu
from jax.sharding import PartitionSpec as P

BF16, F32 = jnp.bfloat16, jnp.float32
VMEM_LIMIT = 48 * 1024 * 1024
WHOLE = pl.BlockSpec(memory_space=pltpu.VMEM)
SCALARS = pl.BlockSpec(memory_space=pltpu.SMEM)


def screen(values, sizes, significant):
    rows, cols = values.shape
    batches = sizes.shape[0]
    blocks = significant.shape[1]
    blocked = (
        values.reshape(batches, rows // batches, blocks, cols // blocks)
        * significant.astype(values.dtype)[:, None, :, None]
    )
    position = lax.broadcasted_iota(jnp.int32, (batches, rows // batches), 1)
    live = (position < sizes[:, None]).astype(jnp.float32).reshape(rows)
    return (blocked.reshape(rows, cols), live)


def any_sizes(orbital_values, occupied, trial, point_weights, batch_sizes, significant):
    screened, live = screen(orbital_values, batch_sizes, significant)
    rows, cols = screened.shape
    grid_count, occ_count = lax.axis_size("grid"), lax.axis_size("occ")
    columns = occupied.shape[1]
    me = lax.axis_index("grid")
    ring = [(i, (i + 1) % grid_count) for i in range(grid_count)]
    occ_ring = [(i, (i + 1) % occ_count) for i in range(occ_count)]

    def project_one(step, carry):
        panel, terms = carry
        term = jnp.dot(screened, panel, preferred_element_type=F32)
        terms = lax.dynamic_update_index_in_dim(terms, term, (me - step) % grid_count, 0)
        return lax.ppermute(panel, "grid", ring), terms

    joined = jnp.concatenate((occupied, trial), axis=1)
    terms = jnp.zeros((grid_count, rows, 2 * columns), F32)
    terms = lax.fori_loop(0, grid_count, project_one, (joined, terms))[1]

    def add_one(step, carry):
        moving, held = carry
        moving = lax.ppermute(moving, "occ", occ_ring)
        return moving, held + moving

    terms = lax.fori_loop(0, occ_count - 1, add_one, (terms, terms))[1]
    orbitals, response = terms[:, :, :columns], terms[:, :, columns:]
    density = jnp.sum(orbitals * response, axis=(0, 2)) * (1.0 / math.sqrt(columns * grid_count))
    weight = (point_weights * live)[None, :, None]
    kernel = (weight * (density[None, :, None] * orbitals + response)).astype(BF16)

    def contract_one(step, held):
        owner = (me + grid_count - 1 - step) % grid_count
        part = lax.dynamic_index_in_dim(kernel, owner, 0, keepdims=False)
        term = lax.dot_general(
            part, screened, (((0,), (0,)), ((), ())), preferred_element_type=F32
        )
        return lax.ppermute(held, "grid", ring) + term

    return lax.fori_loop(0, grid_count, contract_one, jnp.zeros((columns, cols), F32))


def half_of(whole, which):
    rows, columns = whole.shape
    half = rows // 2
    if half % 16:
        return lax.dynamic_slice_in_dim(whole, which * half, half, 0)

    def body(which_ref, whole_ref, out_ref, sem):
        first = pl.multiple_of(which_ref[0] * half, 16)
        copy = pltpu.make_async_copy(whole_ref.at[pl.ds(first, half)], out_ref, sem)
        copy.start()
        copy.wait()

    return pl.pallas_call(
        body,
        out_shape=jax.ShapeDtypeStruct((half, columns), whole.dtype),
        in_specs=[SCALARS, pl.BlockSpec(memory_space=pl.ANY)],
        out_specs=WHOLE,
        scratch_shapes=[pltpu.SemaphoreType.DMA],
        compiler_params=pltpu.CompilerParams(vmem_limit_bytes=VMEM_LIMIT),
        name="half_of",
    )(which[None], whole)


def compact(mine, got, mine_sig, got_sig, mine_to, got_to, width, tile, odd):
    half, rows = mine.shape
    blocks = mine_sig.shape[0]
    count = rows // tile + 2

    def body(odd_ref, mine_ref, got_ref, msig_ref, gsig_ref, mto_ref, gto_ref, *outs):
        block_of = lax.broadcasted_iota(jnp.int32, (half, blocks), 0)
        begin = lax.broadcasted_iota(jnp.int32, (half, blocks), 1) * width
        spread = ((block_of >= begin) & (block_of < begin + width)).astype(F32).astype(BF16)
        slot = lax.broadcasted_iota(jnp.int32, (rows, count * tile), 1)

        def part(value_ref, sig_ref, to_ref):
            kept = jnp.dot(spread, sig_ref[...], preferred_element_type=F32)
            screened = (value_ref[...].astype(F32) * kept).astype(BF16)
            place = (to_ref[...] == slot).astype(F32).astype(BF16)
            return jnp.dot(screened, place, preferred_element_type=F32)

        window = part(mine_ref, msig_ref, mto_ref) + part(got_ref, gsig_ref, gto_ref)
        for j in range(1, count - 1):
            outs[j][...] = window[:, j * tile : (j + 1) * tile].astype(BF16)
        first, last = window[:, :tile], window[:, (count - 1) * tile :]
        outs[0][...] = jnp.where(odd_ref[0] == 0, first, last).astype(BF16)
        outs[-1][...] = jnp.where(odd_ref[0] == 0, last, first).astype(BF16)

    shape = jax.ShapeDtypeStruct((half, tile), BF16)
    return pl.pallas_call(
        body,
        out_shape=(shape,) * count,
        in_specs=[SCALARS] + [WHOLE] * 6,
        out_specs=(WHOLE,) * count,
        compiler_params=pltpu.CompilerParams(vmem_limit_bytes=VMEM_LIMIT),
        name="compact",
        cost_estimate=pl.CostEstimate(
            flops=8 * half * rows * rows, bytes_accessed=8 * half * rows, transcendentals=0
        ),
    )(odd[None], mine, got, mine_sig, got_sig, mine_to, got_to)


def straighten(tiles, by_a, by_b, odd):
    half, tile = by_a.shape
    count = len(tiles)

    def body(odd_ref, *refs):
        tile_refs, a_ref, b_ref, out_ref = refs[:count], *refs[count:]
        even = odd_ref[0] == 0
        for j in range(count):
            value = tile_refs[j][...]
            if j == 0:
                value = value + jnp.where(even, b_ref[...], a_ref[...])
            if j == count - 1:
                value = value + jnp.where(even, a_ref[...], b_ref[...])
            out_ref[:, j * tile : (j + 1) * tile] = value

    return pl.pallas_call(
        body,
        out_shape=jax.ShapeDtypeStruct((half, count * tile), BF16),
        in_specs=[SCALARS] + [WHOLE] * (count + 2),
        out_specs=WHOLE,
        compiler_params=pltpu.CompilerParams(vmem_limit_bytes=VMEM_LIMIT),
        name="straighten",
    )(odd[None], *tiles, by_a, by_b)


def stack_panels(mine, got, core):
    both, half = mine.shape
    columns = both // 2
    width = -(-half // 128) * 128

    def body(core_ref, mine_ref, got_ref, out_ref):
        first = core_ref[0] == 0
        out_ref[...] = jnp.zeros_like(out_ref)
        for j in range(2):
            low = mine_ref[j * columns : (j + 1) * columns]
            high = got_ref[j * columns : (j + 1) * columns]
            q = 2 * j * columns
            out_ref[q : q + columns, :half] = jnp.where(first, low, high)
            out_ref[q + columns : q + 2 * columns, :half] = jnp.where(first, high, low)

    return pl.pallas_call(
        body,
        out_shape=jax.ShapeDtypeStruct((2 * both, width), BF16),
        in_specs=[SCALARS, WHOLE, WHOLE],
        out_specs=WHOLE,
        compiler_params=pltpu.CompilerParams(vmem_limit_bytes=VMEM_LIMIT),
        name="stack_panels",
    )(core[None], mine, got)


def distinct(arrays):
    return list({id(x): x for x in arrays}.values())


def read_window(addends, arrays, refs):
    ref_of = {id(x): ref for x, ref in zip(arrays, refs)}
    total = None
    for x in addends:
        value = ref_of[id(x)][...]
        total = value if total is None else total + value
    return total


def steps_over(half):
    step = half if half <= 512 else 512
    return step, -(-half // step)


def split_sum(pairs, occ):
    _, shares, piece, both = pairs[0][0].shape
    tiles = sum(keep.shape[0] for keep, _ in pairs)

    def body(occ_ref, *refs):
        ins, outs = refs[: 2 * len(pairs)], refs[2 * len(pairs) :]
        for d in range(shares):
            at = 0
            for keep_ref, got_ref in zip(ins[::2], ins[1::2]):
                for q in range(keep_ref.shape[0]):
                    outs[d][at] = keep_ref[q, occ_ref[0] ^ d] + got_ref[q, occ_ref[0] ^ d]
                    at += 1

    shape = jax.ShapeDtypeStruct((tiles, piece, both), F32)
    return pl.pallas_call(
        body,
        out_shape=(shape,) * shares,
        in_specs=[SCALARS] + [WHOLE] * (2 * len(pairs)),
        out_specs=(WHOLE,) * shares,
        compiler_params=pltpu.CompilerParams(vmem_limit_bytes=VMEM_LIMIT),
        name="split_sum",
    )(occ[None], *sum(pairs, ()))


def project(jobs, tile, shares, core):
    both = jobs[0][0].shape[0]
    half, rows = jobs[0][1][0].shape
    piece = tile // shares
    tiles = len(jobs) * rows // tile
    panels = distinct([p for p, _ in jobs])
    arrays = distinct([x for _, window in jobs for x in window])
    count = len(panels)
    step, steps = steps_over(half)
    padded = panels[0].shape[1]

    def body(core_ref, *refs):
        panel_refs, array_refs = refs[:count], refs[count:-4]
        keep_ref, give_ref, total_ref, terms_ref = refs[-4:]
        i = pl.program_id(0)

        @pl.when(i == 0)
        def _():
            total_ref[...] = jnp.zeros_like(total_ref)

        inside = lax.broadcasted_iota(jnp.int32, (step, rows), 0) + i * step < half
        for s, (panel, window) in enumerate(jobs):
            panel_ref = panel_refs[[id(p) for p in panels].index(id(panel))]
            value = read_window(window, arrays, array_refs)
            if steps * step != half:
                value = jnp.where(inside, value, jnp.zeros_like(value))
            part = panel_ref[:, :step]
            total_ref[s] += jnp.dot(part, value, preferred_element_type=F32)

        @pl.when(i == steps - 1)
        def _():
            q = 0
            for s in range(len(jobs)):
                turned = total_ref[s].T
                for j in range(0, rows, tile):
                    terms_ref[q] = turned[j : j + tile].reshape(2, shares // 2, piece, both)
                    keep_ref[q] = terms_ref[q, core_ref[0]]
                    give_ref[q] = terms_ref[q, 1 - core_ref[0]]
                    q += 1

    shape = jax.ShapeDtypeStruct((tiles, shares // 2, piece, both), F32)
    panel_step = step if steps > 1 else padded
    return pl.pallas_call(
        body,
        grid=(steps,),
        out_shape=(shape, shape),
        in_specs=[SCALARS]
        + [pl.BlockSpec((both, panel_step), lambda i: (0, i))] * count
        + [pl.BlockSpec((step, rows), lambda i: (i, 0))] * len(arrays),
        out_specs=(pl.BlockSpec(shape.shape, lambda i: (0, 0, 0, 0)),) * 2,
        scratch_shapes=[
            pltpu.VMEM((len(jobs), both, rows), F32),
            pltpu.VMEM((tiles, 2, shares // 2, piece, both), F32),
        ],
        compiler_params=pltpu.CompilerParams(vmem_limit_bytes=VMEM_LIMIT),
        name="project",
        cost_estimate=pl.CostEstimate(
            flops=2 * both * half * tiles * tile,
            bytes_accessed=2 * half * (both + tiles * tile) + 4 * tiles * tile * both,
            transcendentals=0,
        ),
    )(core[None], *panels, *arrays)


def in_order(parts, occ):
    tiles, _, piece, columns = parts[0].shape

    def body(occ_ref, *refs):
        for d in range(len(parts)):
            refs[-1][:, occ_ref[0] ^ d] = refs[d][:, 0]

    return pl.pallas_call(
        body,
        out_shape=jax.ShapeDtypeStruct((tiles, len(parts), piece, columns), parts[0].dtype),
        in_specs=[SCALARS] + [WHOLE] * len(parts),
        out_specs=WHOLE,
        compiler_params=pltpu.CompilerParams(vmem_limit_bytes=VMEM_LIMIT),
        name="in_order",
    )(occ[None], *parts)


def contract(kernel, got, windows, core):
    tiles, shares, piece, columns = kernel.shape
    half, rows = windows[0][0].shape
    own = columns // 2
    arrays = distinct([x for window in windows for x in window])
    step, steps = steps_over(half)
    per_window = tiles // len(windows)

    def body(core_ref, kernel_ref, got_ref, *refs):
        array_refs = refs[:-4]
        mine_ref, other_ref, order_ref, turned_ref = refs[-4:]
        first = core_ref[0] == 0

        @pl.when(pl.program_id(0) == 0)
        def _():
            order_ref[:, core_ref[0]] = kernel_ref[...].astype(F32)
            order_ref[:, 1 - core_ref[0]] = got_ref[...].astype(F32)
            for s in range(len(windows)):
                part = order_ref[s * per_window : (s + 1) * per_window]
                turned = part.reshape(rows, columns).T
                low, high = turned[:own], turned[own:]
                turned_ref[s, :own] = jnp.where(first, low, high).astype(BF16)
                turned_ref[s, own:] = jnp.where(first, high, low).astype(BF16)

        total = None
        for s, window in enumerate(windows):
            term = lax.dot_general(
                turned_ref[s],
                read_window(window, arrays, array_refs),
                (((1,), (1,)), ((), ())),
                preferred_element_type=F32,
            )
            total = term if total is None else total + term
        mine_ref[...] = total[:own]
        other_ref[...] = total[own:]

    shape = jax.ShapeDtypeStruct((own, half), F32)
    whole = pl.BlockSpec(kernel.shape, lambda i: (0, 0, 0, 0))
    return pl.pallas_call(
        body,
        grid=(steps,),
        out_shape=(shape, shape),
        in_specs=[SCALARS, whole, whole]
        + [pl.BlockSpec((step, rows), lambda i: (i, 0))] * len(arrays),
        out_specs=(pl.BlockSpec((own, step), lambda i: (0, i)),) * 2,
        scratch_shapes=[
            pltpu.VMEM((tiles, 2, shares, piece, columns), F32),
            pltpu.VMEM((len(windows), columns, rows), BF16),
        ],
        compiler_params=pltpu.CompilerParams(vmem_limit_bytes=VMEM_LIMIT),
        name="contract",
        cost_estimate=pl.CostEstimate(
            flops=2 * columns * half * rows * len(windows),
            bytes_accessed=2 * rows * len(windows) * half + 4 * columns * half,
            transcendentals=0,
        ),
    )(core[None], kernel, got, *arrays)


def unwritten(shape):
    def body(out_ref):
        pass

    return pl.pallas_call(
        body,
        out_shape=jax.ShapeDtypeStruct(shape, F32),
        out_specs=pl.BlockSpec(memory_space=pltpu.HBM),
        name="unwritten",
    )()


def finish(core, fits, ours, back, other, scale):
    own, half = ours.shape

    def body(flags_ref, ours_ref, back_ref, other_ref, out_ref, whole_ref, sem):
        @pl.when(flags_ref[1] != 0)
        def _():
            first = flags_ref[0] == 0
            whole_ref[:, :half] = jnp.where(first, ours_ref[...], back_ref[...]) * scale
            whole_ref[:, half:] = jnp.where(first, back_ref[...], ours_ref[...]) * scale
            copy = pltpu.make_async_copy(whole_ref, out_ref, sem)
            copy.start()
            copy.wait()

    return pl.pallas_call(
        body,
        out_shape=jax.ShapeDtypeStruct((own, 2 * half), F32),
        in_specs=[SCALARS, WHOLE, WHOLE, pl.BlockSpec(memory_space=pltpu.HBM)],
        out_specs=pl.BlockSpec(memory_space=pltpu.HBM),
        scratch_shapes=[pltpu.VMEM((own, 2 * half), F32), pltpu.SemaphoreType.DMA],
        input_output_aliases={3: 0},
        compiler_params=pltpu.CompilerParams(vmem_limit_bytes=VMEM_LIMIT),
        name="finish",
    )(jnp.stack((core, fits.astype(jnp.int32))), ours, back, other)


def per_device(orbital_values, occupied, trial, point_weights, batch_sizes, significant):
    rows, cols = orbital_values.shape
    batches = batch_sizes.shape[0]
    slots = rows // batches
    blocks = significant.shape[1]
    columns = occupied.shape[1]
    grid_count = lax.axis_size("grid")
    occ_count = lax.axis_size("occ")
    chips = grid_count // 2
    shares = 2 * occ_count
    half = cols // 2
    total = columns * grid_count
    place = lax.axis_index("grid")
    chip, core = place // 2, place % 2
    occ = lax.axis_index("occ")
    member = core * occ_count + occ

    def flip(x, axis, bit):
        count = lax.axis_size(axis)
        return lax.ppermute(x, axis, [(i, i ^ bit) for i in range(count)])

    def along(pairs):
        return [(2 * a + c, 2 * b + c) for a, b in pairs for c in range(2)]

    def doubled(x, axis, bit, dim):
        got = flip(x, axis, bit)
        mine = (lax.axis_index(axis) & bit) == 0
        return jnp.where(
            mine, jnp.concatenate((x, got), axis=dim), jnp.concatenate((got, x), axis=dim)
        )

    def halves(whole, axis):
        size = whole.shape[axis] // 2
        mine = lax.dynamic_slice_in_dim(whole, core * size, size, axis)
        return mine, lax.dynamic_slice_in_dim(whole, (1 - core) * size, size, axis)

    grid_bits = [1 << b for b in range(grid_count.bit_length() - 1)]
    occ_bits = [1 << b for b in range(occ_count.bit_length() - 1)]

    mine = half_of(orbital_values.T, core)
    got = flip(half_of(orbital_values.T, 1 - core), "grid", 1)
    mine_sig, other_sig = halves(significant.T, 0)
    got_sig = flip(other_sig, "grid", 1)

    told = jnp.concatenate(
        (
            doubled(batch_sizes[None], "grid", 1, 0).astype(F32).reshape(1, -1),
            doubled(point_weights[None], "grid", 1, 0).reshape(1, -1),
        ),
        axis=1,
    )
    if chips <= 4:
        heard = [told]
        for step in range(1, chips):
            around = [(i, (i + 2 * step) % grid_count) for i in range(grid_count)]
            heard.append(lax.ppermute(told, "grid", around))
        heard = jnp.concatenate(heard)
        behind = (chip - lax.iota(jnp.int32, chips)) % chips
        pick = behind[:, None, None] == lax.iota(jnp.int32, chips)[None, :, None]
        told = jnp.sum(jnp.where(pick, heard[None], 0.0), axis=1)
    else:
        for bit in grid_bits[1:]:
            told = doubled(told, "grid", bit, 0)
    sizes = told[:, : 2 * batches].astype(jnp.int32).reshape(-1)
    weights = told[:, 2 * batches :].reshape(-1)

    batch = lax.broadcasted_iota(jnp.int32, (sizes.shape[0], sizes.shape[0]), 0)
    before = lax.broadcasted_iota(jnp.int32, (sizes.shape[0], sizes.shape[0]), 1) < batch
    start = jnp.sum(jnp.where(before, sizes[None, :], 0), axis=1)
    position = lax.broadcasted_iota(jnp.int32, (sizes.shape[0], slots), 1)
    to = jnp.where(position < sizes[:, None], start[:, None] + position, -4 * rows * grid_count)
    to = to.reshape(grid_count, rows)
    first = start.reshape(chips, -1)[:, 0]
    margin = rows // 2 if (rows // 2) % (8 * shares) == 0 else rows
    nominal = rows * lax.iota(jnp.int32, chips)
    fits = jnp.all(jnp.abs(first - nominal) <= margin) & (jnp.sum(sizes) <= rows * chips)

    tile = margin
    piece = tile // shares
    base = rows * chip - margin
    mine_to = lax.dynamic_index_in_dim(to, place, 0, keepdims=False) - base
    got_to = lax.dynamic_index_in_dim(to, place ^ 1, 0, keepdims=False) - base
    odd = chip % 2
    for_b, *own_tiles, for_a = compact(
        mine,
        got,
        jnp.repeat(mine_sig.astype(BF16), slots, axis=1),
        jnp.repeat(got_sig.astype(BF16), slots, axis=1),
        mine_to[:, None],
        got_to[:, None],
        cols // blocks,
        tile,
        odd,
    )

    def sent(x, pairs):
        return lax.ppermute(x, "grid", along(pairs))

    last = chips - 1

    def over(links, t):
        pairs = []
        for a in range(links, last, 2):
            pairs += [(a, a + 1)] if a - t + 1 >= 0 else []
            pairs += [(a + 1, a)] if a + t <= last else []
        return pairs

    own = straighten(own_tiles, sent(for_a, over(0, 1)), sent(for_b, over(1, 1)), odd)

    mine_panel, other_panel = halves(jnp.concatenate((occupied, trial), axis=1).T, 1)
    panels = stack_panels(mine_panel, flip(other_panel, "grid", 1), core)

    per_window = rows // tile
    window_iota = lax.iota(jnp.int32, chips)
    ends = [(0, 1), (last, last - 1)]
    homes = [(b, a) for a, b in ends]
    side = 1 - 2 * odd

    def valid(at):
        return jnp.where((at >= 0) & (at <= last), at, -1)

    stages = [[([own], chip)]]
    by_a = by_b = own
    far_panels = None
    for t in range(1, last):
        by_a, by_b = sent(by_b, over(0, t)), sent(by_a, over(1, t))
        if t == 1:
            far_panels = sent(panels, ends)
        a_at, b_at = valid(chip + side * t), valid(chip - side * t)
        if 2 * t > last:
            stages.append([([by_a, by_b], jnp.maximum(a_at, b_at))])
        else:
            stages.append([([by_a], a_at), ([by_b], b_at)])

    direct = occ_count <= 4
    points = per_window * piece

    def halved(jobs):
        keep, give = project(jobs, tile, shares, core)
        return keep, flip(give, "grid", 1)

    def summed(pairs):
        if direct:
            parts = split_sum(pairs, occ)
            value = parts[0]
            for d in range(1, occ_count):
                value = value + flip(parts[d], "occ", d)
        else:
            value = jnp.concatenate([keep + got for keep, got in pairs])
            for bit in reversed(occ_bits):
                upper = (occ & bit) != 0
                low_part, high_part = value[:, :bit], value[:, bit:]
                got = flip(jnp.where(upper, low_part, high_part), "occ", bit)
                value = jnp.where(upper, high_part, low_part) + got
        return value.reshape(-1, points, 4 * columns)

    def shared_density(value, at):
        product = jnp.sum(value[:, :, : 2 * columns] * value[:, :, 2 * columns :], axis=2)
        here = (at[:, None] == window_iota[None, :])[:, :, None]
        return jnp.sum(jnp.where(here, product[:, None], 0.0), axis=0)

    early_jobs, late_jobs = sum(stages[1:-1], []), stages[-1]
    early_at = jnp.stack([at for _, at in early_jobs])
    late_at = late_jobs[0][1][None]
    early_jobs = stages[0] + early_jobs
    early_at = jnp.concatenate((chip[None], early_at))

    early_pair = halved([(panels, w) for w, _ in early_jobs])

    at = (
        (window_iota * rows)[:, None, None]
        + (lax.iota(jnp.int32, per_window) * tile)[None, :, None]
        + member * piece
        + lax.iota(jnp.int32, piece)[None, None, :]
    ).reshape(-1, 1)
    weight = jnp.sum(jnp.where(to.reshape(1, -1) == at, weights[None, :], 0.0), axis=1)
    weight = weight.reshape(chips, per_window * piece)
    outer = jnp.where(chip == 0, last, jnp.where(chip == last, 0, early_at[2]))
    places = jnp.concatenate((early_at[:2], outer[None], early_at[3:], late_at))
    here = (places[:, None] == window_iota[None, :])[:, :, None]
    weight_here = jnp.sum(jnp.where(here, weight[None], 0.0), axis=1)[:, :, None]

    late, by_a, early_pair, far_panels, weight_here = lax.optimization_barrier(
        (by_b, by_a, early_pair, far_panels, weight_here)
    )
    late = sent(late, homes)
    late_window = [by_a, by_b]
    late_jobs = [(panels, late_window), (far_panels, [by_b])]

    def kernel_of_all():
        value = summed([early_pair, halved(late_jobs)])
        density = shared_density(value, jnp.concatenate((early_at, late_at, late_at)))
        value, far_value = value[:-1], value[-1:]
        packed = jnp.concatenate(
            (far_value[0], jnp.pad(density, ((0, 0), (0, 4 * columns - points)))), axis=0
        )
        packed = flip(packed, "grid", 2)
        home_value, neighbour = packed[None, :points], packed[points:, :points]
        if chips <= 4:
            others = [flip(density, "grid", 2 * d) for d in range(2, chips)]
            density = density + neighbour + sum(others[1:], others[0])
        else:
            density = density + neighbour
            for bit in grid_bits[2:]:
                density = density + flip(density, "grid", bit)
        density = density * (1.0 / math.sqrt(total))

        values = jnp.concatenate((value[:2], value[2:3] + home_value, value[3:]))
        density_here = jnp.sum(jnp.where(here, density[None], 0.0), axis=1)[:, :, None]
        orbitals, response = values[:, :, : 2 * columns], values[:, :, 2 * columns :]
        kernel = (weight_here * (density_here * orbitals + response)).astype(BF16)
        kernel = kernel.reshape(-1, 1, piece, 2 * columns)
        if direct:
            parts = [kernel] + [flip(kernel, "occ", d) for d in range(1, occ_count)]
            kernel = in_order(parts, occ)
        else:
            for bit in occ_bits:
                kernel = doubled(kernel, "occ", bit, 1)
        return kernel, flip(kernel, "grid", 1)

    no_kernel = jnp.zeros((places.shape[0] * per_window, occ_count, piece, 2 * columns), BF16)
    kernel, got_kernel = lax.cond(fits, kernel_of_all, lambda: (no_kernel, no_kernel))
    early_windows = [w for w, _ in early_jobs]
    early_windows[2] = early_windows[2] + [late]
    windows = early_windows + [late_window]
    ours, theirs = contract(kernel, got_kernel, windows, core)
    back = flip(theirs, "grid", 1)
    scale = 1.0 / math.sqrt(rows * grid_count)
    other = lax.cond(
        fits,
        lambda *given: unwritten((columns, cols)),
        lambda *given: any_sizes(*given) * scale,
        orbital_values,
        occupied,
        trial,
        point_weights,
        batch_sizes,
        significant,
    )
    return finish(core, fits, ours, back, other, scale).T


def solution(mesh):
    placed = (
        P("grid", "occ"),
        P("occ", "grid"),
        P("occ", "grid"),
        P("grid"),
        P("grid"),
        P("grid", "occ"),
    )
    return jax.shard_map(
        per_device, mesh=mesh, in_specs=placed, out_specs=P("occ", "grid"), check_vma=False
    )
```

profile of v0, /device:TPU:0, one launch (start us, length us, event | category | flops | bytes accessed | tf_op | source)
XLA Modules:
  0.0 131.6 jit_solution(11406257857682206548)
XLA Ops:
  0.0 1.3 half_of.3
  2.5 1.6 %collective-permute-done.14 = s32[1,8]{1,0:T(1,128)S(1)} collective-permute-done((s32[1,8]{1,0:T(1,128)S(1)}, s32[1,8]{1,0:T(1,128)S(1)}, u32[]{:S(2)}, u32[]{:S(2)}) %collective-permute-start.14) | collective-permute-done | bytes 64 | tf_op jit(solution)/shard_map/ppermute | solution.py:419
  4.3 2.9 %collective-permute-start.16 = (f32[1,528]{1,0:T(1,128)S(1)}, f32[1,528]{1,0:T(1,128)S(1)}, u32[]{:S(2)}, u32[]{:S(2)}) collective-permute-start(f32[1,528]{1,0:T(1,128)S(1)} %pad_maximum_fusion.3), channel_id=1, source_target_pairs={{0,8},{4,12},{8,16},{12,20},{16,24},{20,28},{24,0},{28,4},{1,9},{5... | collective-permute-start | bytes 6344 | tf_op jit(solution)/shard_map/ppermute | solution.py:455
  7.2 2.6 %collective-permute-start.17 = (f32[1,528]{1,0:T(1,128)S(1)}, f32[1,528]{1,0:T(1,128)S(1)}, u32[]{:S(2)}, u32[]{:S(2)}) collective-permute-start(f32[1,528]{1,0:T(1,128)S(1)} %pad_maximum_fusion.3), channel_id=1, source_target_pairs={{0,16},{4,20},{8,24},{12,28},{16,0},{20,4},{24,8},{28,12},{1,17},{... | collective-permute-start | bytes 6344 | tf_op jit(solution)/shard_map/ppermute | solution.py:455
  9.8 1.3 %collective-permute-start.18 = (f32[1,528]{1,0:T(1,128)S(1)}, f32[1,528]{1,0:T(1,128)S(1)}, u32[]{:S(2)}, u32[]{:S(2)}) collective-permute-start(f32[1,528]{1,0:T(1,128)S(1)} %pad_maximum_fusion.3), channel_id=1, source_target_pairs={{0,24},{4,28},{8,0},{12,4},{16,8},{20,12},{24,16},{28,20},{1,25},{... | collective-permute-start | bytes 6344 | tf_op jit(solution)/shard_map/ppermute | solution.py:455
  11.2 1.2 half_of.2.mine_ref
  14.6 1.8 %compact.1 = (bf16[2000,128]{1,0:T(8,128)(2,1)S(1)}, bf16[2000,128]{1,0:T(8,128)(2,1)S(1)}, bf16[2000,128]{1,0:T(8,128)(2,1)S(1)}, bf16[2000,128]{1,0:T(8,128)(2,1)S(1)}) custom-call(s32[1]{0:T(128)} %bitcast.16.odd_ref, bf16[2000,256]{1,0:T(8,128)(2,1)S(1)} %half_of.2.mine_ref, bf16[2000,256]{1,0:T(8,128)(2,1)S(1)} %collective-permute-done.19.got_ref, ...), custom_call_target="tpu_custom_call" | custom-call | flops 1048576000 | bytes 4096000 | tf_op jit(solution)/shard_map/compact/pallas_call | solution.py:118
  17.6 0.8 constant_dynamic-update-slice_fusion.1
  18.4 10.7 %collective-permute-done.21.refs_2_ = bf16[2000,128]{1,0:T(8,128)(2,1)S(1)} collective-permute-done((bf16[2000,128]{1,0:T(8,128)(2,1)S(1)}, bf16[2000,128]{1,0:T(8,128)(2,1)S(1)}, u32[]{:S(2)}, u32[]{:S(2)}) %collective-permute-start.21) | collective-permute-done | bytes 512032 | tf_op jit(solution)/shard_map/ppermute | solution.py:496
  29.4 3.7 %collective-permute-start.23 = (bf16[2000,256]{1,0:T(8,128)(2,1)S(1)}, bf16[2000,256]{1,0:T(8,128)(2,1)S(1)}, u32[]{:S(2)}, u32[]{:S(2)}) collective-permute-start(bf16[2000,256]{1,0:T(8,128)(2,1)S(1)} %straighten.1.refs_1_.refs_0_), channel_id=1, source_target_pairs={{0,8},{4,12},{8,0},{12,4},{16,24},{20,28},{24,16},{28,20},{1,9},{5... | collective-permute-start | bytes 3072008 | tf_op jit(solution)/shard_map/ppermute | solution.py:496
  33.1 0.7 collective-permute-start.25
  33.9 0.8 constant_dynamic-update-slice_fusion
  34.7 2.6 %dynamic-slice_bitcast_fusion = (bf16[128,2000]{1,0:T(8,128)(2,1)}, bf16[128,2000]{1,0:T(8,128)(2,1)}) fusion(bf16[4000,128]{0,1:T(8,128)(2,1)} %constant_dynamic-update-slice_fusion, s32[]{:T(128)S(6)} %select_n.208, s32[]{:T(128)S(6)} %select_n.207), kind=kLoop, calls=%fused_computation.35 | loop fusion | bytes 2048008 | tf_op jit(solution)/shard_map/dynamic_slice | solution.py:434
  37.5 2.1 %collective-permute-done.27.got_ref = bf16[128,2000]{1,0:T(8,128)(2,1)} collective-permute-done((bf16[128,2000]{1,0:T(8,128)(2,1)}, bf16[128,2000]{1,0:T(8,128)(2,1)}, u32[]{:S(2)}, u32[]{:S(2)}) %collective-permute-start.27) | collective-permute-done | bytes 512032 | tf_op jit(solution)/shard_map/ppermute | solution.py:419
  39.6 1.0 copy-done
  40.6 2.1 %stack_panels.1.refs_0_ = bf16[256,2048]{1,0:T(8,128)(2,1)} custom-call(s32[1]{0:T(128)} %bitcast.12.which_ref.core_ref, bf16[128,2000]{1,0:T(8,128)(2,1)S(1)} %copy-done, bf16[128,2000]{1,0:T(8,128)(2,1)} %collective-permute-done.27.got_ref), custom_call_target="tpu_custom_call" | custom-call | tf_op jit(solution)/shard_map/stack_panels/pallas_call | solution.py:171
  42.7 5.8 %collective-permute-start.29 = (bf16[256,2048]{1,0:T(8,128)(2,1)}, bf16[256,2048]{1,0:T(8,128)(2,1)}, u32[]{:S(2)}, u32[]{:S(2)}) collective-permute-start(bf16[256,2048]{1,0:T(8,128)(2,1)} %stack_panels.1.refs_0_), channel_id=1, source_target_pairs={{0,8},{4,12},{24,16},{28,20},{1,9},{5,13},{25,17},{29,21},{2,10},{... | collective-permute-start | bytes 3145736 | tf_op jit(solution)/shard_map/ppermute | solution.py:496
  48.5 7.7 %collective-permute-done.23.refs_2_.refs_1_ = bf16[2000,256]{1,0:T(8,128)(2,1)S(1)} collective-permute-done((bf16[2000,256]{1,0:T(8,128)(2,1)S(1)}, bf16[2000,256]{1,0:T(8,128)(2,1)S(1)}, u32[]{:S(2)}, u32[]{:S(2)}) %collective-permute-start.23) | collective-permute-done | bytes 1024032 | tf_op jit(solution)/shard_map/ppermute | solution.py:496
  56.2 1.6 %collective-permute-start.24 = (bf16[2000,256]{1,0:T(8,128)(2,1)S(1)}, bf16[2000,256]{1,0:T(8,128)(2,1)}, u32[]{:S(2)}, u32[]{:S(2)}) collective-permute-start(bf16[2000,256]{1,0:T(8,128)(2,1)S(1)} %collective-permute-done.23.refs_2_.refs_1_), channel_id=1, source_target_pairs={{8,16},{12,20},{16,8},{20,12},{9,17},{13,21},{17,9},{21,13},{10,18... | collective-permute-start | bytes 3072008 | tf_op jit(solution)/shard_map/ppermute | solution.py:496
  57.9 1.3 collective-permute-start.26
  59.5 4.3 %project.3 = (f32[6,4,16,256]{3,2,1,0:T(8,128)}, f32[6,4,16,256]{3,2,1,0:T(8,128)S(1)}) custom-call(s32[1]{0:T(128)} %bitcast.12.which_ref.core_ref, bf16[256,2048]{1,0:T(8,128)(2,1)} %stack_panels.1.refs_0_, bf16[2000,256]{1,0:T(8,128)(2,1)S(1)} %straighten.1.refs_1_.refs_0_, bf16[2000,256]{1,0:T(8,128)(2,1)S(1)} %collective-permute-done.23.refs_2_.refs_1_, ...), custom_call_target="tpu_custom_call" | custom-call | flops 786432000 | bytes 4882432 | tf_op jit(solution)/shard_map/project/pallas_call | solution.py:265
  64.3 11.0 %collective-permute-done.29 = bf16[256,2048]{1,0:T(8,128)(2,1)} collective-permute-done((bf16[256,2048]{1,0:T(8,128)(2,1)}, bf16[256,2048]{1,0:T(8,128)(2,1)}, u32[]{:S(2)}, u32[]{:S(2)}) %collective-permute-start.29) | collective-permute-done | bytes 1048608 | tf_op jit(solution)/shard_map/ppermute | solution.py:496
  75.4 5.0 %collective-permute-done.26.refs_4_ = bf16[2000,256]{1,0:T(8,128)(2,1)} collective-permute-done((bf16[2000,256]{1,0:T(8,128)(2,1)S(1)}, bf16[2000,256]{1,0:T(8,128)(2,1)}, u32[]{:S(2)}, u32[]{:S(2)}) %collective-permute-start.26) | collective-permute-done | bytes 1024032 | tf_op jit(solution)/shard_map/ppermute | solution.py:496
  80.3 1.3 collective-permute-start.30
  81.8 0.7 fusion.18
  83.3 0.7 compare_reduce_fusion
  84.7 37.3 %conditional.2 = (bf16[8,4,16,128]{3,2,1,0:T(8,128)(2,1)}, bf16[8,4,16,128]{3,2,1,0:T(8,128)(2,1)}) conditional(s32[]{:T(128)} %convert_element_type.46, () %tuple.68, (s32[]{:T(128)}, f32[4,32,1]{1,0,2:T(4,128)S(1)}, s32[4]{0:T(128)S(1)}, s32[4,4,1]{1,0,2:T(4,128)S(1)}, s32[3]{0:T(128)S(1)}, /*index=5*/s32[1]{0:T(128)}, s32[4]{0:T(128)S(1)}, ...), branch_computations={%region_6.7_spmd, %region_7.11_spmd} | conditional | flops 524621184 | bytes 11165124 | solution.py:621
  84.7 3.8 %project.2 = (f32[4,4,16,256]{3,2,1,0:T(8,128)S(1)}, f32[4,4,16,256]{3,2,1,0:T(8,128)S(1)}) custom-call(s32[1]{0:T(128)} %bitcast.3.core_ref, bf16[256,2048]{1,0:T(8,128)(2,1)} %get-tuple-element.328.refs_0_, bf16[256,2048]{1,0:T(8,128)(2,1)} %get-tuple-element.329.refs_1_, bf16[2000,256]{1,0:T(8,128)(2,1)} %get-tuple-element.330.refs_2_, ...), custom_call_target="tpu_custom_call" | custom-call | flops 524288000 | bytes 3596288 | tf_op jit(solution)/shard_map/cond/branch_1_fun/project/pallas_call | solution.py:265
  88.6 1.4 %collective-permute-done.refs_3_ = f32[4,4,16,256]{3,2,1,0:T(8,128)S(1)} collective-permute-done((f32[4,4,16,256]{3,2,1,0:T(8,128)S(1)}, f32[4,4,16,256]{3,2,1,0:T(8,128)S(1)}, u32[]{:S(2)}, u32[]{:S(2)}) %collective-permute-start) | collective-permute-done | bytes 262176 | tf_op jit(solution)/shard_map/cond/branch_1_fun/ppermute | solution.py:419
  90.1 1.1 split_sum.1
  91.2 1.6 %collective-permute-start.1 = (f32[10,16,256]{2,1,0:T(8,128)S(1)}, f32[10,16,256]{2,1,0:T(8,128)S(1)}, u32[]{:S(2)}, u32[]{:S(2)}) collective-permute-start(f32[10,16,256]{2,1,0:T(8,128)S(1)} %get-tuple-element.335), channel_id=1, source_target_pairs={{0,1},{1,0},{2,3},{3,2},{4,5},{5,4},{6,7},{7,6},{8,9},{9,8},{10,11... | collective-permute-start | bytes 491528 | tf_op jit(solution)/shard_map/cond/branch_1_fun/ppermute | solution.py:419
  92.7 1.5 %collective-permute-start.2 = (f32[10,16,256]{2,1,0:T(8,128)S(1)}, f32[10,16,256]{2,1,0:T(8,128)S(1)}, u32[]{:S(2)}, u32[]{:S(2)}) collective-permute-start(f32[10,16,256]{2,1,0:T(8,128)S(1)} %get-tuple-element.336), channel_id=1, source_target_pairs={{0,2},{1,3},{2,0},{3,1},{4,6},{5,7},{6,4},{7,5},{8,10},{9,11},{10,... | collective-permute-start | bytes 491528 | tf_op jit(solution)/shard_map/cond/branch_1_fun/ppermute | solution.py:419
  94.8 3.5 %collective-permute-done.1 = f32[10,16,256]{2,1,0:T(8,128)S(1)} collective-permute-done((f32[10,16,256]{2,1,0:T(8,128)S(1)}, f32[10,16,256]{2,1,0:T(8,128)S(1)}, u32[]{:S(2)}, u32[]{:S(2)}) %collective-permute-start.1) | collective-permute-done | bytes 163872 | tf_op jit(solution)/shard_map/cond/branch_1_fun/ppermute | solution.py:419
  98.3 3.9 %collective-permute-done.2 = f32[10,16,256]{2,1,0:T(8,128)S(1)} collective-permute-done((f32[10,16,256]{2,1,0:T(8,128)S(1)}, f32[10,16,256]{2,1,0:T(8,128)S(1)}, u32[]{:S(2)}, u32[]{:S(2)}) %collective-permute-start.2) | collective-permute-done | bytes 163872 | tf_op jit(solution)/shard_map/cond/branch_1_fun/ppermute | solution.py:419
  102.5 4.4 %collective-permute-start.5 = (f32[4,32]{1,0:T(4,128)S(1)}, f32[4,32]{1,0:T(4,128)S(1)}, u32[]{:S(2)}, u32[]{:S(2)}) collective-permute-start(f32[4,32]{1,0:T(4,128)S(1)} %select_reduce_fusion), channel_id=1, source_target_pairs={{0,16},{4,20},{8,24},{12,28},{16,0},{20,4},{24,8},{28,12},{1,17},{... | collective-permute-start | bytes 1544 | tf_op jit(solution)/shard_map/cond/branch_1_fun/ppermute | solution.py:419
  106.8 1.7 %collective-permute-start.6 = (f32[4,32]{1,0:T(4,128)S(1)}, f32[4,32]{1,0:T(4,128)S(1)}, u32[]{:S(2)}, u32[]{:S(2)}) collective-permute-start(f32[4,32]{1,0:T(4,128)S(1)} %select_reduce_fusion), channel_id=1, source_target_pairs={{0,24},{4,28},{8,16},{12,20},{16,8},{20,12},{24,0},{28,4},{1,25},{... | collective-permute-start | bytes 1544 | tf_op jit(solution)/shard_map/cond/branch_1_fun/ppermute | solution.py:419
  108.6 3.7 %collective-permute-done.6 = f32[4,32]{1,0:T(4,128)S(1)} collective-permute-done((f32[4,32]{1,0:T(4,128)S(1)}, f32[4,32]{1,0:T(4,128)S(1)}, u32[]{:S(2)}, u32[]{:S(2)}) %collective-permute-start.6) | collective-permute-done | bytes 544 | tf_op jit(solution)/shard_map/cond/branch_1_fun/ppermute | solution.py:419
  112.7 1.3 collective-permute-start.7
  114.0 0.8 collective-permute-start.8
  114.8 1.4 %collective-permute-start.9 = (bf16[8,1,16,128]{3,2,1,0:T(8,128)(2,1)S(1)}, bf16[8,1,16,128]{3,2,1,0:T(8,128)(2,1)S(1)}, u32[]{:S(2)}, u32[]{:S(2)}) collective-permute-start(bf16[8,1,16,128]{3,2,1,0:T(8,128)(2,1)S(1)} %bitcast.71), channel_id=1, source_target_pairs={{0,3},{1,2},{2,1},{3,0},{4,7},{5,6},{6,5},{7,4},{8,11},{9,10},{10,... | collective-permute-start | bytes 98312 | tf_op jit(solution)/shard_map/cond/branch_1_fun/ppermute | solution.py:419
  116.7 1.2 collective-permute-done.8.refs_2_
  117.9 1.7 %collective-permute-done.9.refs_3_ = bf16[8,1,16,128]{3,2,1,0:T(8,128)(2,1)S(1)} collective-permute-done((bf16[8,1,16,128]{3,2,1,0:T(8,128)(2,1)S(1)}, bf16[8,1,16,128]{3,2,1,0:T(8,128)(2,1)S(1)}, u32[]{:S(2)}, u32[]{:S(2)}) %collective-permute-start.9) | collective-permute-done | bytes 32800 | tf_op jit(solution)/shard_map/cond/branch_1_fun/ppermute | solution.py:419
  120.3 1.7 %collective-permute-done.10 = bf16[8,4,16,128]{3,2,1,0:T(8,128)(2,1)} collective-permute-done((bf16[8,4,16,128]{3,2,1,0:T(8,128)(2,1)}, bf16[8,4,16,128]{3,2,1,0:T(8,128)(2,1)}, u32[]{:S(2)}, u32[]{:S(2)}) %collective-permute-start.10) | collective-permute-done | bytes 131104 | tf_op jit(solution)/shard_map/cond/branch_1_fun/ppermute | solution.py:419
  122.0 4.8 %contract.1 = (f32[64,2000]{1,0:T(8,128)S(1)}, f32[64,2000]{1,0:T(8,128)}) custom-call(s32[1]{0:T(128)} %bitcast.12.which_ref.core_ref, bf16[8,4,16,128]{3,2,1,0:T(8,128)(2,1)} %get-tuple-element.390.kernel_ref, bf16[8,4,16,128]{3,2,1,0:T(8,128)(2,1)} %get-tuple-element.391.got_ref, bf16[2000,256]{1,0:T(8,128)(2,1)S(1)} %straighten.1.refs_1_.refs_0_, ...), custom_call_target="tpu_custom_call" | custom-call | flops 524288000 | bytes 5120000 | tf_op jit(solution)/shard_map/contract/pallas_call | solution.py:342
  126.8 0.8 copy-done.1
  127.8 1.9 %collective-permute-done.31.back_ref = f32[64,2000]{1,0:T(8,128)S(1)} collective-permute-done((f32[64,2000]{1,0:T(8,128)}, f32[64,2000]{1,0:T(8,128)S(1)}, u32[]{:S(2)}, u32[]{:S(2)}) %collective-permute-start.31) | collective-permute-done | bytes 512032 | tf_op jit(solution)/shard_map/ppermute | solution.py:419
  129.7 0.9 finish.1
  130.6 1.0 copy-done.6
  (115 shorter events, 9.2 us)
Async XLA Ops:
  0.0 1.8 %copy-start.10 = (s32[8,32]{1,0:T(8,128)S(1)}, s32[8,32]{1,0:T(8,128)}, u32[]{:S(2)}) copy-start(s32[8,32]{1,0:T(8,128)} %param.21) | copy-start | bytes 3076
  0.0 1.9 %copy-start.11 = (f32[256]{0:T(256)S(1)}, f32[256]{0:T(256)}, u32[]{:S(2)}) copy-start(f32[256]{0:T(256)} %param.19) | copy-start | bytes 3076
  0.0 2.4 %copy-start.12 = (s32[8]{0:T(128)S(1)}, s32[8]{0:T(128)}, u32[]{:S(2)}) copy-start(s32[8]{0:T(128)} %param.20) | copy-start | bytes 100
  1.3 13.3 %collective-permute-start.19 = (bf16[2000,256]{1,0:T(8,128)(2,1)S(1)}, bf16[2000,256]{1,0:T(8,128)(2,1)S(1)}, u32[]{:S(2)}, u32[]{:S(2)}) collective-permute-start(bf16[2000,256]{1,0:T(8,128)(2,1)S(1)} %half_of.3), channel_id=1, source_target_pairs={{0,4},{4,0},{8,12},{12,8},{16,20},{20,16},{24,28},{28,24},{1,5},{5... | collective-permute-start | bytes 3072008 | tf_op jit(solution)/shard_map/ppermute | solution.py:419
  1.9 10.9 %collective-permute-start.20 = (s32[16,8]{0,1:T(8,128)S(1)}, s32[16,8]{0,1:T(8,128)S(1)}, u32[]{:S(2)}, u32[]{:S(2)}) collective-permute-start(s32[16,8]{0,1:T(8,128)S(1)} %get-tuple-element.466), channel_id=1, source_target_pairs={{0,4},{4,0},{8,12},{12,8},{16,20},{20,16},{24,28},{28,24},{1,5},{5... | collective-permute-start | bytes 1544 | tf_op jit(solution)/shard_map/ppermute | solution.py:419
  1.9 2.2 %collective-permute-start.15 = (f32[1,256]{1,0:T(1,128)S(1)}, f32[1,256]{1,0:T(1,128)S(1)}, u32[]{:S(2)}, u32[]{:S(2)}) collective-permute-start(f32[1,256]{1,0:T(1,128)S(1)} %bitcast.84), channel_id=1, source_target_pairs={{0,4},{4,0},{8,12},{12,8},{16,20},{20,16},{24,28},{28,24},{1,5},{5... | collective-permute-start | bytes 3080 | tf_op jit(solution)/shard_map/ppermute | solution.py:419
  2.4 1.7 %collective-permute-start.14 = (s32[1,8]{1,0:T(1,128)S(1)}, s32[1,8]{1,0:T(1,128)S(1)}, u32[]{:S(2)}, u32[]{:S(2)}) collective-permute-start(s32[1,8]{1,0:T(1,128)S(1)} %bitcast.86), channel_id=1, source_target_pairs={{0,4},{4,0},{8,12},{12,8},{16,20},{20,16},{24,28},{28,24},{1,5},{5... | collective-permute-start | bytes 104 | tf_op jit(solution)/shard_map/ppermute | solution.py:419
  4.3 8.8 %collective-permute-start.16 = (f32[1,528]{1,0:T(1,128)S(1)}, f32[1,528]{1,0:T(1,128)S(1)}, u32[]{:S(2)}, u32[]{:S(2)}) collective-permute-start(f32[1,528]{1,0:T(1,128)S(1)} %pad_maximum_fusion.3), channel_id=1, source_target_pairs={{0,8},{4,12},{8,16},{12,20},{16,24},{20,28},{24,0},{28,4},{1,9},{5... | collective-permute-start | bytes 6344 | tf_op jit(solution)/shard_map/ppermute | solution.py:455
  7.2 5.9 %collective-permute-start.17 = (f32[1,528]{1,0:T(1,128)S(1)}, f32[1,528]{1,0:T(1,128)S(1)}, u32[]{:S(2)}, u32[]{:S(2)}) collective-permute-start(f32[1,528]{1,0:T(1,128)S(1)} %pad_maximum_fusion.3), channel_id=1, source_target_pairs={{0,16},{4,20},{8,24},{12,28},{16,0},{20,4},{24,8},{28,12},{1,17},{... | collective-permute-start | bytes 6344 | tf_op jit(solution)/shard_map/ppermute | solution.py:455
  9.8 3.6 %collective-permute-start.18 = (f32[1,528]{1,0:T(1,128)S(1)}, f32[1,528]{1,0:T(1,128)S(1)}, u32[]{:S(2)}, u32[]{:S(2)}) collective-permute-start(f32[1,528]{1,0:T(1,128)S(1)} %pad_maximum_fusion.3), channel_id=1, source_target_pairs={{0,24},{4,28},{8,0},{12,4},{16,8},{20,12},{24,16},{28,20},{1,25},{... | collective-permute-start | bytes 6344 | tf_op jit(solution)/shard_map/ppermute | solution.py:455
  14.6 3.0 %copy-start.7 = (bf16[4000,64]{0,1:T(8,128)(2,1)S(1)}, bf16[4000,64]{0,1:T(8,128)(2,1)}, u32[]{:S(2)}) copy-start(bf16[4000,64]{0,1:T(8,128)(2,1)} %param.17) | copy-start | bytes 1536004
  16.4 17.5 %copy-start.8 = (bf16[4000,64]{0,1:T(8,128)(2,1)S(1)}, bf16[4000,64]{0,1:T(8,128)(2,1)}, u32[]{:S(2)}) copy-start(bf16[4000,64]{0,1:T(8,128)(2,1)} %param.18) | copy-start | bytes 1536004
  16.4 12.7 %collective-permute-start.21 = (bf16[2000,128]{1,0:T(8,128)(2,1)S(1)}, bf16[2000,128]{1,0:T(8,128)(2,1)S(1)}, u32[]{:S(2)}, u32[]{:S(2)}) collective-permute-start(bf16[2000,128]{1,0:T(8,128)(2,1)S(1)} %get-tuple-element.381), channel_id=1, source_target_pairs={{0,8},{4,12},{8,0},{12,4},{16,24},{20,28},{24,16},{28,20},{1,9},{5... | collective-permute-start | bytes 1536008 | tf_op jit(solution)/shard_map/ppermute | solution.py:496
  16.9 12.2 %collective-permute-start.22 = (bf16[2000,128]{1,0:T(8,128)(2,1)S(1)}, bf16[2000,128]{1,0:T(8,128)(2,1)S(1)}, u32[]{:S(2)}, u32[]{:S(2)}) collective-permute-start(bf16[2000,128]{1,0:T(8,128)(2,1)S(1)} %get-tuple-element.382), channel_id=1, source_target_pairs={{8,16},{12,20},{16,8},{20,12},{9,17},{13,21},{17,9},{21,13},{10,18... | collective-permute-start | bytes 1536008 | tf_op jit(solution)/shard_map/ppermute | solution.py:496
  29.4 26.8 %collective-permute-start.23 = (bf16[2000,256]{1,0:T(8,128)(2,1)S(1)}, bf16[2000,256]{1,0:T(8,128)(2,1)S(1)}, u32[]{:S(2)}, u32[]{:S(2)}) collective-permute-start(bf16[2000,256]{1,0:T(8,128)(2,1)S(1)} %straighten.1.refs_1_.refs_0_), channel_id=1, source_target_pairs={{0,8},{4,12},{8,0},{12,4},{16,24},{20,28},{24,16},{28,20},{1,9},{5... | collective-permute-start | bytes 3072008 | tf_op jit(solution)/shard_map/ppermute | solution.py:496
  33.1 24.7 %collective-permute-start.25 = (bf16[2000,256]{1,0:T(8,128)(2,1)S(1)}, bf16[2000,256]{1,0:T(8,128)(2,1)S(1)}, u32[]{:S(2)}, u32[]{:S(2)}) collective-permute-start(bf16[2000,256]{1,0:T(8,128)(2,1)S(1)} %straighten.1.refs_1_.refs_0_), channel_id=1, source_target_pairs={{8,16},{12,20},{16,8},{20,12},{9,17},{13,21},{17,9},{21,13},{10,18... | collective-permute-start | bytes 3072008 | tf_op jit(solution)/shard_map/ppermute | solution.py:496
  37.3 2.3 %collective-permute-start.27 = (bf16[128,2000]{1,0:T(8,128)(2,1)}, bf16[128,2000]{1,0:T(8,128)(2,1)}, u32[]{:S(2)}, u32[]{:S(2)}) collective-permute-start(bf16[128,2000]{1,0:T(8,128)(2,1)} %get-tuple-element.462), channel_id=1, source_target_pairs={{0,4},{4,0},{8,12},{12,8},{16,20},{20,16},{24,28},{28,24},{1,5},{5... | collective-permute-start | bytes 1536008 | tf_op jit(solution)/shard_map/ppermute | solution.py:419
  39.6 1.0 copy-start
  42.7 32.6 %collective-permute-start.29 = (bf16[256,2048]{1,0:T(8,128)(2,1)}, bf16[256,2048]{1,0:T(8,128)(2,1)}, u32[]{:S(2)}, u32[]{:S(2)}) collective-permute-start(bf16[256,2048]{1,0:T(8,128)(2,1)} %stack_panels.1.refs_0_), channel_id=1, source_target_pairs={{0,8},{4,12},{24,16},{28,20},{1,9},{5,13},{25,17},{29,21},{2,10},{... | collective-permute-start | bytes 3145736 | tf_op jit(solution)/shard_map/ppermute | solution.py:496
  56.2 19.1 %collective-permute-start.24 = (bf16[2000,256]{1,0:T(8,128)(2,1)S(1)}, bf16[2000,256]{1,0:T(8,128)(2,1)}, u32[]{:S(2)}, u32[]{:S(2)}) collective-permute-start(bf16[2000,256]{1,0:T(8,128)(2,1)S(1)} %collective-permute-done.23.refs_2_.refs_1_), channel_id=1, source_target_pairs={{8,16},{12,20},{16,8},{20,12},{9,17},{13,21},{17,9},{21,13},{10,18... | collective-permute-start | bytes 3072008 | tf_op jit(solution)/shard_map/ppermute | solution.py:496
  57.9 22.5 %collective-permute-start.26 = (bf16[2000,256]{1,0:T(8,128)(2,1)S(1)}, bf16[2000,256]{1,0:T(8,128)(2,1)}, u32[]{:S(2)}, u32[]{:S(2)}) collective-permute-start(bf16[2000,256]{1,0:T(8,128)(2,1)S(1)} %collective-permute-done.25.refs_3_.refs_2_), channel_id=1, source_target_pairs={{8,0},{12,4},{16,24},{20,28},{9,1},{13,5},{17,25},{21,29},{10,2},{... | collective-permute-start | bytes 3072008 | tf_op jit(solution)/shard_map/ppermute | solution.py:496
  63.8 11.5 %collective-permute-start.28 = (f32[6,4,16,256]{3,2,1,0:T(8,128)S(1)}, f32[6,4,16,256]{3,2,1,0:T(8,128)}, u32[]{:S(2)}, u32[]{:S(2)}) collective-permute-start(f32[6,4,16,256]{3,2,1,0:T(8,128)S(1)} %get-tuple-element.384), channel_id=1, source_target_pairs={{0,4},{4,0},{8,12},{12,8},{16,20},{20,16},{24,28},{28,24},{1,5},{5... | collective-permute-start | bytes 1179656 | tf_op jit(solution)/shard_map/ppermute | solution.py:419
  80.3 41.7 %collective-permute-start.30 = (bf16[2000,256]{1,0:T(8,128)(2,1)}, bf16[2000,256]{1,0:T(8,128)(2,1)}, u32[]{:S(2)}, u32[]{:S(2)}) collective-permute-start(bf16[2000,256]{1,0:T(8,128)(2,1)} %collective-permute-done.24.refs_5_), channel_id=1, source_target_pairs={{8,0},{12,4},{16,24},{20,28},{9,1},{13,5},{17,25},{21,29},{10,2},{... | collective-permute-start | bytes 3072008 | tf_op jit(solution)/shard_map/ppermute | solution.py:496
  84.7 5.4 %copy-start.9 = (f32[6,4,16,256]{3,2,1,0:T(8,128)S(1)}, f32[6,4,16,256]{3,2,1,0:T(8,128)}, u32[]{:S(2)}) copy-start(f32[6,4,16,256]{3,2,1,0:T(8,128)} %get-tuple-element.325.refs_0_) | copy-start | bytes 1179652 | tf_op jit(solution)/shard_map/cond
  88.5 1.6 %collective-permute-start = (f32[4,4,16,256]{3,2,1,0:T(8,128)S(1)}, f32[4,4,16,256]{3,2,1,0:T(8,128)S(1)}, u32[]{:S(2)}, u32[]{:S(2)}) collective-permute-start(f32[4,4,16,256]{3,2,1,0:T(8,128)S(1)} %get-tuple-element.333), channel_id=1, source_target_pairs={{0,4},{4,0},{8,12},{12,8},{16,20},{20,16},{24,28},{28,24},{1,5},{5... | collective-permute-start | bytes 786440 | tf_op jit(solution)/shard_map/cond/branch_1_fun/ppermute | solution.py:419
  91.2 7.1 %collective-permute-start.1 = (f32[10,16,256]{2,1,0:T(8,128)S(1)}, f32[10,16,256]{2,1,0:T(8,128)S(1)}, u32[]{:S(2)}, u32[]{:S(2)}) collective-permute-start(f32[10,16,256]{2,1,0:T(8,128)S(1)} %get-tuple-element.335), channel_id=1, source_target_pairs={{0,1},{1,0},{2,3},{3,2},{4,5},{5,4},{6,7},{7,6},{8,9},{9,8},{10,11... | collective-permute-start | bytes 491528 | tf_op jit(solution)/shard_map/cond/branch_1_fun/ppermute | solution.py:419
  92.7 9.5 %collective-permute-start.2 = (f32[10,16,256]{2,1,0:T(8,128)S(1)}, f32[10,16,256]{2,1,0:T(8,128)S(1)}, u32[]{:S(2)}, u32[]{:S(2)}) collective-permute-start(f32[10,16,256]{2,1,0:T(8,128)S(1)} %get-tuple-element.336), channel_id=1, source_target_pairs={{0,2},{1,3},{2,0},{3,1},{4,6},{5,7},{6,4},{7,5},{8,10},{9,11},{10,... | collective-permute-start | bytes 491528 | tf_op jit(solution)/shard_map/cond/branch_1_fun/ppermute | solution.py:419
  94.2 8.0 %collective-permute-start.3 = (f32[10,16,256]{2,1,0:T(8,128)S(1)}, f32[10,16,256]{2,1,0:T(8,128)S(1)}, u32[]{:S(2)}, u32[]{:S(2)}) collective-permute-start(f32[10,16,256]{2,1,0:T(8,128)S(1)} %get-tuple-element.337), channel_id=1, source_target_pairs={{0,3},{1,2},{2,1},{3,0},{4,7},{5,6},{6,5},{7,4},{8,11},{9,10},{10,... | collective-permute-start | bytes 491528 | tf_op jit(solution)/shard_map/cond/branch_1_fun/ppermute | solution.py:419
  102.5 6.1 %collective-permute-start.5 = (f32[4,32]{1,0:T(4,128)S(1)}, f32[4,32]{1,0:T(4,128)S(1)}, u32[]{:S(2)}, u32[]{:S(2)}) collective-permute-start(f32[4,32]{1,0:T(4,128)S(1)} %select_reduce_fusion), channel_id=1, source_target_pairs={{0,16},{4,20},{8,24},{12,28},{16,0},{20,4},{24,8},{28,12},{1,17},{... | collective-permute-start | bytes 1544 | tf_op jit(solution)/shard_map/cond/branch_1_fun/ppermute | solution.py:419
  106.8 5.5 %collective-permute-start.6 = (f32[4,32]{1,0:T(4,128)S(1)}, f32[4,32]{1,0:T(4,128)S(1)}, u32[]{:S(2)}, u32[]{:S(2)}) collective-permute-start(f32[4,32]{1,0:T(4,128)S(1)} %select_reduce_fusion), channel_id=1, source_target_pairs={{0,24},{4,28},{8,16},{12,20},{16,8},{20,12},{24,0},{28,4},{1,25},{... | collective-permute-start | bytes 1544 | tf_op jit(solution)/shard_map/cond/branch_1_fun/ppermute | solution.py:419
  108.5 4.0 %collective-permute-start.4 = (f32[36,256]{1,0:T(8,128)S(1)}, f32[36,256]{1,0:T(8,128)S(1)}, u32[]{:S(2)}, u32[]{:S(2)}) collective-permute-start(f32[36,256]{1,0:T(8,128)S(1)} %select_maximum_fusion), channel_id=1, source_target_pairs={{0,8},{4,12},{8,0},{12,4},{16,24},{20,28},{24,16},{28,20},{1,9},{5... | collective-permute-start | bytes 110600 | tf_op jit(solution)/shard_map/cond/branch_1_fun/ppermute | solution.py:419
  112.7 4.0 %collective-permute-start.7 = (bf16[8,1,16,128]{3,2,1,0:T(8,128)(2,1)S(1)}, bf16[8,1,16,128]{3,2,1,0:T(8,128)(2,1)S(1)}, u32[]{:S(2)}, u32[]{:S(2)}) collective-permute-start(bf16[8,1,16,128]{3,2,1,0:T(8,128)(2,1)S(1)} %bitcast.69), channel_id=1, source_target_pairs={{0,1},{1,0},{2,3},{3,2},{4,5},{5,4},{6,7},{7,6},{8,9},{9,8},{10,11... | collective-permute-start | bytes 98312 | tf_op jit(solution)/shard_map/cond/branch_1_fun/ppermute | solution.py:419
  114.0 3.9 %collective-permute-start.8 = (bf16[8,1,16,128]{3,2,1,0:T(8,128)(2,1)S(1)}, bf16[8,1,16,128]{3,2,1,0:T(8,128)(2,1)S(1)}, u32[]{:S(2)}, u32[]{:S(2)}) collective-permute-start(bf16[8,1,16,128]{3,2,1,0:T(8,128)(2,1)S(1)} %bitcast.70), channel_id=1, source_target_pairs={{0,2},{1,3},{2,0},{3,1},{4,6},{5,7},{6,4},{7,5},{8,10},{9,11},{10,... | collective-permute-start | bytes 98312 | tf_op jit(solution)/shard_map/cond/branch_1_fun/ppermute | solution.py:419
  114.8 4.8 %collective-permute-start.9 = (bf16[8,1,16,128]{3,2,1,0:T(8,128)(2,1)S(1)}, bf16[8,1,16,128]{3,2,1,0:T(8,128)(2,1)S(1)}, u32[]{:S(2)}, u32[]{:S(2)}) collective-permute-start(bf16[8,1,16,128]{3,2,1,0:T(8,128)(2,1)S(1)} %bitcast.71), channel_id=1, source_target_pairs={{0,3},{1,2},{2,1},{3,0},{4,7},{5,6},{6,5},{7,4},{8,11},{9,10},{10,... | collective-permute-start | bytes 98312 | tf_op jit(solution)/shard_map/cond/branch_1_fun/ppermute | solution.py:419
  120.3 1.7 %collective-permute-start.10 = (bf16[8,4,16,128]{3,2,1,0:T(8,128)(2,1)}, bf16[8,4,16,128]{3,2,1,0:T(8,128)(2,1)}, u32[]{:S(2)}, u32[]{:S(2)}) collective-permute-start(bf16[8,4,16,128]{3,2,1,0:T(8,128)(2,1)} %in_order.1), channel_id=1, source_target_pairs={{0,4},{4,0},{8,12},{12,8},{16,20},{20,16},{24,28},{28,24},{1,5},{5... | collective-permute-start | bytes 393224 | tf_op jit(solution)/shard_map/cond/branch_1_fun/ppermute | solution.py:419
  126.8 0.8 copy-start.1
  127.6 2.1 %collective-permute-start.31 = (f32[64,2000]{1,0:T(8,128)}, f32[64,2000]{1,0:T(8,128)S(1)}, u32[]{:S(2)}, u32[]{:S(2)}) collective-permute-start(f32[64,2000]{1,0:T(8,128)} %get-tuple-element.394), channel_id=1, source_target_pairs={{0,4},{4,0},{8,12},{12,8},{16,20},{20,16},{24,28},{28,24},{1,5},{5... | collective-permute-start | bytes 1536008 | tf_op jit(solution)/shard_map/ppermute | solution.py:419
  127.7 2.0 %copy-start.2 = (f32[64,2000]{1,0:T(8,128)S(1)}, f32[64,2000]{1,0:T(8,128)}, u32[]{:S(2)}) copy-start(f32[64,2000]{1,0:T(8,128)} %copy-done.1) | copy-start | bytes 1536004
  130.6 1.0 copy-start.6
where the time goes:
time: 132 us
  waiting for transfers between devices  58.1 us (44%)
  starting transfers between devices  36.8 us (28%)
  Pallas kernels  22.2 us (17%)
  local copies, waits for them, and re-layouts  9.2 us (7%)
  other arithmetic  3.54 us (3%)
  between operations  1.62 us (1%)
    ppermute x8, waiting for transfers between devices, sent(): return lax.ppermute(x, 'grid', along(pairs))  34.4 us
    ppermute x18, waiting for transfers between devices, flip(): return lax.ppermute(x, axis, [(i, i ^ bit) for i in range(count)])  23.4 us
    ppermute x8, starting transfers between devices, sent(): return lax.ppermute(x, 'grid', along(pairs))  15.5 us
    ppermute x18, starting transfers between devices, flip(): return lax.ppermute(x, axis, [(i, i ^ bit) for i in range(count)])  14.4 us
    pallas_call x2, Pallas kernels, project(): pl.pallas_call(body, grid=(steps,), out_shape=(shape, shape), in_specs=[S...  8.05 us
    ppermute x3, starting transfers between devices, per_device(): heard.append(lax.ppermute(told, 'grid', around))  6.88 us
    pallas_call x1, Pallas kernels, contract(): pl.pallas_call(body, grid=(steps,), out_shape=(shape, shape), in_specs=[S...  4.78 us
    unnamed x22, local copies, waits for them, and re-layouts  3.75 us
  transfers between devices with their start and end apart: 29, of which 17 were waited for; matrix products, arithmetic and copies ran while one was open for 8% of the time, Pallas kernels for 10%

commit v1 on v0

--- a/solution.py
+++ b/solution.py
@@ -8,7 +8,7 @@
 from jax.sharding import PartitionSpec as P
 
 BF16, F32 = jnp.bfloat16, jnp.float32
-VMEM_LIMIT = 48 * 1024 * 1024
+MIB = 1024 * 1024
 WHOLE = pl.BlockSpec(memory_space=pltpu.VMEM)
 SCALARS = pl.BlockSpec(memory_space=pltpu.SMEM)
 
@@ -85,7 +85,7 @@
         in_specs=[SCALARS, pl.BlockSpec(memory_space=pl.ANY)],
         out_specs=WHOLE,
         scratch_shapes=[pltpu.SemaphoreType.DMA],
-        compiler_params=pltpu.CompilerParams(vmem_limit_bytes=VMEM_LIMIT),
+        compiler_params=pltpu.CompilerParams(vmem_limit_bytes=4 * MIB),
         name="half_of",
     )(which[None], whole)
 
@@ -120,7 +120,7 @@
         out_shape=(shape,) * count,
         in_specs=[SCALARS] + [WHOLE] * 6,
         out_specs=(WHOLE,) * count,
-        compiler_params=pltpu.CompilerParams(vmem_limit_bytes=VMEM_LIMIT),
+        compiler_params=pltpu.CompilerParams(vmem_limit_bytes=24 * MIB),
         name="compact",
         cost_estimate=pl.CostEstimate(
             flops=8 * half * rows * rows, bytes_accessed=8 * half * rows, transcendentals=0
@@ -148,32 +148,55 @@
         out_shape=jax.ShapeDtypeStruct((half, count * tile), BF16),
         in_specs=[SCALARS] + [WHOLE] * (count + 2),
         out_specs=WHOLE,
-        compiler_params=pltpu.CompilerParams(vmem_limit_bytes=VMEM_LIMIT),
+        compiler_params=pltpu.CompilerParams(vmem_limit_bytes=8 * MIB),
         name="straighten",
     )(odd[None], *tiles, by_a, by_b)
 
 
+def panel_halves(occupied, trial, core):
+    columns, cols = occupied.shape
+    half = cols // 2
+    width = -(-half // 128) * 128
+
+    def body(core_ref, occupied_ref, trial_ref, mine_ref, other_ref):
+        first = core_ref[0] == 0
+        mine_ref[...] = jnp.zeros_like(mine_ref)
+        other_ref[...] = jnp.zeros_like(other_ref)
+        for j, ref in enumerate((occupied_ref, trial_ref)):
+            low, high = ref[:, :half], ref[:, half:]
+            mine_ref[j * columns : (j + 1) * columns, :half] = jnp.where(first, low, high)
+            other_ref[j * columns : (j + 1) * columns, :half] = jnp.where(first, high, low)
+
+    shape = jax.ShapeDtypeStruct((2 * columns, width), BF16)
+    return pl.pallas_call(
+        body,
+        out_shape=(shape, shape),
+        in_specs=[SCALARS, WHOLE, WHOLE],
+        out_specs=(WHOLE, WHOLE),
+        compiler_params=pltpu.CompilerParams(vmem_limit_bytes=8 * MIB),
+        name="panel_halves",
+    )(core[None], occupied, trial)
+
+
 def stack_panels(mine, got, core):
-    both, half = mine.shape
+    both, width = mine.shape
     columns = both // 2
-    width = -(-half // 128) * 128
 
     def body(core_ref, mine_ref, got_ref, out_ref):
         first = core_ref[0] == 0
-        out_ref[...] = jnp.zeros_like(out_ref)
         for j in range(2):
             low = mine_ref[j * columns : (j + 1) * columns]
             high = got_ref[j * columns : (j + 1) * columns]
             q = 2 * j * columns
-            out_ref[q : q + columns, :half] = jnp.where(first, low, high)
-            out_ref[q + columns : q + 2 * columns, :half] = jnp.where(first, high, low)
+            out_ref[q : q + columns] = jnp.where(first, low, high)
+            out_ref[q + columns : q + 2 * columns] = jnp.where(first, high, low)
 
     return pl.pallas_call(
         body,
         out_shape=jax.ShapeDtypeStruct((2 * both, width), BF16),
         in_specs=[SCALARS, WHOLE, WHOLE],
         out_specs=WHOLE,
-        compiler_params=pltpu.CompilerParams(vmem_limit_bytes=VMEM_LIMIT),
+        compiler_params=pltpu.CompilerParams(vmem_limit_bytes=8 * MIB),
         name="stack_panels",
     )(core[None], mine, got)
 
@@ -215,7 +238,7 @@
         out_shape=(shape,) * shares,
         in_specs=[SCALARS] + [WHOLE] * (2 * len(pairs)),
         out_specs=(WHOLE,) * shares,
-        compiler_params=pltpu.CompilerParams(vmem_limit_bytes=VMEM_LIMIT),
+        compiler_params=pltpu.CompilerParams(vmem_limit_bytes=8 * MIB),
         name="split_sum",
     )(occ[None], *sum(pairs, ()))
 
@@ -274,7 +297,7 @@
             pltpu.VMEM((len(jobs), both, rows), F32),
             pltpu.VMEM((tiles, 2, shares // 2, piece, both), F32),
         ],
-        compiler_params=pltpu.CompilerParams(vmem_limit_bytes=VMEM_LIMIT),
+        compiler_params=pltpu.CompilerParams(vmem_limit_bytes=12 * MIB),
         name="project",
         cost_estimate=pl.CostEstimate(
             flops=2 * both * half * tiles * tile,
@@ -296,7 +319,7 @@
         out_shape=jax.ShapeDtypeStruct((tiles, len(parts), piece, columns), parts[0].dtype),
         in_specs=[SCALARS] + [WHOLE] * len(parts),
         out_specs=WHOLE,
-        compiler_params=pltpu.CompilerParams(vmem_limit_bytes=VMEM_LIMIT),
+        compiler_params=pltpu.CompilerParams(vmem_limit_bytes=4 * MIB),
         name="in_order",
     )(occ[None], *parts)
 
@@ -320,22 +343,16 @@
             order_ref[:, 1 - core_ref[0]] = got_ref[...].astype(F32)
             for s in range(len(windows)):
                 part = order_ref[s * per_window : (s + 1) * per_window]
-                turned = part.reshape(rows, columns).T
-                low, high = turned[:own], turned[own:]
-                turned_ref[s, :own] = jnp.where(first, low, high).astype(BF16)
-                turned_ref[s, own:] = jnp.where(first, high, low).astype(BF16)
+                turned_ref[s] = part.reshape(rows, columns).astype(BF16)
 
         total = None
         for s, window in enumerate(windows):
-            term = lax.dot_general(
-                turned_ref[s],
-                read_window(window, arrays, array_refs),
-                (((1,), (1,)), ((), ())),
-                preferred_element_type=F32,
-            )
+            value = read_window(window, arrays, array_refs)
+            term = jnp.dot(value, turned_ref[s], preferred_element_type=F32)
             total = term if total is None else total + term
-        mine_ref[...] = total[:own]
-        other_ref[...] = total[own:]
+        total = total.T
+        mine_ref[...] = jnp.where(first, total[:own], total[own:])
+        other_ref[...] = jnp.where(first, total[own:], total[:own])
 
     shape = jax.ShapeDtypeStruct((own, half), F32)
     whole = pl.BlockSpec(kernel.shape, lambda i: (0, 0, 0, 0))
@@ -348,9 +365,9 @@
         out_specs=(pl.BlockSpec((own, step), lambda i: (0, i)),) * 2,
         scratch_shapes=[
             pltpu.VMEM((tiles, 2, shares, piece, columns), F32),
-            pltpu.VMEM((len(windows), columns, rows), BF16),
+            pltpu.VMEM((len(windows), rows, columns), BF16),
         ],
-        compiler_params=pltpu.CompilerParams(vmem_limit_bytes=VMEM_LIMIT),
+        compiler_params=pltpu.CompilerParams(vmem_limit_bytes=12 * MIB),
         name="contract",
         cost_estimate=pl.CostEstimate(
             flops=2 * columns * half * rows * len(windows),
@@ -392,7 +409,7 @@
         out_specs=pl.BlockSpec(memory_space=pltpu.HBM),
         scratch_shapes=[pltpu.VMEM((own, 2 * half), F32), pltpu.SemaphoreType.DMA],
         input_output_aliases={3: 0},
-        compiler_params=pltpu.CompilerParams(vmem_limit_bytes=VMEM_LIMIT),
+        compiler_params=pltpu.CompilerParams(vmem_limit_bytes=8 * MIB),
         name="finish",
     )(jnp.stack((core, fits.astype(jnp.int32))), ours, back, other)
 
@@ -504,9 +521,10 @@
             pairs += [(a + 1, a)] if a + t <= last else []
         return pairs
 
-    own = straighten(own_tiles, sent(for_a, over(0, 1)), sent(for_b, over(1, 1)), odd)
-
-    mine_panel, other_panel = halves(jnp.concatenate((occupied, trial), axis=1).T, 1)
+    by_b = sent(for_b, over(1, 1))
+    own = straighten(own_tiles, sent(for_a, over(0, 1)), by_b, odd)
+
+    mine_panel, other_panel = panel_halves(occupied.T, trial.T, core)
     panels = stack_panels(mine_panel, flip(other_panel, "grid", 1), core)
 
     per_window = rows // tile
@@ -522,7 +540,8 @@
     by_a = by_b = own
     far_panels = None
     for t in range(1, last):
-        by_a, by_b = sent(by_b, over(0, t)), sent(by_a, over(1, t))
+        next_b = sent(by_a, over(1, t))
+        by_a, by_b = sent(by_b, over(0, t)), next_b
         if t == 1:
             far_panels = sent(panels, ends)
         a_at, b_at = valid(chip + side * t), valid(chip - side * t)
@@ -579,9 +598,10 @@
     here = (places[:, None] == window_iota[None, :])[:, :, None]
     weight_here = jnp.sum(jnp.where(here, weight[None], 0.0), axis=1)[:, :, None]
 
-    late, by_a, early_pair, far_panels, weight_here = lax.optimization_barrier(
-        (by_b, by_a, early_pair, far_panels, weight_here)
+    late, by_a, early_pair, far_panels, weight_here, fits = lax.optimization_barrier(
+        (by_b, by_a, early_pair, far_panels, weight_here, fits.astype(jnp.int32))
     )
+    fits = fits != 0
     late = sent(late, homes)
     late_window = [by_a, by_b]
     late_jobs = [(panels, late_window), (far_panels, [by_b])]

time: 132 us -> 127 us (0.962)
  local copies, waits for them, and re-layouts: 9.2 us -> 5.7 us
  waiting for transfers between devices: 58.1 us -> 56.5 us
    dynamic_slice x1 -> x0, local copies, waits for them, and re-layouts: 2.64 us -> none  [halves(): lax.dynamic_slice_in_dim(whole, (1 - core) * size, size, axis)]
    ppermute x18, waiting for transfers between devices: 23.4 us -> 21.2 us  [flip(): return lax.ppermute(x, axis, [(i, i ^ bit) for i in range(count)])]
    ppermute x3, waiting for transfers between devices: 0.29 us -> 2.4 us  [per_device(): heard.append(lax.ppermute(told, 'grid', around))]
    ppermute x8, waiting for transfers between devices: 34.4 us -> 32.9 us  [sent(): return lax.ppermute(x, 'grid', along(pairs))]
    ppermute x8, starting transfers between devices: 15.5 us -> 14.1 us  [sent(): return lax.ppermute(x, 'grid', along(pairs))]
    unnamed x22 -> x23, local copies, waits for them, and re-layouts: 3.75 us -> 3.73 us
  transfers between devices with their start and end apart: 29 -> 29, of which waited for: 17 -> 17; matrix products, arithmetic and copies ran while one was open for 8% -> 5% of each run, Pallas kernels for 10% -> 12%
where the time goes in v1:
time: 127 us
  waiting for transfers between devices  56.5 us (44%)
  starting transfers between devices  35.5 us (28%)
  Pallas kernels  23.5 us (19%)
  local copies, waits for them, and re-layouts  5.7 us (4%)
  other arithmetic  4.1 us (3%)
  between operations  1.38 us (1%)
    ppermute x8, waiting for transfers between devices, sent(): return lax.ppermute(x, 'grid', along(pairs))  32.9 us
    ppermute x18, waiting for transfers between devices, flip(): return lax.ppermute(x, axis, [(i, i ^ bit) for i in range(count)])  21.2 us
    ppermute x18, starting transfers between devices, flip(): return lax.ppermute(x, axis, [(i, i ^ bit) for i in range(count)])  15.3 us
    ppermute x8, starting transfers between devices, sent(): return lax.ppermute(x, 'grid', along(pairs))  14.1 us
    pallas_call x2, Pallas kernels, project(): pl.pallas_call(body, grid=(steps,), out_shape=(shape, shape), in_specs=[S...  8.05 us
    ppermute x3, starting transfers between devices, per_device(): heard.append(lax.ppermute(told, 'grid', around))  6.05 us
    pallas_call x1, Pallas kernels, contract(): pl.pallas_call(body, grid=(steps,), out_shape=(shape, shape), in_specs=[S...  4.8 us
    unnamed x23, local copies, waits for them, and re-layouts  3.73 us
  transfers between devices with their start and end apart: 29, of which 17 were waited for; matrix products, arithmetic and copies ran while one was open for 5% of the time, Pallas kernels for 12%

profile of v1, /device:TPU:0, one launch (start us, length us, event | category | flops | bytes accessed | tf_op | source)
XLA Modules:
  0.0 126.8 jit_solution(9638244666126898719)
XLA Ops:
  0.5 0.8 dynamic-slice_bitcast_fusion
  1.8 1.2 half_of.3
  3.4 5.0 %collective-permute-start.20 = (f32[1,528]{1,0:T(1,128)S(1)}, f32[1,528]{1,0:T(1,128)S(1)}, u32[]{:S(2)}, u32[]{:S(2)}) collective-permute-start(f32[1,528]{1,0:T(1,128)S(1)} %pad_maximum_fusion.3), channel_id=1, source_target_pairs={{0,24},{4,28},{8,0},{12,4},{16,8},{20,12},{24,16},{28,20},{1,25},{... | collective-permute-start | bytes 6344 | tf_op jit(solution)/shard_map/ppermute | solution.py:472
  8.4 1.0 collective-permute-start.18
  9.9 1.2 half_of.2.mine_ref
  11.4 1.5 %collective-permute-done.19 = f32[1,528]{1,0:T(1,128)S(1)} collective-permute-done((f32[1,528]{1,0:T(1,128)S(1)}, f32[1,528]{1,0:T(1,128)S(1)}, u32[]{:S(2)}, u32[]{:S(2)}) %collective-permute-start.19) | collective-permute-done | bytes 2144 | tf_op jit(solution)/shard_map/ppermute | solution.py:472
  12.9 0.9 collective-permute-done.18
  15.0 1.8 %compact.1 = (bf16[2000,128]{1,0:T(8,128)(2,1)S(1)}, bf16[2000,128]{1,0:T(8,128)(2,1)S(1)}, bf16[2000,128]{1,0:T(8,128)(2,1)S(1)}, bf16[2000,128]{1,0:T(8,128)(2,1)S(1)}) custom-call(s32[1]{0:T(128)} %bitcast.13.odd_ref, bf16[2000,256]{1,0:T(8,128)(2,1)S(1)} %half_of.2.mine_ref, bf16[2000,256]{1,0:T(8,128)(2,1)S(1)} %collective-permute-done.14.got_ref, ...), custom_call_target="tpu_custom_call" | custom-call | flops 1048576000 | bytes 4096000 | tf_op jit(solution)/shard_map/compact/pallas_call | solution.py:118
  17.0 0.8 collective-permute-start.22
  17.8 11.3 %collective-permute-done.21.refs_2_ = bf16[2000,128]{1,0:T(8,128)(2,1)S(1)} collective-permute-done((bf16[2000,128]{1,0:T(8,128)(2,1)S(1)}, bf16[2000,128]{1,0:T(8,128)(2,1)S(1)}, u32[]{:S(2)}, u32[]{:S(2)}) %collective-permute-start.21) | collective-permute-done | bytes 512032 | tf_op jit(solution)/shard_map/ppermute | solution.py:513
  29.5 0.7 collective-permute-start.25
  30.3 5.3 %collective-permute-start.23 = (bf16[2000,256]{1,0:T(8,128)(2,1)S(1)}, bf16[2000,256]{1,0:T(8,128)(2,1)S(1)}, u32[]{:S(2)}, u32[]{:S(2)}) collective-permute-start(bf16[2000,256]{1,0:T(8,128)(2,1)S(1)} %straighten.1.refs_1_.refs_0_), channel_id=1, source_target_pairs={{0,8},{4,12},{8,0},{12,4},{16,24},{20,28},{24,16},{28,20},{1,9},{5... | collective-permute-start | bytes 3072008 | tf_op jit(solution)/shard_map/ppermute | solution.py:513
  35.5 1.3 %panel_halves.1 = (bf16[128,2048]{1,0:T(8,128)(2,1)S(1)}, bf16[128,2048]{1,0:T(8,128)(2,1)}) custom-call(s32[1]{0:T(128)} %bitcast.12.which_ref.core_ref, bf16[64,4000]{1,0:T(8,128)(2,1)S(1)} %bitcast.73, bf16[64,4000]{1,0:T(8,128)(2,1)S(1)} %bitcast.74), custom_call_target="tpu_custom_call" | custom-call | tf_op jit(solution)/shard_map/panel_halves/pallas_call | solution.py:171
  36.8 0.8 copy-done
  38.1 1.8 %collective-permute-done.27.got_ref = bf16[128,2048]{1,0:T(8,128)(2,1)} collective-permute-done((bf16[128,2048]{1,0:T(8,128)(2,1)}, bf16[128,2048]{1,0:T(8,128)(2,1)}, u32[]{:S(2)}, u32[]{:S(2)}) %collective-permute-start.27) | collective-permute-done | bytes 524320 | tf_op jit(solution)/shard_map/ppermute | solution.py:436
  39.9 1.0 copy-done.1
  41.0 2.1 %stack_panels.1.refs_0_ = bf16[256,2048]{1,0:T(8,128)(2,1)} custom-call(s32[1]{0:T(128)} %bitcast.12.which_ref.core_ref, bf16[128,2048]{1,0:T(8,128)(2,1)S(1)} %copy-done.1, bf16[128,2048]{1,0:T(8,128)(2,1)} %collective-permute-done.27.got_ref), custom_call_target="tpu_custom_call" | custom-call | tf_op jit(solution)/shard_map/stack_panels/pallas_call | solution.py:194
  43.0 2.9 %collective-permute-start.29 = (bf16[256,2048]{1,0:T(8,128)(2,1)}, bf16[256,2048]{1,0:T(8,128)(2,1)}, u32[]{:S(2)}, u32[]{:S(2)}) collective-permute-start(bf16[256,2048]{1,0:T(8,128)(2,1)} %stack_panels.1.refs_0_), channel_id=1, source_target_pairs={{0,8},{4,12},{24,16},{28,20},{1,9},{5,13},{25,17},{29,21},{2,10},{... | collective-permute-start | bytes 3145736 | tf_op jit(solution)/shard_map/ppermute | solution.py:513
  46.0 1.3 %collective-permute-start.26 = (bf16[2000,256]{1,0:T(8,128)(2,1)S(1)}, bf16[2000,256]{1,0:T(8,128)(2,1)}, u32[]{:S(2)}, u32[]{:S(2)}) collective-permute-start(bf16[2000,256]{1,0:T(8,128)(2,1)S(1)} %collective-permute-done.25.refs_3_.refs_2_), channel_id=1, source_target_pairs={{8,0},{12,4},{16,24},{20,28},{9,1},{13,5},{17,25},{21,29},{10,2},{... | collective-permute-start | bytes 3072008 | tf_op jit(solution)/shard_map/ppermute | solution.py:513
  47.2 11.4 %collective-permute-done.23.refs_2_.refs_1_ = bf16[2000,256]{1,0:T(8,128)(2,1)S(1)} collective-permute-done((bf16[2000,256]{1,0:T(8,128)(2,1)S(1)}, bf16[2000,256]{1,0:T(8,128)(2,1)S(1)}, u32[]{:S(2)}, u32[]{:S(2)}) %collective-permute-start.23) | collective-permute-done | bytes 1024032 | tf_op jit(solution)/shard_map/ppermute | solution.py:513
  58.6 1.6 %collective-permute-start.24 = (bf16[2000,256]{1,0:T(8,128)(2,1)S(1)}, bf16[2000,256]{1,0:T(8,128)(2,1)}, u32[]{:S(2)}, u32[]{:S(2)}) collective-permute-start(bf16[2000,256]{1,0:T(8,128)(2,1)S(1)} %collective-permute-done.23.refs_2_.refs_1_), channel_id=1, source_target_pairs={{8,16},{12,20},{16,8},{20,12},{9,17},{13,21},{17,9},{21,13},{10,18... | collective-permute-start | bytes 3072008 | tf_op jit(solution)/shard_map/ppermute | solution.py:513
  62.8 4.3 %project.3 = (f32[6,4,16,256]{3,2,1,0:T(8,128)}, f32[6,4,16,256]{3,2,1,0:T(8,128)S(1)}) custom-call(s32[1]{0:T(128)} %bitcast.12.which_ref.core_ref, bf16[256,2048]{1,0:T(8,128)(2,1)} %stack_panels.1.refs_0_, bf16[2000,256]{1,0:T(8,128)(2,1)S(1)} %straighten.1.refs_1_.refs_0_, bf16[2000,256]{1,0:T(8,128)(2,1)S(1)} %collective-permute-done.23.refs_2_.refs_1_, ...), custom_call_target="tpu_custom_call" | custom-call | flops 786432000 | bytes 4882432 | tf_op jit(solution)/shard_map/project/pallas_call | solution.py:288
  67.7 10.1 %collective-permute-done.29 = bf16[256,2048]{1,0:T(8,128)(2,1)} collective-permute-done((bf16[256,2048]{1,0:T(8,128)(2,1)}, bf16[256,2048]{1,0:T(8,128)(2,1)}, u32[]{:S(2)}, u32[]{:S(2)}) %collective-permute-start.29) | collective-permute-done | bytes 1048608 | tf_op jit(solution)/shard_map/ppermute | solution.py:513
  77.9 1.3 %collective-permute-start.30 = (bf16[2000,256]{1,0:T(8,128)(2,1)}, bf16[2000,256]{1,0:T(8,128)(2,1)}, u32[]{:S(2)}, u32[]{:S(2)}) collective-permute-start(bf16[2000,256]{1,0:T(8,128)(2,1)} %collective-permute-done.24.refs_5_), channel_id=1, source_target_pairs={{8,0},{12,4},{16,24},{20,28},{9,1},{13,5},{17,25},{21,29},{10,2},{... | collective-permute-start | bytes 3072008 | tf_op jit(solution)/shard_map/ppermute | solution.py:513
  79.3 37.9 %conditional.2 = (bf16[8,4,16,128]{3,2,1,0:T(8,128)(2,1)}, bf16[8,4,16,128]{3,2,1,0:T(8,128)(2,1)}) conditional(s32[]{:T(128)} %convert_element_type.53, () %tuple.69, (s32[]{:T(128)}, f32[4,32,1]{1,0,2:T(4,128)S(1)}, s32[4]{0:T(128)S(1)}, s32[4,4,1]{1,0,2:T(4,128)S(1)}, s32[3]{0:T(128)S(1)}, /*index=5*/s32[1]{0:T(128)}, s32[4]{0:T(128)S(1)}, ...), branch_computations={%region_6.7_spmd, %region_7.11_spmd} | conditional | flops 524621184 | bytes 11165124 | solution.py:641
  79.3 3.8 %project.2 = (f32[4,4,16,256]{3,2,1,0:T(8,128)S(1)}, f32[4,4,16,256]{3,2,1,0:T(8,128)S(1)}) custom-call(s32[1]{0:T(128)} %bitcast.3.core_ref, bf16[256,2048]{1,0:T(8,128)(2,1)} %get-tuple-element.328.refs_0_, bf16[256,2048]{1,0:T(8,128)(2,1)} %get-tuple-element.329.refs_1_, bf16[2000,256]{1,0:T(8,128)(2,1)} %get-tuple-element.330.refs_2_, ...), custom_call_target="tpu_custom_call" | custom-call | flops 524288000 | bytes 3596288 | tf_op jit(solution)/shard_map/cond/branch_1_fun/project/pallas_call | solution.py:288
  83.2 1.4 %collective-permute-done.refs_3_ = f32[4,4,16,256]{3,2,1,0:T(8,128)S(1)} collective-permute-done((f32[4,4,16,256]{3,2,1,0:T(8,128)S(1)}, f32[4,4,16,256]{3,2,1,0:T(8,128)S(1)}, u32[]{:S(2)}, u32[]{:S(2)}) %collective-permute-start) | collective-permute-done | bytes 262176 | tf_op jit(solution)/shard_map/cond/branch_1_fun/ppermute | solution.py:436
  84.7 1.1 split_sum.1
  85.8 1.6 %collective-permute-start.1 = (f32[10,16,256]{2,1,0:T(8,128)S(1)}, f32[10,16,256]{2,1,0:T(8,128)S(1)}, u32[]{:S(2)}, u32[]{:S(2)}) collective-permute-start(f32[10,16,256]{2,1,0:T(8,128)S(1)} %get-tuple-element.335), channel_id=1, source_target_pairs={{0,1},{1,0},{2,3},{3,2},{4,5},{5,4},{6,7},{7,6},{8,9},{9,8},{10,11... | collective-permute-start | bytes 491528 | tf_op jit(solution)/shard_map/cond/branch_1_fun/ppermute | solution.py:436
  87.3 1.5 %collective-permute-start.2 = (f32[10,16,256]{2,1,0:T(8,128)S(1)}, f32[10,16,256]{2,1,0:T(8,128)S(1)}, u32[]{:S(2)}, u32[]{:S(2)}) collective-permute-start(f32[10,16,256]{2,1,0:T(8,128)S(1)} %get-tuple-element.336), channel_id=1, source_target_pairs={{0,2},{1,3},{2,0},{3,1},{4,6},{5,7},{6,4},{7,5},{8,10},{9,11},{10,... | collective-permute-start | bytes 491528 | tf_op jit(solution)/shard_map/cond/branch_1_fun/ppermute | solution.py:436
  89.4 3.5 %collective-permute-done.1 = f32[10,16,256]{2,1,0:T(8,128)S(1)} collective-permute-done((f32[10,16,256]{2,1,0:T(8,128)S(1)}, f32[10,16,256]{2,1,0:T(8,128)S(1)}, u32[]{:S(2)}, u32[]{:S(2)}) %collective-permute-start.1) | collective-permute-done | bytes 163872 | tf_op jit(solution)/shard_map/cond/branch_1_fun/ppermute | solution.py:436
  92.9 3.9 %collective-permute-done.2 = f32[10,16,256]{2,1,0:T(8,128)S(1)} collective-permute-done((f32[10,16,256]{2,1,0:T(8,128)S(1)}, f32[10,16,256]{2,1,0:T(8,128)S(1)}, u32[]{:S(2)}, u32[]{:S(2)}) %collective-permute-start.2) | collective-permute-done | bytes 163872 | tf_op jit(solution)/shard_map/cond/branch_1_fun/ppermute | solution.py:436
  97.0 2.2 %collective-permute-start.6 = (f32[4,32]{1,0:T(4,128)S(1)}, f32[4,32]{1,0:T(4,128)S(1)}, u32[]{:S(2)}, u32[]{:S(2)}) collective-permute-start(f32[4,32]{1,0:T(4,128)S(1)} %select_reduce_fusion), channel_id=1, source_target_pairs={{0,24},{4,28},{8,16},{12,20},{16,8},{20,12},{24,0},{28,4},{1,25},{... | collective-permute-start | bytes 1544 | tf_op jit(solution)/shard_map/cond/branch_1_fun/ppermute | solution.py:436
  99.2 4.7 %collective-permute-start.5 = (f32[4,32]{1,0:T(4,128)S(1)}, f32[4,32]{1,0:T(4,128)S(1)}, u32[]{:S(2)}, u32[]{:S(2)}) collective-permute-start(f32[4,32]{1,0:T(4,128)S(1)} %select_reduce_fusion), channel_id=1, source_target_pairs={{0,16},{4,20},{8,24},{12,28},{16,0},{20,4},{24,8},{28,12},{1,17},{... | collective-permute-start | bytes 1544 | tf_op jit(solution)/shard_map/cond/branch_1_fun/ppermute | solution.py:436
  104.0 1.5 %collective-permute-done.5 = f32[4,32]{1,0:T(4,128)S(1)} collective-permute-done((f32[4,32]{1,0:T(4,128)S(1)}, f32[4,32]{1,0:T(4,128)S(1)}, u32[]{:S(2)}, u32[]{:S(2)}) %collective-permute-start.5) | collective-permute-done | bytes 544 | tf_op jit(solution)/shard_map/cond/branch_1_fun/ppermute | solution.py:436
  105.6 2.4 %collective-permute-done.4 = f32[36,256]{1,0:T(8,128)S(1)} collective-permute-done((f32[36,256]{1,0:T(8,128)S(1)}, f32[36,256]{1,0:T(8,128)S(1)}, u32[]{:S(2)}, u32[]{:S(2)}) %collective-permute-start.4) | collective-permute-done | bytes 36896 | tf_op jit(solution)/shard_map/cond/branch_1_fun/ppermute | solution.py:436
  108.2 1.6 %collective-permute-start.9 = (bf16[8,1,16,128]{3,2,1,0:T(8,128)(2,1)S(1)}, bf16[8,1,16,128]{3,2,1,0:T(8,128)(2,1)S(1)}, u32[]{:S(2)}, u32[]{:S(2)}) collective-permute-start(bf16[8,1,16,128]{3,2,1,0:T(8,128)(2,1)S(1)} %bitcast.67), channel_id=1, source_target_pairs={{0,3},{1,2},{2,1},{3,0},{4,7},{5,6},{6,5},{7,4},{8,11},{9,10},{10,... | collective-permute-start | bytes 98312 | tf_op jit(solution)/shard_map/cond/branch_1_fun/ppermute | solution.py:436
  109.8 1.2 collective-permute-start.8
  111.0 0.8 collective-permute-start.7
  111.7 1.3 %collective-permute-done.9.refs_3_ = bf16[8,1,16,128]{3,2,1,0:T(8,128)(2,1)S(1)} collective-permute-done((bf16[8,1,16,128]{3,2,1,0:T(8,128)(2,1)S(1)}, bf16[8,1,16,128]{3,2,1,0:T(8,128)(2,1)S(1)}, u32[]{:S(2)}, u32[]{:S(2)}) %collective-permute-start.9) | collective-permute-done | bytes 32800 | tf_op jit(solution)/shard_map/cond/branch_1_fun/ppermute | solution.py:436
  113.7 1.2 collective-permute-done.7.refs_1_
  114.9 0.7 in_order.1
  115.5 1.7 %collective-permute-done.10 = bf16[8,4,16,128]{3,2,1,0:T(8,128)(2,1)} collective-permute-done((bf16[8,4,16,128]{3,2,1,0:T(8,128)(2,1)}, bf16[8,4,16,128]{3,2,1,0:T(8,128)(2,1)}, u32[]{:S(2)}, u32[]{:S(2)}) %collective-permute-start.10) | collective-permute-done | bytes 131104 | tf_op jit(solution)/shard_map/cond/branch_1_fun/ppermute | solution.py:436
  117.2 4.8 %contract.1 = (f32[64,2000]{1,0:T(8,128)S(1)}, f32[64,2000]{1,0:T(8,128)}) custom-call(s32[1]{0:T(128)} %bitcast.12.which_ref.core_ref, bf16[8,4,16,128]{3,2,1,0:T(8,128)(2,1)} %get-tuple-element.396.kernel_ref, bf16[8,4,16,128]{3,2,1,0:T(8,128)(2,1)} %get-tuple-element.397.got_ref, bf16[2000,256]{1,0:T(8,128)(2,1)S(1)} %straighten.1.refs_1_.refs_0_, ...), custom_call_target="tpu_custom_call" | custom-call | flops 524288000 | bytes 5120000 | tf_op jit(solution)/shard_map/contract/pallas_call | solution.py:359
  122.0 0.8 copy-done.2
  123.1 1.8 %collective-permute-done.31.back_ref = f32[64,2000]{1,0:T(8,128)S(1)} collective-permute-done((f32[64,2000]{1,0:T(8,128)}, f32[64,2000]{1,0:T(8,128)S(1)}, u32[]{:S(2)}, u32[]{:S(2)}) %collective-permute-start.31) | collective-permute-done | bytes 512032 | tf_op jit(solution)/shard_map/ppermute | solution.py:436
  125.0 0.9 finish.1
  125.8 1.0 copy-done.8
  (115 shorter events, 8.7 us)
Async XLA Ops:
  0.0 3.2 %copy-start.14 = (s32[8]{0:T(128)S(1)}, s32[8]{0:T(128)}, u32[]{:S(2)}) copy-start(s32[8]{0:T(128)} %param.20) | copy-start | bytes 100
  0.0 3.3 %copy-start.13 = (f32[256]{0:T(256)S(1)}, f32[256]{0:T(256)}, u32[]{:S(2)}) copy-start(f32[256]{0:T(256)} %param.19) | copy-start | bytes 3076
  0.0 3.2 %collective-permute-start.16 = (s32[1,8]{1,0:T(1,128)}, s32[1,8]{1,0:T(1,128)S(1)}, u32[]{:S(2)}, u32[]{:S(2)}) collective-permute-start(s32[1,8]{1,0:T(1,128)} %bitcast.86), channel_id=1, source_target_pairs={{0,4},{4,0},{8,12},{12,8},{16,20},{20,16},{24,28},{28,24},{1,5},{5... | collective-permute-start | bytes 104 | tf_op jit(solution)/shard_map/ppermute | solution.py:436
  0.5 2.8 %collective-permute-start.17 = (f32[1,256]{1,0:T(1,128)}, f32[1,256]{1,0:T(1,128)S(1)}, u32[]{:S(2)}, u32[]{:S(2)}) collective-permute-start(f32[1,256]{1,0:T(1,128)} %bitcast.84), channel_id=1, source_target_pairs={{0,4},{4,0},{8,12},{12,8},{16,20},{20,16},{24,28},{28,24},{1,5},{5... | collective-permute-start | bytes 3080 | tf_op jit(solution)/shard_map/ppermute | solution.py:436
  1.4 9.8 %collective-permute-start.15 = (s32[16,8]{0,1:T(8,128)S(1)}, s32[16,8]{0,1:T(8,128)S(1)}, u32[]{:S(2)}, u32[]{:S(2)}) collective-permute-start(s32[16,8]{0,1:T(8,128)S(1)} %get-tuple-element.470), channel_id=1, source_target_pairs={{0,4},{4,0},{8,12},{12,8},{16,20},{20,16},{24,28},{28,24},{1,5},{5... | collective-permute-start | bytes 1544 | tf_op jit(solution)/shard_map/ppermute | solution.py:436
  3.0 12.0 %collective-permute-start.14 = (bf16[2000,256]{1,0:T(8,128)(2,1)S(1)}, bf16[2000,256]{1,0:T(8,128)(2,1)S(1)}, u32[]{:S(2)}, u32[]{:S(2)}) collective-permute-start(bf16[2000,256]{1,0:T(8,128)(2,1)S(1)} %half_of.3), channel_id=1, source_target_pairs={{0,4},{4,0},{8,12},{12,8},{16,20},{20,16},{24,28},{28,24},{1,5},{5... | collective-permute-start | bytes 3072008 | tf_op jit(solution)/shard_map/ppermute | solution.py:436
  3.4 8.0 %collective-permute-start.20 = (f32[1,528]{1,0:T(1,128)S(1)}, f32[1,528]{1,0:T(1,128)S(1)}, u32[]{:S(2)}, u32[]{:S(2)}) collective-permute-start(f32[1,528]{1,0:T(1,128)S(1)} %pad_maximum_fusion.3), channel_id=1, source_target_pairs={{0,24},{4,28},{8,0},{12,4},{16,8},{20,12},{24,16},{28,20},{1,25},{... | collective-permute-start | bytes 6344 | tf_op jit(solution)/shard_map/ppermute | solution.py:472
  8.4 4.5 %collective-permute-start.19 = (f32[1,528]{1,0:T(1,128)S(1)}, f32[1,528]{1,0:T(1,128)S(1)}, u32[]{:S(2)}, u32[]{:S(2)}) collective-permute-start(f32[1,528]{1,0:T(1,128)S(1)} %pad_maximum_fusion.3), channel_id=1, source_target_pairs={{0,16},{4,20},{8,24},{12,28},{16,0},{20,4},{24,8},{28,12},{1,17},{... | collective-permute-start | bytes 6344 | tf_op jit(solution)/shard_map/ppermute | solution.py:472
  8.4 5.4 %collective-permute-start.18 = (f32[1,528]{1,0:T(1,128)S(1)}, f32[1,528]{1,0:T(1,128)S(1)}, u32[]{:S(2)}, u32[]{:S(2)}) collective-permute-start(f32[1,528]{1,0:T(1,128)S(1)} %pad_maximum_fusion.3), channel_id=1, source_target_pairs={{0,8},{4,12},{8,16},{12,20},{16,24},{20,28},{24,0},{28,4},{1,9},{5... | collective-permute-start | bytes 6344 | tf_op jit(solution)/shard_map/ppermute | solution.py:472
  16.8 18.7 %copy-start.9 = (bf16[4000,64]{0,1:T(8,128)(2,1)S(1)}, bf16[4000,64]{0,1:T(8,128)(2,1)}, u32[]{:S(2)}) copy-start(bf16[4000,64]{0,1:T(8,128)(2,1)} %param.17) | copy-start | bytes 1536004
  16.8 18.7 %copy-start.10 = (bf16[4000,64]{0,1:T(8,128)(2,1)S(1)}, bf16[4000,64]{0,1:T(8,128)(2,1)}, u32[]{:S(2)}) copy-start(bf16[4000,64]{0,1:T(8,128)(2,1)} %param.18) | copy-start | bytes 1536004
  16.8 12.3 %collective-permute-start.21 = (bf16[2000,128]{1,0:T(8,128)(2,1)S(1)}, bf16[2000,128]{1,0:T(8,128)(2,1)S(1)}, u32[]{:S(2)}, u32[]{:S(2)}) collective-permute-start(bf16[2000,128]{1,0:T(8,128)(2,1)S(1)} %get-tuple-element.384), channel_id=1, source_target_pairs={{0,8},{4,12},{8,0},{12,4},{16,24},{20,28},{24,16},{28,20},{1,9},{5... | collective-permute-start | bytes 1536008 | tf_op jit(solution)/shard_map/ppermute | solution.py:513
  17.0 12.1 %collective-permute-start.22 = (bf16[2000,128]{1,0:T(8,128)(2,1)S(1)}, bf16[2000,128]{1,0:T(8,128)(2,1)S(1)}, u32[]{:S(2)}, u32[]{:S(2)}) collective-permute-start(bf16[2000,128]{1,0:T(8,128)(2,1)S(1)} %get-tuple-element.385), channel_id=1, source_target_pairs={{8,16},{12,20},{16,8},{20,12},{9,17},{13,21},{17,9},{21,13},{10,18... | collective-permute-start | bytes 1536008 | tf_op jit(solution)/shard_map/ppermute | solution.py:513
  29.5 16.4 %collective-permute-start.25 = (bf16[2000,256]{1,0:T(8,128)(2,1)S(1)}, bf16[2000,256]{1,0:T(8,128)(2,1)S(1)}, u32[]{:S(2)}, u32[]{:S(2)}) collective-permute-start(bf16[2000,256]{1,0:T(8,128)(2,1)S(1)} %straighten.1.refs_1_.refs_0_), channel_id=1, source_target_pairs={{8,16},{12,20},{16,8},{20,12},{9,17},{13,21},{17,9},{21,13},{10,18... | collective-permute-start | bytes 3072008 | tf_op jit(solution)/shard_map/ppermute | solution.py:513
  30.3 28.4 %collective-permute-start.23 = (bf16[2000,256]{1,0:T(8,128)(2,1)S(1)}, bf16[2000,256]{1,0:T(8,128)(2,1)S(1)}, u32[]{:S(2)}, u32[]{:S(2)}) collective-permute-start(bf16[2000,256]{1,0:T(8,128)(2,1)S(1)} %straighten.1.refs_1_.refs_0_), channel_id=1, source_target_pairs={{0,8},{4,12},{8,0},{12,4},{16,24},{20,28},{24,16},{28,20},{1,9},{5... | collective-permute-start | bytes 3072008 | tf_op jit(solution)/shard_map/ppermute | solution.py:513
  36.8 0.8 copy-start
  37.7 2.3 %collective-permute-start.27 = (bf16[128,2048]{1,0:T(8,128)(2,1)}, bf16[128,2048]{1,0:T(8,128)(2,1)}, u32[]{:S(2)}, u32[]{:S(2)}) collective-permute-start(bf16[128,2048]{1,0:T(8,128)(2,1)} %get-tuple-element.387), channel_id=1, source_target_pairs={{0,4},{4,0},{8,12},{12,8},{16,20},{20,16},{24,28},{28,24},{1,5},{5... | collective-permute-start | bytes 1572872 | tf_op jit(solution)/shard_map/ppermute | solution.py:436
  39.9 1.0 copy-start.1
  43.0 34.7 %collective-permute-start.29 = (bf16[256,2048]{1,0:T(8,128)(2,1)}, bf16[256,2048]{1,0:T(8,128)(2,1)}, u32[]{:S(2)}, u32[]{:S(2)}) collective-permute-start(bf16[256,2048]{1,0:T(8,128)(2,1)} %stack_panels.1.refs_0_), channel_id=1, source_target_pairs={{0,8},{4,12},{24,16},{28,20},{1,9},{5,13},{25,17},{29,21},{2,10},{... | collective-permute-start | bytes 3145736 | tf_op jit(solution)/shard_map/ppermute | solution.py:513
  46.0 32.0 %collective-permute-start.26 = (bf16[2000,256]{1,0:T(8,128)(2,1)S(1)}, bf16[2000,256]{1,0:T(8,128)(2,1)}, u32[]{:S(2)}, u32[]{:S(2)}) collective-permute-start(bf16[2000,256]{1,0:T(8,128)(2,1)S(1)} %collective-permute-done.25.refs_3_.refs_2_), channel_id=1, source_target_pairs={{8,0},{12,4},{16,24},{20,28},{9,1},{13,5},{17,25},{21,29},{10,2},{... | collective-permute-start | bytes 3072008 | tf_op jit(solution)/shard_map/ppermute | solution.py:513
  58.6 19.3 %collective-permute-start.24 = (bf16[2000,256]{1,0:T(8,128)(2,1)S(1)}, bf16[2000,256]{1,0:T(8,128)(2,1)}, u32[]{:S(2)}, u32[]{:S(2)}) collective-permute-start(bf16[2000,256]{1,0:T(8,128)(2,1)S(1)} %collective-permute-done.23.refs_2_.refs_1_), channel_id=1, source_target_pairs={{8,16},{12,20},{16,8},{20,12},{9,17},{13,21},{17,9},{21,13},{10,18... | collective-permute-start | bytes 3072008 | tf_op jit(solution)/shard_map/ppermute | solution.py:513
  67.1 10.7 %collective-permute-start.28 = (f32[6,4,16,256]{3,2,1,0:T(8,128)S(1)}, f32[6,4,16,256]{3,2,1,0:T(8,128)}, u32[]{:S(2)}, u32[]{:S(2)}) collective-permute-start(f32[6,4,16,256]{3,2,1,0:T(8,128)S(1)} %get-tuple-element.389), channel_id=1, source_target_pairs={{0,4},{4,0},{8,12},{12,8},{16,20},{20,16},{24,28},{28,24},{1,5},{5... | collective-permute-start | bytes 1179656 | tf_op jit(solution)/shard_map/ppermute | solution.py:436
  77.9 39.3 %collective-permute-start.30 = (bf16[2000,256]{1,0:T(8,128)(2,1)}, bf16[2000,256]{1,0:T(8,128)(2,1)}, u32[]{:S(2)}, u32[]{:S(2)}) collective-permute-start(bf16[2000,256]{1,0:T(8,128)(2,1)} %collective-permute-done.24.refs_5_), channel_id=1, source_target_pairs={{8,0},{12,4},{16,24},{20,28},{9,1},{13,5},{17,25},{21,29},{10,2},{... | collective-permute-start | bytes 3072008 | tf_op jit(solution)/shard_map/ppermute | solution.py:513
  79.3 5.4 %copy-start.11 = (f32[6,4,16,256]{3,2,1,0:T(8,128)S(1)}, f32[6,4,16,256]{3,2,1,0:T(8,128)}, u32[]{:S(2)}) copy-start(f32[6,4,16,256]{3,2,1,0:T(8,128)} %get-tuple-element.325.refs_0_) | copy-start | bytes 1179652 | tf_op jit(solution)/shard_map/cond
  83.1 1.6 %collective-permute-start = (f32[4,4,16,256]{3,2,1,0:T(8,128)S(1)}, f32[4,4,16,256]{3,2,1,0:T(8,128)S(1)}, u32[]{:S(2)}, u32[]{:S(2)}) collective-permute-start(f32[4,4,16,256]{3,2,1,0:T(8,128)S(1)} %get-tuple-element.333), channel_id=1, source_target_pairs={{0,4},{4,0},{8,12},{12,8},{16,20},{20,16},{24,28},{28,24},{1,5},{5... | collective-permute-start | bytes 786440 | tf_op jit(solution)/shard_map/cond/branch_1_fun/ppermute | solution.py:436
  85.8 7.1 %collective-permute-start.1 = (f32[10,16,256]{2,1,0:T(8,128)S(1)}, f32[10,16,256]{2,1,0:T(8,128)S(1)}, u32[]{:S(2)}, u32[]{:S(2)}) collective-permute-start(f32[10,16,256]{2,1,0:T(8,128)S(1)} %get-tuple-element.335), channel_id=1, source_target_pairs={{0,1},{1,0},{2,3},{3,2},{4,5},{5,4},{6,7},{7,6},{8,9},{9,8},{10,11... | collective-permute-start | bytes 491528 | tf_op jit(solution)/shard_map/cond/branch_1_fun/ppermute | solution.py:436
  87.3 9.5 %collective-permute-start.2 = (f32[10,16,256]{2,1,0:T(8,128)S(1)}, f32[10,16,256]{2,1,0:T(8,128)S(1)}, u32[]{:S(2)}, u32[]{:S(2)}) collective-permute-start(f32[10,16,256]{2,1,0:T(8,128)S(1)} %get-tuple-element.336), channel_id=1, source_target_pairs={{0,2},{1,3},{2,0},{3,1},{4,6},{5,7},{6,4},{7,5},{8,10},{9,11},{10,... | collective-permute-start | bytes 491528 | tf_op jit(solution)/shard_map/cond/branch_1_fun/ppermute | solution.py:436
  88.8 8.0 %collective-permute-start.3 = (f32[10,16,256]{2,1,0:T(8,128)S(1)}, f32[10,16,256]{2,1,0:T(8,128)S(1)}, u32[]{:S(2)}, u32[]{:S(2)}) collective-permute-start(f32[10,16,256]{2,1,0:T(8,128)S(1)} %get-tuple-element.337), channel_id=1, source_target_pairs={{0,3},{1,2},{2,1},{3,0},{4,7},{5,6},{6,5},{7,4},{8,11},{9,10},{10,... | collective-permute-start | bytes 491528 | tf_op jit(solution)/shard_map/cond/branch_1_fun/ppermute | solution.py:436
  97.0 7.0 %collective-permute-start.6 = (f32[4,32]{1,0:T(4,128)S(1)}, f32[4,32]{1,0:T(4,128)S(1)}, u32[]{:S(2)}, u32[]{:S(2)}) collective-permute-start(f32[4,32]{1,0:T(4,128)S(1)} %select_reduce_fusion), channel_id=1, source_target_pairs={{0,24},{4,28},{8,16},{12,20},{16,8},{20,12},{24,0},{28,4},{1,25},{... | collective-permute-start | bytes 1544 | tf_op jit(solution)/shard_map/cond/branch_1_fun/ppermute | solution.py:436
  99.2 6.3 %collective-permute-start.5 = (f32[4,32]{1,0:T(4,128)S(1)}, f32[4,32]{1,0:T(4,128)S(1)}, u32[]{:S(2)}, u32[]{:S(2)}) collective-permute-start(f32[4,32]{1,0:T(4,128)S(1)} %select_reduce_fusion), channel_id=1, source_target_pairs={{0,16},{4,20},{8,24},{12,28},{16,0},{20,4},{24,8},{28,12},{1,17},{... | collective-permute-start | bytes 1544 | tf_op jit(solution)/shard_map/cond/branch_1_fun/ppermute | solution.py:436
  103.9 4.1 %collective-permute-start.4 = (f32[36,256]{1,0:T(8,128)S(1)}, f32[36,256]{1,0:T(8,128)S(1)}, u32[]{:S(2)}, u32[]{:S(2)}) collective-permute-start(f32[36,256]{1,0:T(8,128)S(1)} %select_maximum_fusion), channel_id=1, source_target_pairs={{0,8},{4,12},{8,0},{12,4},{16,24},{20,28},{24,16},{28,20},{1,9},{5... | collective-permute-start | bytes 110600 | tf_op jit(solution)/shard_map/cond/branch_1_fun/ppermute | solution.py:436
  108.2 4.9 %collective-permute-start.9 = (bf16[8,1,16,128]{3,2,1,0:T(8,128)(2,1)S(1)}, bf16[8,1,16,128]{3,2,1,0:T(8,128)(2,1)S(1)}, u32[]{:S(2)}, u32[]{:S(2)}) collective-permute-start(bf16[8,1,16,128]{3,2,1,0:T(8,128)(2,1)S(1)} %bitcast.67), channel_id=1, source_target_pairs={{0,3},{1,2},{2,1},{3,0},{4,7},{5,6},{6,5},{7,4},{8,11},{9,10},{10,... | collective-permute-start | bytes 98312 | tf_op jit(solution)/shard_map/cond/branch_1_fun/ppermute | solution.py:436
  109.8 3.9 %collective-permute-start.8 = (bf16[8,1,16,128]{3,2,1,0:T(8,128)(2,1)S(1)}, bf16[8,1,16,128]{3,2,1,0:T(8,128)(2,1)S(1)}, u32[]{:S(2)}, u32[]{:S(2)}) collective-permute-start(bf16[8,1,16,128]{3,2,1,0:T(8,128)(2,1)S(1)} %bitcast.68), channel_id=1, source_target_pairs={{0,2},{1,3},{2,0},{3,1},{4,6},{5,7},{6,4},{7,5},{8,10},{9,11},{10,... | collective-permute-start | bytes 98312 | tf_op jit(solution)/shard_map/cond/branch_1_fun/ppermute | solution.py:436
  111.0 3.9 %collective-permute-start.7 = (bf16[8,1,16,128]{3,2,1,0:T(8,128)(2,1)S(1)}, bf16[8,1,16,128]{3,2,1,0:T(8,128)(2,1)S(1)}, u32[]{:S(2)}, u32[]{:S(2)}) collective-permute-start(bf16[8,1,16,128]{3,2,1,0:T(8,128)(2,1)S(1)} %bitcast.69), channel_id=1, source_target_pairs={{0,1},{1,0},{2,3},{3,2},{4,5},{5,4},{6,7},{7,6},{8,9},{9,8},{10,11... | collective-permute-start | bytes 98312 | tf_op jit(solution)/shard_map/cond/branch_1_fun/ppermute | solution.py:436
  115.5 1.7 %collective-permute-start.10 = (bf16[8,4,16,128]{3,2,1,0:T(8,128)(2,1)}, bf16[8,4,16,128]{3,2,1,0:T(8,128)(2,1)}, u32[]{:S(2)}, u32[]{:S(2)}) collective-permute-start(bf16[8,4,16,128]{3,2,1,0:T(8,128)(2,1)} %in_order.1), channel_id=1, source_target_pairs={{0,4},{4,0},{8,12},{12,8},{16,20},{20,16},{24,28},{28,24},{1,5},{5... | collective-permute-start | bytes 393224 | tf_op jit(solution)/shard_map/cond/branch_1_fun/ppermute | solution.py:436
  117.2 5.8 %copy-start.12 = (s32[8,32]{1,0:T(8,128)S(1)}, s32[8,32]{1,0:T(8,128)}, u32[]{:S(2)}) copy-start(s32[8,32]{1,0:T(8,128)} %param.21) | copy-start | bytes 3076
  122.0 0.8 copy-start.2
  122.8 2.1 %collective-permute-start.31 = (f32[64,2000]{1,0:T(8,128)}, f32[64,2000]{1,0:T(8,128)S(1)}, u32[]{:S(2)}, u32[]{:S(2)}) collective-permute-start(f32[64,2000]{1,0:T(8,128)} %get-tuple-element.400), channel_id=1, source_target_pairs={{0,4},{4,0},{8,12},{12,8},{16,20},{20,16},{24,28},{28,24},{1,5},{5... | collective-permute-start | bytes 1536008 | tf_op jit(solution)/shard_map/ppermute | solution.py:436
  123.0 2.0 %copy-start.3 = (f32[64,2000]{1,0:T(8,128)S(1)}, f32[64,2000]{1,0:T(8,128)}, u32[]{:S(2)}) copy-start(f32[64,2000]{1,0:T(8,128)} %copy-done.2) | copy-start | bytes 1536004
  125.8 1.0 copy-start.8

commit v2 on v1

--- a/solution.py
+++ b/solution.py
@@ -214,11 +214,6 @@
     return total
 
 
-def steps_over(half):
-    step = half if half <= 512 else 512
-    return step, -(-half // step)
-
-
 def split_sum(pairs, occ):
     _, shares, piece, both = pairs[0][0].shape
     tiles = sum(keep.shape[0] for keep, _ in pairs)
@@ -251,52 +246,28 @@
     panels = distinct([p for p, _ in jobs])
     arrays = distinct([x for _, window in jobs for x in window])
     count = len(panels)
-    step, steps = steps_over(half)
-    padded = panels[0].shape[1]
 
     def body(core_ref, *refs):
-        panel_refs, array_refs = refs[:count], refs[count:-4]
-        keep_ref, give_ref, total_ref, terms_ref = refs[-4:]
-        i = pl.program_id(0)
-
-        @pl.when(i == 0)
-        def _():
-            total_ref[...] = jnp.zeros_like(total_ref)
-
-        inside = lax.broadcasted_iota(jnp.int32, (step, rows), 0) + i * step < half
-        for s, (panel, window) in enumerate(jobs):
+        panel_refs, array_refs = refs[:count], refs[count:-3]
+        keep_ref, give_ref, terms_ref = refs[-3:]
+        q = 0
+        for panel, window in jobs:
             panel_ref = panel_refs[[id(p) for p in panels].index(id(panel))]
             value = read_window(window, arrays, array_refs)
-            if steps * step != half:
-                value = jnp.where(inside, value, jnp.zeros_like(value))
-            part = panel_ref[:, :step]
-            total_ref[s] += jnp.dot(part, value, preferred_element_type=F32)
-
-        @pl.when(i == steps - 1)
-        def _():
-            q = 0
-            for s in range(len(jobs)):
-                turned = total_ref[s].T
-                for j in range(0, rows, tile):
-                    terms_ref[q] = turned[j : j + tile].reshape(2, shares // 2, piece, both)
-                    keep_ref[q] = terms_ref[q, core_ref[0]]
-                    give_ref[q] = terms_ref[q, 1 - core_ref[0]]
-                    q += 1
+            turned = jnp.dot(panel_ref[:, :half], value, preferred_element_type=F32).T
+            for j in range(0, rows, tile):
+                terms_ref[q] = turned[j : j + tile].reshape(2, shares // 2, piece, both)
+                keep_ref[q] = terms_ref[q, core_ref[0]]
+                give_ref[q] = terms_ref[q, 1 - core_ref[0]]
+                q += 1
 
     shape = jax.ShapeDtypeStruct((tiles, shares // 2, piece, both), F32)
-    panel_step = step if steps > 1 else padded
-    return pl.pallas_call(
-        body,
-        grid=(steps,),
+    return pl.pallas_call(
+        body,
         out_shape=(shape, shape),
-        in_specs=[SCALARS]
-        + [pl.BlockSpec((both, panel_step), lambda i: (0, i))] * count
-        + [pl.BlockSpec((step, rows), lambda i: (i, 0))] * len(arrays),
-        out_specs=(pl.BlockSpec(shape.shape, lambda i: (0, 0, 0, 0)),) * 2,
-        scratch_shapes=[
-            pltpu.VMEM((len(jobs), both, rows), F32),
-            pltpu.VMEM((tiles, 2, shares // 2, piece, both), F32),
-        ],
+        in_specs=[SCALARS] + [WHOLE] * (count + len(arrays)),
+        out_specs=(WHOLE, WHOLE),
+        scratch_shapes=[pltpu.VMEM((tiles, 2, shares // 2, piece, both), F32)],
         compiler_params=pltpu.CompilerParams(vmem_limit_bytes=12 * MIB),
         name="project",
         cost_estimate=pl.CostEstimate(
@@ -329,45 +300,33 @@
     half, rows = windows[0][0].shape
     own = columns // 2
     arrays = distinct([x for window in windows for x in window])
-    step, steps = steps_over(half)
     per_window = tiles // len(windows)
 
     def body(core_ref, kernel_ref, got_ref, *refs):
-        array_refs = refs[:-4]
-        mine_ref, other_ref, order_ref, turned_ref = refs[-4:]
+        array_refs = refs[:-3]
+        mine_ref, other_ref, order_ref = refs[-3:]
         first = core_ref[0] == 0
-
-        @pl.when(pl.program_id(0) == 0)
-        def _():
-            order_ref[:, core_ref[0]] = kernel_ref[...].astype(F32)
-            order_ref[:, 1 - core_ref[0]] = got_ref[...].astype(F32)
-            for s in range(len(windows)):
-                part = order_ref[s * per_window : (s + 1) * per_window]
-                turned_ref[s] = part.reshape(rows, columns).astype(BF16)
-
+        order_ref[:, core_ref[0]] = kernel_ref[...].astype(F32)
+        order_ref[:, 1 - core_ref[0]] = got_ref[...].astype(F32)
         total = None
         for s, window in enumerate(windows):
+            part = order_ref[s * per_window : (s + 1) * per_window]
+            part = part.reshape(rows, columns).astype(BF16)
             value = read_window(window, arrays, array_refs)
-            term = jnp.dot(value, turned_ref[s], preferred_element_type=F32)
+            term = jnp.dot(value, part, preferred_element_type=F32)
             total = term if total is None else total + term
         total = total.T
         mine_ref[...] = jnp.where(first, total[:own], total[own:])
         other_ref[...] = jnp.where(first, total[own:], total[:own])
 
     shape = jax.ShapeDtypeStruct((own, half), F32)
-    whole = pl.BlockSpec(kernel.shape, lambda i: (0, 0, 0, 0))
-    return pl.pallas_call(
-        body,
-        grid=(steps,),
+    return pl.pallas_call(
+        body,
         out_shape=(shape, shape),
-        in_specs=[SCALARS, whole, whole]
-        + [pl.BlockSpec((step, rows), lambda i: (i, 0))] * len(arrays),
-        out_specs=(pl.BlockSpec((own, step), lambda i: (0, i)),) * 2,
-        scratch_shapes=[
-            pltpu.VMEM((tiles, 2, shares, piece, columns), F32),
-            pltpu.VMEM((len(windows), rows, columns), BF16),
-        ],
-        compiler_params=pltpu.CompilerParams(vmem_limit_bytes=12 * MIB),
+        in_specs=[SCALARS] + [WHOLE] * (2 + len(arrays)),
+        out_specs=(WHOLE, WHOLE),
+        scratch_shapes=[pltpu.VMEM((tiles, 2, shares, piece, columns), F32)],
+        compiler_params=pltpu.CompilerParams(vmem_limit_bytes=20 * MIB),
         name="contract",
         cost_estimate=pl.CostEstimate(
             flops=2 * columns * half * rows * len(windows),
@@ -580,10 +539,14 @@
     early_jobs, late_jobs = sum(stages[1:-1], []), stages[-1]
     early_at = jnp.stack([at for _, at in early_jobs])
     late_at = late_jobs[0][1][None]
+    own_job = stages[0][0]
     early_jobs = stages[0] + early_jobs
     early_at = jnp.concatenate((chip[None], early_at))
 
-    early_pair = halved([(panels, w) for w, _ in early_jobs])
+    early_value = summed(
+        [halved([(panels, own_job[0])]), halved([(panels, w) for w, _ in early_jobs[1:]])]
+    )
+    early_density = shared_density(early_value, early_at)
 
     at = (
         (window_iota * rows)[:, None, None]
@@ -598,8 +561,18 @@
     here = (places[:, None] == window_iota[None, :])[:, :, None]
     weight_here = jnp.sum(jnp.where(here, weight[None], 0.0), axis=1)[:, :, None]
 
-    late, by_a, early_pair, far_panels, weight_here, fits = lax.optimization_barrier(
-        (by_b, by_a, early_pair, far_panels, weight_here, fits.astype(jnp.int32))
+    late, by_a, early_value, early_density, far_panels, weight_here, fits = (
+        lax.optimization_barrier(
+            (
+                by_b,
+                by_a,
+                early_value,
+                early_density,
+                far_panels,
+                weight_here,
+                fits.astype(jnp.int32),
+            )
+        )
     )
     fits = fits != 0
     late = sent(late, homes)
@@ -607,9 +580,9 @@
     late_jobs = [(panels, late_window), (far_panels, [by_b])]
 
     def kernel_of_all():
-        value = summed([early_pair, halved(late_jobs)])
-        density = shared_density(value, jnp.concatenate((early_at, late_at, late_at)))
-        value, far_value = value[:-1], value[-1:]
+        value = summed([halved(late_jobs)])
+        density = early_density + shared_density(value, jnp.concatenate((late_at, late_at)))
+        value, far_value = jnp.concatenate((early_value, value[:1])), value[1:]
         packed = jnp.concatenate(
             (far_value[0], jnp.pad(density, ((0, 0), (0, 4 * columns - points)))), axis=0
         )
@@ -635,27 +608,23 @@
         else:
             for bit in occ_bits:
                 kernel = doubled(kernel, "occ", bit, 1)
-        return kernel, flip(kernel, "grid", 1)
-
-    no_kernel = jnp.zeros((places.shape[0] * per_window, occ_count, piece, 2 * columns), BF16)
-    kernel, got_kernel = lax.cond(fits, kernel_of_all, lambda: (no_kernel, no_kernel))
+        return kernel, flip(kernel, "grid", 1), unwritten((columns, cols))
+
+    scale = 1.0 / math.sqrt(rows * grid_count)
+
+    def result_for_any_sizes():
+        whole = any_sizes(
+            orbital_values, occupied, trial, point_weights, batch_sizes, significant
+        )
+        none = jnp.zeros((places.shape[0] * per_window, occ_count, piece, 2 * columns), BF16)
+        return none, none, whole * scale
+
+    kernel, got_kernel, other = lax.cond(fits, kernel_of_all, result_for_any_sizes)
     early_windows = [w for w, _ in early_jobs]
     early_windows[2] = early_windows[2] + [late]
     windows = early_windows + [late_window]
     ours, theirs = contract(kernel, got_kernel, windows, core)
     back = flip(theirs, "grid", 1)
-    scale = 1.0 / math.sqrt(rows * grid_count)
-    other = lax.cond(
-        fits,
-        lambda *given: unwritten((columns, cols)),
-        lambda *given: any_sizes(*given) * scale,
-        orbital_values,
-        occupied,
-        trial,
-        point_weights,
-        batch_sizes,
-        significant,
-    )
     return finish(core, fits, ours, back, other, scale).T
 
 

time: 127 us -> 139 us (1.094)
  starting transfers between devices: 35.5 us -> 41.8 us
  waiting for transfers between devices: 56.5 us -> 58.9 us
  Pallas kernels: 23.5 us -> 25.1 us
    ppermute x18 -> x22, starting transfers between devices: 15.3 us -> 20.5 us  [flip(): return lax.ppermute(x, axis, [(i, i ^ bit) for i in range(count)])]
    ppermute x18 -> x22, waiting for transfers between devices: 21.2 us -> 25.8 us  [flip(): return lax.ppermute(x, axis, [(i, i ^ bit) for i in range(count)])]
    ppermute x3, waiting for transfers between devices: 2.4 us -> 0.01 us  [per_device(): heard.append(lax.ppermute(told, 'grid', around))]
    pallas_call x3 -> x4, Pallas kernels: 12.9 us -> 11.6 us  [the longest x3 8.3 us: project(): pl.pallas_call(body, out_shape=(shape, shape), in_specs=[SCALARS] + [WHOL...]
    unnamed x23 -> x19, local copies, waits for them, and re-layouts: 3.73 us -> 3.84 us
  transfers between devices with their start and end apart: 29 -> 33, of which waited for: 17 -> 19; matrix products, arithmetic and copies ran while one was open for 5% -> 5% of each run, Pallas kernels for 12% -> 14%
where the time goes in v2:
time: 139 us; the launch traced here: 138 us
  waiting for transfers between devices  58.9 us (42%)
  starting transfers between devices  41.8 us (30%)
  Pallas kernels  25.1 us (18%)
  local copies, waits for them, and re-layouts  5.81 us (4%)
  other arithmetic  4.58 us (3%)
  between operations  1.72 us (1%)
    ppermute x8, waiting for transfers between devices, sent(): return lax.ppermute(x, 'grid', along(pairs))  33.1 us
    ppermute x22, waiting for transfers between devices, flip(): return lax.ppermute(x, axis, [(i, i ^ bit) for i in range(count)])  25.8 us
    ppermute x22, starting transfers between devices, flip(): return lax.ppermute(x, axis, [(i, i ^ bit) for i in range(count)])  20.5 us
    ppermute x8, starting transfers between devices, sent(): return lax.ppermute(x, 'grid', along(pairs))  14.5 us
    pallas_call x3, Pallas kernels, project(): pl.pallas_call(body, out_shape=(shape, shape), in_specs=[SCALARS] + [WHOL...  8.3 us
    ppermute x3, starting transfers between devices, per_device(): heard.append(lax.ppermute(told, 'grid', around))  6.88 us
    unnamed x19, local copies, waits for them, and re-layouts  3.84 us
    pallas_call x1, Pallas kernels, contract(): pl.pallas_call(body, out_shape=(shape, shape), in_specs=[SCALARS] + [WHOL...  3.29 us
  transfers between devices with their start and end apart: 33, of which 19 were waited for; matrix products, arithmetic and copies ran while one was open for 5% of the time, Pallas kernels for 14%

profile of v2, /device:TPU:0, one launch (start us, length us, event | category | flops | bytes accessed | tf_op | source)
XLA Modules:
  0.0 138.2 jit_solution(10642278510988024499)
XLA Ops:
  0.0 1.3 half_of.3
  2.6 1.5 %collective-permute-done.16 = s32[1,8]{1,0:T(1,128)S(1)} collective-permute-done((s32[1,8]{1,0:T(1,128)S(1)}, s32[1,8]{1,0:T(1,128)S(1)}, u32[]{:S(2)}, u32[]{:S(2)}) %collective-permute-start.16) | collective-permute-done | bytes 64 | tf_op jit(solution)/shard_map/ppermute | solution.py:395
  4.2 2.9 %collective-permute-start.18 = (f32[1,528]{1,0:T(1,128)S(1)}, f32[1,528]{1,0:T(1,128)S(1)}, u32[]{:S(2)}, u32[]{:S(2)}) collective-permute-start(f32[1,528]{1,0:T(1,128)S(1)} %pad_maximum_fusion.3), channel_id=1, source_target_pairs={{0,8},{4,12},{8,16},{12,20},{16,24},{20,28},{24,0},{28,4},{1,9},{5... | collective-permute-start | bytes 6344 | tf_op jit(solution)/shard_map/ppermute | solution.py:431
  7.2 2.6 %collective-permute-start.19 = (f32[1,528]{1,0:T(1,128)S(1)}, f32[1,528]{1,0:T(1,128)S(1)}, u32[]{:S(2)}, u32[]{:S(2)}) collective-permute-start(f32[1,528]{1,0:T(1,128)S(1)} %pad_maximum_fusion.3), channel_id=1, source_target_pairs={{0,16},{4,20},{8,24},{12,28},{16,0},{20,4},{24,8},{28,12},{1,17},{... | collective-permute-start | bytes 6344 | tf_op jit(solution)/shard_map/ppermute | solution.py:431
  9.8 1.3 collective-permute-start.20
  11.1 1.2 half_of.2.mine_ref
  12.7 2.5 %panel_halves.1 = (bf16[128,2048]{1,0:T(8,128)(2,1)S(1)}, bf16[128,2048]{1,0:T(8,128)(2,1)}) custom-call(s32[1]{0:T(128)} %bitcast.10.which_ref.core_ref, bf16[64,4000]{1,0:T(8,128)(2,1)} %bitcast.74, bf16[64,4000]{1,0:T(8,128)(2,1)} %bitcast.75), custom_call_target="tpu_custom_call" | custom-call | tf_op jit(solution)/shard_map/panel_halves/pallas_call | solution.py:171
  15.2 0.8 copy-done
  17.5 1.8 %compact.1 = (bf16[2000,128]{1,0:T(8,128)(2,1)S(1)}, bf16[2000,128]{1,0:T(8,128)(2,1)S(1)}, bf16[2000,128]{1,0:T(8,128)(2,1)S(1)}, bf16[2000,128]{1,0:T(8,128)(2,1)S(1)}) custom-call(s32[1]{0:T(128)} %bitcast.11.odd_ref, bf16[2000,256]{1,0:T(8,128)(2,1)S(1)} %half_of.2.mine_ref, bf16[2000,256]{1,0:T(8,128)(2,1)S(1)} %collective-permute-done.14.got_ref, ...), custom_call_target="tpu_custom_call" | custom-call | flops 1048576000 | bytes 4096000 | tf_op jit(solution)/shard_map/compact/pallas_call | solution.py:118
  19.3 0.7 collective-permute-start.21
  20.9 12.5 %collective-permute-done.21.refs_2_ = bf16[2000,128]{1,0:T(8,128)(2,1)S(1)} collective-permute-done((bf16[2000,128]{1,0:T(8,128)(2,1)S(1)}, bf16[2000,128]{1,0:T(8,128)(2,1)S(1)}, u32[]{:S(2)}, u32[]{:S(2)}) %collective-permute-start.21) | collective-permute-done | bytes 512032 | tf_op jit(solution)/shard_map/ppermute | solution.py:472
  33.9 3.7 %collective-permute-start.23 = (bf16[2000,256]{1,0:T(8,128)(2,1)S(1)}, bf16[2000,256]{1,0:T(8,128)(2,1)S(1)}, u32[]{:S(2)}, u32[]{:S(2)}) collective-permute-start(bf16[2000,256]{1,0:T(8,128)(2,1)S(1)} %straighten.1.refs_1_.refs_0_), channel_id=1, source_target_pairs={{0,8},{4,12},{8,0},{12,4},{16,24},{20,28},{24,16},{28,20},{1,9},{5... | collective-permute-start | bytes 3072008 | tf_op jit(solution)/shard_map/ppermute | solution.py:472
  37.6 0.7 collective-permute-start.25
  38.9 1.0 copy-done.1
  40.0 2.2 %stack_panels.1.refs_0_ = bf16[256,2048]{1,0:T(8,128)(2,1)} custom-call(s32[1]{0:T(128)} %bitcast.10.which_ref.core_ref, bf16[128,2048]{1,0:T(8,128)(2,1)S(1)} %copy-done.1, bf16[128,2048]{1,0:T(8,128)(2,1)} %collective-permute-done.27.got_ref), custom_call_target="tpu_custom_call" | custom-call | tf_op jit(solution)/shard_map/stack_panels/pallas_call | solution.py:194
  42.1 4.4 %collective-permute-start.33 = (bf16[256,2048]{1,0:T(8,128)(2,1)}, bf16[256,2048]{1,0:T(8,128)(2,1)}, u32[]{:S(2)}, u32[]{:S(2)}) collective-permute-start(bf16[256,2048]{1,0:T(8,128)(2,1)} %stack_panels.1.refs_0_), channel_id=1, source_target_pairs={{0,8},{4,12},{24,16},{28,20},{1,9},{5,13},{25,17},{29,21},{2,10},{... | collective-permute-start | bytes 3145736 | tf_op jit(solution)/shard_map/ppermute | solution.py:472
  46.5 14.1 %collective-permute-done.23.refs_1_ = bf16[2000,256]{1,0:T(8,128)(2,1)S(1)} collective-permute-done((bf16[2000,256]{1,0:T(8,128)(2,1)S(1)}, bf16[2000,256]{1,0:T(8,128)(2,1)S(1)}, u32[]{:S(2)}, u32[]{:S(2)}) %collective-permute-start.23) | collective-permute-done | bytes 1024032 | tf_op jit(solution)/shard_map/ppermute | solution.py:472
  60.6 2.8 %project.5 = (f32[4,4,16,256]{3,2,1,0:T(8,128)S(1)}, f32[4,4,16,256]{3,2,1,0:T(8,128)}) custom-call(s32[1]{0:T(128)} %bitcast.10.which_ref.core_ref, bf16[256,2048]{1,0:T(8,128)(2,1)} %stack_panels.1.refs_0_, bf16[2000,256]{1,0:T(8,128)(2,1)S(1)} %collective-permute-done.23.refs_1_, bf16[2000,256]{1,0:T(8,128)(2,1)S(1)} %collective-permute-done.25.refs_2_), custom_call_target="tpu_custom_call" | custom-call | flops 524288000 | bytes 3596288 | tf_op jit(solution)/shard_map/project/pallas_call | solution.py:265
  63.5 1.7 %collective-permute-start.24 = (bf16[2000,256]{1,0:T(8,128)(2,1)S(1)}, bf16[2000,256]{1,0:T(8,128)(2,1)}, u32[]{:S(2)}, u32[]{:S(2)}) collective-permute-start(bf16[2000,256]{1,0:T(8,128)(2,1)S(1)} %collective-permute-done.23.refs_1_), channel_id=1, source_target_pairs={{8,16},{12,20},{16,8},{20,12},{9,17},{13,21},{17,9},{21,13},{10,18... | collective-permute-start | bytes 3072008 | tf_op jit(solution)/shard_map/ppermute | solution.py:472
  65.2 1.3 collective-permute-start.26
  66.7 2.4 %project.4 = (f32[2,4,16,256]{3,2,1,0:T(8,128)S(1)}, f32[2,4,16,256]{3,2,1,0:T(8,128)}) custom-call(s32[1]{0:T(128)} %bitcast.10.which_ref.core_ref, bf16[256,2048]{1,0:T(8,128)(2,1)} %stack_panels.1.refs_0_, bf16[2000,256]{1,0:T(8,128)(2,1)S(1)} %straighten.1.refs_1_.refs_0_), custom_call_target="tpu_custom_call" | custom-call | flops 262144000 | bytes 2310144 | tf_op jit(solution)/shard_map/project/pallas_call | solution.py:265
  71.2 1.7 %split_sum.3 = (f32[6,16,256]{2,1,0:T(8,128)S(1)}, f32[6,16,256]{2,1,0:T(8,128)}, f32[6,16,256]{2,1,0:T(8,128)S(1)}, f32[6,16,256]{2,1,0:T(8,128)S(1)}) custom-call(s32[1]{0:T(128)} %bitcast.20.occ_ref, f32[2,4,16,256]{3,2,1,0:T(8,128)S(1)} %get-tuple-element.389.refs_0_, f32[2,4,16,256]{3,2,1,0:T(8,128)} %collective-permute-done.28.refs_1_, ...), custom_call_target="tpu_custom_call" | custom-call | tf_op jit(solution)/shard_map/split_sum/pallas_call | solution.py:231
  74.9 1.5 %collective-permute-start.30 = (f32[6,16,256]{2,1,0:T(8,128)}, f32[6,16,256]{2,1,0:T(8,128)S(1)}, u32[]{:S(2)}, u32[]{:S(2)}) collective-permute-start(f32[6,16,256]{2,1,0:T(8,128)} %get-tuple-element.394), channel_id=1, source_target_pairs={{0,1},{1,0},{2,3},{3,2},{4,5},{5,4},{6,7},{7,6},{8,9},{9,8},{10,11... | collective-permute-start | bytes 294920 | tf_op jit(solution)/shard_map/ppermute | solution.py:395
  77.6 1.6 %collective-permute-start.31 = (f32[6,16,256]{2,1,0:T(8,128)}, f32[6,16,256]{2,1,0:T(8,128)S(1)}, u32[]{:S(2)}, u32[]{:S(2)}) collective-permute-start(f32[6,16,256]{2,1,0:T(8,128)} %copy-done.4), channel_id=1, source_target_pairs={{0,2},{1,3},{2,0},{3,1},{4,6},{5,7},{6,4},{7,5},{8,10},{9,11},{10,... | collective-permute-start | bytes 294920 | tf_op jit(solution)/shard_map/ppermute | solution.py:395
  79.9 2.4 %collective-permute-start.32 = (f32[6,16,256]{2,1,0:T(8,128)}, f32[6,16,256]{2,1,0:T(8,128)S(1)}, u32[]{:S(2)}, u32[]{:S(2)}) collective-permute-start(f32[6,16,256]{2,1,0:T(8,128)} %copy-done.3), channel_id=1, source_target_pairs={{0,3},{1,2},{2,1},{3,0},{4,7},{5,6},{6,5},{7,4},{8,11},{9,10},{10,... | collective-permute-start | bytes 294920 | tf_op jit(solution)/shard_map/ppermute | solution.py:395
  82.5 3.1 %collective-permute-done.32 = f32[6,16,256]{2,1,0:T(8,128)S(1)} collective-permute-done((f32[6,16,256]{2,1,0:T(8,128)}, f32[6,16,256]{2,1,0:T(8,128)S(1)}, u32[]{:S(2)}, u32[]{:S(2)}) %collective-permute-start.32) | collective-permute-done | bytes 98336 | tf_op jit(solution)/shard_map/ppermute | solution.py:395
  85.6 0.9 add_add_fusion.1
  86.7 6.5 %collective-permute-done.26.refs_4_ = bf16[2000,256]{1,0:T(8,128)(2,1)} collective-permute-done((bf16[2000,256]{1,0:T(8,128)(2,1)S(1)}, bf16[2000,256]{1,0:T(8,128)(2,1)}, u32[]{:S(2)}, u32[]{:S(2)}) %collective-permute-start.26) | collective-permute-done | bytes 1024032 | tf_op jit(solution)/shard_map/ppermute | solution.py:472
  93.2 1.3 collective-permute-start.34
  94.5 36.5 %conditional.1 = (bf16[8,4,16,128]{3,2,1,0:T(8,128)(2,1)}, bf16[8,4,16,128]{3,2,1,0:T(8,128)(2,1)}, f32[64,4000]{1,0:T(8,128)}) conditional(s32[]{:T(128)} %convert_element_type.52, (s32[8]{0:T(128)S(1)}, f32[256]{0:T(256)S(1)}, bf16[4000,64]{0,1:T(8,128)(2,1)}, bf16[4000,64]{0,1:T(8,128)(2,1)}, s32[8,32]{1,0:T(8,128)S(1)}, ...), branch_computations={%region_8.16_spmd, %region_16.20_spmd} | conditional | flops 524522304 | bytes 65907736 | solution.py:622
  94.7 3.0 %project.3 = (f32[4,4,16,256]{3,2,1,0:T(8,128)S(1)}, f32[4,4,16,256]{3,2,1,0:T(8,128)S(1)}) custom-call(s32[1]{0:T(128)} %bitcast.4.core_ref, bf16[256,2048]{1,0:T(8,128)(2,1)} %get-tuple-element.346.refs_0_, bf16[256,2048]{1,0:T(8,128)(2,1)} %get-tuple-element.347.refs_1_, bf16[2000,256]{1,0:T(8,128)(2,1)} %get-tuple-element.348.refs_2_, ...), custom_call_target="tpu_custom_call" | custom-call | flops 524288000 | bytes 3596288 | tf_op jit(solution)/shard_map/cond/branch_1_fun/project/pallas_call | solution.py:265
  97.9 1.4 %collective-permute-done.refs_1_ = f32[4,4,16,256]{3,2,1,0:T(8,128)S(1)} collective-permute-done((f32[4,4,16,256]{3,2,1,0:T(8,128)S(1)}, f32[4,4,16,256]{3,2,1,0:T(8,128)S(1)}, u32[]{:S(2)}, u32[]{:S(2)}) %collective-permute-start) | collective-permute-done | bytes 262176 | tf_op jit(solution)/shard_map/cond/branch_1_fun/ppermute | solution.py:395
  99.4 1.6 %collective-permute-start.1 = (f32[4,16,256]{2,1,0:T(8,128)S(1)}, f32[4,16,256]{2,1,0:T(8,128)S(1)}, u32[]{:S(2)}, u32[]{:S(2)}) collective-permute-start(f32[4,16,256]{2,1,0:T(8,128)S(1)} %get-tuple-element.353), channel_id=1, source_target_pairs={{0,1},{1,0},{2,3},{3,2},{4,5},{5,4},{6,7},{7,6},{8,9},{9,8},{10,11... | collective-permute-start | bytes 196616 | tf_op jit(solution)/shard_map/cond/branch_1_fun/ppermute | solution.py:395
  100.9 1.5 %collective-permute-start.2 = (f32[4,16,256]{2,1,0:T(8,128)S(1)}, f32[4,16,256]{2,1,0:T(8,128)S(1)}, u32[]{:S(2)}, u32[]{:S(2)}) collective-permute-start(f32[4,16,256]{2,1,0:T(8,128)S(1)} %get-tuple-element.354), channel_id=1, source_target_pairs={{0,2},{1,3},{2,0},{3,1},{4,6},{5,7},{6,4},{7,5},{8,10},{9,11},{10,... | collective-permute-start | bytes 196616 | tf_op jit(solution)/shard_map/cond/branch_1_fun/ppermute | solution.py:395
  103.7 1.5 %collective-permute-done.2 = f32[4,16,256]{2,1,0:T(8,128)S(1)} collective-permute-done((f32[4,16,256]{2,1,0:T(8,128)S(1)}, f32[4,16,256]{2,1,0:T(8,128)S(1)}, u32[]{:S(2)}, u32[]{:S(2)}) %collective-permute-start.2) | collective-permute-done | bytes 65568 | tf_op jit(solution)/shard_map/cond/branch_1_fun/ppermute | solution.py:395
  105.2 2.4 %collective-permute-done.3 = f32[4,16,256]{2,1,0:T(8,128)S(1)} collective-permute-done((f32[4,16,256]{2,1,0:T(8,128)S(1)}, f32[4,16,256]{2,1,0:T(8,128)S(1)}, u32[]{:S(2)}, u32[]{:S(2)}) %collective-permute-start.3) | collective-permute-done | bytes 65568 | tf_op jit(solution)/shard_map/cond/branch_1_fun/ppermute | solution.py:395
  107.8 4.4 %collective-permute-start.5 = (f32[4,32]{1,0:T(4,128)S(1)}, f32[4,32]{1,0:T(4,128)S(1)}, u32[]{:S(2)}, u32[]{:S(2)}) collective-permute-start(f32[4,32]{1,0:T(4,128)S(1)} %add.231), channel_id=1, source_target_pairs={{0,16},{4,20},{8,24},{12,28},{16,0},{20,4},{24,8},{28,12},{1,17},{... | collective-permute-start | bytes 1544 | tf_op jit(solution)/shard_map/cond/branch_1_fun/ppermute | solution.py:395
  112.2 1.5 %collective-permute-start.6 = (f32[4,32]{1,0:T(4,128)S(1)}, f32[4,32]{1,0:T(4,128)S(1)}, u32[]{:S(2)}, u32[]{:S(2)}) collective-permute-start(f32[4,32]{1,0:T(4,128)S(1)} %add.231), channel_id=1, source_target_pairs={{0,24},{4,28},{8,16},{12,20},{16,8},{20,12},{24,0},{28,4},{1,25},{... | collective-permute-start | bytes 1544 | tf_op jit(solution)/shard_map/cond/branch_1_fun/ppermute | solution.py:395
  113.9 3.8 %collective-permute-done.6 = f32[4,32]{1,0:T(4,128)S(1)} collective-permute-done((f32[4,32]{1,0:T(4,128)S(1)}, f32[4,32]{1,0:T(4,128)S(1)}, u32[]{:S(2)}, u32[]{:S(2)}) %collective-permute-start.6) | collective-permute-done | bytes 544 | tf_op jit(solution)/shard_map/cond/branch_1_fun/ppermute | solution.py:395
  117.7 2.8 %collective-permute-done.4 = f32[36,256]{1,0:T(8,128)S(1)} collective-permute-done((f32[36,256]{1,0:T(8,128)S(1)}, f32[36,256]{1,0:T(8,128)S(1)}, u32[]{:S(2)}, u32[]{:S(2)}) %collective-permute-start.4) | collective-permute-done | bytes 36896 | tf_op jit(solution)/shard_map/cond/branch_1_fun/ppermute | solution.py:395
  120.7 1.6 %collective-permute-start.7 = (bf16[8,1,16,128]{3,2,1,0:T(8,128)(2,1)S(1)}, bf16[8,1,16,128]{3,2,1,0:T(8,128)(2,1)S(1)}, u32[]{:S(2)}, u32[]{:S(2)}) collective-permute-start(bf16[8,1,16,128]{3,2,1,0:T(8,128)(2,1)S(1)} %bitcast.68), channel_id=1, source_target_pairs={{0,1},{1,0},{2,3},{3,2},{4,5},{5,4},{6,7},{7,6},{8,9},{9,8},{10,11... | collective-permute-start | bytes 98312 | tf_op jit(solution)/shard_map/cond/branch_1_fun/ppermute | solution.py:395
  122.3 1.5 %collective-permute-start.8 = (bf16[8,1,16,128]{3,2,1,0:T(8,128)(2,1)S(1)}, bf16[8,1,16,128]{3,2,1,0:T(8,128)(2,1)S(1)}, u32[]{:S(2)}, u32[]{:S(2)}) collective-permute-start(bf16[8,1,16,128]{3,2,1,0:T(8,128)(2,1)S(1)} %bitcast.69), channel_id=1, source_target_pairs={{0,2},{1,3},{2,0},{3,1},{4,6},{5,7},{6,4},{7,5},{8,10},{9,11},{10,... | collective-permute-start | bytes 98312 | tf_op jit(solution)/shard_map/cond/branch_1_fun/ppermute | solution.py:395
  124.7 1.7 %collective-permute-done.8.refs_2_ = bf16[8,1,16,128]{3,2,1,0:T(8,128)(2,1)S(1)} collective-permute-done((bf16[8,1,16,128]{3,2,1,0:T(8,128)(2,1)S(1)}, bf16[8,1,16,128]{3,2,1,0:T(8,128)(2,1)S(1)}, u32[]{:S(2)}, u32[]{:S(2)}) %collective-permute-start.8) | collective-permute-done | bytes 32800 | tf_op jit(solution)/shard_map/cond/branch_1_fun/ppermute | solution.py:395
  126.4 2.2 %collective-permute-done.9.refs_3_ = bf16[8,1,16,128]{3,2,1,0:T(8,128)(2,1)S(1)} collective-permute-done((bf16[8,1,16,128]{3,2,1,0:T(8,128)(2,1)S(1)}, bf16[8,1,16,128]{3,2,1,0:T(8,128)(2,1)S(1)}, u32[]{:S(2)}, u32[]{:S(2)}) %collective-permute-start.9) | collective-permute-done | bytes 32800 | tf_op jit(solution)/shard_map/cond/branch_1_fun/ppermute | solution.py:395
  129.3 1.7 %collective-permute-done.10 = bf16[8,4,16,128]{3,2,1,0:T(8,128)(2,1)} collective-permute-done((bf16[8,4,16,128]{3,2,1,0:T(8,128)(2,1)}, bf16[8,4,16,128]{3,2,1,0:T(8,128)(2,1)}, u32[]{:S(2)}, u32[]{:S(2)}) %collective-permute-start.10) | collective-permute-done | bytes 131104 | tf_op jit(solution)/shard_map/cond/branch_1_fun/ppermute | solution.py:395
  131.0 3.3 %contract.1 = (f32[64,2000]{1,0:T(8,128)S(1)}, f32[64,2000]{1,0:T(8,128)S(1)}) custom-call(s32[1]{0:T(128)} %bitcast.10.which_ref.core_ref, bf16[8,4,16,128]{3,2,1,0:T(8,128)(2,1)} %get-tuple-element.403.kernel_ref, bf16[8,4,16,128]{3,2,1,0:T(8,128)(2,1)} %get-tuple-element.404.got_ref, bf16[2000,256]{1,0:T(8,128)(2,1)S(1)} %straighten.1.refs_1_.refs_0_, ...), custom_call_target="tpu_custom_call" | custom-call | flops 524288000 | bytes 5120000 | tf_op jit(solution)/shard_map/contract/pallas_call | solution.py:323
  134.6 1.7 %collective-permute-done.35.back_ref = f32[64,2000]{1,0:T(8,128)S(1)} collective-permute-done((f32[64,2000]{1,0:T(8,128)S(1)}, f32[64,2000]{1,0:T(8,128)S(1)}, u32[]{:S(2)}, u32[]{:S(2)}) %collective-permute-start.35) | collective-permute-done | bytes 512032 | tf_op jit(solution)/shard_map/ppermute | solution.py:395
  136.2 1.8 %finish.1 = f32[64,4000]{1,0:T(8,128)} custom-call(s32[2]{0:T(128)S(1)} %pad_add_fusion.3.flags_ref, f32[64,2000]{1,0:T(8,128)S(1)} %get-tuple-element.406.ours_ref, f32[64,2000]{1,0:T(8,128)S(1)} %collective-permute-done.35.back_ref, f32[64,4000]{1,0:T(8,128)} %get-tuple-element.408.other_ref), custom_call_target="tpu_custom_call", output_to_operand_aliasing={{}: (3, {})} | custom-call | tf_op jit(solution)/shard_map/finish/pallas_call | solution.py:364
  (123 shorter events, 14.2 us)
Async XLA Ops:
  0.0 1.8 %copy-start.8 = (f32[256]{0:T(256)S(1)}, f32[256]{0:T(256)}, u32[]{:S(2)}) copy-start(f32[256]{0:T(256)} %param.17) | copy-start | bytes 3076
  0.0 1.9 %copy-start.9 = (s32[8]{0:T(128)S(1)}, s32[8]{0:T(128)}, u32[]{:S(2)}) copy-start(s32[8]{0:T(128)} %param.18) | copy-start | bytes 100
  0.0 2.3 %copy-start.7 = (s32[8,32]{1,0:T(8,128)S(1)}, s32[8,32]{1,0:T(8,128)}, u32[]{:S(2)}) copy-start(s32[8,32]{1,0:T(8,128)} %param.19) | copy-start | bytes 3076
  1.3 16.3 %collective-permute-start.14 = (bf16[2000,256]{1,0:T(8,128)(2,1)S(1)}, bf16[2000,256]{1,0:T(8,128)(2,1)S(1)}, u32[]{:S(2)}, u32[]{:S(2)}) collective-permute-start(bf16[2000,256]{1,0:T(8,128)(2,1)S(1)} %half_of.3), channel_id=1, source_target_pairs={{0,4},{4,0},{8,12},{12,8},{16,20},{20,16},{24,28},{28,24},{1,5},{5... | collective-permute-start | bytes 3072008 | tf_op jit(solution)/shard_map/ppermute | solution.py:395
  1.8 2.4 %collective-permute-start.17 = (f32[1,256]{1,0:T(1,128)S(1)}, f32[1,256]{1,0:T(1,128)S(1)}, u32[]{:S(2)}, u32[]{:S(2)}) collective-permute-start(f32[1,256]{1,0:T(1,128)S(1)} %bitcast.86), channel_id=1, source_target_pairs={{0,4},{4,0},{8,12},{12,8},{16,20},{20,16},{24,28},{28,24},{1,5},{5... | collective-permute-start | bytes 3080 | tf_op jit(solution)/shard_map/ppermute | solution.py:395
  1.9 2.2 %collective-permute-start.16 = (s32[1,8]{1,0:T(1,128)S(1)}, s32[1,8]{1,0:T(1,128)S(1)}, u32[]{:S(2)}, u32[]{:S(2)}) collective-permute-start(s32[1,8]{1,0:T(1,128)S(1)} %bitcast.88), channel_id=1, source_target_pairs={{0,4},{4,0},{8,12},{12,8},{16,20},{20,16},{24,28},{28,24},{1,5},{5... | collective-permute-start | bytes 104 | tf_op jit(solution)/shard_map/ppermute | solution.py:395
  2.4 13.7 %collective-permute-start.15 = (s32[16,8]{0,1:T(8,128)S(1)}, s32[16,8]{0,1:T(8,128)S(1)}, u32[]{:S(2)}, u32[]{:S(2)}) collective-permute-start(s32[16,8]{0,1:T(8,128)S(1)} %get-tuple-element.477), channel_id=1, source_target_pairs={{0,4},{4,0},{8,12},{12,8},{16,20},{20,16},{24,28},{28,24},{1,5},{5... | collective-permute-start | bytes 1544 | tf_op jit(solution)/shard_map/ppermute | solution.py:395
  4.2 12.1 %collective-permute-start.18 = (f32[1,528]{1,0:T(1,128)S(1)}, f32[1,528]{1,0:T(1,128)S(1)}, u32[]{:S(2)}, u32[]{:S(2)}) collective-permute-start(f32[1,528]{1,0:T(1,128)S(1)} %pad_maximum_fusion.3), channel_id=1, source_target_pairs={{0,8},{4,12},{8,16},{12,20},{16,24},{20,28},{24,0},{28,4},{1,9},{5... | collective-permute-start | bytes 6344 | tf_op jit(solution)/shard_map/ppermute | solution.py:431
  7.2 9.1 %collective-permute-start.19 = (f32[1,528]{1,0:T(1,128)S(1)}, f32[1,528]{1,0:T(1,128)S(1)}, u32[]{:S(2)}, u32[]{:S(2)}) collective-permute-start(f32[1,528]{1,0:T(1,128)S(1)} %pad_maximum_fusion.3), channel_id=1, source_target_pairs={{0,16},{4,20},{8,24},{12,28},{16,0},{20,4},{24,8},{28,12},{1,17},{... | collective-permute-start | bytes 6344 | tf_op jit(solution)/shard_map/ppermute | solution.py:431
  9.8 6.6 %collective-permute-start.20 = (f32[1,528]{1,0:T(1,128)S(1)}, f32[1,528]{1,0:T(1,128)S(1)}, u32[]{:S(2)}, u32[]{:S(2)}) collective-permute-start(f32[1,528]{1,0:T(1,128)S(1)} %pad_maximum_fusion.3), channel_id=1, source_target_pairs={{0,24},{4,28},{8,0},{12,4},{16,8},{20,12},{24,16},{28,20},{1,25},{... | collective-permute-start | bytes 6344 | tf_op jit(solution)/shard_map/ppermute | solution.py:431
  15.2 0.8 copy-start
  16.0 22.9 %collective-permute-start.27 = (bf16[128,2048]{1,0:T(8,128)(2,1)}, bf16[128,2048]{1,0:T(8,128)(2,1)}, u32[]{:S(2)}, u32[]{:S(2)}) collective-permute-start(bf16[128,2048]{1,0:T(8,128)(2,1)} %get-tuple-element.388), channel_id=1, source_target_pairs={{0,4},{4,0},{8,12},{12,8},{16,20},{20,16},{24,28},{28,24},{1,5},{5... | collective-permute-start | bytes 1572872 | tf_op jit(solution)/shard_map/ppermute | solution.py:395
  19.3 14.1 %collective-permute-start.21 = (bf16[2000,128]{1,0:T(8,128)(2,1)S(1)}, bf16[2000,128]{1,0:T(8,128)(2,1)S(1)}, u32[]{:S(2)}, u32[]{:S(2)}) collective-permute-start(bf16[2000,128]{1,0:T(8,128)(2,1)S(1)} %get-tuple-element.385), channel_id=1, source_target_pairs={{0,8},{4,12},{8,0},{12,4},{16,24},{20,28},{24,16},{28,20},{1,9},{5... | collective-permute-start | bytes 1536008 | tf_op jit(solution)/shard_map/ppermute | solution.py:472
  20.1 13.4 %collective-permute-start.22 = (bf16[2000,128]{1,0:T(8,128)(2,1)S(1)}, bf16[2000,128]{1,0:T(8,128)(2,1)S(1)}, u32[]{:S(2)}, u32[]{:S(2)}) collective-permute-start(bf16[2000,128]{1,0:T(8,128)(2,1)S(1)} %get-tuple-element.386), channel_id=1, source_target_pairs={{8,16},{12,20},{16,8},{20,12},{9,17},{13,21},{17,9},{21,13},{10,18... | collective-permute-start | bytes 1536008 | tf_op jit(solution)/shard_map/ppermute | solution.py:472
  33.9 26.8 %collective-permute-start.23 = (bf16[2000,256]{1,0:T(8,128)(2,1)S(1)}, bf16[2000,256]{1,0:T(8,128)(2,1)S(1)}, u32[]{:S(2)}, u32[]{:S(2)}) collective-permute-start(bf16[2000,256]{1,0:T(8,128)(2,1)S(1)} %straighten.1.refs_1_.refs_0_), channel_id=1, source_target_pairs={{0,8},{4,12},{8,0},{12,4},{16,24},{20,28},{24,16},{28,20},{1,9},{5... | collective-permute-start | bytes 3072008 | tf_op jit(solution)/shard_map/ppermute | solution.py:472
  37.6 23.1 %collective-permute-start.25 = (bf16[2000,256]{1,0:T(8,128)(2,1)S(1)}, bf16[2000,256]{1,0:T(8,128)(2,1)S(1)}, u32[]{:S(2)}, u32[]{:S(2)}) collective-permute-start(bf16[2000,256]{1,0:T(8,128)(2,1)S(1)} %straighten.1.refs_1_.refs_0_), channel_id=1, source_target_pairs={{8,16},{12,20},{16,8},{20,12},{9,17},{13,21},{17,9},{21,13},{10,18... | collective-permute-start | bytes 3072008 | tf_op jit(solution)/shard_map/ppermute | solution.py:472
  38.9 1.0 copy-start.1
  42.1 44.6 %collective-permute-start.33 = (bf16[256,2048]{1,0:T(8,128)(2,1)}, bf16[256,2048]{1,0:T(8,128)(2,1)}, u32[]{:S(2)}, u32[]{:S(2)}) collective-permute-start(bf16[256,2048]{1,0:T(8,128)(2,1)} %stack_panels.1.refs_0_), channel_id=1, source_target_pairs={{0,8},{4,12},{24,16},{28,20},{1,9},{5,13},{25,17},{29,21},{2,10},{... | collective-permute-start | bytes 3145736 | tf_op jit(solution)/shard_map/ppermute | solution.py:472
  63.5 7.7 %collective-permute-start.29 = (f32[4,4,16,256]{3,2,1,0:T(8,128)}, f32[4,4,16,256]{3,2,1,0:T(8,128)}, u32[]{:S(2)}, u32[]{:S(2)}) collective-permute-start(f32[4,4,16,256]{3,2,1,0:T(8,128)} %get-tuple-element.392), channel_id=1, source_target_pairs={{0,4},{4,0},{8,12},{12,8},{16,20},{20,16},{24,28},{28,24},{1,5},{5... | collective-permute-start | bytes 786440 | tf_op jit(solution)/shard_map/ppermute | solution.py:395
  63.5 23.2 %collective-permute-start.24 = (bf16[2000,256]{1,0:T(8,128)(2,1)S(1)}, bf16[2000,256]{1,0:T(8,128)(2,1)}, u32[]{:S(2)}, u32[]{:S(2)}) collective-permute-start(bf16[2000,256]{1,0:T(8,128)(2,1)S(1)} %collective-permute-done.23.refs_1_), channel_id=1, source_target_pairs={{8,16},{12,20},{16,8},{20,12},{9,17},{13,21},{17,9},{21,13},{10,18... | collective-permute-start | bytes 3072008 | tf_op jit(solution)/shard_map/ppermute | solution.py:472
  65.2 28.0 %collective-permute-start.26 = (bf16[2000,256]{1,0:T(8,128)(2,1)S(1)}, bf16[2000,256]{1,0:T(8,128)(2,1)}, u32[]{:S(2)}, u32[]{:S(2)}) collective-permute-start(bf16[2000,256]{1,0:T(8,128)(2,1)S(1)} %collective-permute-done.25.refs_2_), channel_id=1, source_target_pairs={{8,0},{12,4},{16,24},{20,28},{9,1},{13,5},{17,25},{21,29},{10,2},{... | collective-permute-start | bytes 3072008 | tf_op jit(solution)/shard_map/ppermute | solution.py:472
  69.1 2.1 %collective-permute-start.28 = (f32[2,4,16,256]{3,2,1,0:T(8,128)}, f32[2,4,16,256]{3,2,1,0:T(8,128)}, u32[]{:S(2)}, u32[]{:S(2)}) collective-permute-start(f32[2,4,16,256]{3,2,1,0:T(8,128)} %get-tuple-element.390), channel_id=1, source_target_pairs={{0,4},{4,0},{8,12},{12,8},{16,20},{20,16},{24,28},{28,24},{1,5},{5... | collective-permute-start | bytes 393224 | tf_op jit(solution)/shard_map/ppermute | solution.py:395
  73.0 0.6 copy-start.2
  73.6 0.6 copy-start.3
  74.2 0.6 copy-start.4
  74.9 5.0 %collective-permute-start.30 = (f32[6,16,256]{2,1,0:T(8,128)}, f32[6,16,256]{2,1,0:T(8,128)S(1)}, u32[]{:S(2)}, u32[]{:S(2)}) collective-permute-start(f32[6,16,256]{2,1,0:T(8,128)} %get-tuple-element.394), channel_id=1, source_target_pairs={{0,1},{1,0},{2,3},{3,2},{4,5},{5,4},{6,7},{7,6},{8,9},{9,8},{10,11... | collective-permute-start | bytes 294920 | tf_op jit(solution)/shard_map/ppermute | solution.py:395
  77.6 4.9 %collective-permute-start.31 = (f32[6,16,256]{2,1,0:T(8,128)}, f32[6,16,256]{2,1,0:T(8,128)S(1)}, u32[]{:S(2)}, u32[]{:S(2)}) collective-permute-start(f32[6,16,256]{2,1,0:T(8,128)} %copy-done.4), channel_id=1, source_target_pairs={{0,2},{1,3},{2,0},{3,1},{4,6},{5,7},{6,4},{7,5},{8,10},{9,11},{10,... | collective-permute-start | bytes 294920 | tf_op jit(solution)/shard_map/ppermute | solution.py:395
  79.9 5.7 %collective-permute-start.32 = (f32[6,16,256]{2,1,0:T(8,128)}, f32[6,16,256]{2,1,0:T(8,128)S(1)}, u32[]{:S(2)}, u32[]{:S(2)}) collective-permute-start(f32[6,16,256]{2,1,0:T(8,128)} %copy-done.3), channel_id=1, source_target_pairs={{0,3},{1,2},{2,1},{3,0},{4,7},{5,6},{6,5},{7,4},{8,11},{9,10},{10,... | collective-permute-start | bytes 294920 | tf_op jit(solution)/shard_map/ppermute | solution.py:395
  93.2 37.8 %collective-permute-start.34 = (bf16[2000,256]{1,0:T(8,128)(2,1)}, bf16[2000,256]{1,0:T(8,128)(2,1)}, u32[]{:S(2)}, u32[]{:S(2)}) collective-permute-start(bf16[2000,256]{1,0:T(8,128)(2,1)} %collective-permute-done.24.refs_5_), channel_id=1, source_target_pairs={{8,0},{12,4},{16,24},{20,28},{9,1},{13,5},{17,25},{21,29},{10,2},{... | collective-permute-start | bytes 3072008 | tf_op jit(solution)/shard_map/ppermute | solution.py:472
  97.7 1.6 %collective-permute-start = (f32[4,4,16,256]{3,2,1,0:T(8,128)S(1)}, f32[4,4,16,256]{3,2,1,0:T(8,128)S(1)}, u32[]{:S(2)}, u32[]{:S(2)}) collective-permute-start(f32[4,4,16,256]{3,2,1,0:T(8,128)S(1)} %get-tuple-element.351), channel_id=1, source_target_pairs={{0,4},{4,0},{8,12},{12,8},{16,20},{20,16},{24,28},{28,24},{1,5},{5... | collective-permute-start | bytes 786440 | tf_op jit(solution)/shard_map/cond/branch_1_fun/ppermute | solution.py:395
  99.4 4.3 %collective-permute-start.1 = (f32[4,16,256]{2,1,0:T(8,128)S(1)}, f32[4,16,256]{2,1,0:T(8,128)S(1)}, u32[]{:S(2)}, u32[]{:S(2)}) collective-permute-start(f32[4,16,256]{2,1,0:T(8,128)S(1)} %get-tuple-element.353), channel_id=1, source_target_pairs={{0,1},{1,0},{2,3},{3,2},{4,5},{5,4},{6,7},{7,6},{8,9},{9,8},{10,11... | collective-permute-start | bytes 196616 | tf_op jit(solution)/shard_map/cond/branch_1_fun/ppermute | solution.py:395
  100.9 4.3 %collective-permute-start.2 = (f32[4,16,256]{2,1,0:T(8,128)S(1)}, f32[4,16,256]{2,1,0:T(8,128)S(1)}, u32[]{:S(2)}, u32[]{:S(2)}) collective-permute-start(f32[4,16,256]{2,1,0:T(8,128)S(1)} %get-tuple-element.354), channel_id=1, source_target_pairs={{0,2},{1,3},{2,0},{3,1},{4,6},{5,7},{6,4},{7,5},{8,10},{9,11},{10,... | collective-permute-start | bytes 196616 | tf_op jit(solution)/shard_map/cond/branch_1_fun/ppermute | solution.py:395
  102.5 5.2 %collective-permute-start.3 = (f32[4,16,256]{2,1,0:T(8,128)S(1)}, f32[4,16,256]{2,1,0:T(8,128)S(1)}, u32[]{:S(2)}, u32[]{:S(2)}) collective-permute-start(f32[4,16,256]{2,1,0:T(8,128)S(1)} %get-tuple-element.355), channel_id=1, source_target_pairs={{0,3},{1,2},{2,1},{3,0},{4,7},{5,6},{6,5},{7,4},{8,11},{9,10},{10,... | collective-permute-start | bytes 196616 | tf_op jit(solution)/shard_map/cond/branch_1_fun/ppermute | solution.py:395
  107.8 6.1 %collective-permute-start.5 = (f32[4,32]{1,0:T(4,128)S(1)}, f32[4,32]{1,0:T(4,128)S(1)}, u32[]{:S(2)}, u32[]{:S(2)}) collective-permute-start(f32[4,32]{1,0:T(4,128)S(1)} %add.231), channel_id=1, source_target_pairs={{0,16},{4,20},{8,24},{12,28},{16,0},{20,4},{24,8},{28,12},{1,17},{... | collective-permute-start | bytes 1544 | tf_op jit(solution)/shard_map/cond/branch_1_fun/ppermute | solution.py:395
  112.2 5.5 %collective-permute-start.6 = (f32[4,32]{1,0:T(4,128)S(1)}, f32[4,32]{1,0:T(4,128)S(1)}, u32[]{:S(2)}, u32[]{:S(2)}) collective-permute-start(f32[4,32]{1,0:T(4,128)S(1)} %add.231), channel_id=1, source_target_pairs={{0,24},{4,28},{8,16},{12,20},{16,8},{20,12},{24,0},{28,4},{1,25},{... | collective-permute-start | bytes 1544 | tf_op jit(solution)/shard_map/cond/branch_1_fun/ppermute | solution.py:395
  113.7 6.8 %collective-permute-start.4 = (f32[36,256]{1,0:T(8,128)S(1)}, f32[36,256]{1,0:T(8,128)S(1)}, u32[]{:S(2)}, u32[]{:S(2)}) collective-permute-start(f32[36,256]{1,0:T(8,128)S(1)} %select_maximum_fusion), channel_id=1, source_target_pairs={{0,8},{4,12},{8,0},{12,4},{16,24},{20,28},{24,16},{28,20},{1,9},{5... | collective-permute-start | bytes 110600 | tf_op jit(solution)/shard_map/cond/branch_1_fun/ppermute | solution.py:395
  120.7 4.0 %collective-permute-start.7 = (bf16[8,1,16,128]{3,2,1,0:T(8,128)(2,1)S(1)}, bf16[8,1,16,128]{3,2,1,0:T(8,128)(2,1)S(1)}, u32[]{:S(2)}, u32[]{:S(2)}) collective-permute-start(bf16[8,1,16,128]{3,2,1,0:T(8,128)(2,1)S(1)} %bitcast.68), channel_id=1, source_target_pairs={{0,1},{1,0},{2,3},{3,2},{4,5},{5,4},{6,7},{7,6},{8,9},{9,8},{10,11... | collective-permute-start | bytes 98312 | tf_op jit(solution)/shard_map/cond/branch_1_fun/ppermute | solution.py:395
  122.3 4.1 %collective-permute-start.8 = (bf16[8,1,16,128]{3,2,1,0:T(8,128)(2,1)S(1)}, bf16[8,1,16,128]{3,2,1,0:T(8,128)(2,1)S(1)}, u32[]{:S(2)}, u32[]{:S(2)}) collective-permute-start(bf16[8,1,16,128]{3,2,1,0:T(8,128)(2,1)S(1)} %bitcast.69), channel_id=1, source_target_pairs={{0,2},{1,3},{2,0},{3,1},{4,6},{5,7},{6,4},{7,5},{8,10},{9,11},{10,... | collective-permute-start | bytes 98312 | tf_op jit(solution)/shard_map/cond/branch_1_fun/ppermute | solution.py:395
  123.8 4.8 %collective-permute-start.9 = (bf16[8,1,16,128]{3,2,1,0:T(8,128)(2,1)S(1)}, bf16[8,1,16,128]{3,2,1,0:T(8,128)(2,1)S(1)}, u32[]{:S(2)}, u32[]{:S(2)}) collective-permute-start(bf16[8,1,16,128]{3,2,1,0:T(8,128)(2,1)S(1)} %bitcast.70), channel_id=1, source_target_pairs={{0,3},{1,2},{2,1},{3,0},{4,7},{5,6},{6,5},{7,4},{8,11},{9,10},{10,... | collective-permute-start | bytes 98312 | tf_op jit(solution)/shard_map/cond/branch_1_fun/ppermute | solution.py:395
  129.3 1.7 %collective-permute-start.10 = (bf16[8,4,16,128]{3,2,1,0:T(8,128)(2,1)}, bf16[8,4,16,128]{3,2,1,0:T(8,128)(2,1)}, u32[]{:S(2)}, u32[]{:S(2)}) collective-permute-start(bf16[8,4,16,128]{3,2,1,0:T(8,128)(2,1)} %in_order.1), channel_id=1, source_target_pairs={{0,4},{4,0},{8,12},{12,8},{16,20},{20,16},{24,28},{28,24},{1,5},{5... | collective-permute-start | bytes 393224 | tf_op jit(solution)/shard_map/cond/branch_1_fun/ppermute | solution.py:395
  134.3 2.0 %collective-permute-start.35 = (f32[64,2000]{1,0:T(8,128)S(1)}, f32[64,2000]{1,0:T(8,128)S(1)}, u32[]{:S(2)}, u32[]{:S(2)}) collective-permute-start(f32[64,2000]{1,0:T(8,128)S(1)} %get-tuple-element.407), channel_id=1, source_target_pairs={{0,4},{4,0},{8,12},{12,8},{16,20},{20,16},{24,28},{28,24},{1,5},{5... | collective-permute-start | bytes 1536008 | tf_op jit(solution)/shard_map/ppermute | solution.py:395

commit v3 on v2

--- a/solution.py
+++ b/solution.py
@@ -90,10 +90,16 @@
     )(which[None], whole)
 
 
+def basis_cuts(half):
+    cut = -(-half // 256) * 128
+    return [(0, cut), (cut, half)]
+
+
 def compact(mine, got, mine_sig, got_sig, mine_to, got_to, width, tile, odd):
     half, rows = mine.shape
     blocks = mine_sig.shape[0]
     count = rows // tile + 2
+    cuts = basis_cuts(half)
 
     def body(odd_ref, mine_ref, got_ref, msig_ref, gsig_ref, mto_ref, gto_ref, *outs):
         block_of = lax.broadcasted_iota(jnp.int32, (half, blocks), 0)
@@ -108,24 +114,30 @@
             return jnp.dot(screened, place, preferred_element_type=F32)
 
         window = part(mine_ref, msig_ref, mto_ref) + part(got_ref, gsig_ref, gto_ref)
-        for j in range(1, count - 1):
-            outs[j][...] = window[:, j * tile : (j + 1) * tile].astype(BF16)
-        first, last = window[:, :tile], window[:, (count - 1) * tile :]
-        outs[0][...] = jnp.where(odd_ref[0] == 0, first, last).astype(BF16)
-        outs[-1][...] = jnp.where(odd_ref[0] == 0, last, first).astype(BF16)
-
-    shape = jax.ShapeDtypeStruct((half, tile), BF16)
-    return pl.pallas_call(
-        body,
-        out_shape=(shape,) * count,
+        tiles = [window[:, j * tile : (j + 1) * tile] for j in range(count)]
+        even = odd_ref[0] == 0
+        first, last = tiles[0], tiles[-1]
+        tiles[0] = jnp.where(even, first, last)
+        tiles[-1] = jnp.where(even, last, first)
+        for p, (low, high) in enumerate(cuts):
+            for j in range(count):
+                outs[p * count + j][...] = tiles[j][low:high].astype(BF16)
+
+    shapes = [
+        jax.ShapeDtypeStruct((high - low, tile), BF16) for low, high in cuts for _ in range(count)
+    ]
+    out = pl.pallas_call(
+        body,
+        out_shape=shapes,
         in_specs=[SCALARS] + [WHOLE] * 6,
-        out_specs=(WHOLE,) * count,
+        out_specs=[WHOLE] * len(shapes),
         compiler_params=pltpu.CompilerParams(vmem_limit_bytes=24 * MIB),
         name="compact",
         cost_estimate=pl.CostEstimate(
             flops=8 * half * rows * rows, bytes_accessed=8 * half * rows, transcendentals=0
         ),
     )(odd[None], mine, got, mine_sig, got_sig, mine_to, got_to)
+    return [out[p * count : (p + 1) * count] for p in range(len(cuts))]
 
 
 def straighten(tiles, by_a, by_b, odd):
@@ -205,11 +217,11 @@
     return list({id(x): x for x in arrays}.values())
 
 
-def read_window(addends, arrays, refs):
+def read_window(addends, p, arrays, refs):
     ref_of = {id(x): ref for x, ref in zip(arrays, refs)}
     total = None
     for x in addends:
-        value = ref_of[id(x)][...]
+        value = ref_of[id(x[p])][...]
         total = value if total is None else total + value
     return total
 
@@ -240,11 +252,13 @@
 
 def project(jobs, tile, shares, core):
     both = jobs[0][0].shape[0]
-    half, rows = jobs[0][1][0].shape
+    parts = [x.shape[0] for x in jobs[0][1][0]]
+    rows = jobs[0][1][0][0].shape[1]
+    half = sum(parts)
     piece = tile // shares
     tiles = len(jobs) * rows // tile
     panels = distinct([p for p, _ in jobs])
-    arrays = distinct([x for _, window in jobs for x in window])
+    arrays = distinct([x for _, window in jobs for addend in window for x in addend])
     count = len(panels)
 
     def body(core_ref, *refs):
@@ -253,8 +267,15 @@
         q = 0
         for panel, window in jobs:
             panel_ref = panel_refs[[id(p) for p in panels].index(id(panel))]
-            value = read_window(window, arrays, array_refs)
-            turned = jnp.dot(panel_ref[:, :half], value, preferred_element_type=F32).T
+            total, low = None, 0
+            for p, size in enumerate(parts):
+                value = read_window(window, p, arrays, array_refs)
+                term = jnp.dot(
+                    panel_ref[:, low : low + size], value, preferred_element_type=F32
+                )
+                total = term if total is None else total + term
+                low += size
+            turned = total.T
             for j in range(0, rows, tile):
                 terms_ref[q] = turned[j : j + tile].reshape(2, shares // 2, piece, both)
                 keep_ref[q] = terms_ref[q, core_ref[0]]
@@ -297,9 +318,11 @@
 
 def contract(kernel, got, windows, core):
     tiles, shares, piece, columns = kernel.shape
-    half, rows = windows[0][0].shape
+    parts = [x.shape[0] for x in windows[0][0]]
+    rows = windows[0][0][0].shape[1]
+    half = sum(parts)
     own = columns // 2
-    arrays = distinct([x for window in windows for x in window])
+    arrays = distinct([x for window in windows for addend in window for x in addend])
     per_window = tiles // len(windows)
 
     def body(core_ref, kernel_ref, got_ref, *refs):
@@ -308,16 +331,21 @@
         first = core_ref[0] == 0
         order_ref[:, core_ref[0]] = kernel_ref[...].astype(F32)
         order_ref[:, 1 - core_ref[0]] = got_ref[...].astype(F32)
-        total = None
-        for s, window in enumerate(windows):
-            part = order_ref[s * per_window : (s + 1) * per_window]
-            part = part.reshape(rows, columns).astype(BF16)
-            value = read_window(window, arrays, array_refs)
-            term = jnp.dot(value, part, preferred_element_type=F32)
-            total = term if total is None else total + term
-        total = total.T
-        mine_ref[...] = jnp.where(first, total[:own], total[own:])
-        other_ref[...] = jnp.where(first, total[own:], total[:own])
+        kernels = [
+            order_ref[s * per_window : (s + 1) * per_window].reshape(rows, columns).astype(BF16)
+            for s in range(len(windows))
+        ]
+        low = 0
+        for p, size in enumerate(parts):
+            total = None
+            for window, part in zip(windows, kernels):
+                value = read_window(window, p, arrays, array_refs)
+                term = jnp.dot(value, part, preferred_element_type=F32)
+                total = term if total is None else total + term
+            total = total.T
+            mine_ref[:, low : low + size] = jnp.where(first, total[:own], total[own:])
+            other_ref[:, low : low + size] = jnp.where(first, total[own:], total[:own])
+            low += size
 
     shape = jax.ShapeDtypeStruct((own, half), F32)
     return pl.pallas_call(
@@ -456,7 +484,7 @@
     mine_to = lax.dynamic_index_in_dim(to, place, 0, keepdims=False) - base
     got_to = lax.dynamic_index_in_dim(to, place ^ 1, 0, keepdims=False) - base
     odd = chip % 2
-    for_b, *own_tiles, for_a = compact(
+    compacted = compact(
         mine,
         got,
         jnp.repeat(mine_sig.astype(BF16), slots, axis=1),
@@ -480,10 +508,18 @@
             pairs += [(a + 1, a)] if a + t <= last else []
         return pairs
 
-    by_b = sent(for_b, over(1, 1))
-    own = straighten(own_tiles, sent(for_a, over(0, 1)), by_b, odd)
-
-    mine_panel, other_panel = panel_halves(occupied.T, trial.T, core)
+    arrived = [
+        (sent(for_b, over(1, 1)), sent(for_a, over(0, 1))) for for_b, *_, for_a in compacted
+    ]
+    own = tuple(
+        straighten(tiles, by_a, by_b, odd)
+        for (_, *tiles, _), (by_b, by_a) in zip(compacted, arrived)
+    )
+
+    _, occupied_turned, trial_turned = lax.optimization_barrier(
+        (compacted[0][0], occupied.T, trial.T)
+    )
+    mine_panel, other_panel = panel_halves(occupied_turned, trial_turned, core)
     panels = stack_panels(mine_panel, flip(other_panel, "grid", 1), core)
 
     per_window = rows // tile
@@ -499,10 +535,11 @@
     by_a = by_b = own
     far_panels = None
     for t in range(1, last):
-        next_b = sent(by_a, over(1, t))
-        by_a, by_b = sent(by_b, over(0, t)), next_b
+        moved = [(sent(a, over(1, t)), sent(b, over(0, t))) for a, b in zip(by_a, by_b)]
+        by_b, by_a = (tuple(x) for x in zip(*moved))
         if t == 1:
-            far_panels = sent(panels, ends)
+            _, far_panels = lax.optimization_barrier(((by_a[0], by_b[0]), panels))
+            far_panels = sent(far_panels, ends)
         a_at, b_at = valid(chip + side * t), valid(chip - side * t)
         if 2 * t > last:
             stages.append([([by_a, by_b], jnp.maximum(a_at, b_at))])
@@ -511,10 +548,6 @@
 
     direct = occ_count <= 4
     points = per_window * piece
-
-    def halved(jobs):
-        keep, give = project(jobs, tile, shares, core)
-        return keep, flip(give, "grid", 1)
 
     def summed(pairs):
         if direct:
@@ -539,14 +572,10 @@
     early_jobs, late_jobs = sum(stages[1:-1], []), stages[-1]
     early_at = jnp.stack([at for _, at in early_jobs])
     late_at = late_jobs[0][1][None]
-    own_job = stages[0][0]
     early_jobs = stages[0] + early_jobs
     early_at = jnp.concatenate((chip[None], early_at))
 
-    early_value = summed(
-        [halved([(panels, own_job[0])]), halved([(panels, w) for w, _ in early_jobs[1:]])]
-    )
-    early_density = shared_density(early_value, early_at)
+    early_pair = project([(panels, w) for w, _ in early_jobs], tile, shares, core)
 
     at = (
         (window_iota * rows)[:, None, None]
@@ -561,28 +590,19 @@
     here = (places[:, None] == window_iota[None, :])[:, :, None]
     weight_here = jnp.sum(jnp.where(here, weight[None], 0.0), axis=1)[:, :, None]
 
-    late, by_a, early_value, early_density, far_panels, weight_here, fits = (
-        lax.optimization_barrier(
-            (
-                by_b,
-                by_a,
-                early_value,
-                early_density,
-                far_panels,
-                weight_here,
-                fits.astype(jnp.int32),
-            )
-        )
+    late, by_a, early_pair, far_panels, weight_here, fits = lax.optimization_barrier(
+        (by_b, by_a, early_pair, far_panels, weight_here, fits.astype(jnp.int32))
     )
     fits = fits != 0
-    late = sent(late, homes)
+    late = tuple(sent(x, homes) for x in late)
     late_window = [by_a, by_b]
     late_jobs = [(panels, late_window), (far_panels, [by_b])]
 
     def kernel_of_all():
-        value = summed([halved(late_jobs)])
-        density = early_density + shared_density(value, jnp.concatenate((late_at, late_at)))
-        value, far_value = jnp.concatenate((early_value, value[:1])), value[1:]
+        late_pair = project(late_jobs, tile, shares, core)
+        value = summed([(keep, flip(give, "grid", 1)) for keep, give in (early_pair, late_pair)])
+        density = shared_density(value, jnp.concatenate((early_at, late_at, late_at)))
+        value, far_value = value[:-1], value[-1:]
         packed = jnp.concatenate(
             (far_value[0], jnp.pad(density, ((0, 0), (0, 4 * columns - points)))), axis=0
         )

time: 139 us -> 132 us (0.950)
  waiting for transfers between devices: 58.9 us -> 50.6 us
  starting transfers between devices: 41.8 us -> 48.5 us
  local copies, waits for them, and re-layouts: 5.81 us -> 3.91 us
  Pallas kernels: 25.1 us -> 23.4 us
    ppermute x8 -> x15, starting transfers between devices: 14.5 us -> 25.9 us  [sent(): return lax.ppermute(x, 'grid', along(pairs))]
    ppermute x22 -> x18, starting transfers between devices: 20.5 us -> 15.7 us  [flip(): return lax.ppermute(x, axis, [(i, i ^ bit) for i in range(count)])]
    ppermute x22 -> x18, waiting for transfers between devices: 25.8 us -> 21.1 us  [flip(): return lax.ppermute(x, axis, [(i, i ^ bit) for i in range(count)])]
    ppermute x8 -> x15, waiting for transfers between devices: 33.1 us -> 29.2 us  [sent(): return lax.ppermute(x, 'grid', along(pairs))]
    pallas_call x3 -> x2, Pallas kernels: 8.3 us -> 6.17 us  [project(): pl.pallas_call(body, out_shape=(shape, shape), in_specs=[SCALARS] + [WHOL...]
    pallas_call x1, Pallas kernels: 1.78 us -> 3.83 us  [compact(): pl.pallas_call(body, out_shape=shapes, in_specs=[SCALARS] + [WHOLE] * 6,...]
    unnamed x19 -> x13, local copies, waits for them, and re-layouts: 3.84 us -> 1.94 us
    pallas_call x2 -> x1, Pallas kernels: 1.74 us -> 0.08 us  [split_sum(): pl.pallas_call(body, out_shape=(shape,) * shares, in_specs=[SCALARS] + [W...]
  transfers between devices with their start and end apart: 33 -> 36, of which waited for: 19 -> 16; matrix products, arithmetic and copies ran while one was open for 5% -> 4% of each run, Pallas kernels for 14% -> 10%
where the time goes in v3:
time: 132 us
  waiting for transfers between devices  50.6 us (38%)
  starting transfers between devices  48.5 us (37%)
  Pallas kernels  23.4 us (18%)
  local copies, waits for them, and re-layouts  3.91 us (3%)
  other arithmetic  3.39 us (3%)
  between operations  1.79 us (1%)
    ppermute x15, waiting for transfers between devices, sent(): return lax.ppermute(x, 'grid', along(pairs))  29.2 us
    ppermute x15, starting transfers between devices, sent(): return lax.ppermute(x, 'grid', along(pairs))  25.9 us
    ppermute x18, waiting for transfers between devices, flip(): return lax.ppermute(x, axis, [(i, i ^ bit) for i in range(count)])  21.1 us
    ppermute x18, starting transfers between devices, flip(): return lax.ppermute(x, axis, [(i, i ^ bit) for i in range(count)])  15.7 us
    ppermute x3, starting transfers between devices, per_device(): heard.append(lax.ppermute(told, 'grid', around))  6.85 us
    pallas_call x2, Pallas kernels, project(): pl.pallas_call(body, out_shape=(shape, shape), in_specs=[SCALARS] + [WHOL...  6.17 us
    pallas_call x1, Pallas kernels, compact(): pl.pallas_call(body, out_shape=shapes, in_specs=[SCALARS] + [WHOLE] * 6,...  3.83 us
    pallas_call x1, Pallas kernels, contract(): pl.pallas_call(body, out_shape=(shape, shape), in_specs=[SCALARS] + [WHOL...  3.31 us
  transfers between devices with their start and end apart: 36, of which 16 were waited for; matrix products, arithmetic and copies ran while one was open for 4% of the time, Pallas kernels for 10%

profile of v3, /device:TPU:0, one launch (start us, length us, event | category | flops | bytes accessed | tf_op | source)
XLA Modules:
  0.0 131.8 jit_solution(6925724142038712045)
XLA Ops:
  0.0 1.3 half_of.3
  2.6 1.5 %collective-permute-done.17 = s32[1,8]{1,0:T(1,128)S(1)} collective-permute-done((s32[1,8]{1,0:T(1,128)S(1)}, s32[1,8]{1,0:T(1,128)S(1)}, u32[]{:S(2)}, u32[]{:S(2)}) %collective-permute-start.17) | collective-permute-done | bytes 64 | tf_op jit(solution)/shard_map/ppermute | solution.py:423
  4.2 2.9 %collective-permute-start.19 = (f32[1,528]{1,0:T(1,128)S(1)}, f32[1,528]{1,0:T(1,128)S(1)}, u32[]{:S(2)}, u32[]{:S(2)}) collective-permute-start(f32[1,528]{1,0:T(1,128)S(1)} %pad_maximum_fusion.3), channel_id=1, source_target_pairs={{0,8},{4,12},{8,16},{12,20},{16,24},{20,28},{24,0},{28,4},{1,9},{5... | collective-permute-start | bytes 6344 | tf_op jit(solution)/shard_map/ppermute | solution.py:459
  7.2 2.6 %collective-permute-start.20 = (f32[1,528]{1,0:T(1,128)S(1)}, f32[1,528]{1,0:T(1,128)S(1)}, u32[]{:S(2)}, u32[]{:S(2)}) collective-permute-start(f32[1,528]{1,0:T(1,128)S(1)} %pad_maximum_fusion.3), channel_id=1, source_target_pairs={{0,16},{4,20},{8,24},{12,28},{16,0},{20,4},{24,8},{28,12},{1,17},{... | collective-permute-start | bytes 6344 | tf_op jit(solution)/shard_map/ppermute | solution.py:459
  9.7 1.3 %collective-permute-start.21 = (f32[1,528]{1,0:T(1,128)S(1)}, f32[1,528]{1,0:T(1,128)S(1)}, u32[]{:S(2)}, u32[]{:S(2)}) collective-permute-start(f32[1,528]{1,0:T(1,128)S(1)} %pad_maximum_fusion.3), channel_id=1, source_target_pairs={{0,24},{4,28},{8,0},{12,4},{16,8},{20,12},{24,16},{28,20},{1,25},{... | collective-permute-start | bytes 6344 | tf_op jit(solution)/shard_map/ppermute | solution.py:459
  11.1 1.2 half_of.2.mine_ref
  14.5 3.8 %compact.1 = (bf16[1024,128]{1,0:T(8,128)(2,1)S(1)}, bf16[1024,128]{1,0:T(8,128)(2,1)S(1)}, bf16[1024,128]{1,0:T(8,128)(2,1)S(1)}, bf16[1024,128]{1,0:T(8,128)(2...) custom-call(s32[1]{0:T(128)} %bitcast.13.odd_ref, ...), custom_call_target="tpu_custom_call" | custom-call | flops 1048576000 | bytes 4096000 | tf_op jit(solution)/shard_map/compact/pallas_call | solution.py:129
  18.7 0.7 collective-permute-start.23
  19.5 2.5 %panel_halves.1 = (bf16[128,2048]{1,0:T(8,128)(2,1)S(1)}, bf16[128,2048]{1,0:T(8,128)(2,1)}) custom-call(s32[1]{0:T(128)} %bitcast.12.which_ref.core_ref, bf16[64,4000]{1,0:T(8,128)(2,1)} %bitcast.73, bf16[64,4000]{1,0:T(8,128)(2,1)} %bitcast.74), custom_call_target="tpu_custom_call" | custom-call | tf_op jit(solution)/shard_map/panel_halves/pallas_call | solution.py:183
  22.0 0.8 copy-done
  22.8 2.7 %collective-permute-done.22.refs_2_ = bf16[1024,128]{1,0:T(8,128)(2,1)S(1)} collective-permute-done((bf16[1024,128]{1,0:T(8,128)(2,1)S(1)}, bf16[1024,128]{1,0:T(8,128)(2,1)S(1)}, u32[]{:S(2)}, u32[]{:S(2)}) %collective-permute-start.22) | collective-permute-done | bytes 262176 | tf_op jit(solution)/shard_map/ppermute | solution.py:500
  25.8 3.7 %collective-permute-start.24 = (bf16[1024,256]{1,0:T(8,128)(2,1)S(1)}, bf16[1024,256]{1,0:T(8,128)(2,1)S(1)}, u32[]{:S(2)}, u32[]{:S(2)}) collective-permute-start(bf16[1024,256]{1,0:T(8,128)(2,1)S(1)} %straighten.2.refs_1_.refs_0_), channel_id=1, source_target_pairs={{0,8},{4,12},{8,0},{12,4},{16,24},{20,28},{24,16},{28,20},{1,9},{5... | collective-permute-start | bytes 1572872 | tf_op jit(solution)/shard_map/ppermute | solution.py:500
  29.5 0.7 collective-permute-start.30
  30.2 3.0 %collective-permute-start.26 = (bf16[976,128]{1,0:T(8,128)(2,1)}, bf16[976,128]{1,0:T(8,128)(2,1)S(1)}, u32[]{:S(2)}, u32[]{:S(2)}) collective-permute-start(bf16[976,128]{1,0:T(8,128)(2,1)} %get-tuple-element.401), channel_id=1, source_target_pairs={{0,8},{4,12},{8,0},{12,4},{16,24},{20,28},{24,16},{28,20},{1,9},{5... | collective-permute-start | bytes 749576 | tf_op jit(solution)/shard_map/ppermute | solution.py:500
  33.2 0.7 collective-permute-start.27
  34.2 12.0 %collective-permute-done.26.refs_2_ = bf16[976,128]{1,0:T(8,128)(2,1)S(1)} collective-permute-done((bf16[976,128]{1,0:T(8,128)(2,1)}, bf16[976,128]{1,0:T(8,128)(2,1)S(1)}, u32[]{:S(2)}, u32[]{:S(2)}) %collective-permute-start.26) | collective-permute-done | bytes 249888 | tf_op jit(solution)/shard_map/ppermute | solution.py:500
  46.4 3.7 %collective-permute-start.28 = (bf16[976,256]{1,0:T(8,128)(2,1)S(1)}, bf16[976,256]{1,0:T(8,128)(2,1)S(1)}, u32[]{:S(2)}, u32[]{:S(2)}) collective-permute-start(bf16[976,256]{1,0:T(8,128)(2,1)S(1)} %straighten.3.refs_2_.refs_1_), channel_id=1, source_target_pairs={{0,8},{4,12},{8,0},{12,4},{16,24},{20,28},{24,16},{28,20},{1,9},{5... | collective-permute-start | bytes 1499144 | tf_op jit(solution)/shard_map/ppermute | solution.py:500
  50.1 0.7 collective-permute-start.32
  50.8 1.0 copy-done.1
  51.9 2.2 %stack_panels.1.refs_0_ = bf16[256,2048]{1,0:T(8,128)(2,1)} custom-call(s32[1]{0:T(128)} %bitcast.12.which_ref.core_ref, bf16[128,2048]{1,0:T(8,128)(2,1)S(1)} %copy-done.1, bf16[128,2048]{1,0:T(8,128)(2,1)} %collective-permute-done.34.got_ref), custom_call_target="tpu_custom_call" | custom-call | tf_op jit(solution)/shard_map/stack_panels/pallas_call | solution.py:206
  54.1 4.4 %collective-permute-start.35 = (bf16[256,2048]{1,0:T(8,128)(2,1)}, bf16[256,2048]{1,0:T(8,128)(2,1)}, u32[]{:S(2)}, u32[]{:S(2)}) collective-permute-start(bf16[256,2048]{1,0:T(8,128)(2,1)} %stack_panels.1.refs_0_), channel_id=1, source_target_pairs={{0,8},{4,12},{24,16},{28,20},{1,9},{5,13},{25,17},{29,21},{2,10},{... | collective-permute-start | bytes 3145736 | tf_op jit(solution)/shard_map/ppermute | solution.py:500
  59.1 1.5 %collective-permute-start.25 = (bf16[1024,256]{1,0:T(8,128)(2,1)S(1)}, bf16[1024,256]{1,0:T(8,128)(2,1)}, u32[]{:S(2)}, u32[]{:S(2)}) collective-permute-start(bf16[1024,256]{1,0:T(8,128)(2,1)S(1)} %collective-permute-done.24.refs_3_.refs_2_), channel_id=1, source_target_pairs={{8,16},{12,20},{16,8},{20,12},{9,17},{13,21},{17,9},{21,13},{10,18... | collective-permute-start | bytes 1572872 | tf_op jit(solution)/shard_map/ppermute | solution.py:500
  60.5 1.3 collective-permute-start.31
  62.0 1.5 %collective-permute-start.29 = (bf16[976,256]{1,0:T(8,128)(2,1)S(1)}, bf16[976,256]{1,0:T(8,128)(2,1)}, u32[]{:S(2)}, u32[]{:S(2)}) collective-permute-start(bf16[976,256]{1,0:T(8,128)(2,1)S(1)} %collective-permute-done.28.refs_4_.refs_3_), channel_id=1, source_target_pairs={{8,16},{12,20},{16,8},{20,12},{9,17},{13,21},{17,9},{21,13},{10,18... | collective-permute-start | bytes 1499144 | tf_op jit(solution)/shard_map/ppermute | solution.py:500
  63.4 1.3 collective-permute-start.33
  67.5 3.2 %project.3 = (f32[6,4,16,256]{3,2,1,0:T(8,128)S(1)}, f32[6,4,16,256]{3,2,1,0:T(8,128)}) custom-call(s32[1]{0:T(128)} %bitcast.12.which_ref.core_ref, bf16[256,2048]{1,0:T(8,128)(2,1)} %stack_panels.1.refs_0_, bf16[1024,256]{1,0:T(8,128)(2,1)S(1)} %straighten.2.refs_1_.refs_0_, bf16[976,256]{1,0:T(8,128)(2,1)S(1)} %straighten.3.refs_2_.refs_1_, ...), custom_call_target="tpu_custom_call" | custom-call | flops 786432000 | bytes 4882432 | tf_op jit(solution)/shard_map/project/pallas_call | solution.py:286
  70.7 14.2 %collective-permute-done.33.refs_9_ = bf16[976,256]{1,0:T(8,128)(2,1)} collective-permute-done((bf16[976,256]{1,0:T(8,128)(2,1)S(1)}, bf16[976,256]{1,0:T(8,128)(2,1)}, u32[]{:S(2)}, u32[]{:S(2)}) %collective-permute-start.33) | collective-permute-done | bytes 499744 | tf_op jit(solution)/shard_map/ppermute | solution.py:500
  84.9 1.3 collective-permute-start.36
  86.2 1.3 collective-permute-start.37
  87.6 37.0 %conditional.1 = (bf16[8,4,16,128]{3,2,1,0:T(8,128)(2,1)}, bf16[8,4,16,128]{3,2,1,0:T(8,128)(2,1)}, f32[64,4000]{1,0:T(8,128)}) conditional(s32[]{:T(128)} %convert_element_type.52, (s32[8]{0:T(128)S(1)}, f32[256]{0:T(256)S(1)}, bf16[4000,64]{0,1:T(8,128)(2,1)}, bf16[4000,64]{0,1:T(8,128)(2,1)}, s32[8,32]{1,0:T(8,128)S(1)}, ...), branch_computations={%region_6.14_spmd, %region_14.18_spmd} | conditional | flops 524621184 | bytes 65907736 | solution.py:642
  87.8 3.0 %project.2 = (f32[4,4,16,256]{3,2,1,0:T(8,128)S(1)}, f32[4,4,16,256]{3,2,1,0:T(8,128)S(1)}) custom-call(s32[1]{0:T(128)} %bitcast.4.core_ref, bf16[256,2048]{1,0:T(8,128)(2,1)} %get-tuple-element.354.refs_0_, bf16[256,2048]{1,0:T(8,128)(2,1)} %get-tuple-element.355.refs_1_, bf16[1024,256]{1,0:T(8,128)(2,1)} %get-tuple-element.356.refs_2_, ...), custom_call_target="tpu_custom_call" | custom-call | flops 524288000 | bytes 3596288 | tf_op jit(solution)/shard_map/cond/branch_1_fun/project/pallas_call | solution.py:286
  91.5 1.1 collective-permute-done.1.refs_3_
  92.7 1.6 %collective-permute-start.2 = (f32[10,16,256]{2,1,0:T(8,128)S(1)}, f32[10,16,256]{2,1,0:T(8,128)S(1)}, u32[]{:S(2)}, u32[]{:S(2)}) collective-permute-start(f32[10,16,256]{2,1,0:T(8,128)S(1)} %get-tuple-element.363), channel_id=1, source_target_pairs={{0,1},{1,0},{2,3},{3,2},{4,5},{5,4},{6,7},{7,6},{8,9},{9,8},{10,11... | collective-permute-start | bytes 491528 | tf_op jit(solution)/shard_map/cond/branch_1_fun/ppermute | solution.py:423
  94.2 1.5 %collective-permute-start.3 = (f32[10,16,256]{2,1,0:T(8,128)S(1)}, f32[10,16,256]{2,1,0:T(8,128)S(1)}, u32[]{:S(2)}, u32[]{:S(2)}) collective-permute-start(f32[10,16,256]{2,1,0:T(8,128)S(1)} %get-tuple-element.364), channel_id=1, source_target_pairs={{0,2},{1,3},{2,0},{3,1},{4,6},{5,7},{6,4},{7,5},{8,10},{9,11},{10,... | collective-permute-start | bytes 491528 | tf_op jit(solution)/shard_map/cond/branch_1_fun/ppermute | solution.py:423
  96.3 3.5 %collective-permute-done.2 = f32[10,16,256]{2,1,0:T(8,128)S(1)} collective-permute-done((f32[10,16,256]{2,1,0:T(8,128)S(1)}, f32[10,16,256]{2,1,0:T(8,128)S(1)}, u32[]{:S(2)}, u32[]{:S(2)}) %collective-permute-start.2) | collective-permute-done | bytes 163872 | tf_op jit(solution)/shard_map/cond/branch_1_fun/ppermute | solution.py:423
  99.8 4.2 %collective-permute-done.3 = f32[10,16,256]{2,1,0:T(8,128)S(1)} collective-permute-done((f32[10,16,256]{2,1,0:T(8,128)S(1)}, f32[10,16,256]{2,1,0:T(8,128)S(1)}, u32[]{:S(2)}, u32[]{:S(2)}) %collective-permute-start.3) | collective-permute-done | bytes 163872 | tf_op jit(solution)/shard_map/cond/branch_1_fun/ppermute | solution.py:423
  104.2 5.4 %collective-permute-start.6 = (f32[4,32]{1,0:T(4,128)S(1)}, f32[4,32]{1,0:T(4,128)S(1)}, u32[]{:S(2)}, u32[]{:S(2)}) collective-permute-start(f32[4,32]{1,0:T(4,128)S(1)} %select_reduce_fusion), channel_id=1, source_target_pairs={{0,16},{4,20},{8,24},{12,28},{16,0},{20,4},{24,8},{28,12},{1,17},{... | collective-permute-start | bytes 1544 | tf_op jit(solution)/shard_map/cond/branch_1_fun/ppermute | solution.py:423
  109.6 1.2 collective-permute-start.7
  111.2 3.8 %collective-permute-done.7 = f32[4,32]{1,0:T(4,128)S(1)} collective-permute-done((f32[4,32]{1,0:T(4,128)S(1)}, f32[4,32]{1,0:T(4,128)S(1)}, u32[]{:S(2)}, u32[]{:S(2)}) %collective-permute-start.7) | collective-permute-done | bytes 544 | tf_op jit(solution)/shard_map/cond/branch_1_fun/ppermute | solution.py:423
  115.2 1.6 %collective-permute-start.10 = (bf16[8,1,16,128]{3,2,1,0:T(8,128)(2,1)S(1)}, bf16[8,1,16,128]{3,2,1,0:T(8,128)(2,1)S(1)}, u32[]{:S(2)}, u32[]{:S(2)}) collective-permute-start(bf16[8,1,16,128]{3,2,1,0:T(8,128)(2,1)S(1)} %bitcast.67), channel_id=1, source_target_pairs={{0,3},{1,2},{2,1},{3,0},{4,7},{5,6},{6,5},{7,4},{8,11},{9,10},{10,... | collective-permute-start | bytes 98312 | tf_op jit(solution)/shard_map/cond/branch_1_fun/ppermute | solution.py:423
  116.8 1.5 %collective-permute-start.8 = (bf16[8,1,16,128]{3,2,1,0:T(8,128)(2,1)S(1)}, bf16[8,1,16,128]{3,2,1,0:T(8,128)(2,1)S(1)}, u32[]{:S(2)}, u32[]{:S(2)}) collective-permute-start(bf16[8,1,16,128]{3,2,1,0:T(8,128)(2,1)S(1)} %bitcast.68), channel_id=1, source_target_pairs={{0,1},{1,0},{2,3},{3,2},{4,5},{5,4},{6,7},{7,6},{8,9},{9,8},{10,11... | collective-permute-start | bytes 98312 | tf_op jit(solution)/shard_map/cond/branch_1_fun/ppermute | solution.py:423
  118.8 1.3 %collective-permute-done.10.refs_3_ = bf16[8,1,16,128]{3,2,1,0:T(8,128)(2,1)S(1)} collective-permute-done((bf16[8,1,16,128]{3,2,1,0:T(8,128)(2,1)S(1)}, bf16[8,1,16,128]{3,2,1,0:T(8,128)(2,1)S(1)}, u32[]{:S(2)}, u32[]{:S(2)}) %collective-permute-start.10) | collective-permute-done | bytes 32800 | tf_op jit(solution)/shard_map/cond/branch_1_fun/ppermute | solution.py:423
  120.7 1.5 %collective-permute-done.9.refs_2_ = bf16[8,1,16,128]{3,2,1,0:T(8,128)(2,1)S(1)} collective-permute-done((bf16[8,1,16,128]{3,2,1,0:T(8,128)(2,1)S(1)}, bf16[8,1,16,128]{3,2,1,0:T(8,128)(2,1)S(1)}, u32[]{:S(2)}, u32[]{:S(2)}) %collective-permute-start.9) | collective-permute-done | bytes 32800 | tf_op jit(solution)/shard_map/cond/branch_1_fun/ppermute | solution.py:423
  122.2 0.7 in_order.1
  122.9 1.7 %collective-permute-done.11 = bf16[8,4,16,128]{3,2,1,0:T(8,128)(2,1)} collective-permute-done((bf16[8,4,16,128]{3,2,1,0:T(8,128)(2,1)}, bf16[8,4,16,128]{3,2,1,0:T(8,128)(2,1)}, u32[]{:S(2)}, u32[]{:S(2)}) %collective-permute-start.11) | collective-permute-done | bytes 131104 | tf_op jit(solution)/shard_map/cond/branch_1_fun/ppermute | solution.py:423
  124.6 3.3 %contract.1 = (f32[64,2000]{1,0:T(8,128)S(1)}, f32[64,2000]{1,0:T(8,128)S(1)}) custom-call(s32[1]{0:T(128)} %bitcast.12.which_ref.core_ref, bf16[8,4,16,128]{3,2,1,0:T(8,128)(2,1)} %get-tuple-element.417.kernel_ref, bf16[8,4,16,128]{3,2,1,0:T(8,128)(2,1)} %get-tuple-element.418.got_ref, bf16[1024,256]{1,0:T(8,128)(2,1)S(1)} %straighten.2.refs_1_.refs_0_, ...), custom_call_target="tpu_custom_call" | custom-call | flops 524288000 | bytes 5120000 | tf_op jit(solution)/shard_map/contract/pallas_call | solution.py:351
  128.2 1.7 %collective-permute-done.38.back_ref = f32[64,2000]{1,0:T(8,128)S(1)} collective-permute-done((f32[64,2000]{1,0:T(8,128)S(1)}, f32[64,2000]{1,0:T(8,128)S(1)}, u32[]{:S(2)}, u32[]{:S(2)}) %collective-permute-start.38) | collective-permute-done | bytes 512032 | tf_op jit(solution)/shard_map/ppermute | solution.py:423
  129.9 1.8 %finish.1 = f32[64,4000]{1,0:T(8,128)} custom-call(s32[2]{0:T(128)S(1)} %pad_add_fusion.2.flags_ref, f32[64,2000]{1,0:T(8,128)S(1)} %get-tuple-element.421.ours_ref, f32[64,2000]{1,0:T(8,128)S(1)} %collective-permute-done.38.back_ref, f32[64,4000]{1,0:T(8,128)} %get-tuple-element.423.other_ref), custom_call_target="tpu_custom_call", output_to_operand_aliasing={{}: (3, {})} | custom-call | tf_op jit(solution)/shard_map/finish/pallas_call | solution.py:392
  (117 shorter events, 10.7 us)
Async XLA Ops:
  0.0 1.8 %copy-start.5 = (f32[256]{0:T(256)S(1)}, f32[256]{0:T(256)}, u32[]{:S(2)}) copy-start(f32[256]{0:T(256)} %param.17) | copy-start | bytes 3076
  0.0 1.9 %copy-start.6 = (s32[8]{0:T(128)S(1)}, s32[8]{0:T(128)}, u32[]{:S(2)}) copy-start(s32[8]{0:T(128)} %param.18) | copy-start | bytes 100
  0.0 2.3 %copy-start.4 = (s32[8,32]{1,0:T(8,128)S(1)}, s32[8,32]{1,0:T(8,128)}, u32[]{:S(2)}) copy-start(s32[8,32]{1,0:T(8,128)} %param.19) | copy-start | bytes 3076
  1.3 13.2 %collective-permute-start.15 = (bf16[2000,256]{1,0:T(8,128)(2,1)S(1)}, bf16[2000,256]{1,0:T(8,128)(2,1)}, u32[]{:S(2)}, u32[]{:S(2)}) collective-permute-start(bf16[2000,256]{1,0:T(8,128)(2,1)S(1)} %half_of.3), channel_id=1, source_target_pairs={{0,4},{4,0},{8,12},{12,8},{16,20},{20,16},{24,28},{28,24},{1,5},{5... | collective-permute-start | bytes 3072008 | tf_op jit(solution)/shard_map/ppermute | solution.py:423
  1.8 2.3 %collective-permute-start.18 = (f32[1,256]{1,0:T(1,128)S(1)}, f32[1,256]{1,0:T(1,128)S(1)}, u32[]{:S(2)}, u32[]{:S(2)}) collective-permute-start(f32[1,256]{1,0:T(1,128)S(1)} %bitcast.84), channel_id=1, source_target_pairs={{0,4},{4,0},{8,12},{12,8},{16,20},{20,16},{24,28},{28,24},{1,5},{5... | collective-permute-start | bytes 3080 | tf_op jit(solution)/shard_map/ppermute | solution.py:423
  1.9 2.2 %collective-permute-start.17 = (s32[1,8]{1,0:T(1,128)S(1)}, s32[1,8]{1,0:T(1,128)S(1)}, u32[]{:S(2)}, u32[]{:S(2)}) collective-permute-start(s32[1,8]{1,0:T(1,128)S(1)} %bitcast.86), channel_id=1, source_target_pairs={{0,4},{4,0},{8,12},{12,8},{16,20},{20,16},{24,28},{28,24},{1,5},{5... | collective-permute-start | bytes 104 | tf_op jit(solution)/shard_map/ppermute | solution.py:423
  2.4 10.3 %collective-permute-start.16 = (s32[16,8]{0,1:T(8,128)S(1)}, s32[16,8]{0,1:T(8,128)S(1)}, u32[]{:S(2)}, u32[]{:S(2)}) collective-permute-start(s32[16,8]{0,1:T(8,128)S(1)} %get-tuple-element.493), channel_id=1, source_target_pairs={{0,4},{4,0},{8,12},{12,8},{16,20},{20,16},{24,28},{28,24},{1,5},{5... | collective-permute-start | bytes 1544 | tf_op jit(solution)/shard_map/ppermute | solution.py:423
  4.2 8.7 %collective-permute-start.19 = (f32[1,528]{1,0:T(1,128)S(1)}, f32[1,528]{1,0:T(1,128)S(1)}, u32[]{:S(2)}, u32[]{:S(2)}) collective-permute-start(f32[1,528]{1,0:T(1,128)S(1)} %pad_maximum_fusion.3), channel_id=1, source_target_pairs={{0,8},{4,12},{8,16},{12,20},{16,24},{20,28},{24,0},{28,4},{1,9},{5... | collective-permute-start | bytes 6344 | tf_op jit(solution)/shard_map/ppermute | solution.py:459
  7.2 5.8 %collective-permute-start.20 = (f32[1,528]{1,0:T(1,128)S(1)}, f32[1,528]{1,0:T(1,128)S(1)}, u32[]{:S(2)}, u32[]{:S(2)}) collective-permute-start(f32[1,528]{1,0:T(1,128)S(1)} %pad_maximum_fusion.3), channel_id=1, source_target_pairs={{0,16},{4,20},{8,24},{12,28},{16,0},{20,4},{24,8},{28,12},{1,17},{... | collective-permute-start | bytes 6344 | tf_op jit(solution)/shard_map/ppermute | solution.py:459
  9.7 3.6 %collective-permute-start.21 = (f32[1,528]{1,0:T(1,128)S(1)}, f32[1,528]{1,0:T(1,128)S(1)}, u32[]{:S(2)}, u32[]{:S(2)}) collective-permute-start(f32[1,528]{1,0:T(1,128)S(1)} %pad_maximum_fusion.3), channel_id=1, source_target_pairs={{0,24},{4,28},{8,0},{12,4},{16,8},{20,12},{24,16},{28,20},{1,25},{... | collective-permute-start | bytes 6344 | tf_op jit(solution)/shard_map/ppermute | solution.py:459
  18.4 7.2 %collective-permute-start.22 = (bf16[1024,128]{1,0:T(8,128)(2,1)S(1)}, bf16[1024,128]{1,0:T(8,128)(2,1)S(1)}, u32[]{:S(2)}, u32[]{:S(2)}) collective-permute-start(bf16[1024,128]{1,0:T(8,128)(2,1)S(1)} %get-tuple-element.397), channel_id=1, source_target_pairs={{0,8},{4,12},{8,0},{12,4},{16,24},{20,28},{24,16},{28,20},{1,9},{5... | collective-permute-start | bytes 786440 | tf_op jit(solution)/shard_map/ppermute | solution.py:500
  18.7 6.9 %collective-permute-start.23 = (bf16[1024,128]{1,0:T(8,128)(2,1)S(1)}, bf16[1024,128]{1,0:T(8,128)(2,1)S(1)}, u32[]{:S(2)}, u32[]{:S(2)}) collective-permute-start(bf16[1024,128]{1,0:T(8,128)(2,1)S(1)} %get-tuple-element.398), channel_id=1, source_target_pairs={{8,16},{12,20},{16,8},{20,12},{9,17},{13,21},{17,9},{21,13},{10,18... | collective-permute-start | bytes 786440 | tf_op jit(solution)/shard_map/ppermute | solution.py:500
  22.0 0.8 copy-start
  22.8 28.0 %collective-permute-start.34 = (bf16[128,2048]{1,0:T(8,128)(2,1)}, bf16[128,2048]{1,0:T(8,128)(2,1)}, u32[]{:S(2)}, u32[]{:S(2)}) collective-permute-start(bf16[128,2048]{1,0:T(8,128)(2,1)} %get-tuple-element.406), channel_id=1, source_target_pairs={{0,4},{4,0},{8,12},{12,8},{16,20},{20,16},{24,28},{28,24},{1,5},{5... | collective-permute-start | bytes 1572872 | tf_op jit(solution)/shard_map/ppermute | solution.py:423
  25.8 28.3 %collective-permute-start.24 = (bf16[1024,256]{1,0:T(8,128)(2,1)S(1)}, bf16[1024,256]{1,0:T(8,128)(2,1)S(1)}, u32[]{:S(2)}, u32[]{:S(2)}) collective-permute-start(bf16[1024,256]{1,0:T(8,128)(2,1)S(1)} %straighten.2.refs_1_.refs_0_), channel_id=1, source_target_pairs={{0,8},{4,12},{8,0},{12,4},{16,24},{20,28},{24,16},{28,20},{1,9},{5... | collective-permute-start | bytes 1572872 | tf_op jit(solution)/shard_map/ppermute | solution.py:500
  29.5 24.6 %collective-permute-start.30 = (bf16[1024,256]{1,0:T(8,128)(2,1)S(1)}, bf16[1024,256]{1,0:T(8,128)(2,1)S(1)}, u32[]{:S(2)}, u32[]{:S(2)}) collective-permute-start(bf16[1024,256]{1,0:T(8,128)(2,1)S(1)} %straighten.2.refs_1_.refs_0_), channel_id=1, source_target_pairs={{8,16},{12,20},{16,8},{20,12},{9,17},{13,21},{17,9},{21,13},{10,18... | collective-permute-start | bytes 1572872 | tf_op jit(solution)/shard_map/ppermute | solution.py:500
  30.2 16.0 %collective-permute-start.26 = (bf16[976,128]{1,0:T(8,128)(2,1)}, bf16[976,128]{1,0:T(8,128)(2,1)S(1)}, u32[]{:S(2)}, u32[]{:S(2)}) collective-permute-start(bf16[976,128]{1,0:T(8,128)(2,1)} %get-tuple-element.401), channel_id=1, source_target_pairs={{0,8},{4,12},{8,0},{12,4},{16,24},{20,28},{24,16},{28,20},{1,9},{5... | collective-permute-start | bytes 749576 | tf_op jit(solution)/shard_map/ppermute | solution.py:500
  33.2 13.0 %collective-permute-start.27 = (bf16[976,128]{1,0:T(8,128)(2,1)}, bf16[976,128]{1,0:T(8,128)(2,1)S(1)}, u32[]{:S(2)}, u32[]{:S(2)}) collective-permute-start(bf16[976,128]{1,0:T(8,128)(2,1)} %get-tuple-element.402), channel_id=1, source_target_pairs={{8,16},{12,20},{16,8},{20,12},{9,17},{13,21},{17,9},{21,13},{10,18... | collective-permute-start | bytes 749576 | tf_op jit(solution)/shard_map/ppermute | solution.py:500
  46.4 15.6 %collective-permute-start.28 = (bf16[976,256]{1,0:T(8,128)(2,1)S(1)}, bf16[976,256]{1,0:T(8,128)(2,1)S(1)}, u32[]{:S(2)}, u32[]{:S(2)}) collective-permute-start(bf16[976,256]{1,0:T(8,128)(2,1)S(1)} %straighten.3.refs_2_.refs_1_), channel_id=1, source_target_pairs={{0,8},{4,12},{8,0},{12,4},{16,24},{20,28},{24,16},{28,20},{1,9},{5... | collective-permute-start | bytes 1499144 | tf_op jit(solution)/shard_map/ppermute | solution.py:500
  50.1 13.3 %collective-permute-start.32 = (bf16[976,256]{1,0:T(8,128)(2,1)S(1)}, bf16[976,256]{1,0:T(8,128)(2,1)S(1)}, u32[]{:S(2)}, u32[]{:S(2)}) collective-permute-start(bf16[976,256]{1,0:T(8,128)(2,1)S(1)} %straighten.3.refs_2_.refs_1_), channel_id=1, source_target_pairs={{8,16},{12,20},{16,8},{20,12},{9,17},{13,21},{17,9},{21,13},{10,18... | collective-permute-start | bytes 1499144 | tf_op jit(solution)/shard_map/ppermute | solution.py:500
  50.8 1.0 copy-start.1
  54.1 30.8 %collective-permute-start.35 = (bf16[256,2048]{1,0:T(8,128)(2,1)}, bf16[256,2048]{1,0:T(8,128)(2,1)}, u32[]{:S(2)}, u32[]{:S(2)}) collective-permute-start(bf16[256,2048]{1,0:T(8,128)(2,1)} %stack_panels.1.refs_0_), channel_id=1, source_target_pairs={{0,8},{4,12},{24,16},{28,20},{1,9},{5,13},{25,17},{29,21},{2,10},{... | collective-permute-start | bytes 3145736 | tf_op jit(solution)/shard_map/ppermute | solution.py:500
  59.1 25.8 %collective-permute-start.25 = (bf16[1024,256]{1,0:T(8,128)(2,1)S(1)}, bf16[1024,256]{1,0:T(8,128)(2,1)}, u32[]{:S(2)}, u32[]{:S(2)}) collective-permute-start(bf16[1024,256]{1,0:T(8,128)(2,1)S(1)} %collective-permute-done.24.refs_3_.refs_2_), channel_id=1, source_target_pairs={{8,16},{12,20},{16,8},{20,12},{9,17},{13,21},{17,9},{21,13},{10,18... | collective-permute-start | bytes 1572872 | tf_op jit(solution)/shard_map/ppermute | solution.py:500
  60.5 24.4 %collective-permute-start.31 = (bf16[1024,256]{1,0:T(8,128)(2,1)S(1)}, bf16[1024,256]{1,0:T(8,128)(2,1)}, u32[]{:S(2)}, u32[]{:S(2)}) collective-permute-start(bf16[1024,256]{1,0:T(8,128)(2,1)S(1)} %collective-permute-done.30.refs_5_.refs_4_), channel_id=1, source_target_pairs={{8,0},{12,4},{16,24},{20,28},{9,1},{13,5},{17,25},{21,29},{10,2},{... | collective-permute-start | bytes 1572872 | tf_op jit(solution)/shard_map/ppermute | solution.py:500
  62.0 8.7 %collective-permute-start.29 = (bf16[976,256]{1,0:T(8,128)(2,1)S(1)}, bf16[976,256]{1,0:T(8,128)(2,1)}, u32[]{:S(2)}, u32[]{:S(2)}) collective-permute-start(bf16[976,256]{1,0:T(8,128)(2,1)S(1)} %collective-permute-done.28.refs_4_.refs_3_), channel_id=1, source_target_pairs={{8,16},{12,20},{16,8},{20,12},{9,17},{13,21},{17,9},{21,13},{10,18... | collective-permute-start | bytes 1499144 | tf_op jit(solution)/shard_map/ppermute | solution.py:500
  63.4 21.5 %collective-permute-start.33 = (bf16[976,256]{1,0:T(8,128)(2,1)S(1)}, bf16[976,256]{1,0:T(8,128)(2,1)}, u32[]{:S(2)}, u32[]{:S(2)}) collective-permute-start(bf16[976,256]{1,0:T(8,128)(2,1)S(1)} %collective-permute-done.32.refs_6_.refs_5_), channel_id=1, source_target_pairs={{8,0},{12,4},{16,24},{20,28},{9,1},{13,5},{17,25},{21,29},{10,2},{... | collective-permute-start | bytes 1499144 | tf_op jit(solution)/shard_map/ppermute | solution.py:500
  84.9 39.7 %collective-permute-start.36 = (bf16[1024,256]{1,0:T(8,128)(2,1)}, bf16[1024,256]{1,0:T(8,128)(2,1)}, u32[]{:S(2)}, u32[]{:S(2)}) collective-permute-start(bf16[1024,256]{1,0:T(8,128)(2,1)} %collective-permute-done.25.refs_10_), channel_id=1, source_target_pairs={{8,0},{12,4},{16,24},{20,28},{9,1},{13,5},{17,25},{21,29},{10,2},{... | collective-permute-start | bytes 1572872 | tf_op jit(solution)/shard_map/ppermute | solution.py:500
  86.2 38.4 %collective-permute-start.37 = (bf16[976,256]{1,0:T(8,128)(2,1)}, bf16[976,256]{1,0:T(8,128)(2,1)}, u32[]{:S(2)}, u32[]{:S(2)}) collective-permute-start(bf16[976,256]{1,0:T(8,128)(2,1)} %collective-permute-done.29.refs_11_), channel_id=1, source_target_pairs={{8,0},{12,4},{16,24},{20,28},{9,1},{13,5},{17,25},{21,29},{10,2},{... | collective-permute-start | bytes 1499144 | tf_op jit(solution)/shard_map/ppermute | solution.py:500
  87.8 4.8 %collective-permute-start = (f32[6,4,16,256]{3,2,1,0:T(8,128)}, f32[6,4,16,256]{3,2,1,0:T(8,128)S(1)}, u32[]{:S(2)}, u32[]{:S(2)}) collective-permute-start(f32[6,4,16,256]{3,2,1,0:T(8,128)} %get-tuple-element.352), channel_id=1, source_target_pairs={{0,4},{4,0},{8,12},{12,8},{16,20},{20,16},{24,28},{28,24},{1,5},{5... | collective-permute-start | bytes 1179656 | tf_op jit(solution)/shard_map/cond/branch_1_fun/ppermute | solution.py:423
  90.9 1.7 %collective-permute-start.1 = (f32[4,4,16,256]{3,2,1,0:T(8,128)S(1)}, f32[4,4,16,256]{3,2,1,0:T(8,128)S(1)}, u32[]{:S(2)}, u32[]{:S(2)}) collective-permute-start(f32[4,4,16,256]{3,2,1,0:T(8,128)S(1)} %get-tuple-element.361), channel_id=1, source_target_pairs={{0,4},{4,0},{8,12},{12,8},{16,20},{20,16},{24,28},{28,24},{1,5},{5... | collective-permute-start | bytes 786440 | tf_op jit(solution)/shard_map/cond/branch_1_fun/ppermute | solution.py:423
  92.7 7.1 %collective-permute-start.2 = (f32[10,16,256]{2,1,0:T(8,128)S(1)}, f32[10,16,256]{2,1,0:T(8,128)S(1)}, u32[]{:S(2)}, u32[]{:S(2)}) collective-permute-start(f32[10,16,256]{2,1,0:T(8,128)S(1)} %get-tuple-element.363), channel_id=1, source_target_pairs={{0,1},{1,0},{2,3},{3,2},{4,5},{5,4},{6,7},{7,6},{8,9},{9,8},{10,11... | collective-permute-start | bytes 491528 | tf_op jit(solution)/shard_map/cond/branch_1_fun/ppermute | solution.py:423
  94.2 9.7 %collective-permute-start.3 = (f32[10,16,256]{2,1,0:T(8,128)S(1)}, f32[10,16,256]{2,1,0:T(8,128)S(1)}, u32[]{:S(2)}, u32[]{:S(2)}) collective-permute-start(f32[10,16,256]{2,1,0:T(8,128)S(1)} %get-tuple-element.364), channel_id=1, source_target_pairs={{0,2},{1,3},{2,0},{3,1},{4,6},{5,7},{6,4},{7,5},{8,10},{9,11},{10,... | collective-permute-start | bytes 491528 | tf_op jit(solution)/shard_map/cond/branch_1_fun/ppermute | solution.py:423
  95.8 8.2 %collective-permute-start.4 = (f32[10,16,256]{2,1,0:T(8,128)S(1)}, f32[10,16,256]{2,1,0:T(8,128)S(1)}, u32[]{:S(2)}, u32[]{:S(2)}) collective-permute-start(f32[10,16,256]{2,1,0:T(8,128)S(1)} %get-tuple-element.365), channel_id=1, source_target_pairs={{0,3},{1,2},{2,1},{3,0},{4,7},{5,6},{6,5},{7,4},{8,11},{9,10},{10,... | collective-permute-start | bytes 491528 | tf_op jit(solution)/shard_map/cond/branch_1_fun/ppermute | solution.py:423
  104.2 7.0 %collective-permute-start.6 = (f32[4,32]{1,0:T(4,128)S(1)}, f32[4,32]{1,0:T(4,128)S(1)}, u32[]{:S(2)}, u32[]{:S(2)}) collective-permute-start(f32[4,32]{1,0:T(4,128)S(1)} %select_reduce_fusion), channel_id=1, source_target_pairs={{0,16},{4,20},{8,24},{12,28},{16,0},{20,4},{24,8},{28,12},{1,17},{... | collective-permute-start | bytes 1544 | tf_op jit(solution)/shard_map/cond/branch_1_fun/ppermute | solution.py:423
  109.6 5.4 %collective-permute-start.7 = (f32[4,32]{1,0:T(4,128)S(1)}, f32[4,32]{1,0:T(4,128)S(1)}, u32[]{:S(2)}, u32[]{:S(2)}) collective-permute-start(f32[4,32]{1,0:T(4,128)S(1)} %select_reduce_fusion), channel_id=1, source_target_pairs={{0,24},{4,28},{8,16},{12,20},{16,8},{20,12},{24,0},{28,4},{1,25},{... | collective-permute-start | bytes 1544 | tf_op jit(solution)/shard_map/cond/branch_1_fun/ppermute | solution.py:423
  110.8 4.2 %collective-permute-start.5 = (f32[36,256]{1,0:T(8,128)S(1)}, f32[36,256]{1,0:T(8,128)S(1)}, u32[]{:S(2)}, u32[]{:S(2)}) collective-permute-start(f32[36,256]{1,0:T(8,128)S(1)} %select_maximum_fusion), channel_id=1, source_target_pairs={{0,8},{4,12},{8,0},{12,4},{16,24},{20,28},{24,16},{28,20},{1,9},{5... | collective-permute-start | bytes 110600 | tf_op jit(solution)/shard_map/cond/branch_1_fun/ppermute | solution.py:423
  115.2 4.9 %collective-permute-start.10 = (bf16[8,1,16,128]{3,2,1,0:T(8,128)(2,1)S(1)}, bf16[8,1,16,128]{3,2,1,0:T(8,128)(2,1)S(1)}, u32[]{:S(2)}, u32[]{:S(2)}) collective-permute-start(bf16[8,1,16,128]{3,2,1,0:T(8,128)(2,1)S(1)} %bitcast.67), channel_id=1, source_target_pairs={{0,3},{1,2},{2,1},{3,0},{4,7},{5,6},{6,5},{7,4},{8,11},{9,10},{10,... | collective-permute-start | bytes 98312 | tf_op jit(solution)/shard_map/cond/branch_1_fun/ppermute | solution.py:423
  116.8 3.9 %collective-permute-start.8 = (bf16[8,1,16,128]{3,2,1,0:T(8,128)(2,1)S(1)}, bf16[8,1,16,128]{3,2,1,0:T(8,128)(2,1)S(1)}, u32[]{:S(2)}, u32[]{:S(2)}) collective-permute-start(bf16[8,1,16,128]{3,2,1,0:T(8,128)(2,1)S(1)} %bitcast.68), channel_id=1, source_target_pairs={{0,1},{1,0},{2,3},{3,2},{4,5},{5,4},{6,7},{7,6},{8,9},{9,8},{10,11... | collective-permute-start | bytes 98312 | tf_op jit(solution)/shard_map/cond/branch_1_fun/ppermute | solution.py:423
  118.3 3.9 %collective-permute-start.9 = (bf16[8,1,16,128]{3,2,1,0:T(8,128)(2,1)S(1)}, bf16[8,1,16,128]{3,2,1,0:T(8,128)(2,1)S(1)}, u32[]{:S(2)}, u32[]{:S(2)}) collective-permute-start(bf16[8,1,16,128]{3,2,1,0:T(8,128)(2,1)S(1)} %bitcast.69), channel_id=1, source_target_pairs={{0,2},{1,3},{2,0},{3,1},{4,6},{5,7},{6,4},{7,5},{8,10},{9,11},{10,... | collective-permute-start | bytes 98312 | tf_op jit(solution)/shard_map/cond/branch_1_fun/ppermute | solution.py:423
  122.9 1.7 %collective-permute-start.11 = (bf16[8,4,16,128]{3,2,1,0:T(8,128)(2,1)}, bf16[8,4,16,128]{3,2,1,0:T(8,128)(2,1)}, u32[]{:S(2)}, u32[]{:S(2)}) collective-permute-start(bf16[8,4,16,128]{3,2,1,0:T(8,128)(2,1)} %in_order.1), channel_id=1, source_target_pairs={{0,4},{4,0},{8,12},{12,8},{16,20},{20,16},{24,28},{28,24},{1,5},{5... | collective-permute-start | bytes 393224 | tf_op jit(solution)/shard_map/cond/branch_1_fun/ppermute | solution.py:423
  127.9 2.0 %collective-permute-start.38 = (f32[64,2000]{1,0:T(8,128)S(1)}, f32[64,2000]{1,0:T(8,128)S(1)}, u32[]{:S(2)}, u32[]{:S(2)}) collective-permute-start(f32[64,2000]{1,0:T(8,128)S(1)} %get-tuple-element.422), channel_id=1, source_target_pairs={{0,4},{4,0},{8,12},{12,8},{16,20},{20,16},{24,28},{28,24},{1,5},{5... | collective-permute-start | bytes 1536008 | tf_op jit(solution)/shard_map/ppermute | solution.py:423

commit v4 on v3

--- a/solution.py
+++ b/solution.py
@@ -90,16 +90,11 @@
     )(which[None], whole)
 
 
-def basis_cuts(half):
-    cut = -(-half // 256) * 128
-    return [(0, cut), (cut, half)]
-
-
 def compact(mine, got, mine_sig, got_sig, mine_to, got_to, width, tile, odd):
     half, rows = mine.shape
     blocks = mine_sig.shape[0]
     count = rows // tile + 2
-    cuts = basis_cuts(half)
+    cuts = [(0, half)]
 
     def body(odd_ref, mine_ref, got_ref, msig_ref, gsig_ref, mto_ref, gto_ref, *outs):
         block_of = lax.broadcasted_iota(jnp.int32, (half, blocks), 0)
@@ -140,12 +135,12 @@
     return [out[p * count : (p + 1) * count] for p in range(len(cuts))]
 
 
-def straighten(tiles, by_a, by_b, odd):
+def straighten(tiles, by_b, by_a, odd):
     half, tile = by_a.shape
     count = len(tiles)
 
     def body(odd_ref, *refs):
-        tile_refs, a_ref, b_ref, out_ref = refs[:count], *refs[count:]
+        tile_refs, b_ref, a_ref, out_ref = refs[:count], *refs[count:]
         even = odd_ref[0] == 0
         for j in range(count):
             value = tile_refs[j][...]
@@ -162,7 +157,7 @@
         out_specs=WHOLE,
         compiler_params=pltpu.CompilerParams(vmem_limit_bytes=8 * MIB),
         name="straighten",
-    )(odd[None], *tiles, by_a, by_b)
+    )(odd[None], *tiles, by_b, by_a)
 
 
 def panel_halves(occupied, trial, core):
@@ -452,37 +447,34 @@
         ),
         axis=1,
     )
-    if chips <= 4:
-        heard = [told]
-        for step in range(1, chips):
-            around = [(i, (i + 2 * step) % grid_count) for i in range(grid_count)]
-            heard.append(lax.ppermute(told, "grid", around))
-        heard = jnp.concatenate(heard)
-        behind = (chip - lax.iota(jnp.int32, chips)) % chips
-        pick = behind[:, None, None] == lax.iota(jnp.int32, chips)[None, :, None]
-        told = jnp.sum(jnp.where(pick, heard[None], 0.0), axis=1)
-    else:
-        for bit in grid_bits[1:]:
+    live = rows * chips
+    for bit in grid_bits[1:2]:
+        told = doubled(told, "grid", bit, 0)
+    if chips > 4:
+        for bit in grid_bits[2:]:
             told = doubled(told, "grid", bit, 0)
+
+    def places_of(sizes, first):
+        count = sizes.shape[0]
+        batch = lax.broadcasted_iota(jnp.int32, (count, count), 0)
+        before = lax.broadcasted_iota(jnp.int32, (count, count), 1) < batch
+        start = first + jnp.sum(jnp.where(before, sizes[None, :], 0), axis=1)
+        position = lax.broadcasted_iota(jnp.int32, (count, slots), 1)
+        to = jnp.where(position < sizes[:, None], start[:, None] + position, -4 * live)
+        return to.reshape(-1, rows), start
+
     sizes = told[:, : 2 * batches].astype(jnp.int32).reshape(-1)
-    weights = told[:, 2 * batches :].reshape(-1)
-
-    batch = lax.broadcasted_iota(jnp.int32, (sizes.shape[0], sizes.shape[0]), 0)
-    before = lax.broadcasted_iota(jnp.int32, (sizes.shape[0], sizes.shape[0]), 1) < batch
-    start = jnp.sum(jnp.where(before, sizes[None, :], 0), axis=1)
-    position = lax.broadcasted_iota(jnp.int32, (sizes.shape[0], slots), 1)
-    to = jnp.where(position < sizes[:, None], start[:, None] + position, -4 * rows * grid_count)
-    to = to.reshape(grid_count, rows)
-    first = start.reshape(chips, -1)[:, 0]
+    first = jnp.where((chip >= 2) & (chips <= 4), live - jnp.sum(sizes), 0)
+    near_to, _ = places_of(sizes, first)
+    near_place = place if chips > 4 else place % 4
+    for bit in grid_bits[2:] if chips <= 4 else []:
+        told = doubled(told, "grid", bit, 0)
     margin = rows // 2 if (rows // 2) % (8 * shares) == 0 else rows
-    nominal = rows * lax.iota(jnp.int32, chips)
-    fits = jnp.all(jnp.abs(first - nominal) <= margin) & (jnp.sum(sizes) <= rows * chips)
-
     tile = margin
     piece = tile // shares
     base = rows * chip - margin
-    mine_to = lax.dynamic_index_in_dim(to, place, 0, keepdims=False) - base
-    got_to = lax.dynamic_index_in_dim(to, place ^ 1, 0, keepdims=False) - base
+    mine_to = lax.dynamic_index_in_dim(near_to, near_place, 0, keepdims=False) - base
+    got_to = lax.dynamic_index_in_dim(near_to, near_place ^ 1, 0, keepdims=False) - base
     odd = chip % 2
     compacted = compact(
         mine,
@@ -512,9 +504,17 @@
         (sent(for_b, over(1, 1)), sent(for_a, over(0, 1))) for for_b, *_, for_a in compacted
     ]
     own = tuple(
-        straighten(tiles, by_a, by_b, odd)
+        straighten(tiles, by_b, by_a, odd)
         for (_, *tiles, _), (by_b, by_a) in zip(compacted, arrived)
     )
+
+    own, told = lax.optimization_barrier((own, told))
+    sizes = told[:, : 2 * batches].astype(jnp.int32).reshape(-1)
+    weights = told[:, 2 * batches :].reshape(-1)
+    to, start = places_of(sizes, 0)
+    first = start.reshape(chips, -1)[:, 0]
+    nominal = rows * lax.iota(jnp.int32, chips)
+    fits = jnp.all(jnp.abs(first - nominal) <= margin) & (jnp.sum(sizes) == live)
 
     _, occupied_turned, trial_turned = lax.optimization_barrier(
         (compacted[0][0], occupied.T, trial.T)
@@ -538,8 +538,7 @@
         moved = [(sent(a, over(1, t)), sent(b, over(0, t))) for a, b in zip(by_a, by_b)]
         by_b, by_a = (tuple(x) for x in zip(*moved))
         if t == 1:
-            _, far_panels = lax.optimization_barrier(((by_a[0], by_b[0]), panels))
-            far_panels = sent(far_panels, ends)
+            far_panels = sent(panels, ends)
         a_at, b_at = valid(chip + side * t), valid(chip - side * t)
         if 2 * t > last:
             stages.append([([by_a, by_b], jnp.maximum(a_at, b_at))])

time: 132 us -> 128 us (0.970)
  starting transfers between devices: 48.5 us -> 36.1 us
  waiting for transfers between devices: 50.6 us -> 56.4 us
  local copies, waits for them, and re-layouts: 3.91 us -> 6.16 us
  Pallas kernels: 23.4 us -> 21.2 us
  other arithmetic: 3.39 us -> 4.76 us
    ppermute x18 -> x20, waiting for transfers between devices: 21.1 us -> 32.4 us  [flip(): return lax.ppermute(x, axis, [(i, i ^ bit) for i in range(count)])]
    ppermute x15 -> x8, starting transfers between devices: 25.9 us -> 17.8 us  [sent(): return lax.ppermute(x, 'grid', along(pairs))]
    ppermute x3 -> x0, starting transfers between devices: 6.85 us -> none  [per_device(): heard.append(lax.ppermute(told, 'grid', around))]
    ppermute x15 -> x8, waiting for transfers between devices: 29.2 us -> 24 us  [sent(): return lax.ppermute(x, 'grid', along(pairs))]
    ppermute x18 -> x20, starting transfers between devices: 15.7 us -> 18.2 us  [flip(): return lax.ppermute(x, axis, [(i, i ^ bit) for i in range(count)])]
    unnamed x13 -> x17, local copies, waits for them, and re-layouts: 1.94 us -> 4.1 us
    pallas_call x1, Pallas kernels: 3.83 us -> 1.78 us  [compact(): pl.pallas_call(body, out_shape=shapes, in_specs=[SCALARS] + [WHOLE] * 6,...]
  transfers between devices with their start and end apart: 36 -> 28, of which waited for: 16 -> 16; matrix products, arithmetic and copies ran while one was open for 4% -> 5% of each run, Pallas kernels for 10% -> 11%
where the time goes in v4:
time: 128 us; the launch traced here: 127 us
  waiting for transfers between devices  56.4 us (44%)
  starting transfers between devices  36.1 us (28%)
  Pallas kernels  21.2 us (17%)
  local copies, waits for them, and re-layouts  6.16 us (5%)
  other arithmetic  4.76 us (4%)
  between operations  2.42 us (2%)
    ppermute x20, waiting for transfers between devices, flip(): return lax.ppermute(x, axis, [(i, i ^ bit) for i in range(count)])  32.4 us
    ppermute x8, waiting for transfers between devices, sent(): return lax.ppermute(x, 'grid', along(pairs))  24 us
    ppermute x20, starting transfers between devices, flip(): return lax.ppermute(x, axis, [(i, i ^ bit) for i in range(count)])  18.2 us
    ppermute x8, starting transfers between devices, sent(): return lax.ppermute(x, 'grid', along(pairs))  17.8 us
    pallas_call x2, Pallas kernels, project(): pl.pallas_call(body, out_shape=(shape, shape), in_specs=[SCALARS] + [WHOL...  6.19 us
    unnamed x17, local copies, waits for them, and re-layouts  4.1 us
    pallas_call x1, Pallas kernels, contract(): pl.pallas_call(body, out_shape=(shape, shape), in_specs=[SCALARS] + [WHOL...  3.3 us
  transfers between devices with their start and end apart: 28, of which 16 were waited for; matrix products, arithmetic and copies ran while one was open for 5% of the time, Pallas kernels for 11%

profile of v4, /device:TPU:0, one launch (start us, length us, event | category | flops | bytes accessed | tf_op | source)
XLA Modules:
  0.0 127.3 jit_solution(8253583567791520013)
XLA Ops:
  0.5 0.8 dynamic-slice_bitcast_fusion
  1.8 1.2 half_of.3
  3.4 3.0 %collective-permute-start.19 = (f32[1,528]{1,0:T(1,128)S(1)}, f32[1,528]{1,0:T(1,128)S(1)}, u32[]{:S(2)}, u32[]{:S(2)}) collective-permute-start(f32[1,528]{1,0:T(1,128)S(1)} %pad_maximum_fusion.2), channel_id=1, source_target_pairs={{0,8},{4,12},{8,0},{12,4},{16,24},{20,28},{24,16},{28,20},{1,9},{5... | collective-permute-start | bytes 6344 | tf_op jit(solution)/shard_map/ppermute | solution.py:418
  6.8 1.2 half_of.2.mine_ref
  8.6 0.6 fusion.13
  10.7 0.9 copy-done.2
  11.7 1.2 copy-done.3
  12.9 1.8 %compact.1 = (bf16[2000,128]{1,0:T(8,128)(2,1)S(1)}, bf16[2000,128]{1,0:T(8,128)(2,1)S(1)}, bf16[2000,128]{1,0:T(8,128)(2,1)S(1)}, bf16[2000,128]{1,0:T(8,128)(2,1)S(1)}) custom-call(s32[1]{0:T(128)} %bitcast.13.odd_ref, bf16[2000,256]{1,0:T(8,128)(2,1)S(1)} %half_of.2.mine_ref, bf16[2000,256]{1,0:T(8,128)(2,1)S(1)} %copy-done.3, ...), custom_call_target="tpu_custom_call" | custom-call | flops 1048576000 | bytes 4096000 | tf_op jit(solution)/shard_map/compact/pallas_call | solution.py:124
  14.7 0.7 collective-permute-start.20
  15.4 4.5 %collective-permute-start.21 = (bf16[2000,128]{1,0:T(8,128)(2,1)S(1)}, bf16[2000,128]{1,0:T(8,128)(2,1)S(1)}, u32[]{:S(2)}, u32[]{:S(2)}) collective-permute-start(bf16[2000,128]{1,0:T(8,128)(2,1)S(1)} %get-tuple-element.387), channel_id=1, source_target_pairs={{0,8},{4,12},{8,0},{12,4},{16,24},{20,28},{24,16},{28,20},{1,9},{5... | collective-permute-start | bytes 1536008 | tf_op jit(solution)/shard_map/ppermute | solution.py:492
  20.0 11.1 %collective-permute-done.22 = f32[2,528]{1,0:T(2,128)S(1)} collective-permute-done((f32[2,528]{1,0:T(2,128)S(1)}, f32[2,528]{1,0:T(2,128)S(1)}, u32[]{:S(2)}, u32[]{:S(2)}) %collective-permute-start.22) | collective-permute-done | bytes 4256 | tf_op jit(solution)/shard_map/ppermute | solution.py:418
  31.6 1.8 %collective-permute-start.23 = (bf16[2000,256]{1,0:T(8,128)(2,1)S(1)}, bf16[2000,256]{1,0:T(8,128)(2,1)S(1)}, u32[]{:S(2)}, u32[]{:S(2)}) collective-permute-start(bf16[2000,256]{1,0:T(8,128)(2,1)S(1)} %straighten.1.refs_1_.refs_0_), channel_id=1, source_target_pairs={{0,8},{4,12},{8,0},{12,4},{16,24},{20,28},{24,16},{28,20},{1,9},{5... | collective-permute-start | bytes 3072008 | tf_op jit(solution)/shard_map/ppermute | solution.py:492
  33.4 0.7 collective-permute-start.25
  34.4 2.5 %panel_halves.1 = (bf16[128,2048]{1,0:T(8,128)(2,1)S(1)}, bf16[128,2048]{1,0:T(8,128)(2,1)}) custom-call(s32[1]{0:T(128)} %bitcast.12.which_ref.core_ref, bf16[64,4000]{1,0:T(8,128)(2,1)} %bitcast.73, bf16[64,4000]{1,0:T(8,128)(2,1)} %bitcast.74), custom_call_target="tpu_custom_call" | custom-call | tf_op jit(solution)/shard_map/panel_halves/pallas_call | solution.py:178
  36.9 0.8 copy-done
  38.1 1.9 %collective-permute-done.27.got_ref = bf16[128,2048]{1,0:T(8,128)(2,1)} collective-permute-done((bf16[128,2048]{1,0:T(8,128)(2,1)}, bf16[128,2048]{1,0:T(8,128)(2,1)}, u32[]{:S(2)}, u32[]{:S(2)}) %collective-permute-start.27) | collective-permute-done | bytes 524320 | tf_op jit(solution)/shard_map/ppermute | solution.py:418
  40.0 1.0 copy-done.1
  41.0 2.1 %stack_panels.1.refs_0_ = bf16[256,2048]{1,0:T(8,128)(2,1)} custom-call(s32[1]{0:T(128)} %bitcast.12.which_ref.core_ref, bf16[128,2048]{1,0:T(8,128)(2,1)S(1)} %copy-done.1, bf16[128,2048]{1,0:T(8,128)(2,1)} %collective-permute-done.27.got_ref), custom_call_target="tpu_custom_call" | custom-call | tf_op jit(solution)/shard_map/stack_panels/pallas_call | solution.py:201
  43.1 5.9 %collective-permute-start.28 = (bf16[256,2048]{1,0:T(8,128)(2,1)}, bf16[256,2048]{1,0:T(8,128)(2,1)}, u32[]{:S(2)}, u32[]{:S(2)}) collective-permute-start(bf16[256,2048]{1,0:T(8,128)(2,1)} %stack_panels.1.refs_0_), channel_id=1, source_target_pairs={{0,8},{4,12},{24,16},{28,20},{1,9},{5,13},{25,17},{29,21},{2,10},{... | collective-permute-start | bytes 3145736 | tf_op jit(solution)/shard_map/ppermute | solution.py:492
  49.0 7.4 %collective-permute-done.23.refs_2_.refs_1_ = bf16[2000,256]{1,0:T(8,128)(2,1)S(1)} collective-permute-done((bf16[2000,256]{1,0:T(8,128)(2,1)S(1)}, bf16[2000,256]{1,0:T(8,128)(2,1)S(1)}, u32[]{:S(2)}, u32[]{:S(2)}) %collective-permute-start.23) | collective-permute-done | bytes 1024032 | tf_op jit(solution)/shard_map/ppermute | solution.py:492
  56.4 1.7 %collective-permute-start.24 = (bf16[2000,256]{1,0:T(8,128)(2,1)S(1)}, bf16[2000,256]{1,0:T(8,128)(2,1)}, u32[]{:S(2)}, u32[]{:S(2)}) collective-permute-start(bf16[2000,256]{1,0:T(8,128)(2,1)S(1)} %collective-permute-done.23.refs_2_.refs_1_), channel_id=1, source_target_pairs={{8,16},{12,20},{16,8},{20,12},{9,17},{13,21},{17,9},{21,13},{10,18... | collective-permute-start | bytes 3072008 | tf_op jit(solution)/shard_map/ppermute | solution.py:492
  58.1 1.3 %collective-permute-start.26 = (bf16[2000,256]{1,0:T(8,128)(2,1)S(1)}, bf16[2000,256]{1,0:T(8,128)(2,1)}, u32[]{:S(2)}, u32[]{:S(2)}) collective-permute-start(bf16[2000,256]{1,0:T(8,128)(2,1)S(1)} %collective-permute-done.25.refs_3_.refs_2_), channel_id=1, source_target_pairs={{8,0},{12,4},{16,24},{20,28},{9,1},{13,5},{17,25},{21,29},{10,2},{... | collective-permute-start | bytes 3072008 | tf_op jit(solution)/shard_map/ppermute | solution.py:492
  60.0 0.6 fusion.14
  61.4 0.6 compare_reduce_fusion
  62.8 3.2 %project.3 = (f32[6,4,16,256]{3,2,1,0:T(8,128)S(1)}, f32[6,4,16,256]{3,2,1,0:T(8,128)}) custom-call(s32[1]{0:T(128)} %bitcast.12.which_ref.core_ref, bf16[256,2048]{1,0:T(8,128)(2,1)} %stack_panels.1.refs_0_, bf16[2000,256]{1,0:T(8,128)(2,1)S(1)} %straighten.1.refs_1_.refs_0_, bf16[2000,256]{1,0:T(8,128)(2,1)S(1)} %collective-permute-done.23.refs_2_.refs_1_, ...), custom_call_target="tpu_custom_call" | custom-call | flops 786432000 | bytes 4882432 | tf_op jit(solution)/shard_map/project/pallas_call | solution.py:281
  66.0 10.5 %collective-permute-done.28 = bf16[256,2048]{1,0:T(8,128)(2,1)} collective-permute-done((bf16[256,2048]{1,0:T(8,128)(2,1)}, bf16[256,2048]{1,0:T(8,128)(2,1)}, u32[]{:S(2)}, u32[]{:S(2)}) %collective-permute-start.28) | collective-permute-done | bytes 1048608 | tf_op jit(solution)/shard_map/ppermute | solution.py:492
  76.4 5.9 %collective-permute-done.26.refs_4_ = bf16[2000,256]{1,0:T(8,128)(2,1)} collective-permute-done((bf16[2000,256]{1,0:T(8,128)(2,1)S(1)}, bf16[2000,256]{1,0:T(8,128)(2,1)}, u32[]{:S(2)}, u32[]{:S(2)}) %collective-permute-start.26) | collective-permute-done | bytes 1024032 | tf_op jit(solution)/shard_map/ppermute | solution.py:492
  82.4 1.3 %collective-permute-start.29 = (bf16[2000,256]{1,0:T(8,128)(2,1)}, bf16[2000,256]{1,0:T(8,128)(2,1)}, u32[]{:S(2)}, u32[]{:S(2)}) collective-permute-start(bf16[2000,256]{1,0:T(8,128)(2,1)} %collective-permute-done.24.refs_5_), channel_id=1, source_target_pairs={{8,0},{12,4},{16,24},{20,28},{9,1},{13,5},{17,25},{21,29},{10,2},{... | collective-permute-start | bytes 3072008 | tf_op jit(solution)/shard_map/ppermute | solution.py:492
  83.7 36.3 %conditional.1 = (bf16[8,4,16,128]{3,2,1,0:T(8,128)(2,1)}, bf16[8,4,16,128]{3,2,1,0:T(8,128)(2,1)}, f32[64,4000]{1,0:T(8,128)}) conditional(s32[]{:T(128)} %convert_element_type.56, (s32[8]{0:T(128)S(1)}, f32[256]{0:T(256)S(1)}, bf16[4000,64]{0,1:T(8,128)(2,1)}, bf16[4000,64]{0,1:T(8,128)(2,1)}, s32[8,32]{1,0:T(8,128)S(1)}, ...), branch_computations={%region_7.15_spmd, %region_15.19_spmd} | conditional | flops 524621184 | bytes 57519072 | solution.py:641
  84.0 3.0 %project.2 = (f32[4,4,16,256]{3,2,1,0:T(8,128)S(1)}, f32[4,4,16,256]{3,2,1,0:T(8,128)S(1)}) custom-call(s32[1]{0:T(128)} %bitcast.4.core_ref, bf16[256,2048]{1,0:T(8,128)(2,1)} %get-tuple-element.350.refs_0_, bf16[256,2048]{1,0:T(8,128)(2,1)} %get-tuple-element.351.refs_1_, bf16[2000,256]{1,0:T(8,128)(2,1)} %get-tuple-element.352.refs_2_, ...), custom_call_target="tpu_custom_call" | custom-call | flops 524288000 | bytes 3596288 | tf_op jit(solution)/shard_map/cond/branch_1_fun/project/pallas_call | solution.py:281
  87.7 1.1 collective-permute-done.1.refs_3_
  88.9 1.6 %collective-permute-start.2 = (f32[10,16,256]{2,1,0:T(8,128)S(1)}, f32[10,16,256]{2,1,0:T(8,128)S(1)}, u32[]{:S(2)}, u32[]{:S(2)}) collective-permute-start(f32[10,16,256]{2,1,0:T(8,128)S(1)} %get-tuple-element.357), channel_id=1, source_target_pairs={{0,1},{1,0},{2,3},{3,2},{4,5},{5,4},{6,7},{7,6},{8,9},{9,8},{10,11... | collective-permute-start | bytes 491528 | tf_op jit(solution)/shard_map/cond/branch_1_fun/ppermute | solution.py:418
  90.5 1.5 %collective-permute-start.3 = (f32[10,16,256]{2,1,0:T(8,128)S(1)}, f32[10,16,256]{2,1,0:T(8,128)S(1)}, u32[]{:S(2)}, u32[]{:S(2)}) collective-permute-start(f32[10,16,256]{2,1,0:T(8,128)S(1)} %get-tuple-element.358), channel_id=1, source_target_pairs={{0,2},{1,3},{2,0},{3,1},{4,6},{5,7},{6,4},{7,5},{8,10},{9,11},{10,... | collective-permute-start | bytes 491528 | tf_op jit(solution)/shard_map/cond/branch_1_fun/ppermute | solution.py:418
  92.5 3.5 %collective-permute-done.2 = f32[10,16,256]{2,1,0:T(8,128)S(1)} collective-permute-done((f32[10,16,256]{2,1,0:T(8,128)S(1)}, f32[10,16,256]{2,1,0:T(8,128)S(1)}, u32[]{:S(2)}, u32[]{:S(2)}) %collective-permute-start.2) | collective-permute-done | bytes 163872 | tf_op jit(solution)/shard_map/cond/branch_1_fun/ppermute | solution.py:418
  96.0 4.2 %collective-permute-done.3 = f32[10,16,256]{2,1,0:T(8,128)S(1)} collective-permute-done((f32[10,16,256]{2,1,0:T(8,128)S(1)}, f32[10,16,256]{2,1,0:T(8,128)S(1)}, u32[]{:S(2)}, u32[]{:S(2)}) %collective-permute-start.3) | collective-permute-done | bytes 163872 | tf_op jit(solution)/shard_map/cond/branch_1_fun/ppermute | solution.py:418
  100.4 3.7 %collective-permute-start.6 = (f32[4,32]{1,0:T(4,128)S(1)}, f32[4,32]{1,0:T(4,128)S(1)}, u32[]{:S(2)}, u32[]{:S(2)}) collective-permute-start(f32[4,32]{1,0:T(4,128)S(1)} %select_reduce_fusion), channel_id=1, source_target_pairs={{0,16},{4,20},{8,24},{12,28},{16,0},{20,4},{24,8},{28,12},{1,17},{... | collective-permute-start | bytes 1544 | tf_op jit(solution)/shard_map/cond/branch_1_fun/ppermute | solution.py:418
  104.1 2.5 %collective-permute-start.7 = (f32[4,32]{1,0:T(4,128)S(1)}, f32[4,32]{1,0:T(4,128)S(1)}, u32[]{:S(2)}, u32[]{:S(2)}) collective-permute-start(f32[4,32]{1,0:T(4,128)S(1)} %select_reduce_fusion), channel_id=1, source_target_pairs={{0,24},{4,28},{8,16},{12,20},{16,8},{20,12},{24,0},{28,4},{1,25},{... | collective-permute-start | bytes 1544 | tf_op jit(solution)/shard_map/cond/branch_1_fun/ppermute | solution.py:418
  106.6 2.8 %collective-permute-done.7 = f32[4,32]{1,0:T(4,128)S(1)} collective-permute-done((f32[4,32]{1,0:T(4,128)S(1)}, f32[4,32]{1,0:T(4,128)S(1)}, u32[]{:S(2)}, u32[]{:S(2)}) %collective-permute-start.7) | collective-permute-done | bytes 544 | tf_op jit(solution)/shard_map/cond/branch_1_fun/ppermute | solution.py:418
  109.5 1.1 collective-permute-done.5
  110.8 1.6 %collective-permute-start.10 = (bf16[8,1,16,128]{3,2,1,0:T(8,128)(2,1)S(1)}, bf16[8,1,16,128]{3,2,1,0:T(8,128)(2,1)S(1)}, u32[]{:S(2)}, u32[]{:S(2)}) collective-permute-start(bf16[8,1,16,128]{3,2,1,0:T(8,128)(2,1)S(1)} %bitcast.67), channel_id=1, source_target_pairs={{0,3},{1,2},{2,1},{3,0},{4,7},{5,6},{6,5},{7,4},{8,11},{9,10},{10,... | collective-permute-start | bytes 98312 | tf_op jit(solution)/shard_map/cond/branch_1_fun/ppermute | solution.py:418
  112.3 1.5 %collective-permute-start.8 = (bf16[8,1,16,128]{3,2,1,0:T(8,128)(2,1)S(1)}, bf16[8,1,16,128]{3,2,1,0:T(8,128)(2,1)S(1)}, u32[]{:S(2)}, u32[]{:S(2)}) collective-permute-start(bf16[8,1,16,128]{3,2,1,0:T(8,128)(2,1)S(1)} %bitcast.68), channel_id=1, source_target_pairs={{0,1},{1,0},{2,3},{3,2},{4,5},{5,4},{6,7},{7,6},{8,9},{9,8},{10,11... | collective-permute-start | bytes 98312 | tf_op jit(solution)/shard_map/cond/branch_1_fun/ppermute | solution.py:418
  114.3 1.3 %collective-permute-done.10.refs_3_ = bf16[8,1,16,128]{3,2,1,0:T(8,128)(2,1)S(1)} collective-permute-done((bf16[8,1,16,128]{3,2,1,0:T(8,128)(2,1)S(1)}, bf16[8,1,16,128]{3,2,1,0:T(8,128)(2,1)S(1)}, u32[]{:S(2)}, u32[]{:S(2)}) %collective-permute-start.10) | collective-permute-done | bytes 32800 | tf_op jit(solution)/shard_map/cond/branch_1_fun/ppermute | solution.py:418
  116.2 1.5 %collective-permute-done.9.refs_2_ = bf16[8,1,16,128]{3,2,1,0:T(8,128)(2,1)S(1)} collective-permute-done((bf16[8,1,16,128]{3,2,1,0:T(8,128)(2,1)S(1)}, bf16[8,1,16,128]{3,2,1,0:T(8,128)(2,1)S(1)}, u32[]{:S(2)}, u32[]{:S(2)}) %collective-permute-start.9) | collective-permute-done | bytes 32800 | tf_op jit(solution)/shard_map/cond/branch_1_fun/ppermute | solution.py:418
  117.7 0.7 in_order.1
  118.4 1.7 %collective-permute-done.11 = bf16[8,4,16,128]{3,2,1,0:T(8,128)(2,1)} collective-permute-done((bf16[8,4,16,128]{3,2,1,0:T(8,128)(2,1)}, bf16[8,4,16,128]{3,2,1,0:T(8,128)(2,1)}, u32[]{:S(2)}, u32[]{:S(2)}) %collective-permute-start.11) | collective-permute-done | bytes 131104 | tf_op jit(solution)/shard_map/cond/branch_1_fun/ppermute | solution.py:418
  120.1 3.3 %contract.1 = (f32[64,2000]{1,0:T(8,128)S(1)}, f32[64,2000]{1,0:T(8,128)S(1)}) custom-call(s32[1]{0:T(128)} %bitcast.12.which_ref.core_ref, bf16[8,4,16,128]{3,2,1,0:T(8,128)(2,1)} %get-tuple-element.402.kernel_ref, bf16[8,4,16,128]{3,2,1,0:T(8,128)(2,1)} %get-tuple-element.403.got_ref, bf16[2000,256]{1,0:T(8,128)(2,1)S(1)} %straighten.1.refs_1_.refs_0_, ...), custom_call_target="tpu_custom_call" | custom-call | flops 524288000 | bytes 5120000 | tf_op jit(solution)/shard_map/contract/pallas_call | solution.py:346
  123.7 1.7 %collective-permute-done.30.back_ref = f32[64,2000]{1,0:T(8,128)S(1)} collective-permute-done((f32[64,2000]{1,0:T(8,128)S(1)}, f32[64,2000]{1,0:T(8,128)S(1)}, u32[]{:S(2)}, u32[]{:S(2)}) %collective-permute-start.30) | collective-permute-done | bytes 512032 | tf_op jit(solution)/shard_map/ppermute | solution.py:418
  125.4 1.8 %finish.1 = f32[64,4000]{1,0:T(8,128)} custom-call(s32[2]{0:T(128)S(1)} %pad_add_fusion.2.flags_ref, f32[64,2000]{1,0:T(8,128)S(1)} %get-tuple-element.405.ours_ref, f32[64,2000]{1,0:T(8,128)S(1)} %collective-permute-done.30.back_ref, f32[64,4000]{1,0:T(8,128)} %get-tuple-element.407.other_ref), custom_call_target="tpu_custom_call", output_to_operand_aliasing={{}: (3, {})} | custom-call | tf_op jit(solution)/shard_map/finish/pallas_call | solution.py:387
  (107 shorter events, 8.4 us)
Async XLA Ops:
  0.0 3.3 %copy-start.5 = (f32[256]{0:T(256)S(1)}, f32[256]{0:T(256)}, u32[]{:S(2)}) copy-start(f32[256]{0:T(256)} %param.17) | copy-start | bytes 3076
  0.0 3.2 %copy-start.6 = (s32[8]{0:T(128)S(1)}, s32[8]{0:T(128)}, u32[]{:S(2)}) copy-start(s32[8]{0:T(128)} %param.18) | copy-start | bytes 100
  0.0 3.3 %collective-permute-start.18 = (f32[1,256]{1,0:T(1,128)}, f32[1,256]{1,0:T(1,128)S(1)}, u32[]{:S(2)}, u32[]{:S(2)}) collective-permute-start(f32[1,256]{1,0:T(1,128)} %bitcast.84), channel_id=1, source_target_pairs={{0,4},{4,0},{8,12},{12,8},{16,20},{20,16},{24,28},{28,24},{1,5},{5... | collective-permute-start | bytes 3080 | tf_op jit(solution)/shard_map/ppermute | solution.py:418
  0.5 2.7 %collective-permute-start.17 = (s32[1,8]{1,0:T(1,128)}, s32[1,8]{1,0:T(1,128)S(1)}, u32[]{:S(2)}, u32[]{:S(2)}) collective-permute-start(s32[1,8]{1,0:T(1,128)} %bitcast.86), channel_id=1, source_target_pairs={{0,4},{4,0},{8,12},{12,8},{16,20},{20,16},{24,28},{28,24},{1,5},{5... | collective-permute-start | bytes 104 | tf_op jit(solution)/shard_map/ppermute | solution.py:418
  1.4 6.6 %collective-permute-start.16 = (s32[16,8]{0,1:T(8,128)S(1)}, s32[16,8]{0,1:T(8,128)S(1)}, u32[]{:S(2)}, u32[]{:S(2)}) collective-permute-start(s32[16,8]{0,1:T(8,128)S(1)} %get-tuple-element.477), channel_id=1, source_target_pairs={{0,4},{4,0},{8,12},{12,8},{16,20},{20,16},{24,28},{28,24},{1,5},{5... | collective-permute-start | bytes 1544 | tf_op jit(solution)/shard_map/ppermute | solution.py:418
  3.0 7.7 %collective-permute-start.15 = (bf16[2000,256]{1,0:T(8,128)(2,1)S(1)}, bf16[2000,256]{1,0:T(8,128)(2,1)S(1)}, u32[]{:S(2)}, u32[]{:S(2)}) collective-permute-start(bf16[2000,256]{1,0:T(8,128)(2,1)S(1)} %half_of.3), channel_id=1, source_target_pairs={{0,4},{4,0},{8,12},{12,8},{16,20},{20,16},{24,28},{28,24},{1,5},{5... | collective-permute-start | bytes 3072008 | tf_op jit(solution)/shard_map/ppermute | solution.py:418
  3.4 4.9 %collective-permute-start.19 = (f32[1,528]{1,0:T(1,128)S(1)}, f32[1,528]{1,0:T(1,128)S(1)}, u32[]{:S(2)}, u32[]{:S(2)}) collective-permute-start(f32[1,528]{1,0:T(1,128)S(1)} %pad_maximum_fusion.2), channel_id=1, source_target_pairs={{0,8},{4,12},{8,0},{12,4},{16,24},{20,28},{24,16},{28,20},{1,9},{5... | collective-permute-start | bytes 6344 | tf_op jit(solution)/shard_map/ppermute | solution.py:418
  10.7 1.0 copy-start.2
  11.7 1.2 copy-start.3
  14.7 16.4 %collective-permute-start.20 = (bf16[2000,128]{1,0:T(8,128)(2,1)S(1)}, bf16[2000,128]{1,0:T(8,128)(2,1)S(1)}, u32[]{:S(2)}, u32[]{:S(2)}) collective-permute-start(bf16[2000,128]{1,0:T(8,128)(2,1)S(1)} %get-tuple-element.386), channel_id=1, source_target_pairs={{8,16},{12,20},{16,8},{20,12},{9,17},{13,21},{17,9},{21,13},{10,18... | collective-permute-start | bytes 1536008 | tf_op jit(solution)/shard_map/ppermute | solution.py:492
  15.4 15.9 %collective-permute-start.21 = (bf16[2000,128]{1,0:T(8,128)(2,1)S(1)}, bf16[2000,128]{1,0:T(8,128)(2,1)S(1)}, u32[]{:S(2)}, u32[]{:S(2)}) collective-permute-start(bf16[2000,128]{1,0:T(8,128)(2,1)S(1)} %get-tuple-element.387), channel_id=1, source_target_pairs={{0,8},{4,12},{8,0},{12,4},{16,24},{20,28},{24,16},{28,20},{1,9},{5... | collective-permute-start | bytes 1536008 | tf_op jit(solution)/shard_map/ppermute | solution.py:492
  19.9 11.1 %collective-permute-start.22 = (f32[2,528]{1,0:T(2,128)S(1)}, f32[2,528]{1,0:T(2,128)S(1)}, u32[]{:S(2)}, u32[]{:S(2)}) collective-permute-start(f32[2,528]{1,0:T(2,128)S(1)} %maximum_select_fusion.1), channel_id=1, source_target_pairs={{0,16},{4,20},{8,24},{12,28},{16,0},{20,4},{24,8},{28,12},{1,17},{... | collective-permute-start | bytes 12680 | tf_op jit(solution)/shard_map/ppermute | solution.py:418
  31.6 24.8 %collective-permute-start.23 = (bf16[2000,256]{1,0:T(8,128)(2,1)S(1)}, bf16[2000,256]{1,0:T(8,128)(2,1)S(1)}, u32[]{:S(2)}, u32[]{:S(2)}) collective-permute-start(bf16[2000,256]{1,0:T(8,128)(2,1)S(1)} %straighten.1.refs_1_.refs_0_), channel_id=1, source_target_pairs={{0,8},{4,12},{8,0},{12,4},{16,24},{20,28},{24,16},{28,20},{1,9},{5... | collective-permute-start | bytes 3072008 | tf_op jit(solution)/shard_map/ppermute | solution.py:492
  33.4 24.8 %collective-permute-start.25 = (bf16[2000,256]{1,0:T(8,128)(2,1)S(1)}, bf16[2000,256]{1,0:T(8,128)(2,1)S(1)}, u32[]{:S(2)}, u32[]{:S(2)}) collective-permute-start(bf16[2000,256]{1,0:T(8,128)(2,1)S(1)} %straighten.1.refs_1_.refs_0_), channel_id=1, source_target_pairs={{8,16},{12,20},{16,8},{20,12},{9,17},{13,21},{17,9},{21,13},{10,18... | collective-permute-start | bytes 3072008 | tf_op jit(solution)/shard_map/ppermute | solution.py:492
  36.9 0.8 copy-start
  37.7 2.3 %collective-permute-start.27 = (bf16[128,2048]{1,0:T(8,128)(2,1)}, bf16[128,2048]{1,0:T(8,128)(2,1)}, u32[]{:S(2)}, u32[]{:S(2)}) collective-permute-start(bf16[128,2048]{1,0:T(8,128)(2,1)} %get-tuple-element.392), channel_id=1, source_target_pairs={{0,4},{4,0},{8,12},{12,8},{16,20},{20,16},{24,28},{28,24},{1,5},{5... | collective-permute-start | bytes 1572872 | tf_op jit(solution)/shard_map/ppermute | solution.py:418
  40.0 1.0 copy-start.1
  43.1 33.3 %collective-permute-start.28 = (bf16[256,2048]{1,0:T(8,128)(2,1)}, bf16[256,2048]{1,0:T(8,128)(2,1)}, u32[]{:S(2)}, u32[]{:S(2)}) collective-permute-start(bf16[256,2048]{1,0:T(8,128)(2,1)} %stack_panels.1.refs_0_), channel_id=1, source_target_pairs={{0,8},{4,12},{24,16},{28,20},{1,9},{5,13},{25,17},{29,21},{2,10},{... | collective-permute-start | bytes 3145736 | tf_op jit(solution)/shard_map/ppermute | solution.py:492
  56.4 20.0 %collective-permute-start.24 = (bf16[2000,256]{1,0:T(8,128)(2,1)S(1)}, bf16[2000,256]{1,0:T(8,128)(2,1)}, u32[]{:S(2)}, u32[]{:S(2)}) collective-permute-start(bf16[2000,256]{1,0:T(8,128)(2,1)S(1)} %collective-permute-done.23.refs_2_.refs_1_), channel_id=1, source_target_pairs={{8,16},{12,20},{16,8},{20,12},{9,17},{13,21},{17,9},{21,13},{10,18... | collective-permute-start | bytes 3072008 | tf_op jit(solution)/shard_map/ppermute | solution.py:492
  58.1 24.2 %collective-permute-start.26 = (bf16[2000,256]{1,0:T(8,128)(2,1)S(1)}, bf16[2000,256]{1,0:T(8,128)(2,1)}, u32[]{:S(2)}, u32[]{:S(2)}) collective-permute-start(bf16[2000,256]{1,0:T(8,128)(2,1)S(1)} %collective-permute-done.25.refs_3_.refs_2_), channel_id=1, source_target_pairs={{8,0},{12,4},{16,24},{20,28},{9,1},{13,5},{17,25},{21,29},{10,2},{... | collective-permute-start | bytes 3072008 | tf_op jit(solution)/shard_map/ppermute | solution.py:492
  59.7 24.1 %copy-start.4 = (s32[8,32]{1,0:T(8,128)S(1)}, s32[8,32]{1,0:T(8,128)}, u32[]{:S(2)}) copy-start(s32[8,32]{1,0:T(8,128)} %param.19) | copy-start | bytes 3076
  82.4 37.7 %collective-permute-start.29 = (bf16[2000,256]{1,0:T(8,128)(2,1)}, bf16[2000,256]{1,0:T(8,128)(2,1)}, u32[]{:S(2)}, u32[]{:S(2)}) collective-permute-start(bf16[2000,256]{1,0:T(8,128)(2,1)} %collective-permute-done.24.refs_5_), channel_id=1, source_target_pairs={{8,0},{12,4},{16,24},{20,28},{9,1},{13,5},{17,25},{21,29},{10,2},{... | collective-permute-start | bytes 3072008 | tf_op jit(solution)/shard_map/ppermute | solution.py:492
  83.9 4.9 %collective-permute-start = (f32[6,4,16,256]{3,2,1,0:T(8,128)}, f32[6,4,16,256]{3,2,1,0:T(8,128)S(1)}, u32[]{:S(2)}, u32[]{:S(2)}) collective-permute-start(f32[6,4,16,256]{3,2,1,0:T(8,128)} %get-tuple-element.348), channel_id=1, source_target_pairs={{0,4},{4,0},{8,12},{12,8},{16,20},{20,16},{24,28},{28,24},{1,5},{5... | collective-permute-start | bytes 1179656 | tf_op jit(solution)/shard_map/cond/branch_1_fun/ppermute | solution.py:418
  87.1 1.7 %collective-permute-start.1 = (f32[4,4,16,256]{3,2,1,0:T(8,128)S(1)}, f32[4,4,16,256]{3,2,1,0:T(8,128)S(1)}, u32[]{:S(2)}, u32[]{:S(2)}) collective-permute-start(f32[4,4,16,256]{3,2,1,0:T(8,128)S(1)} %get-tuple-element.355), channel_id=1, source_target_pairs={{0,4},{4,0},{8,12},{12,8},{16,20},{20,16},{24,28},{28,24},{1,5},{5... | collective-permute-start | bytes 786440 | tf_op jit(solution)/shard_map/cond/branch_1_fun/ppermute | solution.py:418
  88.9 7.1 %collective-permute-start.2 = (f32[10,16,256]{2,1,0:T(8,128)S(1)}, f32[10,16,256]{2,1,0:T(8,128)S(1)}, u32[]{:S(2)}, u32[]{:S(2)}) collective-permute-start(f32[10,16,256]{2,1,0:T(8,128)S(1)} %get-tuple-element.357), channel_id=1, source_target_pairs={{0,1},{1,0},{2,3},{3,2},{4,5},{5,4},{6,7},{7,6},{8,9},{9,8},{10,11... | collective-permute-start | bytes 491528 | tf_op jit(solution)/shard_map/cond/branch_1_fun/ppermute | solution.py:418
  90.5 9.7 %collective-permute-start.3 = (f32[10,16,256]{2,1,0:T(8,128)S(1)}, f32[10,16,256]{2,1,0:T(8,128)S(1)}, u32[]{:S(2)}, u32[]{:S(2)}) collective-permute-start(f32[10,16,256]{2,1,0:T(8,128)S(1)} %get-tuple-element.358), channel_id=1, source_target_pairs={{0,2},{1,3},{2,0},{3,1},{4,6},{5,7},{6,4},{7,5},{8,10},{9,11},{10,... | collective-permute-start | bytes 491528 | tf_op jit(solution)/shard_map/cond/branch_1_fun/ppermute | solution.py:418
  92.0 8.2 %collective-permute-start.4 = (f32[10,16,256]{2,1,0:T(8,128)S(1)}, f32[10,16,256]{2,1,0:T(8,128)S(1)}, u32[]{:S(2)}, u32[]{:S(2)}) collective-permute-start(f32[10,16,256]{2,1,0:T(8,128)S(1)} %get-tuple-element.359), channel_id=1, source_target_pairs={{0,3},{1,2},{2,1},{3,0},{4,7},{5,6},{6,5},{7,4},{8,11},{9,10},{10,... | collective-permute-start | bytes 491528 | tf_op jit(solution)/shard_map/cond/branch_1_fun/ppermute | solution.py:418
  100.4 6.2 %collective-permute-start.6 = (f32[4,32]{1,0:T(4,128)S(1)}, f32[4,32]{1,0:T(4,128)S(1)}, u32[]{:S(2)}, u32[]{:S(2)}) collective-permute-start(f32[4,32]{1,0:T(4,128)S(1)} %select_reduce_fusion), channel_id=1, source_target_pairs={{0,16},{4,20},{8,24},{12,28},{16,0},{20,4},{24,8},{28,12},{1,17},{... | collective-permute-start | bytes 1544 | tf_op jit(solution)/shard_map/cond/branch_1_fun/ppermute | solution.py:418
  104.1 5.4 %collective-permute-start.7 = (f32[4,32]{1,0:T(4,128)S(1)}, f32[4,32]{1,0:T(4,128)S(1)}, u32[]{:S(2)}, u32[]{:S(2)}) collective-permute-start(f32[4,32]{1,0:T(4,128)S(1)} %select_reduce_fusion), channel_id=1, source_target_pairs={{0,24},{4,28},{8,16},{12,20},{16,8},{20,12},{24,0},{28,4},{1,25},{... | collective-permute-start | bytes 1544 | tf_op jit(solution)/shard_map/cond/branch_1_fun/ppermute | solution.py:418
  106.5 4.0 %collective-permute-start.5 = (f32[36,256]{1,0:T(8,128)S(1)}, f32[36,256]{1,0:T(8,128)S(1)}, u32[]{:S(2)}, u32[]{:S(2)}) collective-permute-start(f32[36,256]{1,0:T(8,128)S(1)} %select_maximum_fusion), channel_id=1, source_target_pairs={{0,8},{4,12},{8,0},{12,4},{16,24},{20,28},{24,16},{28,20},{1,9},{5... | collective-permute-start | bytes 110600 | tf_op jit(solution)/shard_map/cond/branch_1_fun/ppermute | solution.py:418
  110.8 4.9 %collective-permute-start.10 = (bf16[8,1,16,128]{3,2,1,0:T(8,128)(2,1)S(1)}, bf16[8,1,16,128]{3,2,1,0:T(8,128)(2,1)S(1)}, u32[]{:S(2)}, u32[]{:S(2)}) collective-permute-start(bf16[8,1,16,128]{3,2,1,0:T(8,128)(2,1)S(1)} %bitcast.67), channel_id=1, source_target_pairs={{0,3},{1,2},{2,1},{3,0},{4,7},{5,6},{6,5},{7,4},{8,11},{9,10},{10,... | collective-permute-start | bytes 98312 | tf_op jit(solution)/shard_map/cond/branch_1_fun/ppermute | solution.py:418
  112.3 3.9 %collective-permute-start.8 = (bf16[8,1,16,128]{3,2,1,0:T(8,128)(2,1)S(1)}, bf16[8,1,16,128]{3,2,1,0:T(8,128)(2,1)S(1)}, u32[]{:S(2)}, u32[]{:S(2)}) collective-permute-start(bf16[8,1,16,128]{3,2,1,0:T(8,128)(2,1)S(1)} %bitcast.68), channel_id=1, source_target_pairs={{0,1},{1,0},{2,3},{3,2},{4,5},{5,4},{6,7},{7,6},{8,9},{9,8},{10,11... | collective-permute-start | bytes 98312 | tf_op jit(solution)/shard_map/cond/branch_1_fun/ppermute | solution.py:418
  113.8 3.9 %collective-permute-start.9 = (bf16[8,1,16,128]{3,2,1,0:T(8,128)(2,1)S(1)}, bf16[8,1,16,128]{3,2,1,0:T(8,128)(2,1)S(1)}, u32[]{:S(2)}, u32[]{:S(2)}) collective-permute-start(bf16[8,1,16,128]{3,2,1,0:T(8,128)(2,1)S(1)} %bitcast.69), channel_id=1, source_target_pairs={{0,2},{1,3},{2,0},{3,1},{4,6},{5,7},{6,4},{7,5},{8,10},{9,11},{10,... | collective-permute-start | bytes 98312 | tf_op jit(solution)/shard_map/cond/branch_1_fun/ppermute | solution.py:418
  118.4 1.7 %collective-permute-start.11 = (bf16[8,4,16,128]{3,2,1,0:T(8,128)(2,1)}, bf16[8,4,16,128]{3,2,1,0:T(8,128)(2,1)}, u32[]{:S(2)}, u32[]{:S(2)}) collective-permute-start(bf16[8,4,16,128]{3,2,1,0:T(8,128)(2,1)} %in_order.1), channel_id=1, source_target_pairs={{0,4},{4,0},{8,12},{12,8},{16,20},{20,16},{24,28},{28,24},{1,5},{5... | collective-permute-start | bytes 393224 | tf_op jit(solution)/shard_map/cond/branch_1_fun/ppermute | solution.py:418
  123.4 2.0 %collective-permute-start.30 = (f32[64,2000]{1,0:T(8,128)S(1)}, f32[64,2000]{1,0:T(8,128)S(1)}, u32[]{:S(2)}, u32[]{:S(2)}) collective-permute-start(f32[64,2000]{1,0:T(8,128)S(1)} %get-tuple-element.406), channel_id=1, source_target_pairs={{0,4},{4,0},{8,12},{12,8},{16,20},{20,16},{24,28},{28,24},{1,5},{5... | collective-permute-start | bytes 1536008 | tf_op jit(solution)/shard_map/ppermute | solution.py:418

commit v5 on v4

--- a/solution.py
+++ b/solution.py
@@ -126,7 +126,7 @@
         out_shape=shapes,
         in_specs=[SCALARS] + [WHOLE] * 6,
         out_specs=[WHOLE] * len(shapes),
-        compiler_params=pltpu.CompilerParams(vmem_limit_bytes=24 * MIB),
+        compiler_params=pltpu.CompilerParams(vmem_limit_bytes=16 * MIB),
         name="compact",
         cost_estimate=pl.CostEstimate(
             flops=8 * half * rows * rows, bytes_accessed=8 * half * rows, transcendentals=0
@@ -535,8 +535,10 @@
     by_a = by_b = own
     far_panels = None
     for t in range(1, last):
-        moved = [(sent(a, over(1, t)), sent(b, over(0, t))) for a, b in zip(by_a, by_b)]
-        by_b, by_a = (tuple(x) for x in zip(*moved))
+        by_a, by_b = (
+            tuple(sent(x, over(0, t)) for x in by_b),
+            tuple(sent(x, over(1, t)) for x in by_a),
+        )
         if t == 1:
             far_panels = sent(panels, ends)
         a_at, b_at = valid(chip + side * t), valid(chip - side * t)
@@ -589,6 +591,7 @@
     here = (places[:, None] == window_iota[None, :])[:, :, None]
     weight_here = jnp.sum(jnp.where(here, weight[None], 0.0), axis=1)[:, :, None]
 
+    by_a, early_pair = lax.optimization_barrier((by_a, early_pair))
     late, by_a, early_pair, far_panels, weight_here, fits = lax.optimization_barrier(
         (by_b, by_a, early_pair, far_panels, weight_here, fits.astype(jnp.int32))
     )

time: 128 us -> 128 us (level)
  waiting for transfers between devices: 56.4 us -> 54.4 us
  starting transfers between devices: 36.1 us -> 38 us
    ppermute x8, waiting for transfers between devices: 24 us -> 22 us  [sent(): return lax.ppermute(x, 'grid', along(pairs))]
    ppermute x20, starting transfers between devices: 18.2 us -> 20.2 us  [flip(): return lax.ppermute(x, axis, [(i, i ^ bit) for i in range(count)])]
  transfers between devices with their start and end apart: 28 -> 28, of which waited for: 16 -> 15; matrix products, arithmetic and copies ran while one was open for 5% -> 5% of each run, Pallas kernels for 11% -> 11%
where the time goes in v5:
time: 128 us; the launch traced here: 127 us
  waiting for transfers between devices  54.4 us (42%)
  starting transfers between devices  38 us (30%)
  Pallas kernels  21.2 us (17%)
  local copies, waits for them, and re-layouts  6.16 us (5%)
  other arithmetic  4.76 us (4%)
  between operations  2.42 us (2%)
    ppermute x20, waiting for transfers between devices, flip(): return lax.ppermute(x, axis, [(i, i ^ bit) for i in range(count)])  32.4 us
    ppermute x8, waiting for transfers between devices, sent(): return lax.ppermute(x, 'grid', along(pairs))  22 us
    ppermute x20, starting transfers between devices, flip(): return lax.ppermute(x, axis, [(i, i ^ bit) for i in range(count)])  20.2 us
    ppermute x8, starting transfers between devices, sent(): return lax.ppermute(x, 'grid', along(pairs))  17.8 us
    pallas_call x2, Pallas kernels, project(): pl.pallas_call(body, out_shape=(shape, shape), in_specs=[SCALARS] + [WHOL...  6.19 us
    unnamed x17, local copies, waits for them, and re-layouts  4.1 us
    pallas_call x1, Pallas kernels, contract(): pl.pallas_call(body, out_shape=(shape, shape), in_specs=[SCALARS] + [WHOL...  3.3 us
  transfers between devices with their start and end apart: 28, of which 15 were waited for; matrix products, arithmetic and copies ran while one was open for 5% of the time, Pallas kernels for 11%

profile of v5, /device:TPU:0, one launch (start us, length us, event | category | flops | bytes accessed | tf_op | source)
XLA Modules:
  0.0 127.2 jit_solution(15489143707604188363)
XLA Ops:
  0.5 0.8 dynamic-slice_bitcast_fusion
  1.8 1.2 half_of.3
  3.4 3.0 %collective-permute-start.19 = (f32[1,528]{1,0:T(1,128)S(1)}, f32[1,528]{1,0:T(1,128)S(1)}, u32[]{:S(2)}, u32[]{:S(2)}) collective-permute-start(f32[1,528]{1,0:T(1,128)S(1)} %pad_maximum_fusion.2), channel_id=1, source_target_pairs={{0,8},{4,12},{8,0},{12,4},{16,24},{20,28},{24,16},{28,20},{1,9},{5... | collective-permute-start | bytes 6344 | tf_op jit(solution)/shard_map/ppermute | solution.py:418
  6.8 1.2 half_of.2.mine_ref
  8.6 0.6 fusion.13
  10.7 0.9 copy-done.2
  11.7 1.2 copy-done.3
  12.9 1.8 %compact.1 = (bf16[2000,128]{1,0:T(8,128)(2,1)S(1)}, bf16[2000,128]{1,0:T(8,128)(2,1)S(1)}, bf16[2000,128]{1,0:T(8,128)(2,1)S(1)}, bf16[2000,128]{1,0:T(8,128)(2,1)S(1)}) custom-call(s32[1]{0:T(128)} %bitcast.13.odd_ref, bf16[2000,256]{1,0:T(8,128)(2,1)S(1)} %half_of.2.mine_ref, bf16[2000,256]{1,0:T(8,128)(2,1)S(1)} %copy-done.3, ...), custom_call_target="tpu_custom_call" | custom-call | flops 1048576000 | bytes 4096000 | tf_op jit(solution)/shard_map/compact/pallas_call | solution.py:124
  14.7 0.7 collective-permute-start.20
  15.4 4.5 %collective-permute-start.21 = (bf16[2000,128]{1,0:T(8,128)(2,1)S(1)}, bf16[2000,128]{1,0:T(8,128)(2,1)S(1)}, u32[]{:S(2)}, u32[]{:S(2)}) collective-permute-start(bf16[2000,128]{1,0:T(8,128)(2,1)S(1)} %get-tuple-element.390), channel_id=1, source_target_pairs={{0,8},{4,12},{8,0},{12,4},{16,24},{20,28},{24,16},{28,20},{1,9},{5... | collective-permute-start | bytes 1536008 | tf_op jit(solution)/shard_map/ppermute | solution.py:492
  20.0 11.1 %collective-permute-done.22 = f32[2,528]{1,0:T(2,128)S(1)} collective-permute-done((f32[2,528]{1,0:T(2,128)S(1)}, f32[2,528]{1,0:T(2,128)S(1)}, u32[]{:S(2)}, u32[]{:S(2)}) %collective-permute-start.22) | collective-permute-done | bytes 4256 | tf_op jit(solution)/shard_map/ppermute | solution.py:418
  31.6 1.8 %collective-permute-start.23 = (bf16[2000,256]{1,0:T(8,128)(2,1)S(1)}, bf16[2000,256]{1,0:T(8,128)(2,1)S(1)}, u32[]{:S(2)}, u32[]{:S(2)}) collective-permute-start(bf16[2000,256]{1,0:T(8,128)(2,1)S(1)} %straighten.1.refs_1_.refs_0_), channel_id=1, source_target_pairs={{0,8},{4,12},{8,0},{12,4},{16,24},{20,28},{24,16},{28,20},{1,9},{5... | collective-permute-start | bytes 3072008 | tf_op jit(solution)/shard_map/ppermute | solution.py:492
  33.4 0.7 collective-permute-start.25
  34.4 2.5 %panel_halves.1 = (bf16[128,2048]{1,0:T(8,128)(2,1)S(1)}, bf16[128,2048]{1,0:T(8,128)(2,1)}) custom-call(s32[1]{0:T(128)} %bitcast.12.which_ref.core_ref, bf16[64,4000]{1,0:T(8,128)(2,1)} %bitcast.73, bf16[64,4000]{1,0:T(8,128)(2,1)} %bitcast.74), custom_call_target="tpu_custom_call" | custom-call | tf_op jit(solution)/shard_map/panel_halves/pallas_call | solution.py:178
  36.9 0.8 copy-done
  38.1 1.9 %collective-permute-done.27.got_ref = bf16[128,2048]{1,0:T(8,128)(2,1)} collective-permute-done((bf16[128,2048]{1,0:T(8,128)(2,1)}, bf16[128,2048]{1,0:T(8,128)(2,1)}, u32[]{:S(2)}, u32[]{:S(2)}) %collective-permute-start.27) | collective-permute-done | bytes 524320 | tf_op jit(solution)/shard_map/ppermute | solution.py:418
  40.0 1.0 copy-done.1
  41.0 2.1 %stack_panels.1.refs_0_ = bf16[256,2048]{1,0:T(8,128)(2,1)} custom-call(s32[1]{0:T(128)} %bitcast.12.which_ref.core_ref, bf16[128,2048]{1,0:T(8,128)(2,1)S(1)} %copy-done.1, bf16[128,2048]{1,0:T(8,128)(2,1)} %collective-permute-done.27.got_ref), custom_call_target="tpu_custom_call" | custom-call | tf_op jit(solution)/shard_map/stack_panels/pallas_call | solution.py:201
  43.1 5.9 %collective-permute-start.28 = (bf16[256,2048]{1,0:T(8,128)(2,1)}, bf16[256,2048]{1,0:T(8,128)(2,1)}, u32[]{:S(2)}, u32[]{:S(2)}) collective-permute-start(bf16[256,2048]{1,0:T(8,128)(2,1)} %stack_panels.1.refs_0_), channel_id=1, source_target_pairs={{0,8},{4,12},{24,16},{28,20},{1,9},{5,13},{25,17},{29,21},{2,10},{... | collective-permute-start | bytes 3145736 | tf_op jit(solution)/shard_map/ppermute | solution.py:492
  49.0 1.3 %collective-permute-start.26 = (bf16[2000,256]{1,0:T(8,128)(2,1)S(1)}, bf16[2000,256]{1,0:T(8,128)(2,1)}, u32[]{:S(2)}, u32[]{:S(2)}) collective-permute-start(bf16[2000,256]{1,0:T(8,128)(2,1)S(1)} %collective-permute-done.25.refs_3_.refs_2_), channel_id=1, source_target_pairs={{8,0},{12,4},{16,24},{20,28},{9,1},{13,5},{17,25},{21,29},{10,2},{... | collective-permute-start | bytes 3072008 | tf_op jit(solution)/shard_map/ppermute | solution.py:492
  50.3 6.1 %collective-permute-done.23.refs_2_.refs_1_ = bf16[2000,256]{1,0:T(8,128)(2,1)S(1)} collective-permute-done((bf16[2000,256]{1,0:T(8,128)(2,1)S(1)}, bf16[2000,256]{1,0:T(8,128)(2,1)S(1)}, u32[]{:S(2)}, u32[]{:S(2)}) %collective-permute-start.23) | collective-permute-done | bytes 1024032 | tf_op jit(solution)/shard_map/ppermute | solution.py:492
  56.4 1.7 %collective-permute-start.24 = (bf16[2000,256]{1,0:T(8,128)(2,1)S(1)}, bf16[2000,256]{1,0:T(8,128)(2,1)}, u32[]{:S(2)}, u32[]{:S(2)}) collective-permute-start(bf16[2000,256]{1,0:T(8,128)(2,1)S(1)} %collective-permute-done.23.refs_2_.refs_1_), channel_id=1, source_target_pairs={{8,16},{12,20},{16,8},{20,12},{9,17},{13,21},{17,9},{21,13},{10,18... | collective-permute-start | bytes 3072008 | tf_op jit(solution)/shard_map/ppermute | solution.py:492
  58.7 0.6 fusion.14
  60.1 0.6 compare_reduce_fusion
  61.5 3.2 %project.3 = (f32[6,4,16,256]{3,2,1,0:T(8,128)S(1)}, f32[6,4,16,256]{3,2,1,0:T(8,128)}) custom-call(s32[1]{0:T(128)} %bitcast.12.which_ref.core_ref, bf16[256,2048]{1,0:T(8,128)(2,1)} %stack_panels.1.refs_0_, bf16[2000,256]{1,0:T(8,128)(2,1)S(1)} %straighten.1.refs_1_.refs_0_, bf16[2000,256]{1,0:T(8,128)(2,1)S(1)} %collective-permute-done.23.refs_2_.refs_1_, ...), custom_call_target="tpu_custom_call" | custom-call | flops 786432000 | bytes 4882432 | tf_op jit(solution)/shard_map/project/pallas_call | solution.py:281
  64.7 15.6 %collective-permute-done.26.refs_4_ = bf16[2000,256]{1,0:T(8,128)(2,1)} collective-permute-done((bf16[2000,256]{1,0:T(8,128)(2,1)S(1)}, bf16[2000,256]{1,0:T(8,128)(2,1)}, u32[]{:S(2)}, u32[]{:S(2)}) %collective-permute-start.26) | collective-permute-done | bytes 1024032 | tf_op jit(solution)/shard_map/ppermute | solution.py:492
  80.3 1.3 %collective-permute-start.29 = (bf16[2000,256]{1,0:T(8,128)(2,1)}, bf16[2000,256]{1,0:T(8,128)(2,1)}, u32[]{:S(2)}, u32[]{:S(2)}) collective-permute-start(bf16[2000,256]{1,0:T(8,128)(2,1)} %collective-permute-done.24.refs_5_), channel_id=1, source_target_pairs={{8,0},{12,4},{16,24},{20,28},{9,1},{13,5},{17,25},{21,29},{10,2},{... | collective-permute-start | bytes 3072008 | tf_op jit(solution)/shard_map/ppermute | solution.py:492
  81.7 38.3 %conditional.1 = (bf16[8,4,16,128]{3,2,1,0:T(8,128)(2,1)}, bf16[8,4,16,128]{3,2,1,0:T(8,128)(2,1)}, f32[64,4000]{1,0:T(8,128)}) conditional(s32[]{:T(128)} %convert_element_type.56, (s32[8]{0:T(128)S(1)}, f32[256]{0:T(256)S(1)}, bf16[4000,64]{0,1:T(8,128)(2,1)}, bf16[4000,64]{0,1:T(8,128)(2,1)}, s32[8,32]{1,0:T(8,128)S(1)}, ...), branch_computations={%region_7.15_spmd, %region_15.19_spmd} | conditional | flops 524621184 | bytes 57519072 | solution.py:644
  82.0 3.0 %project.2 = (f32[4,4,16,256]{3,2,1,0:T(8,128)S(1)}, f32[4,4,16,256]{3,2,1,0:T(8,128)S(1)}) custom-call(s32[1]{0:T(128)} %bitcast.4.core_ref, bf16[256,2048]{1,0:T(8,128)(2,1)} %get-tuple-element.350.refs_0_, bf16[256,2048]{1,0:T(8,128)(2,1)} %get-tuple-element.351.refs_1_, bf16[2000,256]{1,0:T(8,128)(2,1)} %get-tuple-element.352.refs_2_, ...), custom_call_target="tpu_custom_call" | custom-call | flops 524288000 | bytes 3596288 | tf_op jit(solution)/shard_map/cond/branch_1_fun/project/pallas_call | solution.py:281
  85.6 1.1 collective-permute-done.1.refs_3_
  86.8 1.6 %collective-permute-start.2 = (f32[10,16,256]{2,1,0:T(8,128)S(1)}, f32[10,16,256]{2,1,0:T(8,128)S(1)}, u32[]{:S(2)}, u32[]{:S(2)}) collective-permute-start(f32[10,16,256]{2,1,0:T(8,128)S(1)} %get-tuple-element.357), channel_id=1, source_target_pairs={{0,1},{1,0},{2,3},{3,2},{4,5},{5,4},{6,7},{7,6},{8,9},{9,8},{10,11... | collective-permute-start | bytes 491528 | tf_op jit(solution)/shard_map/cond/branch_1_fun/ppermute | solution.py:418
  88.4 1.5 %collective-permute-start.3 = (f32[10,16,256]{2,1,0:T(8,128)S(1)}, f32[10,16,256]{2,1,0:T(8,128)S(1)}, u32[]{:S(2)}, u32[]{:S(2)}) collective-permute-start(f32[10,16,256]{2,1,0:T(8,128)S(1)} %get-tuple-element.358), channel_id=1, source_target_pairs={{0,2},{1,3},{2,0},{3,1},{4,6},{5,7},{6,4},{7,5},{8,10},{9,11},{10,... | collective-permute-start | bytes 491528 | tf_op jit(solution)/shard_map/cond/branch_1_fun/ppermute | solution.py:418
  90.5 3.5 %collective-permute-done.2 = f32[10,16,256]{2,1,0:T(8,128)S(1)} collective-permute-done((f32[10,16,256]{2,1,0:T(8,128)S(1)}, f32[10,16,256]{2,1,0:T(8,128)S(1)}, u32[]{:S(2)}, u32[]{:S(2)}) %collective-permute-start.2) | collective-permute-done | bytes 163872 | tf_op jit(solution)/shard_map/cond/branch_1_fun/ppermute | solution.py:418
  93.9 4.2 %collective-permute-done.3 = f32[10,16,256]{2,1,0:T(8,128)S(1)} collective-permute-done((f32[10,16,256]{2,1,0:T(8,128)S(1)}, f32[10,16,256]{2,1,0:T(8,128)S(1)}, u32[]{:S(2)}, u32[]{:S(2)}) %collective-permute-start.3) | collective-permute-done | bytes 163872 | tf_op jit(solution)/shard_map/cond/branch_1_fun/ppermute | solution.py:418
  98.4 6.1 %collective-permute-start.6 = (f32[4,32]{1,0:T(4,128)S(1)}, f32[4,32]{1,0:T(4,128)S(1)}, u32[]{:S(2)}, u32[]{:S(2)}) collective-permute-start(f32[4,32]{1,0:T(4,128)S(1)} %select_reduce_fusion), channel_id=1, source_target_pairs={{0,16},{4,20},{8,24},{12,28},{16,0},{20,4},{24,8},{28,12},{1,17},{... | collective-permute-start | bytes 1544 | tf_op jit(solution)/shard_map/cond/branch_1_fun/ppermute | solution.py:418
  104.4 2.0 %collective-permute-start.7 = (f32[4,32]{1,0:T(4,128)S(1)}, f32[4,32]{1,0:T(4,128)S(1)}, u32[]{:S(2)}, u32[]{:S(2)}) collective-permute-start(f32[4,32]{1,0:T(4,128)S(1)} %select_reduce_fusion), channel_id=1, source_target_pairs={{0,24},{4,28},{8,16},{12,20},{16,8},{20,12},{24,0},{28,4},{1,25},{... | collective-permute-start | bytes 1544 | tf_op jit(solution)/shard_map/cond/branch_1_fun/ppermute | solution.py:418
  106.5 3.2 %collective-permute-done.7 = f32[4,32]{1,0:T(4,128)S(1)} collective-permute-done((f32[4,32]{1,0:T(4,128)S(1)}, f32[4,32]{1,0:T(4,128)S(1)}, u32[]{:S(2)}, u32[]{:S(2)}) %collective-permute-start.7) | collective-permute-done | bytes 544 | tf_op jit(solution)/shard_map/cond/branch_1_fun/ppermute | solution.py:418
  109.8 0.7 collective-permute-done.5
  110.7 1.6 %collective-permute-start.10 = (bf16[8,1,16,128]{3,2,1,0:T(8,128)(2,1)S(1)}, bf16[8,1,16,128]{3,2,1,0:T(8,128)(2,1)S(1)}, u32[]{:S(2)}, u32[]{:S(2)}) collective-permute-start(bf16[8,1,16,128]{3,2,1,0:T(8,128)(2,1)S(1)} %bitcast.67), channel_id=1, source_target_pairs={{0,3},{1,2},{2,1},{3,0},{4,7},{5,6},{6,5},{7,4},{8,11},{9,10},{10,... | collective-permute-start | bytes 98312 | tf_op jit(solution)/shard_map/cond/branch_1_fun/ppermute | solution.py:418
  112.2 1.5 %collective-permute-start.8 = (bf16[8,1,16,128]{3,2,1,0:T(8,128)(2,1)S(1)}, bf16[8,1,16,128]{3,2,1,0:T(8,128)(2,1)S(1)}, u32[]{:S(2)}, u32[]{:S(2)}) collective-permute-start(bf16[8,1,16,128]{3,2,1,0:T(8,128)(2,1)S(1)} %bitcast.68), channel_id=1, source_target_pairs={{0,1},{1,0},{2,3},{3,2},{4,5},{5,4},{6,7},{7,6},{8,9},{9,8},{10,11... | collective-permute-start | bytes 98312 | tf_op jit(solution)/shard_map/cond/branch_1_fun/ppermute | solution.py:418
  114.2 1.3 %collective-permute-done.10.refs_3_ = bf16[8,1,16,128]{3,2,1,0:T(8,128)(2,1)S(1)} collective-permute-done((bf16[8,1,16,128]{3,2,1,0:T(8,128)(2,1)S(1)}, bf16[8,1,16,128]{3,2,1,0:T(8,128)(2,1)S(1)}, u32[]{:S(2)}, u32[]{:S(2)}) %collective-permute-start.10) | collective-permute-done | bytes 32800 | tf_op jit(solution)/shard_map/cond/branch_1_fun/ppermute | solution.py:418
  115.6 0.6 collective-permute-done.8.refs_1_
  116.2 1.5 %collective-permute-done.9.refs_2_ = bf16[8,1,16,128]{3,2,1,0:T(8,128)(2,1)S(1)} collective-permute-done((bf16[8,1,16,128]{3,2,1,0:T(8,128)(2,1)S(1)}, bf16[8,1,16,128]{3,2,1,0:T(8,128)(2,1)S(1)}, u32[]{:S(2)}, u32[]{:S(2)}) %collective-permute-start.9) | collective-permute-done | bytes 32800 | tf_op jit(solution)/shard_map/cond/branch_1_fun/ppermute | solution.py:418
  117.7 0.7 in_order.1
  118.3 1.7 %collective-permute-done.11 = bf16[8,4,16,128]{3,2,1,0:T(8,128)(2,1)} collective-permute-done((bf16[8,4,16,128]{3,2,1,0:T(8,128)(2,1)}, bf16[8,4,16,128]{3,2,1,0:T(8,128)(2,1)}, u32[]{:S(2)}, u32[]{:S(2)}) %collective-permute-start.11) | collective-permute-done | bytes 131104 | tf_op jit(solution)/shard_map/cond/branch_1_fun/ppermute | solution.py:418
  120.0 3.3 %contract.1 = (f32[64,2000]{1,0:T(8,128)S(1)}, f32[64,2000]{1,0:T(8,128)S(1)}) custom-call(s32[1]{0:T(128)} %bitcast.12.which_ref.core_ref, bf16[8,4,16,128]{3,2,1,0:T(8,128)(2,1)} %get-tuple-element.408.kernel_ref, bf16[8,4,16,128]{3,2,1,0:T(8,128)(2,1)} %get-tuple-element.409.got_ref, bf16[2000,256]{1,0:T(8,128)(2,1)S(1)} %straighten.1.refs_1_.refs_0_, ...), custom_call_target="tpu_custom_call" | custom-call | flops 524288000 | bytes 5120000 | tf_op jit(solution)/shard_map/contract/pallas_call | solution.py:346
  123.6 1.7 %collective-permute-done.30.back_ref = f32[64,2000]{1,0:T(8,128)S(1)} collective-permute-done((f32[64,2000]{1,0:T(8,128)S(1)}, f32[64,2000]{1,0:T(8,128)S(1)}, u32[]{:S(2)}, u32[]{:S(2)}) %collective-permute-start.30) | collective-permute-done | bytes 512032 | tf_op jit(solution)/shard_map/ppermute | solution.py:418
  125.3 1.8 %finish.1 = f32[64,4000]{1,0:T(8,128)} custom-call(s32[2]{0:T(128)S(1)} %pad_add_fusion.2.flags_ref, f32[64,2000]{1,0:T(8,128)S(1)} %get-tuple-element.411.ours_ref, f32[64,2000]{1,0:T(8,128)S(1)} %collective-permute-done.30.back_ref, f32[64,4000]{1,0:T(8,128)} %get-tuple-element.413.other_ref), custom_call_target="tpu_custom_call", output_to_operand_aliasing={{}: (3, {})} | custom-call | tf_op jit(solution)/shard_map/finish/pallas_call | solution.py:387
  (107 shorter events, 7.8 us)
Async XLA Ops:
  0.0 3.3 %copy-start.5 = (f32[256]{0:T(256)S(1)}, f32[256]{0:T(256)}, u32[]{:S(2)}) copy-start(f32[256]{0:T(256)} %param.17) | copy-start | bytes 3076
  0.0 3.2 %copy-start.6 = (s32[8]{0:T(128)S(1)}, s32[8]{0:T(128)}, u32[]{:S(2)}) copy-start(s32[8]{0:T(128)} %param.18) | copy-start | bytes 100
  0.0 3.3 %collective-permute-start.18 = (f32[1,256]{1,0:T(1,128)}, f32[1,256]{1,0:T(1,128)S(1)}, u32[]{:S(2)}, u32[]{:S(2)}) collective-permute-start(f32[1,256]{1,0:T(1,128)} %bitcast.84), channel_id=1, source_target_pairs={{0,4},{4,0},{8,12},{12,8},{16,20},{20,16},{24,28},{28,24},{1,5},{5... | collective-permute-start | bytes 3080 | tf_op jit(solution)/shard_map/ppermute | solution.py:418
  0.5 2.7 %collective-permute-start.17 = (s32[1,8]{1,0:T(1,128)}, s32[1,8]{1,0:T(1,128)S(1)}, u32[]{:S(2)}, u32[]{:S(2)}) collective-permute-start(s32[1,8]{1,0:T(1,128)} %bitcast.86), channel_id=1, source_target_pairs={{0,4},{4,0},{8,12},{12,8},{16,20},{20,16},{24,28},{28,24},{1,5},{5... | collective-permute-start | bytes 104 | tf_op jit(solution)/shard_map/ppermute | solution.py:418
  1.4 6.6 %collective-permute-start.16 = (s32[16,8]{0,1:T(8,128)S(1)}, s32[16,8]{0,1:T(8,128)S(1)}, u32[]{:S(2)}, u32[]{:S(2)}) collective-permute-start(s32[16,8]{0,1:T(8,128)S(1)} %get-tuple-element.483), channel_id=1, source_target_pairs={{0,4},{4,0},{8,12},{12,8},{16,20},{20,16},{24,28},{28,24},{1,5},{5... | collective-permute-start | bytes 1544 | tf_op jit(solution)/shard_map/ppermute | solution.py:418
  3.0 7.7 %collective-permute-start.15 = (bf16[2000,256]{1,0:T(8,128)(2,1)S(1)}, bf16[2000,256]{1,0:T(8,128)(2,1)S(1)}, u32[]{:S(2)}, u32[]{:S(2)}) collective-permute-start(bf16[2000,256]{1,0:T(8,128)(2,1)S(1)} %half_of.3), channel_id=1, source_target_pairs={{0,4},{4,0},{8,12},{12,8},{16,20},{20,16},{24,28},{28,24},{1,5},{5... | collective-permute-start | bytes 3072008 | tf_op jit(solution)/shard_map/ppermute | solution.py:418
  3.4 4.9 %collective-permute-start.19 = (f32[1,528]{1,0:T(1,128)S(1)}, f32[1,528]{1,0:T(1,128)S(1)}, u32[]{:S(2)}, u32[]{:S(2)}) collective-permute-start(f32[1,528]{1,0:T(1,128)S(1)} %pad_maximum_fusion.2), channel_id=1, source_target_pairs={{0,8},{4,12},{8,0},{12,4},{16,24},{20,28},{24,16},{28,20},{1,9},{5... | collective-permute-start | bytes 6344 | tf_op jit(solution)/shard_map/ppermute | solution.py:418
  10.7 1.0 copy-start.2
  11.7 1.2 copy-start.3
  14.7 16.4 %collective-permute-start.20 = (bf16[2000,128]{1,0:T(8,128)(2,1)S(1)}, bf16[2000,128]{1,0:T(8,128)(2,1)S(1)}, u32[]{:S(2)}, u32[]{:S(2)}) collective-permute-start(bf16[2000,128]{1,0:T(8,128)(2,1)S(1)} %get-tuple-element.389), channel_id=1, source_target_pairs={{8,16},{12,20},{16,8},{20,12},{9,17},{13,21},{17,9},{21,13},{10,18... | collective-permute-start | bytes 1536008 | tf_op jit(solution)/shard_map/ppermute | solution.py:492
  15.4 15.9 %collective-permute-start.21 = (bf16[2000,128]{1,0:T(8,128)(2,1)S(1)}, bf16[2000,128]{1,0:T(8,128)(2,1)S(1)}, u32[]{:S(2)}, u32[]{:S(2)}) collective-permute-start(bf16[2000,128]{1,0:T(8,128)(2,1)S(1)} %get-tuple-element.390), channel_id=1, source_target_pairs={{0,8},{4,12},{8,0},{12,4},{16,24},{20,28},{24,16},{28,20},{1,9},{5... | collective-permute-start | bytes 1536008 | tf_op jit(solution)/shard_map/ppermute | solution.py:492
  19.9 11.1 %collective-permute-start.22 = (f32[2,528]{1,0:T(2,128)S(1)}, f32[2,528]{1,0:T(2,128)S(1)}, u32[]{:S(2)}, u32[]{:S(2)}) collective-permute-start(f32[2,528]{1,0:T(2,128)S(1)} %maximum_select_fusion.1), channel_id=1, source_target_pairs={{0,16},{4,20},{8,24},{12,28},{16,0},{20,4},{24,8},{28,12},{1,17},{... | collective-permute-start | bytes 12680 | tf_op jit(solution)/shard_map/ppermute | solution.py:418
  31.6 24.8 %collective-permute-start.23 = (bf16[2000,256]{1,0:T(8,128)(2,1)S(1)}, bf16[2000,256]{1,0:T(8,128)(2,1)S(1)}, u32[]{:S(2)}, u32[]{:S(2)}) collective-permute-start(bf16[2000,256]{1,0:T(8,128)(2,1)S(1)} %straighten.1.refs_1_.refs_0_), channel_id=1, source_target_pairs={{0,8},{4,12},{8,0},{12,4},{16,24},{20,28},{24,16},{28,20},{1,9},{5... | collective-permute-start | bytes 3072008 | tf_op jit(solution)/shard_map/ppermute | solution.py:492
  33.4 15.7 %collective-permute-start.25 = (bf16[2000,256]{1,0:T(8,128)(2,1)S(1)}, bf16[2000,256]{1,0:T(8,128)(2,1)S(1)}, u32[]{:S(2)}, u32[]{:S(2)}) collective-permute-start(bf16[2000,256]{1,0:T(8,128)(2,1)S(1)} %straighten.1.refs_1_.refs_0_), channel_id=1, source_target_pairs={{8,16},{12,20},{16,8},{20,12},{9,17},{13,21},{17,9},{21,13},{10,18... | collective-permute-start | bytes 3072008 | tf_op jit(solution)/shard_map/ppermute | solution.py:492
  36.9 0.8 copy-start
  37.7 2.3 %collective-permute-start.27 = (bf16[128,2048]{1,0:T(8,128)(2,1)}, bf16[128,2048]{1,0:T(8,128)(2,1)}, u32[]{:S(2)}, u32[]{:S(2)}) collective-permute-start(bf16[128,2048]{1,0:T(8,128)(2,1)} %get-tuple-element.395), channel_id=1, source_target_pairs={{0,4},{4,0},{8,12},{12,8},{16,20},{20,16},{24,28},{28,24},{1,5},{5... | collective-permute-start | bytes 1572872 | tf_op jit(solution)/shard_map/ppermute | solution.py:418
  40.0 1.0 copy-start.1
  43.1 37.2 %collective-permute-start.28 = (bf16[256,2048]{1,0:T(8,128)(2,1)}, bf16[256,2048]{1,0:T(8,128)(2,1)}, u32[]{:S(2)}, u32[]{:S(2)}) collective-permute-start(bf16[256,2048]{1,0:T(8,128)(2,1)} %stack_panels.1.refs_0_), channel_id=1, source_target_pairs={{0,8},{4,12},{24,16},{28,20},{1,9},{5,13},{25,17},{29,21},{2,10},{... | collective-permute-start | bytes 3145736 | tf_op jit(solution)/shard_map/ppermute | solution.py:492
  49.0 31.3 %collective-permute-start.26 = (bf16[2000,256]{1,0:T(8,128)(2,1)S(1)}, bf16[2000,256]{1,0:T(8,128)(2,1)}, u32[]{:S(2)}, u32[]{:S(2)}) collective-permute-start(bf16[2000,256]{1,0:T(8,128)(2,1)S(1)} %collective-permute-done.25.refs_3_.refs_2_), channel_id=1, source_target_pairs={{8,0},{12,4},{16,24},{20,28},{9,1},{13,5},{17,25},{21,29},{10,2},{... | collective-permute-start | bytes 3072008 | tf_op jit(solution)/shard_map/ppermute | solution.py:492
  56.4 23.9 %collective-permute-start.24 = (bf16[2000,256]{1,0:T(8,128)(2,1)S(1)}, bf16[2000,256]{1,0:T(8,128)(2,1)}, u32[]{:S(2)}, u32[]{:S(2)}) collective-permute-start(bf16[2000,256]{1,0:T(8,128)(2,1)S(1)} %collective-permute-done.23.refs_2_.refs_1_), channel_id=1, source_target_pairs={{8,16},{12,20},{16,8},{20,12},{9,17},{13,21},{17,9},{21,13},{10,18... | collective-permute-start | bytes 3072008 | tf_op jit(solution)/shard_map/ppermute | solution.py:492
  58.4 23.3 %copy-start.4 = (s32[8,32]{1,0:T(8,128)S(1)}, s32[8,32]{1,0:T(8,128)}, u32[]{:S(2)}) copy-start(s32[8,32]{1,0:T(8,128)} %param.19) | copy-start | bytes 3076
  80.3 39.7 %collective-permute-start.29 = (bf16[2000,256]{1,0:T(8,128)(2,1)}, bf16[2000,256]{1,0:T(8,128)(2,1)}, u32[]{:S(2)}, u32[]{:S(2)}) collective-permute-start(bf16[2000,256]{1,0:T(8,128)(2,1)} %collective-permute-done.24.refs_5_), channel_id=1, source_target_pairs={{8,0},{12,4},{16,24},{20,28},{9,1},{13,5},{17,25},{21,29},{10,2},{... | collective-permute-start | bytes 3072008 | tf_op jit(solution)/shard_map/ppermute | solution.py:492
  81.9 4.9 %collective-permute-start = (f32[6,4,16,256]{3,2,1,0:T(8,128)}, f32[6,4,16,256]{3,2,1,0:T(8,128)S(1)}, u32[]{:S(2)}, u32[]{:S(2)}) collective-permute-start(f32[6,4,16,256]{3,2,1,0:T(8,128)} %get-tuple-element.348), channel_id=1, source_target_pairs={{0,4},{4,0},{8,12},{12,8},{16,20},{20,16},{24,28},{28,24},{1,5},{5... | collective-permute-start | bytes 1179656 | tf_op jit(solution)/shard_map/cond/branch_1_fun/ppermute | solution.py:418
  85.0 1.7 %collective-permute-start.1 = (f32[4,4,16,256]{3,2,1,0:T(8,128)S(1)}, f32[4,4,16,256]{3,2,1,0:T(8,128)S(1)}, u32[]{:S(2)}, u32[]{:S(2)}) collective-permute-start(f32[4,4,16,256]{3,2,1,0:T(8,128)S(1)} %get-tuple-element.355), channel_id=1, source_target_pairs={{0,4},{4,0},{8,12},{12,8},{16,20},{20,16},{24,28},{28,24},{1,5},{5... | collective-permute-start | bytes 786440 | tf_op jit(solution)/shard_map/cond/branch_1_fun/ppermute | solution.py:418
  86.8 7.1 %collective-permute-start.2 = (f32[10,16,256]{2,1,0:T(8,128)S(1)}, f32[10,16,256]{2,1,0:T(8,128)S(1)}, u32[]{:S(2)}, u32[]{:S(2)}) collective-permute-start(f32[10,16,256]{2,1,0:T(8,128)S(1)} %get-tuple-element.357), channel_id=1, source_target_pairs={{0,1},{1,0},{2,3},{3,2},{4,5},{5,4},{6,7},{7,6},{8,9},{9,8},{10,11... | collective-permute-start | bytes 491528 | tf_op jit(solution)/shard_map/cond/branch_1_fun/ppermute | solution.py:418
  88.4 9.7 %collective-permute-start.3 = (f32[10,16,256]{2,1,0:T(8,128)S(1)}, f32[10,16,256]{2,1,0:T(8,128)S(1)}, u32[]{:S(2)}, u32[]{:S(2)}) collective-permute-start(f32[10,16,256]{2,1,0:T(8,128)S(1)} %get-tuple-element.358), channel_id=1, source_target_pairs={{0,2},{1,3},{2,0},{3,1},{4,6},{5,7},{6,4},{7,5},{8,10},{9,11},{10,... | collective-permute-start | bytes 491528 | tf_op jit(solution)/shard_map/cond/branch_1_fun/ppermute | solution.py:418
  89.9 8.2 %collective-permute-start.4 = (f32[10,16,256]{2,1,0:T(8,128)S(1)}, f32[10,16,256]{2,1,0:T(8,128)S(1)}, u32[]{:S(2)}, u32[]{:S(2)}) collective-permute-start(f32[10,16,256]{2,1,0:T(8,128)S(1)} %get-tuple-element.359), channel_id=1, source_target_pairs={{0,3},{1,2},{2,1},{3,0},{4,7},{5,6},{6,5},{7,4},{8,11},{9,10},{10,... | collective-permute-start | bytes 491528 | tf_op jit(solution)/shard_map/cond/branch_1_fun/ppermute | solution.py:418
  98.4 8.2 %collective-permute-start.6 = (f32[4,32]{1,0:T(4,128)S(1)}, f32[4,32]{1,0:T(4,128)S(1)}, u32[]{:S(2)}, u32[]{:S(2)}) collective-permute-start(f32[4,32]{1,0:T(4,128)S(1)} %select_reduce_fusion), channel_id=1, source_target_pairs={{0,16},{4,20},{8,24},{12,28},{16,0},{20,4},{24,8},{28,12},{1,17},{... | collective-permute-start | bytes 1544 | tf_op jit(solution)/shard_map/cond/branch_1_fun/ppermute | solution.py:418
  104.4 5.4 %collective-permute-start.7 = (f32[4,32]{1,0:T(4,128)S(1)}, f32[4,32]{1,0:T(4,128)S(1)}, u32[]{:S(2)}, u32[]{:S(2)}) collective-permute-start(f32[4,32]{1,0:T(4,128)S(1)} %select_reduce_fusion), channel_id=1, source_target_pairs={{0,24},{4,28},{8,16},{12,20},{16,8},{20,12},{24,0},{28,4},{1,25},{... | collective-permute-start | bytes 1544 | tf_op jit(solution)/shard_map/cond/branch_1_fun/ppermute | solution.py:418
  106.5 4.0 %collective-permute-start.5 = (f32[36,256]{1,0:T(8,128)S(1)}, f32[36,256]{1,0:T(8,128)S(1)}, u32[]{:S(2)}, u32[]{:S(2)}) collective-permute-start(f32[36,256]{1,0:T(8,128)S(1)} %select_maximum_fusion), channel_id=1, source_target_pairs={{0,8},{4,12},{8,0},{12,4},{16,24},{20,28},{24,16},{28,20},{1,9},{5... | collective-permute-start | bytes 110600 | tf_op jit(solution)/shard_map/cond/branch_1_fun/ppermute | solution.py:418
  110.7 4.9 %collective-permute-start.10 = (bf16[8,1,16,128]{3,2,1,0:T(8,128)(2,1)S(1)}, bf16[8,1,16,128]{3,2,1,0:T(8,128)(2,1)S(1)}, u32[]{:S(2)}, u32[]{:S(2)}) collective-permute-start(bf16[8,1,16,128]{3,2,1,0:T(8,128)(2,1)S(1)} %bitcast.67), channel_id=1, source_target_pairs={{0,3},{1,2},{2,1},{3,0},{4,7},{5,6},{6,5},{7,4},{8,11},{9,10},{10,... | collective-permute-start | bytes 98312 | tf_op jit(solution)/shard_map/cond/branch_1_fun/ppermute | solution.py:418
  112.2 3.9 %collective-permute-start.8 = (bf16[8,1,16,128]{3,2,1,0:T(8,128)(2,1)S(1)}, bf16[8,1,16,128]{3,2,1,0:T(8,128)(2,1)S(1)}, u32[]{:S(2)}, u32[]{:S(2)}) collective-permute-start(bf16[8,1,16,128]{3,2,1,0:T(8,128)(2,1)S(1)} %bitcast.68), channel_id=1, source_target_pairs={{0,1},{1,0},{2,3},{3,2},{4,5},{5,4},{6,7},{7,6},{8,9},{9,8},{10,11... | collective-permute-start | bytes 98312 | tf_op jit(solution)/shard_map/cond/branch_1_fun/ppermute | solution.py:418
  113.7 3.9 %collective-permute-start.9 = (bf16[8,1,16,128]{3,2,1,0:T(8,128)(2,1)S(1)}, bf16[8,1,16,128]{3,2,1,0:T(8,128)(2,1)S(1)}, u32[]{:S(2)}, u32[]{:S(2)}) collective-permute-start(bf16[8,1,16,128]{3,2,1,0:T(8,128)(2,1)S(1)} %bitcast.69), channel_id=1, source_target_pairs={{0,2},{1,3},{2,0},{3,1},{4,6},{5,7},{6,4},{7,5},{8,10},{9,11},{10,... | collective-permute-start | bytes 98312 | tf_op jit(solution)/shard_map/cond/branch_1_fun/ppermute | solution.py:418
  118.3 1.7 %collective-permute-start.11 = (bf16[8,4,16,128]{3,2,1,0:T(8,128)(2,1)}, bf16[8,4,16,128]{3,2,1,0:T(8,128)(2,1)}, u32[]{:S(2)}, u32[]{:S(2)}) collective-permute-start(bf16[8,4,16,128]{3,2,1,0:T(8,128)(2,1)} %in_order.1), channel_id=1, source_target_pairs={{0,4},{4,0},{8,12},{12,8},{16,20},{20,16},{24,28},{28,24},{1,5},{5... | collective-permute-start | bytes 393224 | tf_op jit(solution)/shard_map/cond/branch_1_fun/ppermute | solution.py:418
  123.3 2.0 %collective-permute-start.30 = (f32[64,2000]{1,0:T(8,128)S(1)}, f32[64,2000]{1,0:T(8,128)S(1)}, u32[]{:S(2)}, u32[]{:S(2)}) collective-permute-start(f32[64,2000]{1,0:T(8,128)S(1)} %get-tuple-element.412), channel_id=1, source_target_pairs={{0,4},{4,0},{8,12},{12,8},{16,20},{20,16},{24,28},{28,24},{1,5},{5... | collective-permute-start | bytes 1536008 | tf_op jit(solution)/shard_map/ppermute | solution.py:418

commit v6 on v5

--- a/solution.py
+++ b/solution.py
@@ -454,18 +454,17 @@
         for bit in grid_bits[2:]:
             told = doubled(told, "grid", bit, 0)
 
-    def places_of(sizes, first):
+    def places_of(sizes, upper):
         count = sizes.shape[0]
         batch = lax.broadcasted_iota(jnp.int32, (count, count), 0)
         before = lax.broadcasted_iota(jnp.int32, (count, count), 1) < batch
-        start = first + jnp.sum(jnp.where(before, sizes[None, :], 0), axis=1)
+        start = upper * live + jnp.sum((before.astype(jnp.int32) - upper) * sizes[None, :], axis=1)
         position = lax.broadcasted_iota(jnp.int32, (count, slots), 1)
         to = jnp.where(position < sizes[:, None], start[:, None] + position, -4 * live)
         return to.reshape(-1, rows), start
 
     sizes = told[:, : 2 * batches].astype(jnp.int32).reshape(-1)
-    first = jnp.where((chip >= 2) & (chips <= 4), live - jnp.sum(sizes), 0)
-    near_to, _ = places_of(sizes, first)
+    near_to, _ = places_of(sizes, chip // 2 if chips <= 4 else 0)
     near_place = place if chips > 4 else place % 4
     for bit in grid_bits[2:] if chips <= 4 else []:
         told = doubled(told, "grid", bit, 0)
@@ -576,7 +575,13 @@
     early_jobs = stages[0] + early_jobs
     early_at = jnp.concatenate((chip[None], early_at))
 
-    early_pair = project([(panels, w) for w, _ in early_jobs], tile, shares, core)
+    def halved(jobs):
+        keep, give = project(jobs, tile, shares, core)
+        return keep, flip(give, "grid", 1)
+
+    early_value = summed(
+        [halved([(panels, early_jobs[0][0])]), halved([(panels, w) for w, _ in early_jobs[1:]])]
+    )
 
     at = (
         (window_iota * rows)[:, None, None]
@@ -591,9 +596,8 @@
     here = (places[:, None] == window_iota[None, :])[:, :, None]
     weight_here = jnp.sum(jnp.where(here, weight[None], 0.0), axis=1)[:, :, None]
 
-    by_a, early_pair = lax.optimization_barrier((by_a, early_pair))
-    late, by_a, early_pair, far_panels, weight_here, fits = lax.optimization_barrier(
-        (by_b, by_a, early_pair, far_panels, weight_here, fits.astype(jnp.int32))
+    late, by_a, early_value, far_panels, weight_here, fits = lax.optimization_barrier(
+        (by_b, by_a, early_value, far_panels, weight_here, fits.astype(jnp.int32))
     )
     fits = fits != 0
     late = tuple(sent(x, homes) for x in late)
@@ -602,7 +606,8 @@
 
     def kernel_of_all():
         late_pair = project(late_jobs, tile, shares, core)
-        value = summed([(keep, flip(give, "grid", 1)) for keep, give in (early_pair, late_pair)])
+        keep, give = late_pair
+        value = jnp.concatenate((early_value, summed([(keep, flip(give, "grid", 1))])))
         density = shared_density(value, jnp.concatenate((early_at, late_at, late_at)))
         value, far_value = value[:-1], value[-1:]
         packed = jnp.concatenate(

time: 128 us -> 128 us (level)
  waiting for transfers between devices: 54.4 us -> 43.5 us
  starting transfers between devices: 38 us -> 44.1 us
  Pallas kernels: 21.2 us -> 25.1 us
  local copies, waits for them, and re-layouts: 6.16 us -> 8.06 us
    ppermute x8, waiting for transfers between devices: 22 us -> 7.61 us  [sent(): return lax.ppermute(x, 'grid', along(pairs))]
    ppermute x20 -> x24, starting transfers between devices: 20.2 us -> 26.2 us  [flip(): return lax.ppermute(x, axis, [(i, i ^ bit) for i in range(count)])]
    ppermute x20 -> x24, waiting for transfers between devices: 32.4 us -> 35.9 us  [flip(): return lax.ppermute(x, axis, [(i, i ^ bit) for i in range(count)])]
    pallas_call x2 -> x3, Pallas kernels: 6.19 us -> 8.32 us  [project(): pl.pallas_call(body, out_shape=(shape, shape), in_specs=[SCALARS] + [WHOL...]
    unnamed x17 -> x23, local copies, waits for them, and re-layouts: 4.1 us -> 6.01 us
    pallas_call x1 -> x2, Pallas kernels: 0.08 us -> 1.75 us  [split_sum(): pl.pallas_call(body, out_shape=(shape,) * shares, in_specs=[SCALARS] + [W...]
  transfers between devices with their start and end apart: 28 -> 32, of which waited for: 15 -> 17; matrix products, arithmetic and copies ran while one was open for 5% -> 6% of each run, Pallas kernels for 11% -> 14%
where the time goes in v6:
time: 128 us
  starting transfers between devices  44.1 us (34%)
  waiting for transfers between devices  43.5 us (34%)
  Pallas kernels  25.1 us (20%)
  local copies, waits for them, and re-layouts  8.06 us (6%)
  other arithmetic  5.03 us (4%)
  between operations  1.63 us (1%)
    ppermute x24, waiting for transfers between devices, flip(): return lax.ppermute(x, axis, [(i, i ^ bit) for i in range(count)])  35.9 us
    ppermute x24, starting transfers between devices, flip(): return lax.ppermute(x, axis, [(i, i ^ bit) for i in range(count)])  26.2 us
    ppermute x8, starting transfers between devices, sent(): return lax.ppermute(x, 'grid', along(pairs))  17.9 us
    pallas_call x3, Pallas kernels, project(): pl.pallas_call(body, out_shape=(shape, shape), in_specs=[SCALARS] + [WHOL...  8.32 us
    ppermute x8, waiting for transfers between devices, sent(): return lax.ppermute(x, 'grid', along(pairs))  7.61 us
    unnamed x23, local copies, waits for them, and re-layouts  6.01 us
    pallas_call x1, Pallas kernels, contract(): pl.pallas_call(body, out_shape=(shape, shape), in_specs=[SCALARS] + [WHOL...  3.3 us
  transfers between devices with their start and end apart: 32, of which 17 were waited for; matrix products, arithmetic and copies ran while one was open for 6% of the time, Pallas kernels for 14%

profile of v6, /device:TPU:0, one launch (start us, length us, event | category | flops | bytes accessed | tf_op | source)
XLA Modules:
  0.0 127.7 jit_solution(6807801408968582619)
XLA Ops:
  0.5 0.8 dynamic-slice_bitcast_fusion
  1.8 1.2 half_of.3
  3.4 3.0 %collective-permute-start.18 = (f32[1,528]{1,0:T(1,128)S(1)}, f32[1,528]{1,0:T(1,128)S(1)}, u32[]{:S(2)}, u32[]{:S(2)}) collective-permute-start(f32[1,528]{1,0:T(1,128)S(1)} %pad_maximum_fusion.3), channel_id=1, source_target_pairs={{0,8},{4,12},{8,0},{12,4},{16,24},{20,28},{24,16},{28,20},{1,9},{5... | collective-permute-start | bytes 6344 | tf_op jit(solution)/shard_map/ppermute | solution.py:418
  6.8 1.2 half_of.2.mine_ref
  9.4 0.9 copy-done.3
  10.4 1.2 copy-done.4
  11.6 1.8 %compact.1 = (bf16[2000,128]{1,0:T(8,128)(2,1)S(1)}, bf16[2000,128]{1,0:T(8,128)(2,1)S(1)}, bf16[2000,128]{1,0:T(8,128)(2,1)S(1)}, bf16[2000,128]{1,0:T(8,128)(2,1)S(1)}) custom-call(s32[1]{0:T(128)} %bitcast.11.odd_ref, bf16[2000,256]{1,0:T(8,128)(2,1)S(1)} %half_of.2.mine_ref, bf16[2000,256]{1,0:T(8,128)(2,1)S(1)} %copy-done.4, ...), custom_call_target="tpu_custom_call" | custom-call | flops 1048576000 | bytes 4096000 | tf_op jit(solution)/shard_map/compact/pallas_call | solution.py:124
  14.1 4.5 %collective-permute-start.20 = (bf16[2000,128]{1,0:T(8,128)(2,1)S(1)}, bf16[2000,128]{1,0:T(8,128)(2,1)S(1)}, u32[]{:S(2)}, u32[]{:S(2)}) collective-permute-start(bf16[2000,128]{1,0:T(8,128)(2,1)S(1)} %get-tuple-element.389), channel_id=1, source_target_pairs={{0,8},{4,12},{8,0},{12,4},{16,24},{20,28},{24,16},{28,20},{1,9},{5... | collective-permute-start | bytes 1536008 | tf_op jit(solution)/shard_map/ppermute | solution.py:491
  18.7 11.1 %collective-permute-done.21 = f32[2,528]{1,0:T(2,128)S(1)} collective-permute-done((f32[2,528]{1,0:T(2,128)S(1)}, f32[2,528]{1,0:T(2,128)S(1)}, u32[]{:S(2)}, u32[]{:S(2)}) %collective-permute-start.21) | collective-permute-done | bytes 4256 | tf_op jit(solution)/shard_map/ppermute | solution.py:418
  30.3 1.8 %collective-permute-start.22 = (bf16[2000,256]{1,0:T(8,128)(2,1)S(1)}, bf16[2000,256]{1,0:T(8,128)(2,1)S(1)}, u32[]{:S(2)}, u32[]{:S(2)}) collective-permute-start(bf16[2000,256]{1,0:T(8,128)(2,1)S(1)} %straighten.1.refs_1_.refs_0_), channel_id=1, source_target_pairs={{0,8},{4,12},{8,0},{12,4},{16,24},{20,28},{24,16},{28,20},{1,9},{5... | collective-permute-start | bytes 3072008 | tf_op jit(solution)/shard_map/ppermute | solution.py:491
  33.1 2.5 %panel_halves.1 = (bf16[128,2048]{1,0:T(8,128)(2,1)S(1)}, bf16[128,2048]{1,0:T(8,128)(2,1)}) custom-call(s32[1]{0:T(128)} %bitcast.10.which_ref.core_ref, bf16[64,4000]{1,0:T(8,128)(2,1)} %bitcast.74, bf16[64,4000]{1,0:T(8,128)(2,1)} %bitcast.75), custom_call_target="tpu_custom_call" | custom-call | tf_op jit(solution)/shard_map/panel_halves/pallas_call | solution.py:178
  35.6 0.8 copy-done
  36.8 1.9 %collective-permute-done.26.got_ref = bf16[128,2048]{1,0:T(8,128)(2,1)} collective-permute-done((bf16[128,2048]{1,0:T(8,128)(2,1)}, bf16[128,2048]{1,0:T(8,128)(2,1)}, u32[]{:S(2)}, u32[]{:S(2)}) %collective-permute-start.26) | collective-permute-done | bytes 524320 | tf_op jit(solution)/shard_map/ppermute | solution.py:418
  38.7 1.0 copy-done.1
  39.8 2.1 %stack_panels.1.refs_0_ = bf16[256,2048]{1,0:T(8,128)(2,1)} custom-call(s32[1]{0:T(128)} %bitcast.10.which_ref.core_ref, bf16[128,2048]{1,0:T(8,128)(2,1)S(1)} %copy-done.1, bf16[128,2048]{1,0:T(8,128)(2,1)} %collective-permute-done.26.got_ref), custom_call_target="tpu_custom_call" | custom-call | tf_op jit(solution)/shard_map/stack_panels/pallas_call | solution.py:201
  41.9 5.9 %collective-permute-start.32 = (bf16[256,2048]{1,0:T(8,128)(2,1)}, bf16[256,2048]{1,0:T(8,128)(2,1)}, u32[]{:S(2)}, u32[]{:S(2)}) collective-permute-start(bf16[256,2048]{1,0:T(8,128)(2,1)} %stack_panels.1.refs_0_), channel_id=1, source_target_pairs={{0,8},{4,12},{24,16},{28,20},{1,9},{5,13},{25,17},{29,21},{2,10},{... | collective-permute-start | bytes 3145736 | tf_op jit(solution)/shard_map/ppermute | solution.py:491
  47.8 7.4 %collective-permute-done.22.refs_1_ = bf16[2000,256]{1,0:T(8,128)(2,1)S(1)} collective-permute-done((bf16[2000,256]{1,0:T(8,128)(2,1)S(1)}, bf16[2000,256]{1,0:T(8,128)(2,1)S(1)}, u32[]{:S(2)}, u32[]{:S(2)}) %collective-permute-start.22) | collective-permute-done | bytes 1024032 | tf_op jit(solution)/shard_map/ppermute | solution.py:491
  55.2 1.7 %collective-permute-start.23 = (bf16[2000,256]{1,0:T(8,128)(2,1)S(1)}, bf16[2000,256]{1,0:T(8,128)(2,1)}, u32[]{:S(2)}, u32[]{:S(2)}) collective-permute-start(bf16[2000,256]{1,0:T(8,128)(2,1)S(1)} %collective-permute-done.22.refs_1_), channel_id=1, source_target_pairs={{8,16},{12,20},{16,8},{20,12},{9,17},{13,21},{17,9},{21,13},{10,18... | collective-permute-start | bytes 3072008 | tf_op jit(solution)/shard_map/ppermute | solution.py:491
  56.9 1.3 %collective-permute-start.25 = (bf16[2000,256]{1,0:T(8,128)(2,1)S(1)}, bf16[2000,256]{1,0:T(8,128)(2,1)}, u32[]{:S(2)}, u32[]{:S(2)}) collective-permute-start(bf16[2000,256]{1,0:T(8,128)(2,1)S(1)} %collective-permute-done.24.refs_2_), channel_id=1, source_target_pairs={{8,0},{12,4},{16,24},{20,28},{9,1},{13,5},{17,25},{21,29},{10,2},{... | collective-permute-start | bytes 3072008 | tf_op jit(solution)/shard_map/ppermute | solution.py:491
  58.3 2.9 %project.5 = (f32[4,4,16,256]{3,2,1,0:T(8,128)S(1)}, f32[4,4,16,256]{3,2,1,0:T(8,128)}) custom-call(s32[1]{0:T(128)} %bitcast.10.which_ref.core_ref, bf16[256,2048]{1,0:T(8,128)(2,1)} %stack_panels.1.refs_0_, bf16[2000,256]{1,0:T(8,128)(2,1)S(1)} %collective-permute-done.22.refs_1_, bf16[2000,256]{1,0:T(8,128)(2,1)S(1)} %collective-permute-done.24.refs_2_), custom_call_target="tpu_custom_call" | custom-call | flops 524288000 | bytes 3596288 | tf_op jit(solution)/shard_map/project/pallas_call | solution.py:281
  61.4 2.4 %project.4 = (f32[2,4,16,256]{3,2,1,0:T(8,128)S(1)}, f32[2,4,16,256]{3,2,1,0:T(8,128)}) custom-call(s32[1]{0:T(128)} %bitcast.10.which_ref.core_ref, bf16[256,2048]{1,0:T(8,128)(2,1)} %stack_panels.1.refs_0_, bf16[2000,256]{1,0:T(8,128)(2,1)S(1)} %straighten.1.refs_1_.refs_0_), custom_call_target="tpu_custom_call" | custom-call | flops 262144000 | bytes 2310144 | tf_op jit(solution)/shard_map/project/pallas_call | solution.py:281
  65.8 1.7 %split_sum.3 = (f32[6,16,256]{2,1,0:T(8,128)S(1)}, f32[6,16,256]{2,1,0:T(8,128)}, f32[6,16,256]{2,1,0:T(8,128)S(1)}, f32[6,16,256]{2,1,0:T(8,128)S(1)}) custom-call(s32[1]{0:T(128)} %bitcast.20.occ_ref, f32[2,4,16,256]{3,2,1,0:T(8,128)S(1)} %get-tuple-element.395.refs_0_, f32[2,4,16,256]{3,2,1,0:T(8,128)} %collective-permute-done.27.refs_1_, ...), custom_call_target="tpu_custom_call" | custom-call | tf_op jit(solution)/shard_map/split_sum/pallas_call | solution.py:238
  69.4 1.5 %collective-permute-start.29 = (f32[6,16,256]{2,1,0:T(8,128)}, f32[6,16,256]{2,1,0:T(8,128)S(1)}, u32[]{:S(2)}, u32[]{:S(2)}) collective-permute-start(f32[6,16,256]{2,1,0:T(8,128)} %get-tuple-element.400), channel_id=1, source_target_pairs={{0,1},{1,0},{2,3},{3,2},{4,5},{5,4},{6,7},{7,6},{8,9},{9,8},{10,11... | collective-permute-start | bytes 294920 | tf_op jit(solution)/shard_map/ppermute | solution.py:418
  72.2 1.6 %collective-permute-start.30 = (f32[6,16,256]{2,1,0:T(8,128)}, f32[6,16,256]{2,1,0:T(8,128)S(1)}, u32[]{:S(2)}, u32[]{:S(2)}) collective-permute-start(f32[6,16,256]{2,1,0:T(8,128)} %copy-done.6), channel_id=1, source_target_pairs={{0,2},{1,3},{2,0},{3,1},{4,6},{5,7},{6,4},{7,5},{8,10},{9,11},{10,... | collective-permute-start | bytes 294920 | tf_op jit(solution)/shard_map/ppermute | solution.py:418
  73.8 0.8 collective-permute-done.29
  74.5 2.4 %collective-permute-start.31 = (f32[6,16,256]{2,1,0:T(8,128)}, f32[6,16,256]{2,1,0:T(8,128)S(1)}, u32[]{:S(2)}, u32[]{:S(2)}) collective-permute-start(f32[6,16,256]{2,1,0:T(8,128)} %copy-done.5), channel_id=1, source_target_pairs={{0,3},{1,2},{2,1},{3,0},{4,7},{5,6},{6,5},{7,4},{8,11},{9,10},{10,... | collective-permute-start | bytes 294920 | tf_op jit(solution)/shard_map/ppermute | solution.py:418
  77.1 3.2 %collective-permute-done.31 = f32[6,16,256]{2,1,0:T(8,128)S(1)} collective-permute-done((f32[6,16,256]{2,1,0:T(8,128)}, f32[6,16,256]{2,1,0:T(8,128)S(1)}, u32[]{:S(2)}, u32[]{:S(2)}) %collective-permute-start.31) | collective-permute-done | bytes 98336 | tf_op jit(solution)/shard_map/ppermute | solution.py:418
  80.3 0.9 add_add_fusion.1
  81.2 1.3 %collective-permute-start.33 = (bf16[2000,256]{1,0:T(8,128)(2,1)}, bf16[2000,256]{1,0:T(8,128)(2,1)}, u32[]{:S(2)}, u32[]{:S(2)}) collective-permute-start(bf16[2000,256]{1,0:T(8,128)(2,1)} %collective-permute-done.23.refs_5_), channel_id=1, source_target_pairs={{8,0},{12,4},{16,24},{20,28},{9,1},{13,5},{17,25},{21,29},{10,2},{... | collective-permute-start | bytes 3072008 | tf_op jit(solution)/shard_map/ppermute | solution.py:491
  82.6 37.8 %conditional.1 = (bf16[8,4,16,128]{3,2,1,0:T(8,128)(2,1)}, bf16[8,4,16,128]{3,2,1,0:T(8,128)(2,1)}, f32[64,4000]{1,0:T(8,128)}) conditional(s32[]{:T(128)} %convert_element_type.61, (s32[8]{0:T(128)S(1)}, f32[256]{0:T(256)S(1)}, bf16[4000,64]{0,1:T(8,128)(2,1)}, bf16[4000,64]{0,1:T(8,128)(2,1)}, s32[8,32]{1,0:T(8,128)S(1)}, ...), branch_computations={%region_6.14_spmd, %region_14.18_spmd} | conditional | flops 524588416 | bytes 65907736 | solution.py:649
  82.8 3.0 %project.3 = (f32[4,4,16,256]{3,2,1,0:T(8,128)S(1)}, f32[4,4,16,256]{3,2,1,0:T(8,128)S(1)}) custom-call(s32[1]{0:T(128)} %bitcast.4.core_ref, bf16[256,2048]{1,0:T(8,128)(2,1)} %get-tuple-element.347.refs_0_, bf16[256,2048]{1,0:T(8,128)(2,1)} %get-tuple-element.348.refs_1_, bf16[2000,256]{1,0:T(8,128)(2,1)} %get-tuple-element.349.refs_2_, ...), custom_call_target="tpu_custom_call" | custom-call | flops 524288000 | bytes 3596288 | tf_op jit(solution)/shard_map/cond/branch_1_fun/project/pallas_call | solution.py:281
  86.0 1.4 %collective-permute-done.refs_1_ = f32[4,4,16,256]{3,2,1,0:T(8,128)S(1)} collective-permute-done((f32[4,4,16,256]{3,2,1,0:T(8,128)S(1)}, f32[4,4,16,256]{3,2,1,0:T(8,128)S(1)}, u32[]{:S(2)}, u32[]{:S(2)}) %collective-permute-start) | collective-permute-done | bytes 262176 | tf_op jit(solution)/shard_map/cond/branch_1_fun/ppermute | solution.py:418
  87.5 1.6 %collective-permute-start.1 = (f32[4,16,256]{2,1,0:T(8,128)S(1)}, f32[4,16,256]{2,1,0:T(8,128)S(1)}, u32[]{:S(2)}, u32[]{:S(2)}) collective-permute-start(f32[4,16,256]{2,1,0:T(8,128)S(1)} %get-tuple-element.354), channel_id=1, source_target_pairs={{0,1},{1,0},{2,3},{3,2},{4,5},{5,4},{6,7},{7,6},{8,9},{9,8},{10,11... | collective-permute-start | bytes 196616 | tf_op jit(solution)/shard_map/cond/branch_1_fun/ppermute | solution.py:418
  89.1 1.5 %collective-permute-start.2 = (f32[4,16,256]{2,1,0:T(8,128)S(1)}, f32[4,16,256]{2,1,0:T(8,128)S(1)}, u32[]{:S(2)}, u32[]{:S(2)}) collective-permute-start(f32[4,16,256]{2,1,0:T(8,128)S(1)} %get-tuple-element.355), channel_id=1, source_target_pairs={{0,2},{1,3},{2,0},{3,1},{4,6},{5,7},{6,4},{7,5},{8,10},{9,11},{10,... | collective-permute-start | bytes 196616 | tf_op jit(solution)/shard_map/cond/branch_1_fun/ppermute | solution.py:418
  91.8 1.5 %collective-permute-done.2 = f32[4,16,256]{2,1,0:T(8,128)S(1)} collective-permute-done((f32[4,16,256]{2,1,0:T(8,128)S(1)}, f32[4,16,256]{2,1,0:T(8,128)S(1)}, u32[]{:S(2)}, u32[]{:S(2)}) %collective-permute-start.2) | collective-permute-done | bytes 65568 | tf_op jit(solution)/shard_map/cond/branch_1_fun/ppermute | solution.py:418
  93.3 2.4 %collective-permute-done.3 = f32[4,16,256]{2,1,0:T(8,128)S(1)} collective-permute-done((f32[4,16,256]{2,1,0:T(8,128)S(1)}, f32[4,16,256]{2,1,0:T(8,128)S(1)}, u32[]{:S(2)}, u32[]{:S(2)}) %collective-permute-start.3) | collective-permute-done | bytes 65568 | tf_op jit(solution)/shard_map/cond/branch_1_fun/ppermute | solution.py:418
  96.0 6.2 %collective-permute-start.5 = (f32[4,32]{1,0:T(4,128)S(1)}, f32[4,32]{1,0:T(4,128)S(1)}, u32[]{:S(2)}, u32[]{:S(2)}) collective-permute-start(f32[4,32]{1,0:T(4,128)S(1)} %select_reduce_fusion), channel_id=1, source_target_pairs={{0,16},{4,20},{8,24},{12,28},{16,0},{20,4},{24,8},{28,12},{1,17},{... | collective-permute-start | bytes 1544 | tf_op jit(solution)/shard_map/cond/branch_1_fun/ppermute | solution.py:418
  102.2 2.5 %collective-permute-start.6 = (f32[4,32]{1,0:T(4,128)S(1)}, f32[4,32]{1,0:T(4,128)S(1)}, u32[]{:S(2)}, u32[]{:S(2)}) collective-permute-start(f32[4,32]{1,0:T(4,128)S(1)} %select_reduce_fusion), channel_id=1, source_target_pairs={{0,24},{4,28},{8,16},{12,20},{16,8},{20,12},{24,0},{28,4},{1,25},{... | collective-permute-start | bytes 1544 | tf_op jit(solution)/shard_map/cond/branch_1_fun/ppermute | solution.py:418
  104.7 2.9 %collective-permute-done.6 = f32[4,32]{1,0:T(4,128)S(1)} collective-permute-done((f32[4,32]{1,0:T(4,128)S(1)}, f32[4,32]{1,0:T(4,128)S(1)}, u32[]{:S(2)}, u32[]{:S(2)}) %collective-permute-start.6) | collective-permute-done | bytes 544 | tf_op jit(solution)/shard_map/cond/branch_1_fun/ppermute | solution.py:418
  107.6 2.3 %collective-permute-done.4 = f32[36,256]{1,0:T(8,128)S(1)} collective-permute-done((f32[36,256]{1,0:T(8,128)S(1)}, f32[36,256]{1,0:T(8,128)S(1)}, u32[]{:S(2)}, u32[]{:S(2)}) %collective-permute-start.4) | collective-permute-done | bytes 36896 | tf_op jit(solution)/shard_map/cond/branch_1_fun/ppermute | solution.py:418
  110.2 1.6 %collective-permute-start.7 = (bf16[8,1,16,128]{3,2,1,0:T(8,128)(2,1)S(1)}, bf16[8,1,16,128]{3,2,1,0:T(8,128)(2,1)S(1)}, u32[]{:S(2)}, u32[]{:S(2)}) collective-permute-start(bf16[8,1,16,128]{3,2,1,0:T(8,128)(2,1)S(1)} %bitcast.68), channel_id=1, source_target_pairs={{0,1},{1,0},{2,3},{3,2},{4,5},{5,4},{6,7},{7,6},{8,9},{9,8},{10,11... | collective-permute-start | bytes 98312 | tf_op jit(solution)/shard_map/cond/branch_1_fun/ppermute | solution.py:418
  111.8 1.5 %collective-permute-start.8 = (bf16[8,1,16,128]{3,2,1,0:T(8,128)(2,1)S(1)}, bf16[8,1,16,128]{3,2,1,0:T(8,128)(2,1)S(1)}, u32[]{:S(2)}, u32[]{:S(2)}) collective-permute-start(bf16[8,1,16,128]{3,2,1,0:T(8,128)(2,1)S(1)} %bitcast.69), channel_id=1, source_target_pairs={{0,2},{1,3},{2,0},{3,1},{4,6},{5,7},{6,4},{7,5},{8,10},{9,11},{10,... | collective-permute-start | bytes 98312 | tf_op jit(solution)/shard_map/cond/branch_1_fun/ppermute | solution.py:418
  114.2 1.5 %collective-permute-done.8.refs_2_ = bf16[8,1,16,128]{3,2,1,0:T(8,128)(2,1)S(1)} collective-permute-done((bf16[8,1,16,128]{3,2,1,0:T(8,128)(2,1)S(1)}, bf16[8,1,16,128]{3,2,1,0:T(8,128)(2,1)S(1)}, u32[]{:S(2)}, u32[]{:S(2)}) %collective-permute-start.8) | collective-permute-done | bytes 32800 | tf_op jit(solution)/shard_map/cond/branch_1_fun/ppermute | solution.py:418
  115.7 2.4 %collective-permute-done.9.refs_3_ = bf16[8,1,16,128]{3,2,1,0:T(8,128)(2,1)S(1)} collective-permute-done((bf16[8,1,16,128]{3,2,1,0:T(8,128)(2,1)S(1)}, bf16[8,1,16,128]{3,2,1,0:T(8,128)(2,1)S(1)}, u32[]{:S(2)}, u32[]{:S(2)}) %collective-permute-start.9) | collective-permute-done | bytes 32800 | tf_op jit(solution)/shard_map/cond/branch_1_fun/ppermute | solution.py:418
  118.8 1.7 %collective-permute-done.10 = bf16[8,4,16,128]{3,2,1,0:T(8,128)(2,1)} collective-permute-done((bf16[8,4,16,128]{3,2,1,0:T(8,128)(2,1)}, bf16[8,4,16,128]{3,2,1,0:T(8,128)(2,1)}, u32[]{:S(2)}, u32[]{:S(2)}) %collective-permute-start.10) | collective-permute-done | bytes 131104 | tf_op jit(solution)/shard_map/cond/branch_1_fun/ppermute | solution.py:418
  120.4 3.3 %contract.1 = (f32[64,2000]{1,0:T(8,128)S(1)}, f32[64,2000]{1,0:T(8,128)S(1)}) custom-call(s32[1]{0:T(128)} %bitcast.10.which_ref.core_ref, bf16[8,4,16,128]{3,2,1,0:T(8,128)(2,1)} %get-tuple-element.409.kernel_ref, bf16[8,4,16,128]{3,2,1,0:T(8,128)(2,1)} %get-tuple-element.410.got_ref, bf16[2000,256]{1,0:T(8,128)(2,1)S(1)} %straighten.1.refs_1_.refs_0_, ...), custom_call_target="tpu_custom_call" | custom-call | flops 524288000 | bytes 5120000 | tf_op jit(solution)/shard_map/contract/pallas_call | solution.py:346
  124.0 1.7 %collective-permute-done.34.back_ref = f32[64,2000]{1,0:T(8,128)S(1)} collective-permute-done((f32[64,2000]{1,0:T(8,128)S(1)}, f32[64,2000]{1,0:T(8,128)S(1)}, u32[]{:S(2)}, u32[]{:S(2)}) %collective-permute-start.34) | collective-permute-done | bytes 512032 | tf_op jit(solution)/shard_map/ppermute | solution.py:418
  125.7 1.8 %finish.1 = f32[64,4000]{1,0:T(8,128)} custom-call(s32[2]{0:T(128)S(1)} %pad_add_fusion.2.flags_ref, f32[64,2000]{1,0:T(8,128)S(1)} %get-tuple-element.412.ours_ref, f32[64,2000]{1,0:T(8,128)S(1)} %collective-permute-done.34.back_ref, f32[64,4000]{1,0:T(8,128)} %get-tuple-element.414.other_ref), custom_call_target="tpu_custom_call", output_to_operand_aliasing={{}: (3, {})} | custom-call | tf_op jit(solution)/shard_map/finish/pallas_call | solution.py:387
  (123 shorter events, 14.0 us)
Async XLA Ops:
  0.0 3.3 %copy-start.10 = (f32[256]{0:T(256)S(1)}, f32[256]{0:T(256)}, u32[]{:S(2)}) copy-start(f32[256]{0:T(256)} %param.17) | copy-start | bytes 3076
  0.0 3.2 %copy-start.11 = (s32[8]{0:T(128)S(1)}, s32[8]{0:T(128)}, u32[]{:S(2)}) copy-start(s32[8]{0:T(128)} %param.18) | copy-start | bytes 100
  0.0 3.3 %collective-permute-start.17 = (f32[1,256]{1,0:T(1,128)}, f32[1,256]{1,0:T(1,128)S(1)}, u32[]{:S(2)}, u32[]{:S(2)}) collective-permute-start(f32[1,256]{1,0:T(1,128)} %bitcast.85), channel_id=1, source_target_pairs={{0,4},{4,0},{8,12},{12,8},{16,20},{20,16},{24,28},{28,24},{1,5},{5... | collective-permute-start | bytes 3080 | tf_op jit(solution)/shard_map/ppermute | solution.py:418
  0.5 2.7 %collective-permute-start.16 = (s32[1,8]{1,0:T(1,128)}, s32[1,8]{1,0:T(1,128)S(1)}, u32[]{:S(2)}, u32[]{:S(2)}) collective-permute-start(s32[1,8]{1,0:T(1,128)} %bitcast.87), channel_id=1, source_target_pairs={{0,4},{4,0},{8,12},{12,8},{16,20},{20,16},{24,28},{28,24},{1,5},{5... | collective-permute-start | bytes 104 | tf_op jit(solution)/shard_map/ppermute | solution.py:418
  1.4 6.7 %collective-permute-start.15 = (s32[16,8]{0,1:T(8,128)S(1)}, s32[16,8]{0,1:T(8,128)S(1)}, u32[]{:S(2)}, u32[]{:S(2)}) collective-permute-start(s32[16,8]{0,1:T(8,128)S(1)} %get-tuple-element.483), channel_id=1, source_target_pairs={{0,4},{4,0},{8,12},{12,8},{16,20},{20,16},{24,28},{28,24},{1,5},{5... | collective-permute-start | bytes 1544 | tf_op jit(solution)/shard_map/ppermute | solution.py:418
  3.0 6.4 %collective-permute-start.14 = (bf16[2000,256]{1,0:T(8,128)(2,1)S(1)}, bf16[2000,256]{1,0:T(8,128)(2,1)S(1)}, u32[]{:S(2)}, u32[]{:S(2)}) collective-permute-start(bf16[2000,256]{1,0:T(8,128)(2,1)S(1)} %half_of.3), channel_id=1, source_target_pairs={{0,4},{4,0},{8,12},{12,8},{16,20},{20,16},{24,28},{28,24},{1,5},{5... | collective-permute-start | bytes 3072008 | tf_op jit(solution)/shard_map/ppermute | solution.py:418
  3.4 4.9 %collective-permute-start.18 = (f32[1,528]{1,0:T(1,128)S(1)}, f32[1,528]{1,0:T(1,128)S(1)}, u32[]{:S(2)}, u32[]{:S(2)}) collective-permute-start(f32[1,528]{1,0:T(1,128)S(1)} %pad_maximum_fusion.3), channel_id=1, source_target_pairs={{0,8},{4,12},{8,0},{12,4},{16,24},{20,28},{24,16},{28,20},{1,9},{5... | collective-permute-start | bytes 6344 | tf_op jit(solution)/shard_map/ppermute | solution.py:418
  9.4 1.0 copy-start.3
  10.4 1.2 copy-start.4
  13.4 16.4 %collective-permute-start.19 = (bf16[2000,128]{1,0:T(8,128)(2,1)S(1)}, bf16[2000,128]{1,0:T(8,128)(2,1)S(1)}, u32[]{:S(2)}, u32[]{:S(2)}) collective-permute-start(bf16[2000,128]{1,0:T(8,128)(2,1)S(1)} %get-tuple-element.388), channel_id=1, source_target_pairs={{8,16},{12,20},{16,8},{20,12},{9,17},{13,21},{17,9},{21,13},{10,18... | collective-permute-start | bytes 1536008 | tf_op jit(solution)/shard_map/ppermute | solution.py:491
  14.1 15.9 %collective-permute-start.20 = (bf16[2000,128]{1,0:T(8,128)(2,1)S(1)}, bf16[2000,128]{1,0:T(8,128)(2,1)S(1)}, u32[]{:S(2)}, u32[]{:S(2)}) collective-permute-start(bf16[2000,128]{1,0:T(8,128)(2,1)S(1)} %get-tuple-element.389), channel_id=1, source_target_pairs={{0,8},{4,12},{8,0},{12,4},{16,24},{20,28},{24,16},{28,20},{1,9},{5... | collective-permute-start | bytes 1536008 | tf_op jit(solution)/shard_map/ppermute | solution.py:491
  18.6 11.1 %collective-permute-start.21 = (f32[2,528]{1,0:T(2,128)S(1)}, f32[2,528]{1,0:T(2,128)S(1)}, u32[]{:S(2)}, u32[]{:S(2)}) collective-permute-start(f32[2,528]{1,0:T(2,128)S(1)} %maximum_select_fusion.1), channel_id=1, source_target_pairs={{0,16},{4,20},{8,24},{12,28},{16,0},{20,4},{24,8},{28,12},{1,17},{... | collective-permute-start | bytes 12680 | tf_op jit(solution)/shard_map/ppermute | solution.py:418
  30.3 24.8 %collective-permute-start.22 = (bf16[2000,256]{1,0:T(8,128)(2,1)S(1)}, bf16[2000,256]{1,0:T(8,128)(2,1)S(1)}, u32[]{:S(2)}, u32[]{:S(2)}) collective-permute-start(bf16[2000,256]{1,0:T(8,128)(2,1)S(1)} %straighten.1.refs_1_.refs_0_), channel_id=1, source_target_pairs={{0,8},{4,12},{8,0},{12,4},{16,24},{20,28},{24,16},{28,20},{1,9},{5... | collective-permute-start | bytes 3072008 | tf_op jit(solution)/shard_map/ppermute | solution.py:491
  32.1 24.8 %collective-permute-start.24 = (bf16[2000,256]{1,0:T(8,128)(2,1)S(1)}, bf16[2000,256]{1,0:T(8,128)(2,1)S(1)}, u32[]{:S(2)}, u32[]{:S(2)}) collective-permute-start(bf16[2000,256]{1,0:T(8,128)(2,1)S(1)} %straighten.1.refs_1_.refs_0_), channel_id=1, source_target_pairs={{8,16},{12,20},{16,8},{20,12},{9,17},{13,21},{17,9},{21,13},{10,18... | collective-permute-start | bytes 3072008 | tf_op jit(solution)/shard_map/ppermute | solution.py:491
  35.6 0.8 copy-start
  36.5 2.3 %collective-permute-start.26 = (bf16[128,2048]{1,0:T(8,128)(2,1)}, bf16[128,2048]{1,0:T(8,128)(2,1)}, u32[]{:S(2)}, u32[]{:S(2)}) collective-permute-start(bf16[128,2048]{1,0:T(8,128)(2,1)} %get-tuple-element.394), channel_id=1, source_target_pairs={{0,4},{4,0},{8,12},{12,8},{16,20},{20,16},{24,28},{28,24},{1,5},{5... | collective-permute-start | bytes 1572872 | tf_op jit(solution)/shard_map/ppermute | solution.py:418
  38.7 1.0 copy-start.1
  41.9 39.3 %collective-permute-start.32 = (bf16[256,2048]{1,0:T(8,128)(2,1)}, bf16[256,2048]{1,0:T(8,128)(2,1)}, u32[]{:S(2)}, u32[]{:S(2)}) collective-permute-start(bf16[256,2048]{1,0:T(8,128)(2,1)} %stack_panels.1.refs_0_), channel_id=1, source_target_pairs={{0,8},{4,12},{24,16},{28,20},{1,9},{5,13},{25,17},{29,21},{2,10},{... | collective-permute-start | bytes 3145736 | tf_op jit(solution)/shard_map/ppermute | solution.py:491
  55.2 26.0 %collective-permute-start.23 = (bf16[2000,256]{1,0:T(8,128)(2,1)S(1)}, bf16[2000,256]{1,0:T(8,128)(2,1)}, u32[]{:S(2)}, u32[]{:S(2)}) collective-permute-start(bf16[2000,256]{1,0:T(8,128)(2,1)S(1)} %collective-permute-done.22.refs_1_), channel_id=1, source_target_pairs={{8,16},{12,20},{16,8},{20,12},{9,17},{13,21},{17,9},{21,13},{10,18... | collective-permute-start | bytes 3072008 | tf_op jit(solution)/shard_map/ppermute | solution.py:491
  56.9 24.3 %collective-permute-start.25 = (bf16[2000,256]{1,0:T(8,128)(2,1)S(1)}, bf16[2000,256]{1,0:T(8,128)(2,1)}, u32[]{:S(2)}, u32[]{:S(2)}) collective-permute-start(bf16[2000,256]{1,0:T(8,128)(2,1)S(1)} %collective-permute-done.24.refs_2_), channel_id=1, source_target_pairs={{8,0},{12,4},{16,24},{20,28},{9,1},{13,5},{17,25},{21,29},{10,2},{... | collective-permute-start | bytes 3072008 | tf_op jit(solution)/shard_map/ppermute | solution.py:491
  61.1 21.5 %copy-start.9 = (s32[8,32]{1,0:T(8,128)S(1)}, s32[8,32]{1,0:T(8,128)}, u32[]{:S(2)}) copy-start(s32[8,32]{1,0:T(8,128)} %param.19) | copy-start | bytes 3076
  61.1 4.7 %collective-permute-start.28 = (f32[4,4,16,256]{3,2,1,0:T(8,128)}, f32[4,4,16,256]{3,2,1,0:T(8,128)}, u32[]{:S(2)}, u32[]{:S(2)}) collective-permute-start(f32[4,4,16,256]{3,2,1,0:T(8,128)} %get-tuple-element.398), channel_id=1, source_target_pairs={{0,4},{4,0},{8,12},{12,8},{16,20},{20,16},{24,28},{28,24},{1,5},{5... | collective-permute-start | bytes 786440 | tf_op jit(solution)/shard_map/ppermute | solution.py:418
  63.8 2.0 %collective-permute-start.27 = (f32[2,4,16,256]{3,2,1,0:T(8,128)}, f32[2,4,16,256]{3,2,1,0:T(8,128)}, u32[]{:S(2)}, u32[]{:S(2)}) collective-permute-start(f32[2,4,16,256]{3,2,1,0:T(8,128)} %get-tuple-element.396), channel_id=1, source_target_pairs={{0,4},{4,0},{8,12},{12,8},{16,20},{20,16},{24,28},{28,24},{1,5},{5... | collective-permute-start | bytes 393224 | tf_op jit(solution)/shard_map/ppermute | solution.py:418
  67.6 0.6 copy-start.2
  68.2 0.6 copy-start.5
  68.8 0.6 copy-start.6
  69.4 5.1 %collective-permute-start.29 = (f32[6,16,256]{2,1,0:T(8,128)}, f32[6,16,256]{2,1,0:T(8,128)S(1)}, u32[]{:S(2)}, u32[]{:S(2)}) collective-permute-start(f32[6,16,256]{2,1,0:T(8,128)} %get-tuple-element.400), channel_id=1, source_target_pairs={{0,1},{1,0},{2,3},{3,2},{4,5},{5,4},{6,7},{7,6},{8,9},{9,8},{10,11... | collective-permute-start | bytes 294920 | tf_op jit(solution)/shard_map/ppermute | solution.py:418
  72.2 4.9 %collective-permute-start.30 = (f32[6,16,256]{2,1,0:T(8,128)}, f32[6,16,256]{2,1,0:T(8,128)S(1)}, u32[]{:S(2)}, u32[]{:S(2)}) collective-permute-start(f32[6,16,256]{2,1,0:T(8,128)} %copy-done.6), channel_id=1, source_target_pairs={{0,2},{1,3},{2,0},{3,1},{4,6},{5,7},{6,4},{7,5},{8,10},{9,11},{10,... | collective-permute-start | bytes 294920 | tf_op jit(solution)/shard_map/ppermute | solution.py:418
  74.5 5.7 %collective-permute-start.31 = (f32[6,16,256]{2,1,0:T(8,128)}, f32[6,16,256]{2,1,0:T(8,128)S(1)}, u32[]{:S(2)}, u32[]{:S(2)}) collective-permute-start(f32[6,16,256]{2,1,0:T(8,128)} %copy-done.5), channel_id=1, source_target_pairs={{0,3},{1,2},{2,1},{3,0},{4,7},{5,6},{6,5},{7,4},{8,11},{9,10},{10,... | collective-permute-start | bytes 294920 | tf_op jit(solution)/shard_map/ppermute | solution.py:418
  81.2 39.2 %collective-permute-start.33 = (bf16[2000,256]{1,0:T(8,128)(2,1)}, bf16[2000,256]{1,0:T(8,128)(2,1)}, u32[]{:S(2)}, u32[]{:S(2)}) collective-permute-start(bf16[2000,256]{1,0:T(8,128)(2,1)} %collective-permute-done.23.refs_5_), channel_id=1, source_target_pairs={{8,0},{12,4},{16,24},{20,28},{9,1},{13,5},{17,25},{21,29},{10,2},{... | collective-permute-start | bytes 3072008 | tf_op jit(solution)/shard_map/ppermute | solution.py:491
  85.9 1.6 %collective-permute-start = (f32[4,4,16,256]{3,2,1,0:T(8,128)S(1)}, f32[4,4,16,256]{3,2,1,0:T(8,128)S(1)}, u32[]{:S(2)}, u32[]{:S(2)}) collective-permute-start(f32[4,4,16,256]{3,2,1,0:T(8,128)S(1)} %get-tuple-element.352), channel_id=1, source_target_pairs={{0,4},{4,0},{8,12},{12,8},{16,20},{20,16},{24,28},{28,24},{1,5},{5... | collective-permute-start | bytes 786440 | tf_op jit(solution)/shard_map/cond/branch_1_fun/ppermute | solution.py:418
  87.5 4.3 %collective-permute-start.1 = (f32[4,16,256]{2,1,0:T(8,128)S(1)}, f32[4,16,256]{2,1,0:T(8,128)S(1)}, u32[]{:S(2)}, u32[]{:S(2)}) collective-permute-start(f32[4,16,256]{2,1,0:T(8,128)S(1)} %get-tuple-element.354), channel_id=1, source_target_pairs={{0,1},{1,0},{2,3},{3,2},{4,5},{5,4},{6,7},{7,6},{8,9},{9,8},{10,11... | collective-permute-start | bytes 196616 | tf_op jit(solution)/shard_map/cond/branch_1_fun/ppermute | solution.py:418
  89.1 4.3 %collective-permute-start.2 = (f32[4,16,256]{2,1,0:T(8,128)S(1)}, f32[4,16,256]{2,1,0:T(8,128)S(1)}, u32[]{:S(2)}, u32[]{:S(2)}) collective-permute-start(f32[4,16,256]{2,1,0:T(8,128)S(1)} %get-tuple-element.355), channel_id=1, source_target_pairs={{0,2},{1,3},{2,0},{3,1},{4,6},{5,7},{6,4},{7,5},{8,10},{9,11},{10,... | collective-permute-start | bytes 196616 | tf_op jit(solution)/shard_map/cond/branch_1_fun/ppermute | solution.py:418
  90.6 5.2 %collective-permute-start.3 = (f32[4,16,256]{2,1,0:T(8,128)S(1)}, f32[4,16,256]{2,1,0:T(8,128)S(1)}, u32[]{:S(2)}, u32[]{:S(2)}) collective-permute-start(f32[4,16,256]{2,1,0:T(8,128)S(1)} %get-tuple-element.356), channel_id=1, source_target_pairs={{0,3},{1,2},{2,1},{3,0},{4,7},{5,6},{6,5},{7,4},{8,11},{9,10},{10,... | collective-permute-start | bytes 196616 | tf_op jit(solution)/shard_map/cond/branch_1_fun/ppermute | solution.py:418
  96.0 8.8 %collective-permute-start.5 = (f32[4,32]{1,0:T(4,128)S(1)}, f32[4,32]{1,0:T(4,128)S(1)}, u32[]{:S(2)}, u32[]{:S(2)}) collective-permute-start(f32[4,32]{1,0:T(4,128)S(1)} %select_reduce_fusion), channel_id=1, source_target_pairs={{0,16},{4,20},{8,24},{12,28},{16,0},{20,4},{24,8},{28,12},{1,17},{... | collective-permute-start | bytes 1544 | tf_op jit(solution)/shard_map/cond/branch_1_fun/ppermute | solution.py:418
  102.2 5.5 %collective-permute-start.6 = (f32[4,32]{1,0:T(4,128)S(1)}, f32[4,32]{1,0:T(4,128)S(1)}, u32[]{:S(2)}, u32[]{:S(2)}) collective-permute-start(f32[4,32]{1,0:T(4,128)S(1)} %select_reduce_fusion), channel_id=1, source_target_pairs={{0,24},{4,28},{8,16},{12,20},{16,8},{20,12},{24,0},{28,4},{1,25},{... | collective-permute-start | bytes 1544 | tf_op jit(solution)/shard_map/cond/branch_1_fun/ppermute | solution.py:418
  104.6 5.3 %collective-permute-start.4 = (f32[36,256]{1,0:T(8,128)S(1)}, f32[36,256]{1,0:T(8,128)S(1)}, u32[]{:S(2)}, u32[]{:S(2)}) collective-permute-start(f32[36,256]{1,0:T(8,128)S(1)} %select_maximum_fusion), channel_id=1, source_target_pairs={{0,8},{4,12},{8,0},{12,4},{16,24},{20,28},{24,16},{28,20},{1,9},{5... | collective-permute-start | bytes 110600 | tf_op jit(solution)/shard_map/cond/branch_1_fun/ppermute | solution.py:418
  110.2 4.0 %collective-permute-start.7 = (bf16[8,1,16,128]{3,2,1,0:T(8,128)(2,1)S(1)}, bf16[8,1,16,128]{3,2,1,0:T(8,128)(2,1)S(1)}, u32[]{:S(2)}, u32[]{:S(2)}) collective-permute-start(bf16[8,1,16,128]{3,2,1,0:T(8,128)(2,1)S(1)} %bitcast.68), channel_id=1, source_target_pairs={{0,1},{1,0},{2,3},{3,2},{4,5},{5,4},{6,7},{7,6},{8,9},{9,8},{10,11... | collective-permute-start | bytes 98312 | tf_op jit(solution)/shard_map/cond/branch_1_fun/ppermute | solution.py:418
  111.8 3.9 %collective-permute-start.8 = (bf16[8,1,16,128]{3,2,1,0:T(8,128)(2,1)S(1)}, bf16[8,1,16,128]{3,2,1,0:T(8,128)(2,1)S(1)}, u32[]{:S(2)}, u32[]{:S(2)}) collective-permute-start(bf16[8,1,16,128]{3,2,1,0:T(8,128)(2,1)S(1)} %bitcast.69), channel_id=1, source_target_pairs={{0,2},{1,3},{2,0},{3,1},{4,6},{5,7},{6,4},{7,5},{8,10},{9,11},{10,... | collective-permute-start | bytes 98312 | tf_op jit(solution)/shard_map/cond/branch_1_fun/ppermute | solution.py:418
  113.3 4.8 %collective-permute-start.9 = (bf16[8,1,16,128]{3,2,1,0:T(8,128)(2,1)S(1)}, bf16[8,1,16,128]{3,2,1,0:T(8,128)(2,1)S(1)}, u32[]{:S(2)}, u32[]{:S(2)}) collective-permute-start(bf16[8,1,16,128]{3,2,1,0:T(8,128)(2,1)S(1)} %bitcast.70), channel_id=1, source_target_pairs={{0,3},{1,2},{2,1},{3,0},{4,7},{5,6},{6,5},{7,4},{8,11},{9,10},{10,... | collective-permute-start | bytes 98312 | tf_op jit(solution)/shard_map/cond/branch_1_fun/ppermute | solution.py:418
  118.8 1.7 %collective-permute-start.10 = (bf16[8,4,16,128]{3,2,1,0:T(8,128)(2,1)}, bf16[8,4,16,128]{3,2,1,0:T(8,128)(2,1)}, u32[]{:S(2)}, u32[]{:S(2)}) collective-permute-start(bf16[8,4,16,128]{3,2,1,0:T(8,128)(2,1)} %in_order.1), channel_id=1, source_target_pairs={{0,4},{4,0},{8,12},{12,8},{16,20},{20,16},{24,28},{28,24},{1,5},{5... | collective-permute-start | bytes 393224 | tf_op jit(solution)/shard_map/cond/branch_1_fun/ppermute | solution.py:418
  123.8 2.0 %collective-permute-start.34 = (f32[64,2000]{1,0:T(8,128)S(1)}, f32[64,2000]{1,0:T(8,128)S(1)}, u32[]{:S(2)}, u32[]{:S(2)}) collective-permute-start(f32[64,2000]{1,0:T(8,128)S(1)} %get-tuple-element.413), channel_id=1, source_target_pairs={{0,4},{4,0},{8,12},{12,8},{16,20},{20,16},{24,28},{28,24},{1,5},{5... | collective-permute-start | bytes 1536008 | tf_op jit(solution)/shard_map/ppermute | solution.py:418

commit v7 on v6

--- a/solution.py
+++ b/solution.py
@@ -487,6 +487,24 @@
         odd,
     )
 
+    compacted, told = lax.optimization_barrier((compacted, told))
+    sizes = told[:, : 2 * batches].astype(jnp.int32).reshape(-1)
+    weights = told[:, 2 * batches :].reshape(-1)
+    to, start = places_of(sizes, 0)
+    first = start.reshape(chips, -1)[:, 0]
+    nominal = rows * lax.iota(jnp.int32, chips)
+    fits = jnp.all(jnp.abs(first - nominal) <= margin) & (jnp.sum(sizes) == live)
+
+    per_window = rows // tile
+    window_iota = lax.iota(jnp.int32, chips)
+    at = (
+        (window_iota * rows)[:, None, None]
+        + (lax.iota(jnp.int32, per_window) * tile)[None, :, None]
+        + member * piece
+        + lax.iota(jnp.int32, piece)[None, None, :]
+    ).reshape(-1, 1)
+    weight = jnp.sum(jnp.where(to.reshape(1, -1) == at, weights[None, :], 0.0), axis=1)
+    weight = weight.reshape(chips, per_window * piece)
     def sent(x, pairs):
         return lax.ppermute(x, "grid", along(pairs))
 
@@ -507,13 +525,7 @@
         for (_, *tiles, _), (by_b, by_a) in zip(compacted, arrived)
     )
 
-    own, told = lax.optimization_barrier((own, told))
-    sizes = told[:, : 2 * batches].astype(jnp.int32).reshape(-1)
-    weights = told[:, 2 * batches :].reshape(-1)
-    to, start = places_of(sizes, 0)
-    first = start.reshape(chips, -1)[:, 0]
-    nominal = rows * lax.iota(jnp.int32, chips)
-    fits = jnp.all(jnp.abs(first - nominal) <= margin) & (jnp.sum(sizes) == live)
+    own, fits, weight = lax.optimization_barrier((own, fits.astype(jnp.int32), weight))
 
     _, occupied_turned, trial_turned = lax.optimization_barrier(
         (compacted[0][0], occupied.T, trial.T)
@@ -521,8 +533,6 @@
     mine_panel, other_panel = panel_halves(occupied_turned, trial_turned, core)
     panels = stack_panels(mine_panel, flip(other_panel, "grid", 1), core)
 
-    per_window = rows // tile
-    window_iota = lax.iota(jnp.int32, chips)
     ends = [(0, 1), (last, last - 1)]
     homes = [(b, a) for a, b in ends]
     side = 1 - 2 * odd
@@ -575,29 +585,19 @@
     early_jobs = stages[0] + early_jobs
     early_at = jnp.concatenate((chip[None], early_at))
 
-    def halved(jobs):
-        keep, give = project(jobs, tile, shares, core)
-        return keep, flip(give, "grid", 1)
-
+    own_pair = project([(panels, early_jobs[0][0])], tile, shares, core)
+    early_pair = project([(panels, w) for w, _ in early_jobs[1:]], tile, shares, core)
     early_value = summed(
-        [halved([(panels, early_jobs[0][0])]), halved([(panels, w) for w, _ in early_jobs[1:]])]
-    )
-
-    at = (
-        (window_iota * rows)[:, None, None]
-        + (lax.iota(jnp.int32, per_window) * tile)[None, :, None]
-        + member * piece
-        + lax.iota(jnp.int32, piece)[None, None, :]
-    ).reshape(-1, 1)
-    weight = jnp.sum(jnp.where(to.reshape(1, -1) == at, weights[None, :], 0.0), axis=1)
-    weight = weight.reshape(chips, per_window * piece)
+        [(keep, flip(give, "grid", 1)) for keep, give in (own_pair, early_pair)]
+    )
+
     outer = jnp.where(chip == 0, last, jnp.where(chip == last, 0, early_at[2]))
     places = jnp.concatenate((early_at[:2], outer[None], early_at[3:], late_at))
     here = (places[:, None] == window_iota[None, :])[:, :, None]
     weight_here = jnp.sum(jnp.where(here, weight[None], 0.0), axis=1)[:, :, None]
 
     late, by_a, early_value, far_panels, weight_here, fits = lax.optimization_barrier(
-        (by_b, by_a, early_value, far_panels, weight_here, fits.astype(jnp.int32))
+        (by_b, by_a, early_value, far_panels, weight_here, fits)
     )
     fits = fits != 0
     late = tuple(sent(x, homes) for x in late)

time: 128 us -> 126 us (0.984)
  waiting for transfers between devices: 43.5 us -> 49.8 us
  local copies, waits for them, and re-layouts: 8.06 us -> 4.32 us
  Pallas kernels: 25.1 us -> 21.4 us
    ppermute x8, waiting for transfers between devices: 7.61 us -> 21.5 us  [sent(): return lax.ppermute(x, 'grid', along(pairs))]
    ppermute x24, waiting for transfers between devices: 35.9 us -> 28.3 us  [flip(): return lax.ppermute(x, axis, [(i, i ^ bit) for i in range(count)])]
    unnamed x23 -> x17, local copies, waits for them, and re-layouts: 6.01 us -> 2.27 us
    pallas_call x1, Pallas kernels: 2.52 us -> 0.52 us  [panel_halves(): pl.pallas_call(body, out_shape=(shape, shape), in_specs=[SCALARS, WHOLE,...]
  transfers between devices with their start and end apart: 32 -> 32, of which waited for: 17 -> 20; matrix products, arithmetic and copies ran while one was open for 6% -> 5% of each run, Pallas kernels for 14% -> 11%
where the time goes in v7:
time: 126 us; the launch traced here: 125 us
  waiting for transfers between devices  49.8 us (40%)
  starting transfers between devices  43.8 us (35%)
  Pallas kernels  21.4 us (17%)
  local copies, waits for them, and re-layouts  4.32 us (3%)
  other arithmetic  4.14 us (3%)
  between operations  1.78 us (1%)
    ppermute x24, waiting for transfers between devices, flip(): return lax.ppermute(x, axis, [(i, i ^ bit) for i in range(count)])  28.3 us
    ppermute x24, starting transfers between devices, flip(): return lax.ppermute(x, axis, [(i, i ^ bit) for i in range(count)])  27.2 us
    ppermute x8, waiting for transfers between devices, sent(): return lax.ppermute(x, 'grid', along(pairs))  21.5 us
    ppermute x8, starting transfers between devices, sent(): return lax.ppermute(x, 'grid', along(pairs))  16.6 us
    pallas_call x3, Pallas kernels, project(): pl.pallas_call(body, out_shape=(shape, shape), in_specs=[SCALARS] + [WHOL...  8.32 us
    pallas_call x1, Pallas kernels, contract(): pl.pallas_call(body, out_shape=(shape, shape), in_specs=[SCALARS] + [WHOL...  3.3 us
  transfers between devices with their start and end apart: 32, of which 20 were waited for; matrix products, arithmetic and copies ran while one was open for 5% of the time, Pallas kernels for 11%

profile of v7, /device:TPU:0, one launch (start us, length us, event | category | flops | bytes accessed | tf_op | source)
XLA Modules:
  0.0 125.5 jit_solution(17719734095948317261)
XLA Ops:
  0.5 0.8 dynamic-slice_bitcast_fusion
  1.8 1.2 half_of.3
  3.5 3.0 %collective-permute-start.18 = (f32[1,528]{1,0:T(1,128)S(1)}, f32[1,528]{1,0:T(1,128)S(1)}, u32[]{:S(2)}, u32[]{:S(2)}) collective-permute-start(f32[1,528]{1,0:T(1,128)S(1)} %pad_maximum_fusion.3), channel_id=1, source_target_pairs={{0,8},{4,12},{8,0},{12,4},{16,24},{20,28},{24,16},{28,20},{1,9},{5... | collective-permute-start | bytes 6344 | tf_op jit(solution)/shard_map/ppermute | solution.py:418
  6.9 1.2 half_of.2.mine_ref
  8.8 2.6 %collective-permute-start.19 = (f32[2,528]{1,0:T(2,128)S(1)}, f32[2,528]{1,0:T(2,128)S(1)}, u32[]{:S(2)}, u32[]{:S(2)}) collective-permute-start(f32[2,528]{1,0:T(2,128)S(1)} %maximum_select_fusion.1), channel_id=1, source_target_pairs={{0,16},{4,20},{8,24},{12,28},{16,0},{20,4},{24,8},{28,12},{1,17},{... | collective-permute-start | bytes 12680 | tf_op jit(solution)/shard_map/ppermute | solution.py:418
  12.2 1.1 collective-permute-done.19
  13.3 0.9 copy-done
  14.3 1.2 copy-done.1
  15.5 1.8 %compact.1 = (bf16[2000,128]{1,0:T(8,128)(2,1)S(1)}, bf16[2000,128]{1,0:T(8,128)(2,1)S(1)}, bf16[2000,128]{1,0:T(8,128)(2,1)S(1)}, bf16[2000,128]{1,0:T(8,128)(2,1)S(1)}) custom-call(s32[1]{0:T(128)} %bitcast.11.odd_ref, bf16[2000,256]{1,0:T(8,128)(2,1)S(1)} %half_of.2.mine_ref, bf16[2000,256]{1,0:T(8,128)(2,1)S(1)} %copy-done.1, ...), custom_call_target="tpu_custom_call" | custom-call | flops 1048576000 | bytes 4096000 | tf_op jit(solution)/shard_map/compact/pallas_call | solution.py:124
  18.3 4.5 %collective-permute-start.21 = (bf16[2000,128]{1,0:T(8,128)(2,1)S(1)}, bf16[2000,128]{1,0:T(8,128)(2,1)S(1)}, u32[]{:S(2)}, u32[]{:S(2)}) collective-permute-start(bf16[2000,128]{1,0:T(8,128)(2,1)S(1)} %get-tuple-element.399), channel_id=1, source_target_pairs={{0,8},{4,12},{8,0},{12,4},{16,24},{20,28},{24,16},{28,20},{1,9},{5... | collective-permute-start | bytes 1536008 | tf_op jit(solution)/shard_map/ppermute | solution.py:509
  26.1 6.8 %collective-permute-done.21.refs_3_ = bf16[2000,128]{1,0:T(8,128)(2,1)S(1)} collective-permute-done((bf16[2000,128]{1,0:T(8,128)(2,1)S(1)}, bf16[2000,128]{1,0:T(8,128)(2,1)S(1)}, u32[]{:S(2)}, u32[]{:S(2)}) %collective-permute-start.21) | collective-permute-done | bytes 512032 | tf_op jit(solution)/shard_map/ppermute | solution.py:509
  33.3 1.8 %collective-permute-start.22 = (bf16[2000,256]{1,0:T(8,128)(2,1)S(1)}, bf16[2000,256]{1,0:T(8,128)(2,1)S(1)}, u32[]{:S(2)}, u32[]{:S(2)}) collective-permute-start(bf16[2000,256]{1,0:T(8,128)(2,1)S(1)} %straighten.1.refs_1_.refs_0_), channel_id=1, source_target_pairs={{0,8},{4,12},{8,0},{12,4},{16,24},{20,28},{24,16},{28,20},{1,9},{5... | collective-permute-start | bytes 3072008 | tf_op jit(solution)/shard_map/ppermute | solution.py:509
  35.1 0.7 collective-permute-start.24
  36.4 1.9 %collective-permute-done.26.got_ref = bf16[128,2048]{1,0:T(8,128)(2,1)S(1)} collective-permute-done((bf16[128,2048]{1,0:T(8,128)(2,1)S(1)}, bf16[128,2048]{1,0:T(8,128)(2,1)S(1)}, u32[]{:S(2)}, u32[]{:S(2)}) %collective-permute-start.26) | collective-permute-done | bytes 524320 | tf_op jit(solution)/shard_map/ppermute | solution.py:418
  38.3 1.1 stack_panels.1.refs_0_
  39.4 4.6 %collective-permute-start.32 = (bf16[256,2048]{1,0:T(8,128)(2,1)}, bf16[256,2048]{1,0:T(8,128)(2,1)}, u32[]{:S(2)}, u32[]{:S(2)}) collective-permute-start(bf16[256,2048]{1,0:T(8,128)(2,1)} %stack_panels.1.refs_0_), channel_id=1, source_target_pairs={{0,8},{4,12},{24,16},{28,20},{1,9},{5,13},{25,17},{29,21},{2,10},{... | collective-permute-start | bytes 3145736 | tf_op jit(solution)/shard_map/ppermute | solution.py:509
  44.1 14.1 %collective-permute-done.22.refs_1_ = bf16[2000,256]{1,0:T(8,128)(2,1)S(1)} collective-permute-done((bf16[2000,256]{1,0:T(8,128)(2,1)S(1)}, bf16[2000,256]{1,0:T(8,128)(2,1)S(1)}, u32[]{:S(2)}, u32[]{:S(2)}) %collective-permute-start.22) | collective-permute-done | bytes 1024032 | tf_op jit(solution)/shard_map/ppermute | solution.py:509
  58.2 1.7 %collective-permute-start.23 = (bf16[2000,256]{1,0:T(8,128)(2,1)S(1)}, bf16[2000,256]{1,0:T(8,128)(2,1)}, u32[]{:S(2)}, u32[]{:S(2)}) collective-permute-start(bf16[2000,256]{1,0:T(8,128)(2,1)S(1)} %collective-permute-done.22.refs_1_), channel_id=1, source_target_pairs={{8,16},{12,20},{16,8},{20,12},{9,17},{13,21},{17,9},{21,13},{10,18... | collective-permute-start | bytes 3072008 | tf_op jit(solution)/shard_map/ppermute | solution.py:509
  59.9 1.3 %collective-permute-start.25 = (bf16[2000,256]{1,0:T(8,128)(2,1)S(1)}, bf16[2000,256]{1,0:T(8,128)(2,1)}, u32[]{:S(2)}, u32[]{:S(2)}) collective-permute-start(bf16[2000,256]{1,0:T(8,128)(2,1)S(1)} %collective-permute-done.24.refs_2_), channel_id=1, source_target_pairs={{8,0},{12,4},{16,24},{20,28},{9,1},{13,5},{17,25},{21,29},{10,2},{... | collective-permute-start | bytes 3072008 | tf_op jit(solution)/shard_map/ppermute | solution.py:509
  61.2 2.9 %project.5 = (f32[4,4,16,256]{3,2,1,0:T(8,128)S(1)}, f32[4,4,16,256]{3,2,1,0:T(8,128)}) custom-call(s32[1]{0:T(128)} %bitcast.10.which_ref.core_ref, bf16[256,2048]{1,0:T(8,128)(2,1)} %stack_panels.1.refs_0_, bf16[2000,256]{1,0:T(8,128)(2,1)S(1)} %collective-permute-done.22.refs_1_, bf16[2000,256]{1,0:T(8,128)(2,1)S(1)} %collective-permute-done.24.refs_2_), custom_call_target="tpu_custom_call" | custom-call | flops 524288000 | bytes 3596288 | tf_op jit(solution)/shard_map/project/pallas_call | solution.py:281
  64.1 2.4 %project.4 = (f32[2,4,16,256]{3,2,1,0:T(8,128)S(1)}, f32[2,4,16,256]{3,2,1,0:T(8,128)}) custom-call(s32[1]{0:T(128)} %bitcast.10.which_ref.core_ref, bf16[256,2048]{1,0:T(8,128)(2,1)} %stack_panels.1.refs_0_, bf16[2000,256]{1,0:T(8,128)(2,1)S(1)} %straighten.1.refs_1_.refs_0_), custom_call_target="tpu_custom_call" | custom-call | flops 262144000 | bytes 2310144 | tf_op jit(solution)/shard_map/project/pallas_call | solution.py:281
  67.1 1.3 collective-permute-done.27.refs_1_
  68.3 1.1 split_sum.3
  69.4 1.6 %collective-permute-start.29 = (f32[6,16,256]{2,1,0:T(8,128)S(1)}, f32[6,16,256]{2,1,0:T(8,128)S(1)}, u32[]{:S(2)}, u32[]{:S(2)}) collective-permute-start(f32[6,16,256]{2,1,0:T(8,128)S(1)} %get-tuple-element.411), channel_id=1, source_target_pairs={{0,1},{1,0},{2,3},{3,2},{4,5},{5,4},{6,7},{7,6},{8,9},{9,8},{10,11... | collective-permute-start | bytes 294920 | tf_op jit(solution)/shard_map/ppermute | solution.py:418
  71.0 1.5 %collective-permute-start.30 = (f32[6,16,256]{2,1,0:T(8,128)S(1)}, f32[6,16,256]{2,1,0:T(8,128)S(1)}, u32[]{:S(2)}, u32[]{:S(2)}) collective-permute-start(f32[6,16,256]{2,1,0:T(8,128)S(1)} %get-tuple-element.412), channel_id=1, source_target_pairs={{0,2},{1,3},{2,0},{3,1},{4,6},{5,7},{6,4},{7,5},{8,10},{9,11},{10,... | collective-permute-start | bytes 294920 | tf_op jit(solution)/shard_map/ppermute | solution.py:418
  72.6 2.0 %collective-permute-done.29 = f32[6,16,256]{2,1,0:T(8,128)S(1)} collective-permute-done((f32[6,16,256]{2,1,0:T(8,128)S(1)}, f32[6,16,256]{2,1,0:T(8,128)S(1)}, u32[]{:S(2)}, u32[]{:S(2)}) %collective-permute-start.29) | collective-permute-done | bytes 98336 | tf_op jit(solution)/shard_map/ppermute | solution.py:418
  74.5 2.4 %collective-permute-start.31 = (f32[6,16,256]{2,1,0:T(8,128)S(1)}, f32[6,16,256]{2,1,0:T(8,128)S(1)}, u32[]{:S(2)}, u32[]{:S(2)}) collective-permute-start(f32[6,16,256]{2,1,0:T(8,128)S(1)} %get-tuple-element.413), channel_id=1, source_target_pairs={{0,3},{1,2},{2,1},{3,0},{4,7},{5,6},{6,5},{7,4},{8,11},{9,10},{10,... | collective-permute-start | bytes 294920 | tf_op jit(solution)/shard_map/ppermute | solution.py:418
  77.1 3.0 %collective-permute-done.31 = f32[6,16,256]{2,1,0:T(8,128)S(1)} collective-permute-done((f32[6,16,256]{2,1,0:T(8,128)S(1)}, f32[6,16,256]{2,1,0:T(8,128)S(1)}, u32[]{:S(2)}, u32[]{:S(2)}) %collective-permute-start.31) | collective-permute-done | bytes 98336 | tf_op jit(solution)/shard_map/ppermute | solution.py:418
  80.6 1.3 %collective-permute-start.33 = (bf16[2000,256]{1,0:T(8,128)(2,1)}, bf16[2000,256]{1,0:T(8,128)(2,1)}, u32[]{:S(2)}, u32[]{:S(2)}) collective-permute-start(bf16[2000,256]{1,0:T(8,128)(2,1)} %collective-permute-done.23.refs_5_), channel_id=1, source_target_pairs={{8,0},{12,4},{16,24},{20,28},{9,1},{13,5},{17,25},{21,29},{10,2},{... | collective-permute-start | bytes 3072008 | tf_op jit(solution)/shard_map/ppermute | solution.py:509
  82.0 36.3 %conditional.1 = (bf16[8,4,16,128]{3,2,1,0:T(8,128)(2,1)}, bf16[8,4,16,128]{3,2,1,0:T(8,128)(2,1)}, f32[64,4000]{1,0:T(8,128)}) conditional(s32[]{:T(128)} %convert_element_type.61, (s32[8]{0:T(128)S(1)}, f32[256]{0:T(256)S(1)}, bf16[4000,64]{0,1:T(8,128)(2,1)}, bf16[4000,64]{0,1:T(8,128)(2,1)}, s32[8,32]{1,0:T(8,128)S(1)}, ...), branch_computations={%region_6.14_spmd, %region_14.18_spmd} | conditional | flops 524588416 | bytes 65907736 | solution.py:649
  82.2 3.0 %project.3 = (f32[4,4,16,256]{3,2,1,0:T(8,128)S(1)}, f32[4,4,16,256]{3,2,1,0:T(8,128)S(1)}) custom-call(s32[1]{0:T(128)} %bitcast.4.core_ref, bf16[256,2048]{1,0:T(8,128)(2,1)} %get-tuple-element.347.refs_0_, bf16[256,2048]{1,0:T(8,128)(2,1)} %get-tuple-element.348.refs_1_, bf16[2000,256]{1,0:T(8,128)(2,1)} %get-tuple-element.349.refs_2_, ...), custom_call_target="tpu_custom_call" | custom-call | flops 524288000 | bytes 3596288 | tf_op jit(solution)/shard_map/cond/branch_1_fun/project/pallas_call | solution.py:281
  85.4 1.4 %collective-permute-done.refs_1_ = f32[4,4,16,256]{3,2,1,0:T(8,128)S(1)} collective-permute-done((f32[4,4,16,256]{3,2,1,0:T(8,128)S(1)}, f32[4,4,16,256]{3,2,1,0:T(8,128)S(1)}, u32[]{:S(2)}, u32[]{:S(2)}) %collective-permute-start) | collective-permute-done | bytes 262176 | tf_op jit(solution)/shard_map/cond/branch_1_fun/ppermute | solution.py:418
  86.9 1.6 %collective-permute-start.1 = (f32[4,16,256]{2,1,0:T(8,128)S(1)}, f32[4,16,256]{2,1,0:T(8,128)S(1)}, u32[]{:S(2)}, u32[]{:S(2)}) collective-permute-start(f32[4,16,256]{2,1,0:T(8,128)S(1)} %get-tuple-element.354), channel_id=1, source_target_pairs={{0,1},{1,0},{2,3},{3,2},{4,5},{5,4},{6,7},{7,6},{8,9},{9,8},{10,11... | collective-permute-start | bytes 196616 | tf_op jit(solution)/shard_map/cond/branch_1_fun/ppermute | solution.py:418
  88.4 1.5 %collective-permute-start.2 = (f32[4,16,256]{2,1,0:T(8,128)S(1)}, f32[4,16,256]{2,1,0:T(8,128)S(1)}, u32[]{:S(2)}, u32[]{:S(2)}) collective-permute-start(f32[4,16,256]{2,1,0:T(8,128)S(1)} %get-tuple-element.355), channel_id=1, source_target_pairs={{0,2},{1,3},{2,0},{3,1},{4,6},{5,7},{6,4},{7,5},{8,10},{9,11},{10,... | collective-permute-start | bytes 196616 | tf_op jit(solution)/shard_map/cond/branch_1_fun/ppermute | solution.py:418
  91.2 1.5 %collective-permute-done.2 = f32[4,16,256]{2,1,0:T(8,128)S(1)} collective-permute-done((f32[4,16,256]{2,1,0:T(8,128)S(1)}, f32[4,16,256]{2,1,0:T(8,128)S(1)}, u32[]{:S(2)}, u32[]{:S(2)}) %collective-permute-start.2) | collective-permute-done | bytes 65568 | tf_op jit(solution)/shard_map/cond/branch_1_fun/ppermute | solution.py:418
  92.7 2.4 %collective-permute-done.3 = f32[4,16,256]{2,1,0:T(8,128)S(1)} collective-permute-done((f32[4,16,256]{2,1,0:T(8,128)S(1)}, f32[4,16,256]{2,1,0:T(8,128)S(1)}, u32[]{:S(2)}, u32[]{:S(2)}) %collective-permute-start.3) | collective-permute-done | bytes 65568 | tf_op jit(solution)/shard_map/cond/branch_1_fun/ppermute | solution.py:418
  95.4 5.7 %collective-permute-start.5 = (f32[4,32]{1,0:T(4,128)S(1)}, f32[4,32]{1,0:T(4,128)S(1)}, u32[]{:S(2)}, u32[]{:S(2)}) collective-permute-start(f32[4,32]{1,0:T(4,128)S(1)} %select_reduce_fusion), channel_id=1, source_target_pairs={{0,16},{4,20},{8,24},{12,28},{16,0},{20,4},{24,8},{28,12},{1,17},{... | collective-permute-start | bytes 1544 | tf_op jit(solution)/shard_map/cond/branch_1_fun/ppermute | solution.py:418
  101.1 1.2 collective-permute-start.6
  102.7 3.8 %collective-permute-done.6 = f32[4,32]{1,0:T(4,128)S(1)} collective-permute-done((f32[4,32]{1,0:T(4,128)S(1)}, f32[4,32]{1,0:T(4,128)S(1)}, u32[]{:S(2)}, u32[]{:S(2)}) %collective-permute-start.6) | collective-permute-done | bytes 544 | tf_op jit(solution)/shard_map/cond/branch_1_fun/ppermute | solution.py:418
  106.6 1.2 collective-permute-done.4
  108.0 1.6 %collective-permute-start.7 = (bf16[8,1,16,128]{3,2,1,0:T(8,128)(2,1)S(1)}, bf16[8,1,16,128]{3,2,1,0:T(8,128)(2,1)S(1)}, u32[]{:S(2)}, u32[]{:S(2)}) collective-permute-start(bf16[8,1,16,128]{3,2,1,0:T(8,128)(2,1)S(1)} %bitcast.68), channel_id=1, source_target_pairs={{0,1},{1,0},{2,3},{3,2},{4,5},{5,4},{6,7},{7,6},{8,9},{9,8},{10,11... | collective-permute-start | bytes 98312 | tf_op jit(solution)/shard_map/cond/branch_1_fun/ppermute | solution.py:418
  109.6 1.5 %collective-permute-start.8 = (bf16[8,1,16,128]{3,2,1,0:T(8,128)(2,1)S(1)}, bf16[8,1,16,128]{3,2,1,0:T(8,128)(2,1)S(1)}, u32[]{:S(2)}, u32[]{:S(2)}) collective-permute-start(bf16[8,1,16,128]{3,2,1,0:T(8,128)(2,1)S(1)} %bitcast.69), channel_id=1, source_target_pairs={{0,2},{1,3},{2,0},{3,1},{4,6},{5,7},{6,4},{7,5},{8,10},{9,11},{10,... | collective-permute-start | bytes 98312 | tf_op jit(solution)/shard_map/cond/branch_1_fun/ppermute | solution.py:418
  112.0 1.5 %collective-permute-done.8.refs_2_ = bf16[8,1,16,128]{3,2,1,0:T(8,128)(2,1)S(1)} collective-permute-done((bf16[8,1,16,128]{3,2,1,0:T(8,128)(2,1)S(1)}, bf16[8,1,16,128]{3,2,1,0:T(8,128)(2,1)S(1)}, u32[]{:S(2)}, u32[]{:S(2)}) %collective-permute-start.8) | collective-permute-done | bytes 32800 | tf_op jit(solution)/shard_map/cond/branch_1_fun/ppermute | solution.py:418
  113.5 2.4 %collective-permute-done.9.refs_3_ = bf16[8,1,16,128]{3,2,1,0:T(8,128)(2,1)S(1)} collective-permute-done((bf16[8,1,16,128]{3,2,1,0:T(8,128)(2,1)S(1)}, bf16[8,1,16,128]{3,2,1,0:T(8,128)(2,1)S(1)}, u32[]{:S(2)}, u32[]{:S(2)}) %collective-permute-start.9) | collective-permute-done | bytes 32800 | tf_op jit(solution)/shard_map/cond/branch_1_fun/ppermute | solution.py:418
  116.6 1.7 %collective-permute-done.10 = bf16[8,4,16,128]{3,2,1,0:T(8,128)(2,1)} collective-permute-done((bf16[8,4,16,128]{3,2,1,0:T(8,128)(2,1)}, bf16[8,4,16,128]{3,2,1,0:T(8,128)(2,1)}, u32[]{:S(2)}, u32[]{:S(2)}) %collective-permute-start.10) | collective-permute-done | bytes 131104 | tf_op jit(solution)/shard_map/cond/branch_1_fun/ppermute | solution.py:418
  118.3 3.3 %contract.1 = (f32[64,2000]{1,0:T(8,128)S(1)}, f32[64,2000]{1,0:T(8,128)S(1)}) custom-call(s32[1]{0:T(128)} %bitcast.10.which_ref.core_ref, bf16[8,4,16,128]{3,2,1,0:T(8,128)(2,1)} %get-tuple-element.421.kernel_ref, bf16[8,4,16,128]{3,2,1,0:T(8,128)(2,1)} %get-tuple-element.422.got_ref, bf16[2000,256]{1,0:T(8,128)(2,1)S(1)} %straighten.1.refs_1_.refs_0_, ...), custom_call_target="tpu_custom_call" | custom-call | flops 524288000 | bytes 5120000 | tf_op jit(solution)/shard_map/contract/pallas_call | solution.py:346
  121.9 1.7 %collective-permute-done.34.back_ref = f32[64,2000]{1,0:T(8,128)S(1)} collective-permute-done((f32[64,2000]{1,0:T(8,128)S(1)}, f32[64,2000]{1,0:T(8,128)S(1)}, u32[]{:S(2)}, u32[]{:S(2)}) %collective-permute-start.34) | collective-permute-done | bytes 512032 | tf_op jit(solution)/shard_map/ppermute | solution.py:418
  123.5 1.8 %finish.1 = f32[64,4000]{1,0:T(8,128)} custom-call(s32[2]{0:T(128)S(1)} %pad_add_fusion.2.flags_ref, f32[64,2000]{1,0:T(8,128)S(1)} %get-tuple-element.424.ours_ref, f32[64,2000]{1,0:T(8,128)S(1)} %collective-permute-done.34.back_ref, f32[64,4000]{1,0:T(8,128)} %get-tuple-element.426.other_ref), custom_call_target="tpu_custom_call", output_to_operand_aliasing={{}: (3, {})} | custom-call | tf_op jit(solution)/shard_map/finish/pallas_call | solution.py:387
  (117 shorter events, 12.7 us)
Async XLA Ops:
  0.0 3.4 %copy-start.7 = (f32[256]{0:T(256)S(1)}, f32[256]{0:T(256)}, u32[]{:S(2)}) copy-start(f32[256]{0:T(256)} %param.17) | copy-start | bytes 3076
  0.0 3.3 %copy-start.8 = (s32[8]{0:T(128)S(1)}, s32[8]{0:T(128)}, u32[]{:S(2)}) copy-start(s32[8]{0:T(128)} %param.18) | copy-start | bytes 100
  0.0 3.4 %collective-permute-start.17 = (f32[1,256]{1,0:T(1,128)}, f32[1,256]{1,0:T(1,128)S(1)}, u32[]{:S(2)}, u32[]{:S(2)}) collective-permute-start(f32[1,256]{1,0:T(1,128)} %bitcast.85), channel_id=1, source_target_pairs={{0,4},{4,0},{8,12},{12,8},{16,20},{20,16},{24,28},{28,24},{1,5},{5... | collective-permute-start | bytes 3080 | tf_op jit(solution)/shard_map/ppermute | solution.py:418
  0.5 2.9 %collective-permute-start.16 = (s32[1,8]{1,0:T(1,128)}, s32[1,8]{1,0:T(1,128)S(1)}, u32[]{:S(2)}, u32[]{:S(2)}) collective-permute-start(s32[1,8]{1,0:T(1,128)} %bitcast.87), channel_id=1, source_target_pairs={{0,4},{4,0},{8,12},{12,8},{16,20},{20,16},{24,28},{28,24},{1,5},{5... | collective-permute-start | bytes 104 | tf_op jit(solution)/shard_map/ppermute | solution.py:418
  1.4 6.9 %collective-permute-start.15 = (s32[16,8]{0,1:T(8,128)S(1)}, s32[16,8]{0,1:T(8,128)S(1)}, u32[]{:S(2)}, u32[]{:S(2)}) collective-permute-start(s32[16,8]{0,1:T(8,128)S(1)} %get-tuple-element.495), channel_id=1, source_target_pairs={{0,4},{4,0},{8,12},{12,8},{16,20},{20,16},{24,28},{28,24},{1,5},{5... | collective-permute-start | bytes 1544 | tf_op jit(solution)/shard_map/ppermute | solution.py:418
  3.0 10.3 %collective-permute-start.14 = (bf16[2000,256]{1,0:T(8,128)(2,1)S(1)}, bf16[2000,256]{1,0:T(8,128)(2,1)S(1)}, u32[]{:S(2)}, u32[]{:S(2)}) collective-permute-start(bf16[2000,256]{1,0:T(8,128)(2,1)S(1)} %half_of.3), channel_id=1, source_target_pairs={{0,4},{4,0},{8,12},{12,8},{16,20},{20,16},{24,28},{28,24},{1,5},{5... | collective-permute-start | bytes 3072008 | tf_op jit(solution)/shard_map/ppermute | solution.py:418
  3.5 5.0 %collective-permute-start.18 = (f32[1,528]{1,0:T(1,128)S(1)}, f32[1,528]{1,0:T(1,128)S(1)}, u32[]{:S(2)}, u32[]{:S(2)}) collective-permute-start(f32[1,528]{1,0:T(1,128)S(1)} %pad_maximum_fusion.3), channel_id=1, source_target_pairs={{0,8},{4,12},{8,0},{12,4},{16,24},{20,28},{24,16},{28,20},{1,9},{5... | collective-permute-start | bytes 6344 | tf_op jit(solution)/shard_map/ppermute | solution.py:418
  8.8 4.5 %collective-permute-start.19 = (f32[2,528]{1,0:T(2,128)S(1)}, f32[2,528]{1,0:T(2,128)S(1)}, u32[]{:S(2)}, u32[]{:S(2)}) collective-permute-start(f32[2,528]{1,0:T(2,128)S(1)} %maximum_select_fusion.1), channel_id=1, source_target_pairs={{0,16},{4,20},{8,24},{12,28},{16,0},{20,4},{24,8},{28,12},{1,17},{... | collective-permute-start | bytes 12680 | tf_op jit(solution)/shard_map/ppermute | solution.py:418
  13.3 1.0 copy-start
  14.3 1.2 copy-start.1
  17.6 8.5 %collective-permute-start.20 = (bf16[2000,128]{1,0:T(8,128)(2,1)S(1)}, bf16[2000,128]{1,0:T(8,128)(2,1)S(1)}, u32[]{:S(2)}, u32[]{:S(2)}) collective-permute-start(bf16[2000,128]{1,0:T(8,128)(2,1)S(1)} %get-tuple-element.398), channel_id=1, source_target_pairs={{8,16},{12,20},{16,8},{20,12},{9,17},{13,21},{17,9},{21,13},{10,18... | collective-permute-start | bytes 1536008 | tf_op jit(solution)/shard_map/ppermute | solution.py:509
  18.3 14.6 %collective-permute-start.21 = (bf16[2000,128]{1,0:T(8,128)(2,1)S(1)}, bf16[2000,128]{1,0:T(8,128)(2,1)S(1)}, u32[]{:S(2)}, u32[]{:S(2)}) collective-permute-start(bf16[2000,128]{1,0:T(8,128)(2,1)S(1)} %get-tuple-element.399), channel_id=1, source_target_pairs={{0,8},{4,12},{8,0},{12,4},{16,24},{20,28},{24,16},{28,20},{1,9},{5... | collective-permute-start | bytes 1536008 | tf_op jit(solution)/shard_map/ppermute | solution.py:509
  26.1 9.8 %copy-start.4 = (bf16[4000,64]{0,1:T(8,128)(2,1)S(1)}, bf16[4000,64]{0,1:T(8,128)(2,1)}, u32[]{:S(2)}) copy-start(bf16[4000,64]{0,1:T(8,128)(2,1)} %param.15) | copy-start | bytes 1536004
  26.1 9.8 %copy-start.5 = (bf16[4000,64]{0,1:T(8,128)(2,1)S(1)}, bf16[4000,64]{0,1:T(8,128)(2,1)}, u32[]{:S(2)}) copy-start(bf16[4000,64]{0,1:T(8,128)(2,1)} %param.16) | copy-start | bytes 1536004
  33.3 24.9 %collective-permute-start.22 = (bf16[2000,256]{1,0:T(8,128)(2,1)S(1)}, bf16[2000,256]{1,0:T(8,128)(2,1)S(1)}, u32[]{:S(2)}, u32[]{:S(2)}) collective-permute-start(bf16[2000,256]{1,0:T(8,128)(2,1)S(1)} %straighten.1.refs_1_.refs_0_), channel_id=1, source_target_pairs={{0,8},{4,12},{8,0},{12,4},{16,24},{20,28},{24,16},{28,20},{1,9},{5... | collective-permute-start | bytes 3072008 | tf_op jit(solution)/shard_map/ppermute | solution.py:509
  35.1 24.8 %collective-permute-start.24 = (bf16[2000,256]{1,0:T(8,128)(2,1)S(1)}, bf16[2000,256]{1,0:T(8,128)(2,1)S(1)}, u32[]{:S(2)}, u32[]{:S(2)}) collective-permute-start(bf16[2000,256]{1,0:T(8,128)(2,1)S(1)} %straighten.1.refs_1_.refs_0_), channel_id=1, source_target_pairs={{8,16},{12,20},{16,8},{20,12},{9,17},{13,21},{17,9},{21,13},{10,18... | collective-permute-start | bytes 3072008 | tf_op jit(solution)/shard_map/ppermute | solution.py:509
  36.4 2.0 %collective-permute-start.26 = (bf16[128,2048]{1,0:T(8,128)(2,1)S(1)}, bf16[128,2048]{1,0:T(8,128)(2,1)S(1)}, u32[]{:S(2)}, u32[]{:S(2)}) collective-permute-start(bf16[128,2048]{1,0:T(8,128)(2,1)S(1)} %get-tuple-element.405), channel_id=1, source_target_pairs={{0,4},{4,0},{8,12},{12,8},{16,20},{20,16},{24,28},{28,24},{1,5},{5... | collective-permute-start | bytes 1572872 | tf_op jit(solution)/shard_map/ppermute | solution.py:418
  39.4 40.7 %collective-permute-start.32 = (bf16[256,2048]{1,0:T(8,128)(2,1)}, bf16[256,2048]{1,0:T(8,128)(2,1)}, u32[]{:S(2)}, u32[]{:S(2)}) collective-permute-start(bf16[256,2048]{1,0:T(8,128)(2,1)} %stack_panels.1.refs_0_), channel_id=1, source_target_pairs={{0,8},{4,12},{24,16},{28,20},{1,9},{5,13},{25,17},{29,21},{2,10},{... | collective-permute-start | bytes 3145736 | tf_op jit(solution)/shard_map/ppermute | solution.py:509
  58.2 21.9 %collective-permute-start.23 = (bf16[2000,256]{1,0:T(8,128)(2,1)S(1)}, bf16[2000,256]{1,0:T(8,128)(2,1)}, u32[]{:S(2)}, u32[]{:S(2)}) collective-permute-start(bf16[2000,256]{1,0:T(8,128)(2,1)S(1)} %collective-permute-done.22.refs_1_), channel_id=1, source_target_pairs={{8,16},{12,20},{16,8},{20,12},{9,17},{13,21},{17,9},{21,13},{10,18... | collective-permute-start | bytes 3072008 | tf_op jit(solution)/shard_map/ppermute | solution.py:509
  59.9 20.7 %collective-permute-start.25 = (bf16[2000,256]{1,0:T(8,128)(2,1)S(1)}, bf16[2000,256]{1,0:T(8,128)(2,1)}, u32[]{:S(2)}, u32[]{:S(2)}) collective-permute-start(bf16[2000,256]{1,0:T(8,128)(2,1)S(1)} %collective-permute-done.24.refs_2_), channel_id=1, source_target_pairs={{8,0},{12,4},{16,24},{20,28},{9,1},{13,5},{17,25},{21,29},{10,2},{... | collective-permute-start | bytes 3072008 | tf_op jit(solution)/shard_map/ppermute | solution.py:509
  64.1 17.9 %copy-start.6 = (s32[8,32]{1,0:T(8,128)S(1)}, s32[8,32]{1,0:T(8,128)}, u32[]{:S(2)}) copy-start(s32[8,32]{1,0:T(8,128)} %param.19) | copy-start | bytes 3076
  64.1 4.3 %collective-permute-start.28 = (f32[4,4,16,256]{3,2,1,0:T(8,128)}, f32[4,4,16,256]{3,2,1,0:T(8,128)}, u32[]{:S(2)}, u32[]{:S(2)}) collective-permute-start(f32[4,4,16,256]{3,2,1,0:T(8,128)} %get-tuple-element.409), channel_id=1, source_target_pairs={{0,4},{4,0},{8,12},{12,8},{16,20},{20,16},{24,28},{28,24},{1,5},{5... | collective-permute-start | bytes 786440 | tf_op jit(solution)/shard_map/ppermute | solution.py:418
  66.5 1.8 %collective-permute-start.27 = (f32[2,4,16,256]{3,2,1,0:T(8,128)}, f32[2,4,16,256]{3,2,1,0:T(8,128)}, u32[]{:S(2)}, u32[]{:S(2)}) collective-permute-start(f32[2,4,16,256]{3,2,1,0:T(8,128)} %get-tuple-element.407), channel_id=1, source_target_pairs={{0,4},{4,0},{8,12},{12,8},{16,20},{20,16},{24,28},{28,24},{1,5},{5... | collective-permute-start | bytes 393224 | tf_op jit(solution)/shard_map/ppermute | solution.py:418
  69.4 5.1 %collective-permute-start.29 = (f32[6,16,256]{2,1,0:T(8,128)S(1)}, f32[6,16,256]{2,1,0:T(8,128)S(1)}, u32[]{:S(2)}, u32[]{:S(2)}) collective-permute-start(f32[6,16,256]{2,1,0:T(8,128)S(1)} %get-tuple-element.411), channel_id=1, source_target_pairs={{0,1},{1,0},{2,3},{3,2},{4,5},{5,4},{6,7},{7,6},{8,9},{9,8},{10,11... | collective-permute-start | bytes 294920 | tf_op jit(solution)/shard_map/ppermute | solution.py:418
  71.0 6.0 %collective-permute-start.30 = (f32[6,16,256]{2,1,0:T(8,128)S(1)}, f32[6,16,256]{2,1,0:T(8,128)S(1)}, u32[]{:S(2)}, u32[]{:S(2)}) collective-permute-start(f32[6,16,256]{2,1,0:T(8,128)S(1)} %get-tuple-element.412), channel_id=1, source_target_pairs={{0,2},{1,3},{2,0},{3,1},{4,6},{5,7},{6,4},{7,5},{8,10},{9,11},{10,... | collective-permute-start | bytes 294920 | tf_op jit(solution)/shard_map/ppermute | solution.py:418
  74.5 5.5 %collective-permute-start.31 = (f32[6,16,256]{2,1,0:T(8,128)S(1)}, f32[6,16,256]{2,1,0:T(8,128)S(1)}, u32[]{:S(2)}, u32[]{:S(2)}) collective-permute-start(f32[6,16,256]{2,1,0:T(8,128)S(1)} %get-tuple-element.413), channel_id=1, source_target_pairs={{0,3},{1,2},{2,1},{3,0},{4,7},{5,6},{6,5},{7,4},{8,11},{9,10},{10,... | collective-permute-start | bytes 294920 | tf_op jit(solution)/shard_map/ppermute | solution.py:418
  80.6 37.6 %collective-permute-start.33 = (bf16[2000,256]{1,0:T(8,128)(2,1)}, bf16[2000,256]{1,0:T(8,128)(2,1)}, u32[]{:S(2)}, u32[]{:S(2)}) collective-permute-start(bf16[2000,256]{1,0:T(8,128)(2,1)} %collective-permute-done.23.refs_5_), channel_id=1, source_target_pairs={{8,0},{12,4},{16,24},{20,28},{9,1},{13,5},{17,25},{21,29},{10,2},{... | collective-permute-start | bytes 3072008 | tf_op jit(solution)/shard_map/ppermute | solution.py:509
  85.2 1.6 %collective-permute-start = (f32[4,4,16,256]{3,2,1,0:T(8,128)S(1)}, f32[4,4,16,256]{3,2,1,0:T(8,128)S(1)}, u32[]{:S(2)}, u32[]{:S(2)}) collective-permute-start(f32[4,4,16,256]{3,2,1,0:T(8,128)S(1)} %get-tuple-element.352), channel_id=1, source_target_pairs={{0,4},{4,0},{8,12},{12,8},{16,20},{20,16},{24,28},{28,24},{1,5},{5... | collective-permute-start | bytes 786440 | tf_op jit(solution)/shard_map/cond/branch_1_fun/ppermute | solution.py:418
  86.9 4.3 %collective-permute-start.1 = (f32[4,16,256]{2,1,0:T(8,128)S(1)}, f32[4,16,256]{2,1,0:T(8,128)S(1)}, u32[]{:S(2)}, u32[]{:S(2)}) collective-permute-start(f32[4,16,256]{2,1,0:T(8,128)S(1)} %get-tuple-element.354), channel_id=1, source_target_pairs={{0,1},{1,0},{2,3},{3,2},{4,5},{5,4},{6,7},{7,6},{8,9},{9,8},{10,11... | collective-permute-start | bytes 196616 | tf_op jit(solution)/shard_map/cond/branch_1_fun/ppermute | solution.py:418
  88.4 4.3 %collective-permute-start.2 = (f32[4,16,256]{2,1,0:T(8,128)S(1)}, f32[4,16,256]{2,1,0:T(8,128)S(1)}, u32[]{:S(2)}, u32[]{:S(2)}) collective-permute-start(f32[4,16,256]{2,1,0:T(8,128)S(1)} %get-tuple-element.355), channel_id=1, source_target_pairs={{0,2},{1,3},{2,0},{3,1},{4,6},{5,7},{6,4},{7,5},{8,10},{9,11},{10,... | collective-permute-start | bytes 196616 | tf_op jit(solution)/shard_map/cond/branch_1_fun/ppermute | solution.py:418
  90.0 5.2 %collective-permute-start.3 = (f32[4,16,256]{2,1,0:T(8,128)S(1)}, f32[4,16,256]{2,1,0:T(8,128)S(1)}, u32[]{:S(2)}, u32[]{:S(2)}) collective-permute-start(f32[4,16,256]{2,1,0:T(8,128)S(1)} %get-tuple-element.356), channel_id=1, source_target_pairs={{0,3},{1,2},{2,1},{3,0},{4,7},{5,6},{6,5},{7,4},{8,11},{9,10},{10,... | collective-permute-start | bytes 196616 | tf_op jit(solution)/shard_map/cond/branch_1_fun/ppermute | solution.py:418
  95.4 7.4 %collective-permute-start.5 = (f32[4,32]{1,0:T(4,128)S(1)}, f32[4,32]{1,0:T(4,128)S(1)}, u32[]{:S(2)}, u32[]{:S(2)}) collective-permute-start(f32[4,32]{1,0:T(4,128)S(1)} %select_reduce_fusion), channel_id=1, source_target_pairs={{0,16},{4,20},{8,24},{12,28},{16,0},{20,4},{24,8},{28,12},{1,17},{... | collective-permute-start | bytes 1544 | tf_op jit(solution)/shard_map/cond/branch_1_fun/ppermute | solution.py:418
  101.1 5.5 %collective-permute-start.6 = (f32[4,32]{1,0:T(4,128)S(1)}, f32[4,32]{1,0:T(4,128)S(1)}, u32[]{:S(2)}, u32[]{:S(2)}) collective-permute-start(f32[4,32]{1,0:T(4,128)S(1)} %select_reduce_fusion), channel_id=1, source_target_pairs={{0,24},{4,28},{8,16},{12,20},{16,8},{20,12},{24,0},{28,4},{1,25},{... | collective-permute-start | bytes 1544 | tf_op jit(solution)/shard_map/cond/branch_1_fun/ppermute | solution.py:418
  102.3 5.5 %collective-permute-start.4 = (f32[36,256]{1,0:T(8,128)S(1)}, f32[36,256]{1,0:T(8,128)S(1)}, u32[]{:S(2)}, u32[]{:S(2)}) collective-permute-start(f32[36,256]{1,0:T(8,128)S(1)} %select_maximum_fusion), channel_id=1, source_target_pairs={{0,8},{4,12},{8,0},{12,4},{16,24},{20,28},{24,16},{28,20},{1,9},{5... | collective-permute-start | bytes 110600 | tf_op jit(solution)/shard_map/cond/branch_1_fun/ppermute | solution.py:418
  108.0 4.0 %collective-permute-start.7 = (bf16[8,1,16,128]{3,2,1,0:T(8,128)(2,1)S(1)}, bf16[8,1,16,128]{3,2,1,0:T(8,128)(2,1)S(1)}, u32[]{:S(2)}, u32[]{:S(2)}) collective-permute-start(bf16[8,1,16,128]{3,2,1,0:T(8,128)(2,1)S(1)} %bitcast.68), channel_id=1, source_target_pairs={{0,1},{1,0},{2,3},{3,2},{4,5},{5,4},{6,7},{7,6},{8,9},{9,8},{10,11... | collective-permute-start | bytes 98312 | tf_op jit(solution)/shard_map/cond/branch_1_fun/ppermute | solution.py:418
  109.6 3.9 %collective-permute-start.8 = (bf16[8,1,16,128]{3,2,1,0:T(8,128)(2,1)S(1)}, bf16[8,1,16,128]{3,2,1,0:T(8,128)(2,1)S(1)}, u32[]{:S(2)}, u32[]{:S(2)}) collective-permute-start(bf16[8,1,16,128]{3,2,1,0:T(8,128)(2,1)S(1)} %bitcast.69), channel_id=1, source_target_pairs={{0,2},{1,3},{2,0},{3,1},{4,6},{5,7},{6,4},{7,5},{8,10},{9,11},{10,... | collective-permute-start | bytes 98312 | tf_op jit(solution)/shard_map/cond/branch_1_fun/ppermute | solution.py:418
  111.1 4.8 %collective-permute-start.9 = (bf16[8,1,16,128]{3,2,1,0:T(8,128)(2,1)S(1)}, bf16[8,1,16,128]{3,2,1,0:T(8,128)(2,1)S(1)}, u32[]{:S(2)}, u32[]{:S(2)}) collective-permute-start(bf16[8,1,16,128]{3,2,1,0:T(8,128)(2,1)S(1)} %bitcast.70), channel_id=1, source_target_pairs={{0,3},{1,2},{2,1},{3,0},{4,7},{5,6},{6,5},{7,4},{8,11},{9,10},{10,... | collective-permute-start | bytes 98312 | tf_op jit(solution)/shard_map/cond/branch_1_fun/ppermute | solution.py:418
  116.6 1.7 %collective-permute-start.10 = (bf16[8,4,16,128]{3,2,1,0:T(8,128)(2,1)}, bf16[8,4,16,128]{3,2,1,0:T(8,128)(2,1)}, u32[]{:S(2)}, u32[]{:S(2)}) collective-permute-start(bf16[8,4,16,128]{3,2,1,0:T(8,128)(2,1)} %in_order.1), channel_id=1, source_target_pairs={{0,4},{4,0},{8,12},{12,8},{16,20},{20,16},{24,28},{28,24},{1,5},{5... | collective-permute-start | bytes 393224 | tf_op jit(solution)/shard_map/cond/branch_1_fun/ppermute | solution.py:418
  121.6 2.0 %collective-permute-start.34 = (f32[64,2000]{1,0:T(8,128)S(1)}, f32[64,2000]{1,0:T(8,128)S(1)}, u32[]{:S(2)}, u32[]{:S(2)}) collective-permute-start(f32[64,2000]{1,0:T(8,128)S(1)} %get-tuple-element.425), channel_id=1, source_target_pairs={{0,4},{4,0},{8,12},{12,8},{16,20},{20,16},{24,28},{28,24},{1,5},{5... | collective-permute-start | bytes 1536008 | tf_op jit(solution)/shard_map/ppermute | solution.py:418

commit v8 on v7

--- a/solution.py
+++ b/solution.py
@@ -126,7 +126,7 @@
         out_shape=shapes,
         in_specs=[SCALARS] + [WHOLE] * 6,
         out_specs=[WHOLE] * len(shapes),
-        compiler_params=pltpu.CompilerParams(vmem_limit_bytes=16 * MIB),
+        compiler_params=pltpu.CompilerParams(vmem_limit_bytes=10 * MIB),
         name="compact",
         cost_estimate=pl.CostEstimate(
             flops=8 * half * rows * rows, bytes_accessed=8 * half * rows, transcendentals=0
@@ -466,8 +466,6 @@
     sizes = told[:, : 2 * batches].astype(jnp.int32).reshape(-1)
     near_to, _ = places_of(sizes, chip // 2 if chips <= 4 else 0)
     near_place = place if chips > 4 else place % 4
-    for bit in grid_bits[2:] if chips <= 4 else []:
-        told = doubled(told, "grid", bit, 0)
     margin = rows // 2 if (rows // 2) % (8 * shares) == 0 else rows
     tile = margin
     piece = tile // shares
@@ -487,7 +485,9 @@
         odd,
     )
 
-    compacted, told = lax.optimization_barrier((compacted, told))
+    told, _ = lax.optimization_barrier((told, compacted))
+    for bit in grid_bits[2:] if chips <= 4 else []:
+        told = doubled(told, "grid", bit, 0)
     sizes = told[:, : 2 * batches].astype(jnp.int32).reshape(-1)
     weights = told[:, 2 * batches :].reshape(-1)
     to, start = places_of(sizes, 0)

time: 126 us -> 125 us (level)
  waiting for transfers between devices: 49.8 us -> 47.9 us
  transfers between devices with their start and end apart: 32 -> 32, of which waited for: 20 -> 18; matrix products, arithmetic and copies ran while one was open for 5% -> 5% of each run, Pallas kernels for 11% -> 11%
where the time goes in v8:
time: 125 us; the launch traced here: 124 us
  waiting for transfers between devices  47.9 us (38%)
  starting transfers between devices  44.6 us (36%)
  Pallas kernels  21.4 us (17%)
  local copies, waits for them, and re-layouts  4.32 us (3%)
  other arithmetic  4.14 us (3%)
  between operations  1.8 us (1%)
    ppermute x24, starting transfers between devices, flip(): return lax.ppermute(x, axis, [(i, i ^ bit) for i in range(count)])  28.1 us
    ppermute x24, waiting for transfers between devices, flip(): return lax.ppermute(x, axis, [(i, i ^ bit) for i in range(count)])  27.3 us
    ppermute x8, waiting for transfers between devices, sent(): return lax.ppermute(x, 'grid', along(pairs))  20.7 us
    ppermute x8, starting transfers between devices, sent(): return lax.ppermute(x, 'grid', along(pairs))  16.4 us
    pallas_call x3, Pallas kernels, project(): pl.pallas_call(body, out_shape=(shape, shape), in_specs=[SCALARS] + [WHOL...  8.32 us
    pallas_call x1, Pallas kernels, contract(): pl.pallas_call(body, out_shape=(shape, shape), in_specs=[SCALARS] + [WHOL...  3.3 us
  transfers between devices with their start and end apart: 32, of which 18 were waited for; matrix products, arithmetic and copies ran while one was open for 5% of the time, Pallas kernels for 11%

profile of v8, /device:TPU:0, one launch (start us, length us, event | category | flops | bytes accessed | tf_op | source)
XLA Modules:
  0.0 124.4 jit_solution(18436275673980398503)
XLA Ops:
  0.5 0.8 dynamic-slice_bitcast_fusion
  1.8 1.2 half_of.3
  3.5 3.0 %collective-permute-start.18 = (f32[1,528]{1,0:T(1,128)S(1)}, f32[1,528]{1,0:T(1,128)S(1)}, u32[]{:S(2)}, u32[]{:S(2)}) collective-permute-start(f32[1,528]{1,0:T(1,128)S(1)} %pad_maximum_fusion.3), channel_id=1, source_target_pairs={{0,8},{4,12},{8,0},{12,4},{16,24},{20,28},{24,16},{28,20},{1,9},{5... | collective-permute-start | bytes 6344 | tf_op jit(solution)/shard_map/ppermute | solution.py:418
  6.8 1.2 half_of.2.mine_ref
  9.5 0.9 copy-done
  10.5 1.2 copy-done.1
  11.7 1.8 %compact.1 = (bf16[2000,128]{1,0:T(8,128)(2,1)S(1)}, bf16[2000,128]{1,0:T(8,128)(2,1)S(1)}, bf16[2000,128]{1,0:T(8,128)(2,1)S(1)}, bf16[2000,128]{1,0:T(8,128)(2,1)S(1)}) custom-call(s32[1]{0:T(128)} %bitcast.11.odd_ref, bf16[2000,256]{1,0:T(8,128)(2,1)S(1)} %half_of.2.mine_ref, bf16[2000,256]{1,0:T(8,128)(2,1)S(1)} %copy-done.1, ...), custom_call_target="tpu_custom_call" | custom-call | flops 1048576000 | bytes 4096000 | tf_op jit(solution)/shard_map/compact/pallas_call | solution.py:124
  13.5 2.8 %collective-permute-start.21 = (f32[2,528]{1,0:T(2,128)S(1)}, f32[2,528]{1,0:T(2,128)S(1)}, u32[]{:S(2)}, u32[]{:S(2)}) collective-permute-start(f32[2,528]{1,0:T(2,128)S(1)} %maximum_select_fusion.1), channel_id=1, source_target_pairs={{0,16},{4,20},{8,24},{12,28},{16,0},{20,4},{24,8},{28,12},{1,17},{... | collective-permute-start | bytes 12680 | tf_op jit(solution)/shard_map/ppermute | solution.py:418
  17.1 2.9 %collective-permute-start.20 = (bf16[2000,128]{1,0:T(8,128)(2,1)S(1)}, bf16[2000,128]{1,0:T(8,128)(2,1)S(1)}, u32[]{:S(2)}, u32[]{:S(2)}) collective-permute-start(bf16[2000,128]{1,0:T(8,128)(2,1)S(1)} %get-tuple-element.391), channel_id=1, source_target_pairs={{0,8},{4,12},{8,0},{12,4},{16,24},{20,28},{24,16},{28,20},{1,9},{5... | collective-permute-start | bytes 1536008 | tf_op jit(solution)/shard_map/ppermute | solution.py:509
  23.6 6.8 %collective-permute-done.20.refs_3_ = bf16[2000,128]{1,0:T(8,128)(2,1)S(1)} collective-permute-done((bf16[2000,128]{1,0:T(8,128)(2,1)S(1)}, bf16[2000,128]{1,0:T(8,128)(2,1)S(1)}, u32[]{:S(2)}, u32[]{:S(2)}) %collective-permute-start.20) | collective-permute-done | bytes 512032 | tf_op jit(solution)/shard_map/ppermute | solution.py:509
  30.8 1.8 %collective-permute-start.22 = (bf16[2000,256]{1,0:T(8,128)(2,1)S(1)}, bf16[2000,256]{1,0:T(8,128)(2,1)S(1)}, u32[]{:S(2)}, u32[]{:S(2)}) collective-permute-start(bf16[2000,256]{1,0:T(8,128)(2,1)S(1)} %straighten.1.refs_1_.refs_0_), channel_id=1, source_target_pairs={{0,8},{4,12},{8,0},{12,4},{16,24},{20,28},{24,16},{28,20},{1,9},{5... | collective-permute-start | bytes 3072008 | tf_op jit(solution)/shard_map/ppermute | solution.py:509
  32.6 0.7 collective-permute-start.24
  33.9 1.9 %collective-permute-done.26.got_ref = bf16[128,2048]{1,0:T(8,128)(2,1)S(1)} collective-permute-done((bf16[128,2048]{1,0:T(8,128)(2,1)S(1)}, bf16[128,2048]{1,0:T(8,128)(2,1)S(1)}, u32[]{:S(2)}, u32[]{:S(2)}) %collective-permute-start.26) | collective-permute-done | bytes 524320 | tf_op jit(solution)/shard_map/ppermute | solution.py:418
  35.8 1.1 stack_panels.1.refs_0_
  36.9 6.1 %collective-permute-start.32 = (bf16[256,2048]{1,0:T(8,128)(2,1)}, bf16[256,2048]{1,0:T(8,128)(2,1)}, u32[]{:S(2)}, u32[]{:S(2)}) collective-permute-start(bf16[256,2048]{1,0:T(8,128)(2,1)} %stack_panels.1.refs_0_), channel_id=1, source_target_pairs={{0,8},{4,12},{24,16},{28,20},{1,9},{5,13},{25,17},{29,21},{2,10},{... | collective-permute-start | bytes 3145736 | tf_op jit(solution)/shard_map/ppermute | solution.py:509
  43.0 12.7 %collective-permute-done.22.refs_1_ = bf16[2000,256]{1,0:T(8,128)(2,1)S(1)} collective-permute-done((bf16[2000,256]{1,0:T(8,128)(2,1)S(1)}, bf16[2000,256]{1,0:T(8,128)(2,1)S(1)}, u32[]{:S(2)}, u32[]{:S(2)}) %collective-permute-start.22) | collective-permute-done | bytes 1024032 | tf_op jit(solution)/shard_map/ppermute | solution.py:509
  55.7 1.7 %collective-permute-start.23 = (bf16[2000,256]{1,0:T(8,128)(2,1)S(1)}, bf16[2000,256]{1,0:T(8,128)(2,1)}, u32[]{:S(2)}, u32[]{:S(2)}) collective-permute-start(bf16[2000,256]{1,0:T(8,128)(2,1)S(1)} %collective-permute-done.22.refs_1_), channel_id=1, source_target_pairs={{8,16},{12,20},{16,8},{20,12},{9,17},{13,21},{17,9},{21,13},{10,18... | collective-permute-start | bytes 3072008 | tf_op jit(solution)/shard_map/ppermute | solution.py:509
  57.4 1.3 %collective-permute-start.25 = (bf16[2000,256]{1,0:T(8,128)(2,1)S(1)}, bf16[2000,256]{1,0:T(8,128)(2,1)}, u32[]{:S(2)}, u32[]{:S(2)}) collective-permute-start(bf16[2000,256]{1,0:T(8,128)(2,1)S(1)} %collective-permute-done.24.refs_2_), channel_id=1, source_target_pairs={{8,0},{12,4},{16,24},{20,28},{9,1},{13,5},{17,25},{21,29},{10,2},{... | collective-permute-start | bytes 3072008 | tf_op jit(solution)/shard_map/ppermute | solution.py:509
  58.7 2.9 %project.5 = (f32[4,4,16,256]{3,2,1,0:T(8,128)S(1)}, f32[4,4,16,256]{3,2,1,0:T(8,128)}) custom-call(s32[1]{0:T(128)} %bitcast.10.which_ref.core_ref, bf16[256,2048]{1,0:T(8,128)(2,1)} %stack_panels.1.refs_0_, bf16[2000,256]{1,0:T(8,128)(2,1)S(1)} %collective-permute-done.22.refs_1_, bf16[2000,256]{1,0:T(8,128)(2,1)S(1)} %collective-permute-done.24.refs_2_), custom_call_target="tpu_custom_call" | custom-call | flops 524288000 | bytes 3596288 | tf_op jit(solution)/shard_map/project/pallas_call | solution.py:281
  61.5 2.4 %project.4 = (f32[2,4,16,256]{3,2,1,0:T(8,128)S(1)}, f32[2,4,16,256]{3,2,1,0:T(8,128)}) custom-call(s32[1]{0:T(128)} %bitcast.10.which_ref.core_ref, bf16[256,2048]{1,0:T(8,128)(2,1)} %stack_panels.1.refs_0_, bf16[2000,256]{1,0:T(8,128)(2,1)S(1)} %straighten.1.refs_1_.refs_0_), custom_call_target="tpu_custom_call" | custom-call | flops 262144000 | bytes 2310144 | tf_op jit(solution)/shard_map/project/pallas_call | solution.py:281
  64.5 1.3 %collective-permute-done.27.refs_1_ = f32[2,4,16,256]{3,2,1,0:T(8,128)} collective-permute-done((f32[2,4,16,256]{3,2,1,0:T(8,128)}, f32[2,4,16,256]{3,2,1,0:T(8,128)}, u32[]{:S(2)}, u32[]{:S(2)}) %collective-permute-start.27) | collective-permute-done | bytes 131104 | tf_op jit(solution)/shard_map/ppermute | solution.py:418
  65.8 1.1 split_sum.3
  66.9 1.6 %collective-permute-start.29 = (f32[6,16,256]{2,1,0:T(8,128)S(1)}, f32[6,16,256]{2,1,0:T(8,128)S(1)}, u32[]{:S(2)}, u32[]{:S(2)}) collective-permute-start(f32[6,16,256]{2,1,0:T(8,128)S(1)} %get-tuple-element.403), channel_id=1, source_target_pairs={{0,1},{1,0},{2,3},{3,2},{4,5},{5,4},{6,7},{7,6},{8,9},{9,8},{10,11... | collective-permute-start | bytes 294920 | tf_op jit(solution)/shard_map/ppermute | solution.py:418
  68.5 1.5 %collective-permute-start.30 = (f32[6,16,256]{2,1,0:T(8,128)S(1)}, f32[6,16,256]{2,1,0:T(8,128)S(1)}, u32[]{:S(2)}, u32[]{:S(2)}) collective-permute-start(f32[6,16,256]{2,1,0:T(8,128)S(1)} %get-tuple-element.404), channel_id=1, source_target_pairs={{0,2},{1,3},{2,0},{3,1},{4,6},{5,7},{6,4},{7,5},{8,10},{9,11},{10,... | collective-permute-start | bytes 294920 | tf_op jit(solution)/shard_map/ppermute | solution.py:418
  70.0 2.0 %collective-permute-done.29 = f32[6,16,256]{2,1,0:T(8,128)S(1)} collective-permute-done((f32[6,16,256]{2,1,0:T(8,128)S(1)}, f32[6,16,256]{2,1,0:T(8,128)S(1)}, u32[]{:S(2)}, u32[]{:S(2)}) %collective-permute-start.29) | collective-permute-done | bytes 98336 | tf_op jit(solution)/shard_map/ppermute | solution.py:418
  72.0 2.4 %collective-permute-start.31 = (f32[6,16,256]{2,1,0:T(8,128)S(1)}, f32[6,16,256]{2,1,0:T(8,128)S(1)}, u32[]{:S(2)}, u32[]{:S(2)}) collective-permute-start(f32[6,16,256]{2,1,0:T(8,128)S(1)} %get-tuple-element.405), channel_id=1, source_target_pairs={{0,3},{1,2},{2,1},{3,0},{4,7},{5,6},{6,5},{7,4},{8,11},{9,10},{10,... | collective-permute-start | bytes 294920 | tf_op jit(solution)/shard_map/ppermute | solution.py:418
  74.5 3.0 %collective-permute-done.31 = f32[6,16,256]{2,1,0:T(8,128)S(1)} collective-permute-done((f32[6,16,256]{2,1,0:T(8,128)S(1)}, f32[6,16,256]{2,1,0:T(8,128)S(1)}, u32[]{:S(2)}, u32[]{:S(2)}) %collective-permute-start.31) | collective-permute-done | bytes 98336 | tf_op jit(solution)/shard_map/ppermute | solution.py:418
  77.6 1.1 collective-permute-done.25.refs_4_
  78.7 1.3 %collective-permute-start.33 = (bf16[2000,256]{1,0:T(8,128)(2,1)}, bf16[2000,256]{1,0:T(8,128)(2,1)}, u32[]{:S(2)}, u32[]{:S(2)}) collective-permute-start(bf16[2000,256]{1,0:T(8,128)(2,1)} %collective-permute-done.23.refs_5_), channel_id=1, source_target_pairs={{8,0},{12,4},{16,24},{20,28},{9,1},{13,5},{17,25},{21,29},{10,2},{... | collective-permute-start | bytes 3072008 | tf_op jit(solution)/shard_map/ppermute | solution.py:509
  80.1 37.1 %conditional.1 = (bf16[8,4,16,128]{3,2,1,0:T(8,128)(2,1)}, bf16[8,4,16,128]{3,2,1,0:T(8,128)(2,1)}, f32[64,4000]{1,0:T(8,128)}) conditional(s32[]{:T(128)} %convert_element_type.61, (s32[8]{0:T(128)S(1)}, f32[256]{0:T(256)S(1)}, bf16[4000,64]{0,1:T(8,128)(2,1)}, bf16[4000,64]{0,1:T(8,128)(2,1)}, s32[8,32]{1,0:T(8,128)S(1)}, ...), branch_computations={%region_6.14_spmd, %region_14.18_spmd} | conditional | flops 524588416 | bytes 65907736 | solution.py:649
  80.3 3.0 %project.3 = (f32[4,4,16,256]{3,2,1,0:T(8,128)S(1)}, f32[4,4,16,256]{3,2,1,0:T(8,128)S(1)}) custom-call(s32[1]{0:T(128)} %bitcast.4.core_ref, bf16[256,2048]{1,0:T(8,128)(2,1)} %get-tuple-element.347.refs_0_, bf16[256,2048]{1,0:T(8,128)(2,1)} %get-tuple-element.348.refs_1_, bf16[2000,256]{1,0:T(8,128)(2,1)} %get-tuple-element.349.refs_2_, ...), custom_call_target="tpu_custom_call" | custom-call | flops 524288000 | bytes 3596288 | tf_op jit(solution)/shard_map/cond/branch_1_fun/project/pallas_call | solution.py:281
  83.5 1.4 %collective-permute-done.refs_1_ = f32[4,4,16,256]{3,2,1,0:T(8,128)S(1)} collective-permute-done((f32[4,4,16,256]{3,2,1,0:T(8,128)S(1)}, f32[4,4,16,256]{3,2,1,0:T(8,128)S(1)}, u32[]{:S(2)}, u32[]{:S(2)}) %collective-permute-start) | collective-permute-done | bytes 262176 | tf_op jit(solution)/shard_map/cond/branch_1_fun/ppermute | solution.py:418
  85.0 1.6 %collective-permute-start.1 = (f32[4,16,256]{2,1,0:T(8,128)S(1)}, f32[4,16,256]{2,1,0:T(8,128)S(1)}, u32[]{:S(2)}, u32[]{:S(2)}) collective-permute-start(f32[4,16,256]{2,1,0:T(8,128)S(1)} %get-tuple-element.354), channel_id=1, source_target_pairs={{0,1},{1,0},{2,3},{3,2},{4,5},{5,4},{6,7},{7,6},{8,9},{9,8},{10,11... | collective-permute-start | bytes 196616 | tf_op jit(solution)/shard_map/cond/branch_1_fun/ppermute | solution.py:418
  86.5 1.5 %collective-permute-start.2 = (f32[4,16,256]{2,1,0:T(8,128)S(1)}, f32[4,16,256]{2,1,0:T(8,128)S(1)}, u32[]{:S(2)}, u32[]{:S(2)}) collective-permute-start(f32[4,16,256]{2,1,0:T(8,128)S(1)} %get-tuple-element.355), channel_id=1, source_target_pairs={{0,2},{1,3},{2,0},{3,1},{4,6},{5,7},{6,4},{7,5},{8,10},{9,11},{10,... | collective-permute-start | bytes 196616 | tf_op jit(solution)/shard_map/cond/branch_1_fun/ppermute | solution.py:418
  89.3 1.5 %collective-permute-done.2 = f32[4,16,256]{2,1,0:T(8,128)S(1)} collective-permute-done((f32[4,16,256]{2,1,0:T(8,128)S(1)}, f32[4,16,256]{2,1,0:T(8,128)S(1)}, u32[]{:S(2)}, u32[]{:S(2)}) %collective-permute-start.2) | collective-permute-done | bytes 65568 | tf_op jit(solution)/shard_map/cond/branch_1_fun/ppermute | solution.py:418
  90.8 2.4 %collective-permute-done.3 = f32[4,16,256]{2,1,0:T(8,128)S(1)} collective-permute-done((f32[4,16,256]{2,1,0:T(8,128)S(1)}, f32[4,16,256]{2,1,0:T(8,128)S(1)}, u32[]{:S(2)}, u32[]{:S(2)}) %collective-permute-start.3) | collective-permute-done | bytes 65568 | tf_op jit(solution)/shard_map/cond/branch_1_fun/ppermute | solution.py:418
  93.4 5.1 %collective-permute-start.5 = (f32[4,32]{1,0:T(4,128)S(1)}, f32[4,32]{1,0:T(4,128)S(1)}, u32[]{:S(2)}, u32[]{:S(2)}) collective-permute-start(f32[4,32]{1,0:T(4,128)S(1)} %select_reduce_fusion), channel_id=1, source_target_pairs={{0,16},{4,20},{8,24},{12,28},{16,0},{20,4},{24,8},{28,12},{1,17},{... | collective-permute-start | bytes 1544 | tf_op jit(solution)/shard_map/cond/branch_1_fun/ppermute | solution.py:418
  98.5 2.6 %collective-permute-start.6 = (f32[4,32]{1,0:T(4,128)S(1)}, f32[4,32]{1,0:T(4,128)S(1)}, u32[]{:S(2)}, u32[]{:S(2)}) collective-permute-start(f32[4,32]{1,0:T(4,128)S(1)} %select_reduce_fusion), channel_id=1, source_target_pairs={{0,24},{4,28},{8,16},{12,20},{16,8},{20,12},{24,0},{28,4},{1,25},{... | collective-permute-start | bytes 1544 | tf_op jit(solution)/shard_map/cond/branch_1_fun/ppermute | solution.py:418
  101.3 2.7 %collective-permute-done.6 = f32[4,32]{1,0:T(4,128)S(1)} collective-permute-done((f32[4,32]{1,0:T(4,128)S(1)}, f32[4,32]{1,0:T(4,128)S(1)}, u32[]{:S(2)}, u32[]{:S(2)}) %collective-permute-start.6) | collective-permute-done | bytes 544 | tf_op jit(solution)/shard_map/cond/branch_1_fun/ppermute | solution.py:418
  104.0 2.7 %collective-permute-done.4 = f32[36,256]{1,0:T(8,128)S(1)} collective-permute-done((f32[36,256]{1,0:T(8,128)S(1)}, f32[36,256]{1,0:T(8,128)S(1)}, u32[]{:S(2)}, u32[]{:S(2)}) %collective-permute-start.4) | collective-permute-done | bytes 36896 | tf_op jit(solution)/shard_map/cond/branch_1_fun/ppermute | solution.py:418
  106.9 1.6 %collective-permute-start.7 = (bf16[8,1,16,128]{3,2,1,0:T(8,128)(2,1)S(1)}, bf16[8,1,16,128]{3,2,1,0:T(8,128)(2,1)S(1)}, u32[]{:S(2)}, u32[]{:S(2)}) collective-permute-start(bf16[8,1,16,128]{3,2,1,0:T(8,128)(2,1)S(1)} %bitcast.68), channel_id=1, source_target_pairs={{0,1},{1,0},{2,3},{3,2},{4,5},{5,4},{6,7},{7,6},{8,9},{9,8},{10,11... | collective-permute-start | bytes 98312 | tf_op jit(solution)/shard_map/cond/branch_1_fun/ppermute | solution.py:418
  108.5 1.5 %collective-permute-start.8 = (bf16[8,1,16,128]{3,2,1,0:T(8,128)(2,1)S(1)}, bf16[8,1,16,128]{3,2,1,0:T(8,128)(2,1)S(1)}, u32[]{:S(2)}, u32[]{:S(2)}) collective-permute-start(bf16[8,1,16,128]{3,2,1,0:T(8,128)(2,1)S(1)} %bitcast.69), channel_id=1, source_target_pairs={{0,2},{1,3},{2,0},{3,1},{4,6},{5,7},{6,4},{7,5},{8,10},{9,11},{10,... | collective-permute-start | bytes 98312 | tf_op jit(solution)/shard_map/cond/branch_1_fun/ppermute | solution.py:418
  110.9 1.5 %collective-permute-done.8.refs_2_ = bf16[8,1,16,128]{3,2,1,0:T(8,128)(2,1)S(1)} collective-permute-done((bf16[8,1,16,128]{3,2,1,0:T(8,128)(2,1)S(1)}, bf16[8,1,16,128]{3,2,1,0:T(8,128)(2,1)S(1)}, u32[]{:S(2)}, u32[]{:S(2)}) %collective-permute-start.8) | collective-permute-done | bytes 32800 | tf_op jit(solution)/shard_map/cond/branch_1_fun/ppermute | solution.py:418
  112.4 2.4 %collective-permute-done.9.refs_3_ = bf16[8,1,16,128]{3,2,1,0:T(8,128)(2,1)S(1)} collective-permute-done((bf16[8,1,16,128]{3,2,1,0:T(8,128)(2,1)S(1)}, bf16[8,1,16,128]{3,2,1,0:T(8,128)(2,1)S(1)}, u32[]{:S(2)}, u32[]{:S(2)}) %collective-permute-start.9) | collective-permute-done | bytes 32800 | tf_op jit(solution)/shard_map/cond/branch_1_fun/ppermute | solution.py:418
  115.5 1.7 %collective-permute-done.10 = bf16[8,4,16,128]{3,2,1,0:T(8,128)(2,1)} collective-permute-done((bf16[8,4,16,128]{3,2,1,0:T(8,128)(2,1)}, bf16[8,4,16,128]{3,2,1,0:T(8,128)(2,1)}, u32[]{:S(2)}, u32[]{:S(2)}) %collective-permute-start.10) | collective-permute-done | bytes 131104 | tf_op jit(solution)/shard_map/cond/branch_1_fun/ppermute | solution.py:418
  117.2 3.3 %contract.1 = (f32[64,2000]{1,0:T(8,128)S(1)}, f32[64,2000]{1,0:T(8,128)S(1)}) custom-call(s32[1]{0:T(128)} %bitcast.10.which_ref.core_ref, bf16[8,4,16,128]{3,2,1,0:T(8,128)(2,1)} %get-tuple-element.413.kernel_ref, bf16[8,4,16,128]{3,2,1,0:T(8,128)(2,1)} %get-tuple-element.414.got_ref, bf16[2000,256]{1,0:T(8,128)(2,1)S(1)} %straighten.1.refs_1_.refs_0_, ...), custom_call_target="tpu_custom_call" | custom-call | flops 524288000 | bytes 5120000 | tf_op jit(solution)/shard_map/contract/pallas_call | solution.py:346
  120.8 1.7 %collective-permute-done.34.back_ref = f32[64,2000]{1,0:T(8,128)S(1)} collective-permute-done((f32[64,2000]{1,0:T(8,128)S(1)}, f32[64,2000]{1,0:T(8,128)S(1)}, u32[]{:S(2)}, u32[]{:S(2)}) %collective-permute-start.34) | collective-permute-done | bytes 512032 | tf_op jit(solution)/shard_map/ppermute | solution.py:418
  122.5 1.8 %finish.1 = f32[64,4000]{1,0:T(8,128)} custom-call(s32[2]{0:T(128)S(1)} %pad_add_fusion.2.flags_ref, f32[64,2000]{1,0:T(8,128)S(1)} %get-tuple-element.416.ours_ref, f32[64,2000]{1,0:T(8,128)S(1)} %collective-permute-done.34.back_ref, f32[64,4000]{1,0:T(8,128)} %get-tuple-element.418.other_ref), custom_call_target="tpu_custom_call", output_to_operand_aliasing={{}: (3, {})} | custom-call | tf_op jit(solution)/shard_map/finish/pallas_call | solution.py:387
  (117 shorter events, 11.8 us)
Async XLA Ops:
  0.0 3.4 %copy-start.7 = (f32[256]{0:T(256)S(1)}, f32[256]{0:T(256)}, u32[]{:S(2)}) copy-start(f32[256]{0:T(256)} %param.17) | copy-start | bytes 3076
  0.0 3.3 %copy-start.8 = (s32[8]{0:T(128)S(1)}, s32[8]{0:T(128)}, u32[]{:S(2)}) copy-start(s32[8]{0:T(128)} %param.18) | copy-start | bytes 100
  0.0 3.4 %collective-permute-start.17 = (f32[1,256]{1,0:T(1,128)}, f32[1,256]{1,0:T(1,128)S(1)}, u32[]{:S(2)}, u32[]{:S(2)}) collective-permute-start(f32[1,256]{1,0:T(1,128)} %bitcast.85), channel_id=1, source_target_pairs={{0,4},{4,0},{8,12},{12,8},{16,20},{20,16},{24,28},{28,24},{1,5},{5... | collective-permute-start | bytes 3080 | tf_op jit(solution)/shard_map/ppermute | solution.py:418
  0.5 2.8 %collective-permute-start.16 = (s32[1,8]{1,0:T(1,128)}, s32[1,8]{1,0:T(1,128)S(1)}, u32[]{:S(2)}, u32[]{:S(2)}) collective-permute-start(s32[1,8]{1,0:T(1,128)} %bitcast.87), channel_id=1, source_target_pairs={{0,4},{4,0},{8,12},{12,8},{16,20},{20,16},{24,28},{28,24},{1,5},{5... | collective-permute-start | bytes 104 | tf_op jit(solution)/shard_map/ppermute | solution.py:418
  1.4 6.7 %collective-permute-start.15 = (s32[16,8]{0,1:T(8,128)S(1)}, s32[16,8]{0,1:T(8,128)S(1)}, u32[]{:S(2)}, u32[]{:S(2)}) collective-permute-start(s32[16,8]{0,1:T(8,128)S(1)} %get-tuple-element.487), channel_id=1, source_target_pairs={{0,4},{4,0},{8,12},{12,8},{16,20},{20,16},{24,28},{28,24},{1,5},{5... | collective-permute-start | bytes 1544 | tf_op jit(solution)/shard_map/ppermute | solution.py:418
  3.0 6.5 %collective-permute-start.14 = (bf16[2000,256]{1,0:T(8,128)(2,1)S(1)}, bf16[2000,256]{1,0:T(8,128)(2,1)S(1)}, u32[]{:S(2)}, u32[]{:S(2)}) collective-permute-start(bf16[2000,256]{1,0:T(8,128)(2,1)S(1)} %half_of.3), channel_id=1, source_target_pairs={{0,4},{4,0},{8,12},{12,8},{16,20},{20,16},{24,28},{28,24},{1,5},{5... | collective-permute-start | bytes 3072008 | tf_op jit(solution)/shard_map/ppermute | solution.py:418
  3.5 4.9 %collective-permute-start.18 = (f32[1,528]{1,0:T(1,128)S(1)}, f32[1,528]{1,0:T(1,128)S(1)}, u32[]{:S(2)}, u32[]{:S(2)}) collective-permute-start(f32[1,528]{1,0:T(1,128)S(1)} %pad_maximum_fusion.3), channel_id=1, source_target_pairs={{0,8},{4,12},{8,0},{12,4},{16,24},{20,28},{24,16},{28,20},{1,9},{5... | collective-permute-start | bytes 6344 | tf_op jit(solution)/shard_map/ppermute | solution.py:418
  9.5 1.0 copy-start
  10.5 1.2 copy-start.1
  13.5 6.5 %collective-permute-start.21 = (f32[2,528]{1,0:T(2,128)S(1)}, f32[2,528]{1,0:T(2,128)S(1)}, u32[]{:S(2)}, u32[]{:S(2)}) collective-permute-start(f32[2,528]{1,0:T(2,128)S(1)} %maximum_select_fusion.1), channel_id=1, source_target_pairs={{0,16},{4,20},{8,24},{12,28},{16,0},{20,4},{24,8},{28,12},{1,17},{... | collective-permute-start | bytes 12680 | tf_op jit(solution)/shard_map/ppermute | solution.py:418
  16.4 7.2 %collective-permute-start.19 = (bf16[2000,128]{1,0:T(8,128)(2,1)S(1)}, bf16[2000,128]{1,0:T(8,128)(2,1)S(1)}, u32[]{:S(2)}, u32[]{:S(2)}) collective-permute-start(bf16[2000,128]{1,0:T(8,128)(2,1)S(1)} %get-tuple-element.390), channel_id=1, source_target_pairs={{8,16},{12,20},{16,8},{20,12},{9,17},{13,21},{17,9},{21,13},{10,18... | collective-permute-start | bytes 1536008 | tf_op jit(solution)/shard_map/ppermute | solution.py:509
  17.1 13.3 %collective-permute-start.20 = (bf16[2000,128]{1,0:T(8,128)(2,1)S(1)}, bf16[2000,128]{1,0:T(8,128)(2,1)S(1)}, u32[]{:S(2)}, u32[]{:S(2)}) collective-permute-start(bf16[2000,128]{1,0:T(8,128)(2,1)S(1)} %get-tuple-element.391), channel_id=1, source_target_pairs={{0,8},{4,12},{8,0},{12,4},{16,24},{20,28},{24,16},{28,20},{1,9},{5... | collective-permute-start | bytes 1536008 | tf_op jit(solution)/shard_map/ppermute | solution.py:509
  23.5 9.8 %copy-start.4 = (bf16[4000,64]{0,1:T(8,128)(2,1)S(1)}, bf16[4000,64]{0,1:T(8,128)(2,1)}, u32[]{:S(2)}) copy-start(bf16[4000,64]{0,1:T(8,128)(2,1)} %param.15) | copy-start | bytes 1536004
  23.6 9.8 %copy-start.5 = (bf16[4000,64]{0,1:T(8,128)(2,1)S(1)}, bf16[4000,64]{0,1:T(8,128)(2,1)}, u32[]{:S(2)}) copy-start(bf16[4000,64]{0,1:T(8,128)(2,1)} %param.16) | copy-start | bytes 1536004
  30.8 24.9 %collective-permute-start.22 = (bf16[2000,256]{1,0:T(8,128)(2,1)S(1)}, bf16[2000,256]{1,0:T(8,128)(2,1)S(1)}, u32[]{:S(2)}, u32[]{:S(2)}) collective-permute-start(bf16[2000,256]{1,0:T(8,128)(2,1)S(1)} %straighten.1.refs_1_.refs_0_), channel_id=1, source_target_pairs={{0,8},{4,12},{8,0},{12,4},{16,24},{20,28},{24,16},{28,20},{1,9},{5... | collective-permute-start | bytes 3072008 | tf_op jit(solution)/shard_map/ppermute | solution.py:509
  32.6 24.8 %collective-permute-start.24 = (bf16[2000,256]{1,0:T(8,128)(2,1)S(1)}, bf16[2000,256]{1,0:T(8,128)(2,1)S(1)}, u32[]{:S(2)}, u32[]{:S(2)}) collective-permute-start(bf16[2000,256]{1,0:T(8,128)(2,1)S(1)} %straighten.1.refs_1_.refs_0_), channel_id=1, source_target_pairs={{8,16},{12,20},{16,8},{20,12},{9,17},{13,21},{17,9},{21,13},{10,18... | collective-permute-start | bytes 3072008 | tf_op jit(solution)/shard_map/ppermute | solution.py:509
  33.8 2.0 %collective-permute-start.26 = (bf16[128,2048]{1,0:T(8,128)(2,1)S(1)}, bf16[128,2048]{1,0:T(8,128)(2,1)S(1)}, u32[]{:S(2)}, u32[]{:S(2)}) collective-permute-start(bf16[128,2048]{1,0:T(8,128)(2,1)S(1)} %get-tuple-element.397), channel_id=1, source_target_pairs={{0,4},{4,0},{8,12},{12,8},{16,20},{20,16},{24,28},{28,24},{1,5},{5... | collective-permute-start | bytes 1572872 | tf_op jit(solution)/shard_map/ppermute | solution.py:418
  36.9 40.7 %collective-permute-start.32 = (bf16[256,2048]{1,0:T(8,128)(2,1)}, bf16[256,2048]{1,0:T(8,128)(2,1)}, u32[]{:S(2)}, u32[]{:S(2)}) collective-permute-start(bf16[256,2048]{1,0:T(8,128)(2,1)} %stack_panels.1.refs_0_), channel_id=1, source_target_pairs={{0,8},{4,12},{24,16},{28,20},{1,9},{5,13},{25,17},{29,21},{2,10},{... | collective-permute-start | bytes 3145736 | tf_op jit(solution)/shard_map/ppermute | solution.py:509
  55.7 21.9 %collective-permute-start.23 = (bf16[2000,256]{1,0:T(8,128)(2,1)S(1)}, bf16[2000,256]{1,0:T(8,128)(2,1)}, u32[]{:S(2)}, u32[]{:S(2)}) collective-permute-start(bf16[2000,256]{1,0:T(8,128)(2,1)S(1)} %collective-permute-done.22.refs_1_), channel_id=1, source_target_pairs={{8,16},{12,20},{16,8},{20,12},{9,17},{13,21},{17,9},{21,13},{10,18... | collective-permute-start | bytes 3072008 | tf_op jit(solution)/shard_map/ppermute | solution.py:509
  57.4 21.3 %collective-permute-start.25 = (bf16[2000,256]{1,0:T(8,128)(2,1)S(1)}, bf16[2000,256]{1,0:T(8,128)(2,1)}, u32[]{:S(2)}, u32[]{:S(2)}) collective-permute-start(bf16[2000,256]{1,0:T(8,128)(2,1)S(1)} %collective-permute-done.24.refs_2_), channel_id=1, source_target_pairs={{8,0},{12,4},{16,24},{20,28},{9,1},{13,5},{17,25},{21,29},{10,2},{... | collective-permute-start | bytes 3072008 | tf_op jit(solution)/shard_map/ppermute | solution.py:509
  61.5 18.5 %copy-start.6 = (s32[8,32]{1,0:T(8,128)S(1)}, s32[8,32]{1,0:T(8,128)}, u32[]{:S(2)}) copy-start(s32[8,32]{1,0:T(8,128)} %param.19) | copy-start | bytes 3076
  61.5 4.3 %collective-permute-start.28 = (f32[4,4,16,256]{3,2,1,0:T(8,128)}, f32[4,4,16,256]{3,2,1,0:T(8,128)}, u32[]{:S(2)}, u32[]{:S(2)}) collective-permute-start(f32[4,4,16,256]{3,2,1,0:T(8,128)} %get-tuple-element.401), channel_id=1, source_target_pairs={{0,4},{4,0},{8,12},{12,8},{16,20},{20,16},{24,28},{28,24},{1,5},{5... | collective-permute-start | bytes 786440 | tf_op jit(solution)/shard_map/ppermute | solution.py:418
  64.0 1.8 %collective-permute-start.27 = (f32[2,4,16,256]{3,2,1,0:T(8,128)}, f32[2,4,16,256]{3,2,1,0:T(8,128)}, u32[]{:S(2)}, u32[]{:S(2)}) collective-permute-start(f32[2,4,16,256]{3,2,1,0:T(8,128)} %get-tuple-element.399), channel_id=1, source_target_pairs={{0,4},{4,0},{8,12},{12,8},{16,20},{20,16},{24,28},{28,24},{1,5},{5... | collective-permute-start | bytes 393224 | tf_op jit(solution)/shard_map/ppermute | solution.py:418
  66.9 5.1 %collective-permute-start.29 = (f32[6,16,256]{2,1,0:T(8,128)S(1)}, f32[6,16,256]{2,1,0:T(8,128)S(1)}, u32[]{:S(2)}, u32[]{:S(2)}) collective-permute-start(f32[6,16,256]{2,1,0:T(8,128)S(1)} %get-tuple-element.403), channel_id=1, source_target_pairs={{0,1},{1,0},{2,3},{3,2},{4,5},{5,4},{6,7},{7,6},{8,9},{9,8},{10,11... | collective-permute-start | bytes 294920 | tf_op jit(solution)/shard_map/ppermute | solution.py:418
  68.5 6.0 %collective-permute-start.30 = (f32[6,16,256]{2,1,0:T(8,128)S(1)}, f32[6,16,256]{2,1,0:T(8,128)S(1)}, u32[]{:S(2)}, u32[]{:S(2)}) collective-permute-start(f32[6,16,256]{2,1,0:T(8,128)S(1)} %get-tuple-element.404), channel_id=1, source_target_pairs={{0,2},{1,3},{2,0},{3,1},{4,6},{5,7},{6,4},{7,5},{8,10},{9,11},{10,... | collective-permute-start | bytes 294920 | tf_op jit(solution)/shard_map/ppermute | solution.py:418
  72.0 5.5 %collective-permute-start.31 = (f32[6,16,256]{2,1,0:T(8,128)S(1)}, f32[6,16,256]{2,1,0:T(8,128)S(1)}, u32[]{:S(2)}, u32[]{:S(2)}) collective-permute-start(f32[6,16,256]{2,1,0:T(8,128)S(1)} %get-tuple-element.405), channel_id=1, source_target_pairs={{0,3},{1,2},{2,1},{3,0},{4,7},{5,6},{6,5},{7,4},{8,11},{9,10},{10,... | collective-permute-start | bytes 294920 | tf_op jit(solution)/shard_map/ppermute | solution.py:418
  78.7 38.5 %collective-permute-start.33 = (bf16[2000,256]{1,0:T(8,128)(2,1)}, bf16[2000,256]{1,0:T(8,128)(2,1)}, u32[]{:S(2)}, u32[]{:S(2)}) collective-permute-start(bf16[2000,256]{1,0:T(8,128)(2,1)} %collective-permute-done.23.refs_5_), channel_id=1, source_target_pairs={{8,0},{12,4},{16,24},{20,28},{9,1},{13,5},{17,25},{21,29},{10,2},{... | collective-permute-start | bytes 3072008 | tf_op jit(solution)/shard_map/ppermute | solution.py:509
  83.3 1.6 %collective-permute-start = (f32[4,4,16,256]{3,2,1,0:T(8,128)S(1)}, f32[4,4,16,256]{3,2,1,0:T(8,128)S(1)}, u32[]{:S(2)}, u32[]{:S(2)}) collective-permute-start(f32[4,4,16,256]{3,2,1,0:T(8,128)S(1)} %get-tuple-element.352), channel_id=1, source_target_pairs={{0,4},{4,0},{8,12},{12,8},{16,20},{20,16},{24,28},{28,24},{1,5},{5... | collective-permute-start | bytes 786440 | tf_op jit(solution)/shard_map/cond/branch_1_fun/ppermute | solution.py:418
  85.0 4.3 %collective-permute-start.1 = (f32[4,16,256]{2,1,0:T(8,128)S(1)}, f32[4,16,256]{2,1,0:T(8,128)S(1)}, u32[]{:S(2)}, u32[]{:S(2)}) collective-permute-start(f32[4,16,256]{2,1,0:T(8,128)S(1)} %get-tuple-element.354), channel_id=1, source_target_pairs={{0,1},{1,0},{2,3},{3,2},{4,5},{5,4},{6,7},{7,6},{8,9},{9,8},{10,11... | collective-permute-start | bytes 196616 | tf_op jit(solution)/shard_map/cond/branch_1_fun/ppermute | solution.py:418
  86.5 4.3 %collective-permute-start.2 = (f32[4,16,256]{2,1,0:T(8,128)S(1)}, f32[4,16,256]{2,1,0:T(8,128)S(1)}, u32[]{:S(2)}, u32[]{:S(2)}) collective-permute-start(f32[4,16,256]{2,1,0:T(8,128)S(1)} %get-tuple-element.355), channel_id=1, source_target_pairs={{0,2},{1,3},{2,0},{3,1},{4,6},{5,7},{6,4},{7,5},{8,10},{9,11},{10,... | collective-permute-start | bytes 196616 | tf_op jit(solution)/shard_map/cond/branch_1_fun/ppermute | solution.py:418
  88.1 5.2 %collective-permute-start.3 = (f32[4,16,256]{2,1,0:T(8,128)S(1)}, f32[4,16,256]{2,1,0:T(8,128)S(1)}, u32[]{:S(2)}, u32[]{:S(2)}) collective-permute-start(f32[4,16,256]{2,1,0:T(8,128)S(1)} %get-tuple-element.356), channel_id=1, source_target_pairs={{0,3},{1,2},{2,1},{3,0},{4,7},{5,6},{6,5},{7,4},{8,11},{9,10},{10,... | collective-permute-start | bytes 196616 | tf_op jit(solution)/shard_map/cond/branch_1_fun/ppermute | solution.py:418
  93.4 7.8 %collective-permute-start.5 = (f32[4,32]{1,0:T(4,128)S(1)}, f32[4,32]{1,0:T(4,128)S(1)}, u32[]{:S(2)}, u32[]{:S(2)}) collective-permute-start(f32[4,32]{1,0:T(4,128)S(1)} %select_reduce_fusion), channel_id=1, source_target_pairs={{0,16},{4,20},{8,24},{12,28},{16,0},{20,4},{24,8},{28,12},{1,17},{... | collective-permute-start | bytes 1544 | tf_op jit(solution)/shard_map/cond/branch_1_fun/ppermute | solution.py:418
  98.5 5.5 %collective-permute-start.6 = (f32[4,32]{1,0:T(4,128)S(1)}, f32[4,32]{1,0:T(4,128)S(1)}, u32[]{:S(2)}, u32[]{:S(2)}) collective-permute-start(f32[4,32]{1,0:T(4,128)S(1)} %select_reduce_fusion), channel_id=1, source_target_pairs={{0,24},{4,28},{8,16},{12,20},{16,8},{20,12},{24,0},{28,4},{1,25},{... | collective-permute-start | bytes 1544 | tf_op jit(solution)/shard_map/cond/branch_1_fun/ppermute | solution.py:418
  101.2 5.5 %collective-permute-start.4 = (f32[36,256]{1,0:T(8,128)S(1)}, f32[36,256]{1,0:T(8,128)S(1)}, u32[]{:S(2)}, u32[]{:S(2)}) collective-permute-start(f32[36,256]{1,0:T(8,128)S(1)} %select_maximum_fusion), channel_id=1, source_target_pairs={{0,8},{4,12},{8,0},{12,4},{16,24},{20,28},{24,16},{28,20},{1,9},{5... | collective-permute-start | bytes 110600 | tf_op jit(solution)/shard_map/cond/branch_1_fun/ppermute | solution.py:418
  106.9 4.0 %collective-permute-start.7 = (bf16[8,1,16,128]{3,2,1,0:T(8,128)(2,1)S(1)}, bf16[8,1,16,128]{3,2,1,0:T(8,128)(2,1)S(1)}, u32[]{:S(2)}, u32[]{:S(2)}) collective-permute-start(bf16[8,1,16,128]{3,2,1,0:T(8,128)(2,1)S(1)} %bitcast.68), channel_id=1, source_target_pairs={{0,1},{1,0},{2,3},{3,2},{4,5},{5,4},{6,7},{7,6},{8,9},{9,8},{10,11... | collective-permute-start | bytes 98312 | tf_op jit(solution)/shard_map/cond/branch_1_fun/ppermute | solution.py:418
  108.5 3.9 %collective-permute-start.8 = (bf16[8,1,16,128]{3,2,1,0:T(8,128)(2,1)S(1)}, bf16[8,1,16,128]{3,2,1,0:T(8,128)(2,1)S(1)}, u32[]{:S(2)}, u32[]{:S(2)}) collective-permute-start(bf16[8,1,16,128]{3,2,1,0:T(8,128)(2,1)S(1)} %bitcast.69), channel_id=1, source_target_pairs={{0,2},{1,3},{2,0},{3,1},{4,6},{5,7},{6,4},{7,5},{8,10},{9,11},{10,... | collective-permute-start | bytes 98312 | tf_op jit(solution)/shard_map/cond/branch_1_fun/ppermute | solution.py:418
  110.0 4.8 %collective-permute-start.9 = (bf16[8,1,16,128]{3,2,1,0:T(8,128)(2,1)S(1)}, bf16[8,1,16,128]{3,2,1,0:T(8,128)(2,1)S(1)}, u32[]{:S(2)}, u32[]{:S(2)}) collective-permute-start(bf16[8,1,16,128]{3,2,1,0:T(8,128)(2,1)S(1)} %bitcast.70), channel_id=1, source_target_pairs={{0,3},{1,2},{2,1},{3,0},{4,7},{5,6},{6,5},{7,4},{8,11},{9,10},{10,... | collective-permute-start | bytes 98312 | tf_op jit(solution)/shard_map/cond/branch_1_fun/ppermute | solution.py:418
  115.5 1.7 %collective-permute-start.10 = (bf16[8,4,16,128]{3,2,1,0:T(8,128)(2,1)}, bf16[8,4,16,128]{3,2,1,0:T(8,128)(2,1)}, u32[]{:S(2)}, u32[]{:S(2)}) collective-permute-start(bf16[8,4,16,128]{3,2,1,0:T(8,128)(2,1)} %in_order.1), channel_id=1, source_target_pairs={{0,4},{4,0},{8,12},{12,8},{16,20},{20,16},{24,28},{28,24},{1,5},{5... | collective-permute-start | bytes 393224 | tf_op jit(solution)/shard_map/cond/branch_1_fun/ppermute | solution.py:418
  120.5 2.0 %collective-permute-start.34 = (f32[64,2000]{1,0:T(8,128)S(1)}, f32[64,2000]{1,0:T(8,128)S(1)}, u32[]{:S(2)}, u32[]{:S(2)}) collective-permute-start(f32[64,2000]{1,0:T(8,128)S(1)} %get-tuple-element.417), channel_id=1, source_target_pairs={{0,4},{4,0},{8,12},{12,8},{16,20},{20,16},{24,28},{28,24},{1,5},{5... | collective-permute-start | bytes 1536008 | tf_op jit(solution)/shard_map/ppermute | solution.py:418

commit v9 on v8

--- a/solution.py
+++ b/solution.py
@@ -585,11 +585,8 @@
     early_jobs = stages[0] + early_jobs
     early_at = jnp.concatenate((chip[None], early_at))
 
-    own_pair = project([(panels, early_jobs[0][0])], tile, shares, core)
-    early_pair = project([(panels, w) for w, _ in early_jobs[1:]], tile, shares, core)
-    early_value = summed(
-        [(keep, flip(give, "grid", 1)) for keep, give in (own_pair, early_pair)]
-    )
+    keep, give = project([(panels, w) for w, _ in early_jobs], tile, shares, core)
+    early_value = summed([(keep, flip(give, "grid", 1))])
 
     outer = jnp.where(chip == 0, last, jnp.where(chip == last, 0, early_at[2]))
     places = jnp.concatenate((early_at[:2], outer[None], early_at[3:], late_at))

time: 125 us -> 123 us (0.984)
  Pallas kernels: 21.4 us -> 19.2 us
  starting transfers between devices: 44.6 us -> 42.5 us
  waiting for transfers between devices: 47.9 us -> 49.8 us
    ppermute x24 -> x23, starting transfers between devices: 28.1 us -> 26 us  [flip(): return lax.ppermute(x, axis, [(i, i ^ bit) for i in range(count)])]
    pallas_call x3 -> x2, Pallas kernels: 8.32 us -> 6.2 us  [project(): pl.pallas_call(body, out_shape=(shape, shape), in_specs=[SCALARS] + [WHOL...]
    ppermute x8, waiting for transfers between devices: 20.7 us -> 22.7 us  [sent(): return lax.ppermute(x, 'grid', along(pairs))]
    ppermute x24 -> x23, waiting for transfers between devices: 27.3 us -> 27.1 us  [flip(): return lax.ppermute(x, axis, [(i, i ^ bit) for i in range(count)])]
  transfers between devices with their start and end apart: 32 -> 31, of which waited for: 18 -> 18; matrix products, arithmetic and copies ran while one was open for 5% -> 5% of each run, Pallas kernels for 11% -> 10%
where the time goes in v9:
time: 123 us; the launch traced here: 122 us
  waiting for transfers between devices  49.8 us (40%)
  starting transfers between devices  42.5 us (35%)
  Pallas kernels  19.2 us (16%)
  local copies, waits for them, and re-layouts  4.32 us (4%)
  other arithmetic  4.14 us (3%)
  between operations  1.79 us (1%)
    ppermute x23, waiting for transfers between devices, flip(): return lax.ppermute(x, axis, [(i, i ^ bit) for i in range(count)])  27.1 us
    ppermute x23, starting transfers between devices, flip(): return lax.ppermute(x, axis, [(i, i ^ bit) for i in range(count)])  26 us
    ppermute x8, waiting for transfers between devices, sent(): return lax.ppermute(x, 'grid', along(pairs))  22.7 us
    ppermute x8, starting transfers between devices, sent(): return lax.ppermute(x, 'grid', along(pairs))  16.6 us
    pallas_call x2, Pallas kernels, project(): pl.pallas_call(body, out_shape=(shape, shape), in_specs=[SCALARS] + [WHOL...  6.2 us
    pallas_call x1, Pallas kernels, contract(): pl.pallas_call(body, out_shape=(shape, shape), in_specs=[SCALARS] + [WHOL...  3.3 us
  transfers between devices with their start and end apart: 31, of which 18 were waited for; matrix products, arithmetic and copies ran while one was open for 5% of the time, Pallas kernels for 10%

profile of v9, /device:TPU:0, one launch (start us, length us, event | category | flops | bytes accessed | tf_op | source)
XLA Modules:
  0.0 122.0 jit_solution(4259932588716750409)
XLA Ops:
  0.5 0.8 dynamic-slice_bitcast_fusion
  1.8 1.2 %half_of.3 = bf16[2000,256]{1,0:T(8,128)(2,1)S(1)} custom-call(s32[1]{0:T(128)} %bitcast.13.which_ref, bf16[4000,256]{1,0:T(8,128)(2,1)} %bitcast.72), custom_call_target="tpu_custom_call" | custom-call | tf_op jit(solution)/shard_map/half_of/pallas_call | solution.py:82
  3.5 3.0 %collective-permute-start.18 = (f32[1,528]{1,0:T(1,128)S(1)}, f32[1,528]{1,0:T(1,128)S(1)}, u32[]{:S(2)}, u32[]{:S(2)}) collective-permute-start(f32[1,528]{1,0:T(1,128)S(1)} %pad_maximum_fusion.3), channel_id=1, source_target_pairs={{0,8},{4,12},{8,0},{12,4},{16,24},{20,28},{24,16},{28,20},{1,9},{5... | collective-permute-start | bytes 6344 | tf_op jit(solution)/shard_map/ppermute | solution.py:418
  6.8 1.2 %half_of.2.mine_ref = bf16[2000,256]{1,0:T(8,128)(2,1)S(1)} custom-call(s32[1]{0:T(128)} %bitcast.10.which_ref.core_ref, bf16[4000,256]{1,0:T(8,128)(2,1)} %bitcast.73), custom_call_target="tpu_custom_call" | custom-call | tf_op jit(solution)/shard_map/half_of/pallas_call | solution.py:82
  9.5 0.9 copy-done
  10.5 1.2 copy-done.1
  11.7 1.8 %compact.1 = (bf16[2000,128]{1,0:T(8,128)(2,1)S(1)}, bf16[2000,128]{1,0:T(8,128)(2,1)S(1)}, bf16[2000,128]{1,0:T(8,128)(2,1)S(1)}, bf16[2000,128]{1,0:T(8,128)(2,1)S(1)}) custom-call(s32[1]{0:T(128)} %bitcast.11.odd_ref, bf16[2000,256]{1,0:T(8,128)(2,1)S(1)} %half_of.2.mine_ref, bf16[2000,256]{1,0:T(8,128)(2,1)S(1)} %copy-done.1, ...), custom_call_target="tpu_custom_call" | custom-call | flops 1048576000 | bytes 4096000 | tf_op jit(solution)/shard_map/compact/pallas_call | solution.py:124
  13.5 2.7 %collective-permute-start.21 = (f32[2,528]{1,0:T(2,128)S(1)}, f32[2,528]{1,0:T(2,128)S(1)}, u32[]{:S(2)}, u32[]{:S(2)}) collective-permute-start(f32[2,528]{1,0:T(2,128)S(1)} %maximum_select_fusion.1), channel_id=1, source_target_pairs={{0,16},{4,20},{8,24},{12,28},{16,0},{20,4},{24,8},{28,12},{1,17},{... | collective-permute-start | bytes 12680 | tf_op jit(solution)/shard_map/ppermute | solution.py:418
  17.1 2.9 %collective-permute-start.20 = (bf16[2000,128]{1,0:T(8,128)(2,1)S(1)}, bf16[2000,128]{1,0:T(8,128)(2,1)S(1)}, u32[]{:S(2)}, u32[]{:S(2)}) collective-permute-start(bf16[2000,128]{1,0:T(8,128)(2,1)S(1)} %get-tuple-element.389), channel_id=1, source_target_pairs={{0,8},{4,12},{8,0},{12,4},{16,24},{20,28},{24,16},{28,20},{1,9},{5... | collective-permute-start | bytes 1536008 | tf_op jit(solution)/shard_map/ppermute | solution.py:509
  23.6 6.8 %collective-permute-done.20.refs_3_ = bf16[2000,128]{1,0:T(8,128)(2,1)S(1)} collective-permute-done((bf16[2000,128]{1,0:T(8,128)(2,1)S(1)}, bf16[2000,128]{1,0:T(8,128)(2,1)S(1)}, u32[]{:S(2)}, u32[]{:S(2)}) %collective-permute-start.20) | collective-permute-done | bytes 512032 | tf_op jit(solution)/shard_map/ppermute | solution.py:509
  30.8 1.8 %collective-permute-start.22 = (bf16[2000,256]{1,0:T(8,128)(2,1)S(1)}, bf16[2000,256]{1,0:T(8,128)(2,1)S(1)}, u32[]{:S(2)}, u32[]{:S(2)}) collective-permute-start(bf16[2000,256]{1,0:T(8,128)(2,1)S(1)} %straighten.1.refs_1_.refs_0_), channel_id=1, source_target_pairs={{0,8},{4,12},{8,0},{12,4},{16,24},{20,28},{24,16},{28,20},{1,9},{5... | collective-permute-start | bytes 3072008 | tf_op jit(solution)/shard_map/ppermute | solution.py:509
  32.6 0.7 collective-permute-start.24
  33.9 1.9 %collective-permute-done.26.got_ref = bf16[128,2048]{1,0:T(8,128)(2,1)S(1)} collective-permute-done((bf16[128,2048]{1,0:T(8,128)(2,1)S(1)}, bf16[128,2048]{1,0:T(8,128)(2,1)S(1)}, u32[]{:S(2)}, u32[]{:S(2)}) %collective-permute-start.26) | collective-permute-done | bytes 524320 | tf_op jit(solution)/shard_map/ppermute | solution.py:418
  35.8 1.1 stack_panels.1.refs_0_
  36.9 6.2 %collective-permute-start.31 = (bf16[256,2048]{1,0:T(8,128)(2,1)}, bf16[256,2048]{1,0:T(8,128)(2,1)}, u32[]{:S(2)}, u32[]{:S(2)}) collective-permute-start(bf16[256,2048]{1,0:T(8,128)(2,1)} %stack_panels.1.refs_0_), channel_id=1, source_target_pairs={{0,8},{4,12},{24,16},{28,20},{1,9},{5,13},{25,17},{29,21},{2,10},{... | collective-permute-start | bytes 3145736 | tf_op jit(solution)/shard_map/ppermute | solution.py:509
  43.1 12.5 %collective-permute-done.22.refs_2_.refs_1_ = bf16[2000,256]{1,0:T(8,128)(2,1)S(1)} collective-permute-done((bf16[2000,256]{1,0:T(8,128)(2,1)S(1)}, bf16[2000,256]{1,0:T(8,128)(2,1)S(1)}, u32[]{:S(2)}, u32[]{:S(2)}) %collective-permute-start.22) | collective-permute-done | bytes 1024032 | tf_op jit(solution)/shard_map/ppermute | solution.py:509
  55.7 1.7 %collective-permute-start.23 = (bf16[2000,256]{1,0:T(8,128)(2,1)S(1)}, bf16[2000,256]{1,0:T(8,128)(2,1)}, u32[]{:S(2)}, u32[]{:S(2)}) collective-permute-start(bf16[2000,256]{1,0:T(8,128)(2,1)S(1)} %collective-permute-done.22.refs_2_.refs_1_), channel_id=1, source_target_pairs={{8,16},{12,20},{16,8},{20,12},{9,17},{13,21},{17,9},{21,13},{10,18... | collective-permute-start | bytes 3072008 | tf_op jit(solution)/shard_map/ppermute | solution.py:509
  57.4 1.3 %collective-permute-start.25 = (bf16[2000,256]{1,0:T(8,128)(2,1)S(1)}, bf16[2000,256]{1,0:T(8,128)(2,1)}, u32[]{:S(2)}, u32[]{:S(2)}) collective-permute-start(bf16[2000,256]{1,0:T(8,128)(2,1)S(1)} %collective-permute-done.24.refs_3_.refs_2_), channel_id=1, source_target_pairs={{8,0},{12,4},{16,24},{20,28},{9,1},{13,5},{17,25},{21,29},{10,2},{... | collective-permute-start | bytes 3072008 | tf_op jit(solution)/shard_map/ppermute | solution.py:509
  58.6 3.2 %project.3 = (f32[6,4,16,256]{3,2,1,0:T(8,128)S(1)}, f32[6,4,16,256]{3,2,1,0:T(8,128)}) custom-call(s32[1]{0:T(128)} %bitcast.10.which_ref.core_ref, bf16[256,2048]{1,0:T(8,128)(2,1)} %stack_panels.1.refs_0_, bf16[2000,256]{1,0:T(8,128)(2,1)S(1)} %straighten.1.refs_1_.refs_0_, bf16[2000,256]{1,0:T(8,128)(2,1)S(1)} %collective-permute-done.22.refs_2_.refs_1_, ...), custom_call_target="tpu_custom_call" | custom-call | flops 786432000 | bytes 4882432 | tf_op jit(solution)/shard_map/project/pallas_call | solution.py:281
  61.9 2.0 %collective-permute-done.27.refs_1_ = f32[6,4,16,256]{3,2,1,0:T(8,128)} collective-permute-done((f32[6,4,16,256]{3,2,1,0:T(8,128)}, f32[6,4,16,256]{3,2,1,0:T(8,128)}, u32[]{:S(2)}, u32[]{:S(2)}) %collective-permute-start.27) | collective-permute-done | bytes 393248 | tf_op jit(solution)/shard_map/ppermute | solution.py:418
  63.9 1.0 split_sum.3
  64.9 1.6 %collective-permute-start.28 = (f32[6,16,256]{2,1,0:T(8,128)S(1)}, f32[6,16,256]{2,1,0:T(8,128)S(1)}, u32[]{:S(2)}, u32[]{:S(2)}) collective-permute-start(f32[6,16,256]{2,1,0:T(8,128)S(1)} %get-tuple-element.399), channel_id=1, source_target_pairs={{0,1},{1,0},{2,3},{3,2},{4,5},{5,4},{6,7},{7,6},{8,9},{9,8},{10,11... | collective-permute-start | bytes 294920 | tf_op jit(solution)/shard_map/ppermute | solution.py:418
  66.6 1.5 %collective-permute-start.29 = (f32[6,16,256]{2,1,0:T(8,128)S(1)}, f32[6,16,256]{2,1,0:T(8,128)S(1)}, u32[]{:S(2)}, u32[]{:S(2)}) collective-permute-start(f32[6,16,256]{2,1,0:T(8,128)S(1)} %get-tuple-element.400), channel_id=1, source_target_pairs={{0,2},{1,3},{2,0},{3,1},{4,6},{5,7},{6,4},{7,5},{8,10},{9,11},{10,... | collective-permute-start | bytes 294920 | tf_op jit(solution)/shard_map/ppermute | solution.py:418
  68.1 1.8 %collective-permute-done.28 = f32[6,16,256]{2,1,0:T(8,128)S(1)} collective-permute-done((f32[6,16,256]{2,1,0:T(8,128)S(1)}, f32[6,16,256]{2,1,0:T(8,128)S(1)}, u32[]{:S(2)}, u32[]{:S(2)}) %collective-permute-start.28) | collective-permute-done | bytes 98336 | tf_op jit(solution)/shard_map/ppermute | solution.py:418
  69.8 2.4 %collective-permute-start.30 = (f32[6,16,256]{2,1,0:T(8,128)S(1)}, f32[6,16,256]{2,1,0:T(8,128)S(1)}, u32[]{:S(2)}, u32[]{:S(2)}) collective-permute-start(f32[6,16,256]{2,1,0:T(8,128)S(1)} %get-tuple-element.401), channel_id=1, source_target_pairs={{0,3},{1,2},{2,1},{3,0},{4,7},{5,6},{6,5},{7,4},{8,11},{9,10},{10,... | collective-permute-start | bytes 294920 | tf_op jit(solution)/shard_map/ppermute | solution.py:418
  72.4 3.0 %collective-permute-done.30 = f32[6,16,256]{2,1,0:T(8,128)S(1)} collective-permute-done((f32[6,16,256]{2,1,0:T(8,128)S(1)}, f32[6,16,256]{2,1,0:T(8,128)S(1)}, u32[]{:S(2)}, u32[]{:S(2)}) %collective-permute-start.30) | collective-permute-done | bytes 98336 | tf_op jit(solution)/shard_map/ppermute | solution.py:418
  75.4 3.3 %collective-permute-done.25.refs_4_ = bf16[2000,256]{1,0:T(8,128)(2,1)} collective-permute-done((bf16[2000,256]{1,0:T(8,128)(2,1)S(1)}, bf16[2000,256]{1,0:T(8,128)(2,1)}, u32[]{:S(2)}, u32[]{:S(2)}) %collective-permute-start.25) | collective-permute-done | bytes 1024032 | tf_op jit(solution)/shard_map/ppermute | solution.py:509
  78.7 1.3 %collective-permute-start.32 = (bf16[2000,256]{1,0:T(8,128)(2,1)}, bf16[2000,256]{1,0:T(8,128)(2,1)}, u32[]{:S(2)}, u32[]{:S(2)}) collective-permute-start(bf16[2000,256]{1,0:T(8,128)(2,1)} %collective-permute-done.23.refs_5_), channel_id=1, source_target_pairs={{8,0},{12,4},{16,24},{20,28},{9,1},{13,5},{17,25},{21,29},{10,2},{... | collective-permute-start | bytes 3072008 | tf_op jit(solution)/shard_map/ppermute | solution.py:509
  80.0 34.7 %conditional.1 = (bf16[8,4,16,128]{3,2,1,0:T(8,128)(2,1)}, bf16[8,4,16,128]{3,2,1,0:T(8,128)(2,1)}, f32[64,4000]{1,0:T(8,128)}) conditional(s32[]{:T(128)} %convert_element_type.61, (s32[8]{0:T(128)S(1)}, f32[256]{0:T(256)S(1)}, bf16[4000,64]{0,1:T(8,128)(2,1)}, bf16[4000,64]{0,1:T(8,128)(2,1)}, s32[8,32]{1,0:T(8,128)S(1)}, ...), branch_computations={%region_6.14_spmd, %region_14.18_spmd} | conditional | flops 524588416 | bytes 57519072 | solution.py:646
  80.2 3.0 %project.2 = (f32[4,4,16,256]{3,2,1,0:T(8,128)S(1)}, f32[4,4,16,256]{3,2,1,0:T(8,128)S(1)}) custom-call(s32[1]{0:T(128)} %bitcast.4.core_ref, bf16[256,2048]{1,0:T(8,128)(2,1)} %get-tuple-element.347.refs_0_, bf16[256,2048]{1,0:T(8,128)(2,1)} %get-tuple-element.348.refs_1_, bf16[2000,256]{1,0:T(8,128)(2,1)} %get-tuple-element.349.refs_2_, ...), custom_call_target="tpu_custom_call" | custom-call | flops 524288000 | bytes 3596288 | tf_op jit(solution)/shard_map/cond/branch_1_fun/project/pallas_call | solution.py:281
  83.5 1.4 %collective-permute-done.refs_1_ = f32[4,4,16,256]{3,2,1,0:T(8,128)S(1)} collective-permute-done((f32[4,4,16,256]{3,2,1,0:T(8,128)S(1)}, f32[4,4,16,256]{3,2,1,0:T(8,128)S(1)}, u32[]{:S(2)}, u32[]{:S(2)}) %collective-permute-start) | collective-permute-done | bytes 262176 | tf_op jit(solution)/shard_map/cond/branch_1_fun/ppermute | solution.py:418
  84.9 1.6 %collective-permute-start.1 = (f32[4,16,256]{2,1,0:T(8,128)S(1)}, f32[4,16,256]{2,1,0:T(8,128)S(1)}, u32[]{:S(2)}, u32[]{:S(2)}) collective-permute-start(f32[4,16,256]{2,1,0:T(8,128)S(1)} %get-tuple-element.354), channel_id=1, source_target_pairs={{0,1},{1,0},{2,3},{3,2},{4,5},{5,4},{6,7},{7,6},{8,9},{9,8},{10,11... | collective-permute-start | bytes 196616 | tf_op jit(solution)/shard_map/cond/branch_1_fun/ppermute | solution.py:418
  86.5 1.5 %collective-permute-start.2 = (f32[4,16,256]{2,1,0:T(8,128)S(1)}, f32[4,16,256]{2,1,0:T(8,128)S(1)}, u32[]{:S(2)}, u32[]{:S(2)}) collective-permute-start(f32[4,16,256]{2,1,0:T(8,128)S(1)} %get-tuple-element.355), channel_id=1, source_target_pairs={{0,2},{1,3},{2,0},{3,1},{4,6},{5,7},{6,4},{7,5},{8,10},{9,11},{10,... | collective-permute-start | bytes 196616 | tf_op jit(solution)/shard_map/cond/branch_1_fun/ppermute | solution.py:418
  88.6 0.7 collective-permute-done.1
  89.3 1.5 %collective-permute-done.2 = f32[4,16,256]{2,1,0:T(8,128)S(1)} collective-permute-done((f32[4,16,256]{2,1,0:T(8,128)S(1)}, f32[4,16,256]{2,1,0:T(8,128)S(1)}, u32[]{:S(2)}, u32[]{:S(2)}) %collective-permute-start.2) | collective-permute-done | bytes 65568 | tf_op jit(solution)/shard_map/cond/branch_1_fun/ppermute | solution.py:418
  90.8 2.4 %collective-permute-done.3 = f32[4,16,256]{2,1,0:T(8,128)S(1)} collective-permute-done((f32[4,16,256]{2,1,0:T(8,128)S(1)}, f32[4,16,256]{2,1,0:T(8,128)S(1)}, u32[]{:S(2)}, u32[]{:S(2)}) %collective-permute-start.3) | collective-permute-done | bytes 65568 | tf_op jit(solution)/shard_map/cond/branch_1_fun/ppermute | solution.py:418
  93.4 4.4 %collective-permute-start.5 = (f32[4,32]{1,0:T(4,128)S(1)}, f32[4,32]{1,0:T(4,128)S(1)}, u32[]{:S(2)}, u32[]{:S(2)}) collective-permute-start(f32[4,32]{1,0:T(4,128)S(1)} %select_reduce_fusion), channel_id=1, source_target_pairs={{0,16},{4,20},{8,24},{12,28},{16,0},{20,4},{24,8},{28,12},{1,17},{... | collective-permute-start | bytes 1544 | tf_op jit(solution)/shard_map/cond/branch_1_fun/ppermute | solution.py:418
  97.8 1.8 %collective-permute-start.6 = (f32[4,32]{1,0:T(4,128)S(1)}, f32[4,32]{1,0:T(4,128)S(1)}, u32[]{:S(2)}, u32[]{:S(2)}) collective-permute-start(f32[4,32]{1,0:T(4,128)S(1)} %select_reduce_fusion), channel_id=1, source_target_pairs={{0,24},{4,28},{8,16},{12,20},{16,8},{20,12},{24,0},{28,4},{1,25},{... | collective-permute-start | bytes 1544 | tf_op jit(solution)/shard_map/cond/branch_1_fun/ppermute | solution.py:418
  99.6 3.6 %collective-permute-done.6 = f32[4,32]{1,0:T(4,128)S(1)} collective-permute-done((f32[4,32]{1,0:T(4,128)S(1)}, f32[4,32]{1,0:T(4,128)S(1)}, u32[]{:S(2)}, u32[]{:S(2)}) %collective-permute-start.6) | collective-permute-done | bytes 544 | tf_op jit(solution)/shard_map/cond/branch_1_fun/ppermute | solution.py:418
  103.2 1.1 collective-permute-done.4
  104.6 1.6 %collective-permute-start.7 = (bf16[8,1,16,128]{3,2,1,0:T(8,128)(2,1)S(1)}, bf16[8,1,16,128]{3,2,1,0:T(8,128)(2,1)S(1)}, u32[]{:S(2)}, u32[]{:S(2)}) collective-permute-start(bf16[8,1,16,128]{3,2,1,0:T(8,128)(2,1)S(1)} %bitcast.68), channel_id=1, source_target_pairs={{0,1},{1,0},{2,3},{3,2},{4,5},{5,4},{6,7},{7,6},{8,9},{9,8},{10,11... | collective-permute-start | bytes 98312 | tf_op jit(solution)/shard_map/cond/branch_1_fun/ppermute | solution.py:418
  106.1 1.5 %collective-permute-start.8 = (bf16[8,1,16,128]{3,2,1,0:T(8,128)(2,1)S(1)}, bf16[8,1,16,128]{3,2,1,0:T(8,128)(2,1)S(1)}, u32[]{:S(2)}, u32[]{:S(2)}) collective-permute-start(bf16[8,1,16,128]{3,2,1,0:T(8,128)(2,1)S(1)} %bitcast.69), channel_id=1, source_target_pairs={{0,2},{1,3},{2,0},{3,1},{4,6},{5,7},{6,4},{7,5},{8,10},{9,11},{10,... | collective-permute-start | bytes 98312 | tf_op jit(solution)/shard_map/cond/branch_1_fun/ppermute | solution.py:418
  108.5 1.5 %collective-permute-done.8.refs_2_ = bf16[8,1,16,128]{3,2,1,0:T(8,128)(2,1)S(1)} collective-permute-done((bf16[8,1,16,128]{3,2,1,0:T(8,128)(2,1)S(1)}, bf16[8,1,16,128]{3,2,1,0:T(8,128)(2,1)S(1)}, u32[]{:S(2)}, u32[]{:S(2)}) %collective-permute-start.8) | collective-permute-done | bytes 32800 | tf_op jit(solution)/shard_map/cond/branch_1_fun/ppermute | solution.py:418
  110.0 2.4 %collective-permute-done.9.refs_3_ = bf16[8,1,16,128]{3,2,1,0:T(8,128)(2,1)S(1)} collective-permute-done((bf16[8,1,16,128]{3,2,1,0:T(8,128)(2,1)S(1)}, bf16[8,1,16,128]{3,2,1,0:T(8,128)(2,1)S(1)}, u32[]{:S(2)}, u32[]{:S(2)}) %collective-permute-start.9) | collective-permute-done | bytes 32800 | tf_op jit(solution)/shard_map/cond/branch_1_fun/ppermute | solution.py:418
  113.1 1.7 %collective-permute-done.10 = bf16[8,4,16,128]{3,2,1,0:T(8,128)(2,1)} collective-permute-done((bf16[8,4,16,128]{3,2,1,0:T(8,128)(2,1)}, bf16[8,4,16,128]{3,2,1,0:T(8,128)(2,1)}, u32[]{:S(2)}, u32[]{:S(2)}) %collective-permute-start.10) | collective-permute-done | bytes 131104 | tf_op jit(solution)/shard_map/cond/branch_1_fun/ppermute | solution.py:418
  114.8 3.3 %contract.1 = (f32[64,2000]{1,0:T(8,128)S(1)}, f32[64,2000]{1,0:T(8,128)S(1)}) custom-call(s32[1]{0:T(128)} %bitcast.10.which_ref.core_ref, bf16[8,4,16,128]{3,2,1,0:T(8,128)(2,1)} %get-tuple-element.409.kernel_ref, bf16[8,4,16,128]{3,2,1,0:T(8,128)(2,1)} %get-tuple-element.410.got_ref, bf16[2000,256]{1,0:T(8,128)(2,1)S(1)} %straighten.1.refs_1_.refs_0_, ...), custom_call_target="tpu_custom_call" | custom-call | flops 524288000 | bytes 5120000 | tf_op jit(solution)/shard_map/contract/pallas_call | solution.py:346
  118.4 1.7 %collective-permute-done.33.back_ref = f32[64,2000]{1,0:T(8,128)S(1)} collective-permute-done((f32[64,2000]{1,0:T(8,128)S(1)}, f32[64,2000]{1,0:T(8,128)S(1)}, u32[]{:S(2)}, u32[]{:S(2)}) %collective-permute-start.33) | collective-permute-done | bytes 512032 | tf_op jit(solution)/shard_map/ppermute | solution.py:418
  120.1 1.8 %finish.1 = f32[64,4000]{1,0:T(8,128)} custom-call(s32[2]{0:T(128)S(1)} %pad_add_fusion.2.flags_ref, f32[64,2000]{1,0:T(8,128)S(1)} %get-tuple-element.412.ours_ref, f32[64,2000]{1,0:T(8,128)S(1)} %collective-permute-done.33.back_ref, f32[64,4000]{1,0:T(8,128)} %get-tuple-element.414.other_ref), custom_call_target="tpu_custom_call", output_to_operand_aliasing={{}: (3, {})} | custom-call | tf_op jit(solution)/shard_map/finish/pallas_call | solution.py:387
  (114 shorter events, 10.6 us)
Async XLA Ops:
  0.0 3.4 %copy-start.5 = (f32[256]{0:T(256)S(1)}, f32[256]{0:T(256)}, u32[]{:S(2)}) copy-start(f32[256]{0:T(256)} %param.17) | copy-start | bytes 3076
  0.0 3.3 %copy-start.6 = (s32[8]{0:T(128)S(1)}, s32[8]{0:T(128)}, u32[]{:S(2)}) copy-start(s32[8]{0:T(128)} %param.18) | copy-start | bytes 100
  0.0 3.4 %collective-permute-start.17 = (f32[1,256]{1,0:T(1,128)}, f32[1,256]{1,0:T(1,128)S(1)}, u32[]{:S(2)}, u32[]{:S(2)}) collective-permute-start(f32[1,256]{1,0:T(1,128)} %bitcast.85), channel_id=1, source_target_pairs={{0,4},{4,0},{8,12},{12,8},{16,20},{20,16},{24,28},{28,24},{1,5},{5... | collective-permute-start | bytes 3080 | tf_op jit(solution)/shard_map/ppermute | solution.py:418
  0.5 2.8 %collective-permute-start.16 = (s32[1,8]{1,0:T(1,128)}, s32[1,8]{1,0:T(1,128)S(1)}, u32[]{:S(2)}, u32[]{:S(2)}) collective-permute-start(s32[1,8]{1,0:T(1,128)} %bitcast.87), channel_id=1, source_target_pairs={{0,4},{4,0},{8,12},{12,8},{16,20},{20,16},{24,28},{28,24},{1,5},{5... | collective-permute-start | bytes 104 | tf_op jit(solution)/shard_map/ppermute | solution.py:418
  1.4 6.7 %collective-permute-start.15 = (s32[16,8]{0,1:T(8,128)S(1)}, s32[16,8]{0,1:T(8,128)S(1)}, u32[]{:S(2)}, u32[]{:S(2)}) collective-permute-start(s32[16,8]{0,1:T(8,128)S(1)} %get-tuple-element.483), channel_id=1, source_target_pairs={{0,4},{4,0},{8,12},{12,8},{16,20},{20,16},{24,28},{28,24},{1,5},{5... | collective-permute-start | bytes 1544 | tf_op jit(solution)/shard_map/ppermute | solution.py:418
  3.0 6.5 %collective-permute-start.14 = (bf16[2000,256]{1,0:T(8,128)(2,1)S(1)}, bf16[2000,256]{1,0:T(8,128)(2,1)S(1)}, u32[]{:S(2)}, u32[]{:S(2)}) collective-permute-start(bf16[2000,256]{1,0:T(8,128)(2,1)S(1)} %half_of.3), channel_id=1, source_target_pairs={{0,4},{4,0},{8,12},{12,8},{16,20},{20,16},{24,28},{28,24},{1,5},{5... | collective-permute-start | bytes 3072008 | tf_op jit(solution)/shard_map/ppermute | solution.py:418
  3.5 4.9 %collective-permute-start.18 = (f32[1,528]{1,0:T(1,128)S(1)}, f32[1,528]{1,0:T(1,128)S(1)}, u32[]{:S(2)}, u32[]{:S(2)}) collective-permute-start(f32[1,528]{1,0:T(1,128)S(1)} %pad_maximum_fusion.3), channel_id=1, source_target_pairs={{0,8},{4,12},{8,0},{12,4},{16,24},{20,28},{24,16},{28,20},{1,9},{5... | collective-permute-start | bytes 6344 | tf_op jit(solution)/shard_map/ppermute | solution.py:418
  9.5 1.0 copy-start
  10.5 1.2 copy-start.1
  13.5 6.5 %collective-permute-start.21 = (f32[2,528]{1,0:T(2,128)S(1)}, f32[2,528]{1,0:T(2,128)S(1)}, u32[]{:S(2)}, u32[]{:S(2)}) collective-permute-start(f32[2,528]{1,0:T(2,128)S(1)} %maximum_select_fusion.1), channel_id=1, source_target_pairs={{0,16},{4,20},{8,24},{12,28},{16,0},{20,4},{24,8},{28,12},{1,17},{... | collective-permute-start | bytes 12680 | tf_op jit(solution)/shard_map/ppermute | solution.py:418
  16.4 7.2 %collective-permute-start.19 = (bf16[2000,128]{1,0:T(8,128)(2,1)S(1)}, bf16[2000,128]{1,0:T(8,128)(2,1)S(1)}, u32[]{:S(2)}, u32[]{:S(2)}) collective-permute-start(bf16[2000,128]{1,0:T(8,128)(2,1)S(1)} %get-tuple-element.388), channel_id=1, source_target_pairs={{8,16},{12,20},{16,8},{20,12},{9,17},{13,21},{17,9},{21,13},{10,18... | collective-permute-start | bytes 1536008 | tf_op jit(solution)/shard_map/ppermute | solution.py:509
  17.1 13.3 %collective-permute-start.20 = (bf16[2000,128]{1,0:T(8,128)(2,1)S(1)}, bf16[2000,128]{1,0:T(8,128)(2,1)S(1)}, u32[]{:S(2)}, u32[]{:S(2)}) collective-permute-start(bf16[2000,128]{1,0:T(8,128)(2,1)S(1)} %get-tuple-element.389), channel_id=1, source_target_pairs={{0,8},{4,12},{8,0},{12,4},{16,24},{20,28},{24,16},{28,20},{1,9},{5... | collective-permute-start | bytes 1536008 | tf_op jit(solution)/shard_map/ppermute | solution.py:509
  23.5 9.8 %copy-start.2 = (bf16[4000,64]{0,1:T(8,128)(2,1)S(1)}, bf16[4000,64]{0,1:T(8,128)(2,1)}, u32[]{:S(2)}) copy-start(bf16[4000,64]{0,1:T(8,128)(2,1)} %param.15) | copy-start | bytes 1536004
  23.6 9.7 %copy-start.3 = (bf16[4000,64]{0,1:T(8,128)(2,1)S(1)}, bf16[4000,64]{0,1:T(8,128)(2,1)}, u32[]{:S(2)}) copy-start(bf16[4000,64]{0,1:T(8,128)(2,1)} %param.16) | copy-start | bytes 1536004
  30.8 24.9 %collective-permute-start.22 = (bf16[2000,256]{1,0:T(8,128)(2,1)S(1)}, bf16[2000,256]{1,0:T(8,128)(2,1)S(1)}, u32[]{:S(2)}, u32[]{:S(2)}) collective-permute-start(bf16[2000,256]{1,0:T(8,128)(2,1)S(1)} %straighten.1.refs_1_.refs_0_), channel_id=1, source_target_pairs={{0,8},{4,12},{8,0},{12,4},{16,24},{20,28},{24,16},{28,20},{1,9},{5... | collective-permute-start | bytes 3072008 | tf_op jit(solution)/shard_map/ppermute | solution.py:509
  32.6 24.8 %collective-permute-start.24 = (bf16[2000,256]{1,0:T(8,128)(2,1)S(1)}, bf16[2000,256]{1,0:T(8,128)(2,1)S(1)}, u32[]{:S(2)}, u32[]{:S(2)}) collective-permute-start(bf16[2000,256]{1,0:T(8,128)(2,1)S(1)} %straighten.1.refs_1_.refs_0_), channel_id=1, source_target_pairs={{8,16},{12,20},{16,8},{20,12},{9,17},{13,21},{17,9},{21,13},{10,18... | collective-permute-start | bytes 3072008 | tf_op jit(solution)/shard_map/ppermute | solution.py:509
  33.8 2.0 %collective-permute-start.26 = (bf16[128,2048]{1,0:T(8,128)(2,1)S(1)}, bf16[128,2048]{1,0:T(8,128)(2,1)S(1)}, u32[]{:S(2)}, u32[]{:S(2)}) collective-permute-start(bf16[128,2048]{1,0:T(8,128)(2,1)S(1)} %get-tuple-element.395), channel_id=1, source_target_pairs={{0,4},{4,0},{8,12},{12,8},{16,20},{20,16},{24,28},{28,24},{1,5},{5... | collective-permute-start | bytes 1572872 | tf_op jit(solution)/shard_map/ppermute | solution.py:418
  36.9 43.2 %copy-start.4 = (s32[8,32]{1,0:T(8,128)S(1)}, s32[8,32]{1,0:T(8,128)}, u32[]{:S(2)}) copy-start(s32[8,32]{1,0:T(8,128)} %param.19) | copy-start | bytes 3076
  36.9 38.5 %collective-permute-start.31 = (bf16[256,2048]{1,0:T(8,128)(2,1)}, bf16[256,2048]{1,0:T(8,128)(2,1)}, u32[]{:S(2)}, u32[]{:S(2)}) collective-permute-start(bf16[256,2048]{1,0:T(8,128)(2,1)} %stack_panels.1.refs_0_), channel_id=1, source_target_pairs={{0,8},{4,12},{24,16},{28,20},{1,9},{5,13},{25,17},{29,21},{2,10},{... | collective-permute-start | bytes 3145736 | tf_op jit(solution)/shard_map/ppermute | solution.py:509
  55.7 19.7 %collective-permute-start.23 = (bf16[2000,256]{1,0:T(8,128)(2,1)S(1)}, bf16[2000,256]{1,0:T(8,128)(2,1)}, u32[]{:S(2)}, u32[]{:S(2)}) collective-permute-start(bf16[2000,256]{1,0:T(8,128)(2,1)S(1)} %collective-permute-done.22.refs_2_.refs_1_), channel_id=1, source_target_pairs={{8,16},{12,20},{16,8},{20,12},{9,17},{13,21},{17,9},{21,13},{10,18... | collective-permute-start | bytes 3072008 | tf_op jit(solution)/shard_map/ppermute | solution.py:509
  57.4 21.3 %collective-permute-start.25 = (bf16[2000,256]{1,0:T(8,128)(2,1)S(1)}, bf16[2000,256]{1,0:T(8,128)(2,1)}, u32[]{:S(2)}, u32[]{:S(2)}) collective-permute-start(bf16[2000,256]{1,0:T(8,128)(2,1)S(1)} %collective-permute-done.24.refs_3_.refs_2_), channel_id=1, source_target_pairs={{8,0},{12,4},{16,24},{20,28},{9,1},{13,5},{17,25},{21,29},{10,2},{... | collective-permute-start | bytes 3072008 | tf_op jit(solution)/shard_map/ppermute | solution.py:509
  61.8 2.1 %collective-permute-start.27 = (f32[6,4,16,256]{3,2,1,0:T(8,128)}, f32[6,4,16,256]{3,2,1,0:T(8,128)}, u32[]{:S(2)}, u32[]{:S(2)}) collective-permute-start(f32[6,4,16,256]{3,2,1,0:T(8,128)} %get-tuple-element.397), channel_id=1, source_target_pairs={{0,4},{4,0},{8,12},{12,8},{16,20},{20,16},{24,28},{28,24},{1,5},{5... | collective-permute-start | bytes 1179656 | tf_op jit(solution)/shard_map/ppermute | solution.py:418
  64.9 4.9 %collective-permute-start.28 = (f32[6,16,256]{2,1,0:T(8,128)S(1)}, f32[6,16,256]{2,1,0:T(8,128)S(1)}, u32[]{:S(2)}, u32[]{:S(2)}) collective-permute-start(f32[6,16,256]{2,1,0:T(8,128)S(1)} %get-tuple-element.399), channel_id=1, source_target_pairs={{0,1},{1,0},{2,3},{3,2},{4,5},{5,4},{6,7},{7,6},{8,9},{9,8},{10,11... | collective-permute-start | bytes 294920 | tf_op jit(solution)/shard_map/ppermute | solution.py:418
  66.6 5.8 %collective-permute-start.29 = (f32[6,16,256]{2,1,0:T(8,128)S(1)}, f32[6,16,256]{2,1,0:T(8,128)S(1)}, u32[]{:S(2)}, u32[]{:S(2)}) collective-permute-start(f32[6,16,256]{2,1,0:T(8,128)S(1)} %get-tuple-element.400), channel_id=1, source_target_pairs={{0,2},{1,3},{2,0},{3,1},{4,6},{5,7},{6,4},{7,5},{8,10},{9,11},{10,... | collective-permute-start | bytes 294920 | tf_op jit(solution)/shard_map/ppermute | solution.py:418
  69.8 5.5 %collective-permute-start.30 = (f32[6,16,256]{2,1,0:T(8,128)S(1)}, f32[6,16,256]{2,1,0:T(8,128)S(1)}, u32[]{:S(2)}, u32[]{:S(2)}) collective-permute-start(f32[6,16,256]{2,1,0:T(8,128)S(1)} %get-tuple-element.401), channel_id=1, source_target_pairs={{0,3},{1,2},{2,1},{3,0},{4,7},{5,6},{6,5},{7,4},{8,11},{9,10},{10,... | collective-permute-start | bytes 294920 | tf_op jit(solution)/shard_map/ppermute | solution.py:418
  78.7 36.1 %collective-permute-start.32 = (bf16[2000,256]{1,0:T(8,128)(2,1)}, bf16[2000,256]{1,0:T(8,128)(2,1)}, u32[]{:S(2)}, u32[]{:S(2)}) collective-permute-start(bf16[2000,256]{1,0:T(8,128)(2,1)} %collective-permute-done.23.refs_5_), channel_id=1, source_target_pairs={{8,0},{12,4},{16,24},{20,28},{9,1},{13,5},{17,25},{21,29},{10,2},{... | collective-permute-start | bytes 3072008 | tf_op jit(solution)/shard_map/ppermute | solution.py:509
  83.3 1.6 %collective-permute-start = (f32[4,4,16,256]{3,2,1,0:T(8,128)S(1)}, f32[4,4,16,256]{3,2,1,0:T(8,128)S(1)}, u32[]{:S(2)}, u32[]{:S(2)}) collective-permute-start(f32[4,4,16,256]{3,2,1,0:T(8,128)S(1)} %get-tuple-element.352), channel_id=1, source_target_pairs={{0,4},{4,0},{8,12},{12,8},{16,20},{20,16},{24,28},{28,24},{1,5},{5... | collective-permute-start | bytes 786440 | tf_op jit(solution)/shard_map/cond/branch_1_fun/ppermute | solution.py:418
  84.9 4.3 %collective-permute-start.1 = (f32[4,16,256]{2,1,0:T(8,128)S(1)}, f32[4,16,256]{2,1,0:T(8,128)S(1)}, u32[]{:S(2)}, u32[]{:S(2)}) collective-permute-start(f32[4,16,256]{2,1,0:T(8,128)S(1)} %get-tuple-element.354), channel_id=1, source_target_pairs={{0,1},{1,0},{2,3},{3,2},{4,5},{5,4},{6,7},{7,6},{8,9},{9,8},{10,11... | collective-permute-start | bytes 196616 | tf_op jit(solution)/shard_map/cond/branch_1_fun/ppermute | solution.py:418
  86.5 4.3 %collective-permute-start.2 = (f32[4,16,256]{2,1,0:T(8,128)S(1)}, f32[4,16,256]{2,1,0:T(8,128)S(1)}, u32[]{:S(2)}, u32[]{:S(2)}) collective-permute-start(f32[4,16,256]{2,1,0:T(8,128)S(1)} %get-tuple-element.355), channel_id=1, source_target_pairs={{0,2},{1,3},{2,0},{3,1},{4,6},{5,7},{6,4},{7,5},{8,10},{9,11},{10,... | collective-permute-start | bytes 196616 | tf_op jit(solution)/shard_map/cond/branch_1_fun/ppermute | solution.py:418
  88.0 5.2 %collective-permute-start.3 = (f32[4,16,256]{2,1,0:T(8,128)S(1)}, f32[4,16,256]{2,1,0:T(8,128)S(1)}, u32[]{:S(2)}, u32[]{:S(2)}) collective-permute-start(f32[4,16,256]{2,1,0:T(8,128)S(1)} %get-tuple-element.356), channel_id=1, source_target_pairs={{0,3},{1,2},{2,1},{3,0},{4,7},{5,6},{6,5},{7,4},{8,11},{9,10},{10,... | collective-permute-start | bytes 196616 | tf_op jit(solution)/shard_map/cond/branch_1_fun/ppermute | solution.py:418
  93.4 6.2 %collective-permute-start.5 = (f32[4,32]{1,0:T(4,128)S(1)}, f32[4,32]{1,0:T(4,128)S(1)}, u32[]{:S(2)}, u32[]{:S(2)}) collective-permute-start(f32[4,32]{1,0:T(4,128)S(1)} %select_reduce_fusion), channel_id=1, source_target_pairs={{0,16},{4,20},{8,24},{12,28},{16,0},{20,4},{24,8},{28,12},{1,17},{... | collective-permute-start | bytes 1544 | tf_op jit(solution)/shard_map/cond/branch_1_fun/ppermute | solution.py:418
  97.8 5.5 %collective-permute-start.6 = (f32[4,32]{1,0:T(4,128)S(1)}, f32[4,32]{1,0:T(4,128)S(1)}, u32[]{:S(2)}, u32[]{:S(2)}) collective-permute-start(f32[4,32]{1,0:T(4,128)S(1)} %select_reduce_fusion), channel_id=1, source_target_pairs={{0,24},{4,28},{8,16},{12,20},{16,8},{20,12},{24,0},{28,4},{1,25},{... | collective-permute-start | bytes 1544 | tf_op jit(solution)/shard_map/cond/branch_1_fun/ppermute | solution.py:418
  99.5 4.8 %collective-permute-start.4 = (f32[36,256]{1,0:T(8,128)S(1)}, f32[36,256]{1,0:T(8,128)S(1)}, u32[]{:S(2)}, u32[]{:S(2)}) collective-permute-start(f32[36,256]{1,0:T(8,128)S(1)} %select_maximum_fusion), channel_id=1, source_target_pairs={{0,8},{4,12},{8,0},{12,4},{16,24},{20,28},{24,16},{28,20},{1,9},{5... | collective-permute-start | bytes 110600 | tf_op jit(solution)/shard_map/cond/branch_1_fun/ppermute | solution.py:418
  104.6 4.0 %collective-permute-start.7 = (bf16[8,1,16,128]{3,2,1,0:T(8,128)(2,1)S(1)}, bf16[8,1,16,128]{3,2,1,0:T(8,128)(2,1)S(1)}, u32[]{:S(2)}, u32[]{:S(2)}) collective-permute-start(bf16[8,1,16,128]{3,2,1,0:T(8,128)(2,1)S(1)} %bitcast.68), channel_id=1, source_target_pairs={{0,1},{1,0},{2,3},{3,2},{4,5},{5,4},{6,7},{7,6},{8,9},{9,8},{10,11... | collective-permute-start | bytes 98312 | tf_op jit(solution)/shard_map/cond/branch_1_fun/ppermute | solution.py:418
  106.1 3.9 %collective-permute-start.8 = (bf16[8,1,16,128]{3,2,1,0:T(8,128)(2,1)S(1)}, bf16[8,1,16,128]{3,2,1,0:T(8,128)(2,1)S(1)}, u32[]{:S(2)}, u32[]{:S(2)}) collective-permute-start(bf16[8,1,16,128]{3,2,1,0:T(8,128)(2,1)S(1)} %bitcast.69), channel_id=1, source_target_pairs={{0,2},{1,3},{2,0},{3,1},{4,6},{5,7},{6,4},{7,5},{8,10},{9,11},{10,... | collective-permute-start | bytes 98312 | tf_op jit(solution)/shard_map/cond/branch_1_fun/ppermute | solution.py:418
  107.6 4.8 %collective-permute-start.9 = (bf16[8,1,16,128]{3,2,1,0:T(8,128)(2,1)S(1)}, bf16[8,1,16,128]{3,2,1,0:T(8,128)(2,1)S(1)}, u32[]{:S(2)}, u32[]{:S(2)}) collective-permute-start(bf16[8,1,16,128]{3,2,1,0:T(8,128)(2,1)S(1)} %bitcast.70), channel_id=1, source_target_pairs={{0,3},{1,2},{2,1},{3,0},{4,7},{5,6},{6,5},{7,4},{8,11},{9,10},{10,... | collective-permute-start | bytes 98312 | tf_op jit(solution)/shard_map/cond/branch_1_fun/ppermute | solution.py:418
  113.1 1.7 %collective-permute-start.10 = (bf16[8,4,16,128]{3,2,1,0:T(8,128)(2,1)}, bf16[8,4,16,128]{3,2,1,0:T(8,128)(2,1)}, u32[]{:S(2)}, u32[]{:S(2)}) collective-permute-start(bf16[8,4,16,128]{3,2,1,0:T(8,128)(2,1)} %in_order.1), channel_id=1, source_target_pairs={{0,4},{4,0},{8,12},{12,8},{16,20},{20,16},{24,28},{28,24},{1,5},{5... | collective-permute-start | bytes 393224 | tf_op jit(solution)/shard_map/cond/branch_1_fun/ppermute | solution.py:418
  118.1 2.0 %collective-permute-start.33 = (f32[64,2000]{1,0:T(8,128)S(1)}, f32[64,2000]{1,0:T(8,128)S(1)}, u32[]{:S(2)}, u32[]{:S(2)}) collective-permute-start(f32[64,2000]{1,0:T(8,128)S(1)} %get-tuple-element.413), channel_id=1, source_target_pairs={{0,4},{4,0},{8,12},{12,8},{16,20},{20,16},{24,28},{28,24},{1,5},{5... | collective-permute-start | bytes 1536008 | tf_op jit(solution)/shard_map/ppermute | solution.py:418

commit v10 on v9

--- a/solution.py
+++ b/solution.py
@@ -90,13 +90,20 @@
     )(which[None], whole)
 
 
-def compact(mine, got, mine_sig, got_sig, mine_to, got_to, width, tile, odd):
-    half, rows = mine.shape
+def compact(values, core, got, mine_sig, got_sig, mine_to, got_to, width, tile, odd):
+    half, rows = got.shape
     blocks = mine_sig.shape[0]
+    if half % 16:
+        values = lax.dynamic_slice_in_dim(values, core * half, half, 0)
     count = rows // tile + 2
     cuts = [(0, half)]
 
-    def body(odd_ref, mine_ref, got_ref, msig_ref, gsig_ref, mto_ref, gto_ref, *outs):
+    def body(flags_ref, values_ref, got_ref, msig_ref, gsig_ref, mto_ref, gto_ref, *rest):
+        outs, mine_ref, sem = rest[:-2], rest[-2], rest[-1]
+        if values_ref.shape[0] != half:
+            values_ref = values_ref.at[pl.ds(pl.multiple_of(flags_ref[1] * half, 16), half)]
+        copy = pltpu.make_async_copy(values_ref, mine_ref, sem)
+        copy.start()
         block_of = lax.broadcasted_iota(jnp.int32, (half, blocks), 0)
         begin = lax.broadcasted_iota(jnp.int32, (half, blocks), 1) * width
         spread = ((block_of >= begin) & (block_of < begin + width)).astype(F32).astype(BF16)
@@ -108,9 +115,11 @@
             place = (to_ref[...] == slot).astype(F32).astype(BF16)
             return jnp.dot(screened, place, preferred_element_type=F32)
 
-        window = part(mine_ref, msig_ref, mto_ref) + part(got_ref, gsig_ref, gto_ref)
+        window = part(got_ref, gsig_ref, gto_ref)
+        copy.wait()
+        window = window + part(mine_ref, msig_ref, mto_ref)
         tiles = [window[:, j * tile : (j + 1) * tile] for j in range(count)]
-        even = odd_ref[0] == 0
+        even = flags_ref[0] == 0
         first, last = tiles[0], tiles[-1]
         tiles[0] = jnp.where(even, first, last)
         tiles[-1] = jnp.where(even, last, first)
@@ -124,14 +133,15 @@
     out = pl.pallas_call(
         body,
         out_shape=shapes,
-        in_specs=[SCALARS] + [WHOLE] * 6,
+        in_specs=[SCALARS, pl.BlockSpec(memory_space=pl.ANY)] + [WHOLE] * 5,
         out_specs=[WHOLE] * len(shapes),
+        scratch_shapes=[pltpu.VMEM((half, rows), BF16), pltpu.SemaphoreType.DMA],
         compiler_params=pltpu.CompilerParams(vmem_limit_bytes=10 * MIB),
         name="compact",
         cost_estimate=pl.CostEstimate(
             flops=8 * half * rows * rows, bytes_accessed=8 * half * rows, transcendentals=0
         ),
-    )(odd[None], mine, got, mine_sig, got_sig, mine_to, got_to)
+    )(jnp.stack((odd, core)), values, got, mine_sig, got_sig, mine_to, got_to)
     return [out[p * count : (p + 1) * count] for p in range(len(cuts))]
 
 
@@ -435,7 +445,6 @@
     grid_bits = [1 << b for b in range(grid_count.bit_length() - 1)]
     occ_bits = [1 << b for b in range(occ_count.bit_length() - 1)]
 
-    mine = half_of(orbital_values.T, core)
     got = flip(half_of(orbital_values.T, 1 - core), "grid", 1)
     mine_sig, other_sig = halves(significant.T, 0)
     got_sig = flip(other_sig, "grid", 1)
@@ -474,7 +483,8 @@
     got_to = lax.dynamic_index_in_dim(near_to, near_place ^ 1, 0, keepdims=False) - base
     odd = chip % 2
     compacted = compact(
-        mine,
+        orbital_values.T,
+        core,
         got,
         jnp.repeat(mine_sig.astype(BF16), slots, axis=1),
         jnp.repeat(got_sig.astype(BF16), slots, axis=1),

time: 123 us -> 122 us (level)
  local copies, waits for them, and re-layouts: 4.32 us -> 2.15 us
    unnamed x17 -> x13, local copies, waits for them, and re-layouts: 2.27 us -> 0.1 us
    pallas_call x1, Pallas kernels: 1.78 us -> 3.5 us  [compact(): pl.pallas_call(body, out_shape=shapes, in_specs=[SCALARS, pl.BlockSpec(me...]
  transfers between devices with their start and end apart: 31 -> 31, of which waited for: 18 -> 19; matrix products, arithmetic and copies ran while one was open for 5% -> 5% of each run, Pallas kernels for 10% -> 9%
where the time goes in v10:
time: 122 us
  waiting for transfers between devices  50.7 us (42%)
  starting transfers between devices  42.9 us (35%)
  Pallas kernels  19.7 us (16%)
  other arithmetic  4.2 us (3%)
  local copies, waits for them, and re-layouts  2.15 us (2%)
  between operations  1.75 us (1%)
    ppermute x23, waiting for transfers between devices, flip(): return lax.ppermute(x, axis, [(i, i ^ bit) for i in range(count)])  28 us
    ppermute x23, starting transfers between devices, flip(): return lax.ppermute(x, axis, [(i, i ^ bit) for i in range(count)])  26.3 us
    ppermute x8, waiting for transfers between devices, sent(): return lax.ppermute(x, 'grid', along(pairs))  22.7 us
    ppermute x8, starting transfers between devices, sent(): return lax.ppermute(x, 'grid', along(pairs))  16.6 us
    pallas_call x2, Pallas kernels, project(): pl.pallas_call(body, out_shape=(shape, shape), in_specs=[SCALARS] + [WHOL...  6.2 us
    pallas_call x1, Pallas kernels, compact(): pl.pallas_call(body, out_shape=shapes, in_specs=[SCALARS, pl.BlockSpec(me...  3.5 us
    pallas_call x1, Pallas kernels, contract(): pl.pallas_call(body, out_shape=(shape, shape), in_specs=[SCALARS] + [WHOL...  3.3 us
  transfers between devices with their start and end apart: 31, of which 19 were waited for; matrix products, arithmetic and copies ran while one was open for 5% of the time, Pallas kernels for 9%

profile of v10, /device:TPU:0, one launch (start us, length us, event | category | flops | bytes accessed | tf_op | source)
XLA Modules:
  0.0 121.7 jit_solution(1197771165076661321)
XLA Ops:
  0.5 0.8 dynamic-slice_bitcast_fusion
  1.8 1.2 %half_of.1 = bf16[2000,256]{1,0:T(8,128)(2,1)S(1)} custom-call(s32[1]{0:T(128)} %bitcast.13.which_ref, bf16[4000,256]{1,0:T(8,128)(2,1)} %bitcast.72), custom_call_target="tpu_custom_call" | custom-call | tf_op jit(solution)/shard_map/half_of/pallas_call | solution.py:82
  3.5 3.0 %collective-permute-start.18 = (f32[1,528]{1,0:T(1,128)S(1)}, f32[1,528]{1,0:T(1,128)S(1)}, u32[]{:S(2)}, u32[]{:S(2)}) collective-permute-start(f32[1,528]{1,0:T(1,128)S(1)} %pad_maximum_fusion.3), channel_id=1, source_target_pairs={{0,8},{4,12},{8,0},{12,4},{16,24},{20,28},{24,16},{28,20},{1,9},{5... | collective-permute-start | bytes 6344 | tf_op jit(solution)/shard_map/ppermute | solution.py:428
  7.2 0.9 collective-permute-done.18
  9.2 3.5 %compact.1 = (bf16[2000,128]{1,0:T(8,128)(2,1)S(1)}, bf16[2000,128]{1,0:T(8,128)(2,1)S(1)}, bf16[2000,128]{1,0:T(8,128)(2,1)S(1)}, bf16[2000,128]{1,0:T(8,128)(2,1)S(1)}) custom-call(s32[2]{0:T(128)S(1)} %pad_add_fusion.1.flags_ref, bf16[4000,256]{1,0:T(8,128)(2,1)} %bitcast.73, bf16[2000,256]{1,0:T(8,128)(2,1)S(1)} %collective-permute-done.14.got_ref, ...), custom_call_target="tpu_custom_call" | custom-call | flops 1048576000 | bytes 4096000 | tf_op jit(solution)/shard_map/compact/pallas_call | solution.py:133
  12.7 3.1 %collective-permute-start.21 = (f32[2,528]{1,0:T(2,128)S(1)}, f32[2,528]{1,0:T(2,128)S(1)}, u32[]{:S(2)}, u32[]{:S(2)}) collective-permute-start(f32[2,528]{1,0:T(2,128)S(1)} %maximum_select_fusion.1), channel_id=1, source_target_pairs={{0,16},{4,20},{8,24},{12,28},{16,0},{20,4},{24,8},{28,12},{1,17},{... | collective-permute-start | bytes 12680 | tf_op jit(solution)/shard_map/ppermute | solution.py:428
  16.0 0.7 collective-permute-start.19
  16.7 2.9 %collective-permute-start.20 = (bf16[2000,128]{1,0:T(8,128)(2,1)S(1)}, bf16[2000,128]{1,0:T(8,128)(2,1)S(1)}, u32[]{:S(2)}, u32[]{:S(2)}) collective-permute-start(bf16[2000,128]{1,0:T(8,128)(2,1)S(1)} %get-tuple-element.389), channel_id=1, source_target_pairs={{0,8},{4,12},{8,0},{12,4},{16,24},{20,28},{24,16},{28,20},{1,9},{5... | collective-permute-start | bytes 1536008 | tf_op jit(solution)/shard_map/ppermute | solution.py:519
  23.2 6.8 %collective-permute-done.20.refs_3_ = bf16[2000,128]{1,0:T(8,128)(2,1)S(1)} collective-permute-done((bf16[2000,128]{1,0:T(8,128)(2,1)S(1)}, bf16[2000,128]{1,0:T(8,128)(2,1)S(1)}, u32[]{:S(2)}, u32[]{:S(2)}) %collective-permute-start.20) | collective-permute-done | bytes 512032 | tf_op jit(solution)/shard_map/ppermute | solution.py:519
  30.4 1.8 %collective-permute-start.22 = (bf16[2000,256]{1,0:T(8,128)(2,1)S(1)}, bf16[2000,256]{1,0:T(8,128)(2,1)S(1)}, u32[]{:S(2)}, u32[]{:S(2)}) collective-permute-start(bf16[2000,256]{1,0:T(8,128)(2,1)S(1)} %straighten.1.refs_1_.refs_0_), channel_id=1, source_target_pairs={{0,8},{4,12},{8,0},{12,4},{16,24},{20,28},{24,16},{28,20},{1,9},{5... | collective-permute-start | bytes 3072008 | tf_op jit(solution)/shard_map/ppermute | solution.py:519
  32.2 0.7 collective-permute-start.24
  33.5 1.9 %collective-permute-done.26.got_ref = bf16[128,2048]{1,0:T(8,128)(2,1)S(1)} collective-permute-done((bf16[128,2048]{1,0:T(8,128)(2,1)S(1)}, bf16[128,2048]{1,0:T(8,128)(2,1)S(1)}, u32[]{:S(2)}, u32[]{:S(2)}) %collective-permute-start.26) | collective-permute-done | bytes 524320 | tf_op jit(solution)/shard_map/ppermute | solution.py:428
  35.4 1.1 stack_panels.1.refs_0_
  36.5 6.2 %collective-permute-start.31 = (bf16[256,2048]{1,0:T(8,128)(2,1)}, bf16[256,2048]{1,0:T(8,128)(2,1)}, u32[]{:S(2)}, u32[]{:S(2)}) collective-permute-start(bf16[256,2048]{1,0:T(8,128)(2,1)} %stack_panels.1.refs_0_), channel_id=1, source_target_pairs={{0,8},{4,12},{24,16},{28,20},{1,9},{5,13},{25,17},{29,21},{2,10},{... | collective-permute-start | bytes 3145736 | tf_op jit(solution)/shard_map/ppermute | solution.py:519
  42.7 12.6 %collective-permute-done.22.refs_2_.refs_1_ = bf16[2000,256]{1,0:T(8,128)(2,1)S(1)} collective-permute-done((bf16[2000,256]{1,0:T(8,128)(2,1)S(1)}, bf16[2000,256]{1,0:T(8,128)(2,1)S(1)}, u32[]{:S(2)}, u32[]{:S(2)}) %collective-permute-start.22) | collective-permute-done | bytes 1024032 | tf_op jit(solution)/shard_map/ppermute | solution.py:519
  55.3 1.7 %collective-permute-start.23 = (bf16[2000,256]{1,0:T(8,128)(2,1)S(1)}, bf16[2000,256]{1,0:T(8,128)(2,1)}, u32[]{:S(2)}, u32[]{:S(2)}) collective-permute-start(bf16[2000,256]{1,0:T(8,128)(2,1)S(1)} %collective-permute-done.22.refs_2_.refs_1_), channel_id=1, source_target_pairs={{8,16},{12,20},{16,8},{20,12},{9,17},{13,21},{17,9},{21,13},{10,18... | collective-permute-start | bytes 3072008 | tf_op jit(solution)/shard_map/ppermute | solution.py:519
  57.0 1.3 %collective-permute-start.25 = (bf16[2000,256]{1,0:T(8,128)(2,1)S(1)}, bf16[2000,256]{1,0:T(8,128)(2,1)}, u32[]{:S(2)}, u32[]{:S(2)}) collective-permute-start(bf16[2000,256]{1,0:T(8,128)(2,1)S(1)} %collective-permute-done.24.refs_3_.refs_2_), channel_id=1, source_target_pairs={{8,0},{12,4},{16,24},{20,28},{9,1},{13,5},{17,25},{21,29},{10,2},{... | collective-permute-start | bytes 3072008 | tf_op jit(solution)/shard_map/ppermute | solution.py:519
  58.3 3.2 %project.3 = (f32[6,4,16,256]{3,2,1,0:T(8,128)S(1)}, f32[6,4,16,256]{3,2,1,0:T(8,128)}) custom-call(s32[1]{0:T(128)} %bitcast.10.core_ref, bf16[256,2048]{1,0:T(8,128)(2,1)} %stack_panels.1.refs_0_, bf16[2000,256]{1,0:T(8,128)(2,1)S(1)} %straighten.1.refs_1_.refs_0_, bf16[2000,256]{1,0:T(8,128)(2,1)S(1)} %collective-permute-done.22.refs_2_.refs_1_, ...), custom_call_target="tpu_custom_call" | custom-call | flops 786432000 | bytes 4882432 | tf_op jit(solution)/shard_map/project/pallas_call | solution.py:291
  61.5 2.0 %collective-permute-done.27.refs_1_ = f32[6,4,16,256]{3,2,1,0:T(8,128)} collective-permute-done((f32[6,4,16,256]{3,2,1,0:T(8,128)}, f32[6,4,16,256]{3,2,1,0:T(8,128)}, u32[]{:S(2)}, u32[]{:S(2)}) %collective-permute-start.27) | collective-permute-done | bytes 393248 | tf_op jit(solution)/shard_map/ppermute | solution.py:428
  63.5 1.0 split_sum.3
  64.6 1.6 %collective-permute-start.28 = (f32[6,16,256]{2,1,0:T(8,128)S(1)}, f32[6,16,256]{2,1,0:T(8,128)S(1)}, u32[]{:S(2)}, u32[]{:S(2)}) collective-permute-start(f32[6,16,256]{2,1,0:T(8,128)S(1)} %get-tuple-element.399), channel_id=1, source_target_pairs={{0,1},{1,0},{2,3},{3,2},{4,5},{5,4},{6,7},{7,6},{8,9},{9,8},{10,11... | collective-permute-start | bytes 294920 | tf_op jit(solution)/shard_map/ppermute | solution.py:428
  66.2 1.5 %collective-permute-start.29 = (f32[6,16,256]{2,1,0:T(8,128)S(1)}, f32[6,16,256]{2,1,0:T(8,128)S(1)}, u32[]{:S(2)}, u32[]{:S(2)}) collective-permute-start(f32[6,16,256]{2,1,0:T(8,128)S(1)} %get-tuple-element.400), channel_id=1, source_target_pairs={{0,2},{1,3},{2,0},{3,1},{4,6},{5,7},{6,4},{7,5},{8,10},{9,11},{10,... | collective-permute-start | bytes 294920 | tf_op jit(solution)/shard_map/ppermute | solution.py:428
  67.7 1.7 %collective-permute-done.28 = f32[6,16,256]{2,1,0:T(8,128)S(1)} collective-permute-done((f32[6,16,256]{2,1,0:T(8,128)S(1)}, f32[6,16,256]{2,1,0:T(8,128)S(1)}, u32[]{:S(2)}, u32[]{:S(2)}) %collective-permute-start.28) | collective-permute-done | bytes 98336 | tf_op jit(solution)/shard_map/ppermute | solution.py:428
  69.5 2.4 %collective-permute-start.30 = (f32[6,16,256]{2,1,0:T(8,128)S(1)}, f32[6,16,256]{2,1,0:T(8,128)S(1)}, u32[]{:S(2)}, u32[]{:S(2)}) collective-permute-start(f32[6,16,256]{2,1,0:T(8,128)S(1)} %get-tuple-element.401), channel_id=1, source_target_pairs={{0,3},{1,2},{2,1},{3,0},{4,7},{5,6},{6,5},{7,4},{8,11},{9,10},{10,... | collective-permute-start | bytes 294920 | tf_op jit(solution)/shard_map/ppermute | solution.py:428
  72.0 3.0 %collective-permute-done.30 = f32[6,16,256]{2,1,0:T(8,128)S(1)} collective-permute-done((f32[6,16,256]{2,1,0:T(8,128)S(1)}, f32[6,16,256]{2,1,0:T(8,128)S(1)}, u32[]{:S(2)}, u32[]{:S(2)}) %collective-permute-start.30) | collective-permute-done | bytes 98336 | tf_op jit(solution)/shard_map/ppermute | solution.py:428
  75.0 3.3 %collective-permute-done.25.refs_4_ = bf16[2000,256]{1,0:T(8,128)(2,1)} collective-permute-done((bf16[2000,256]{1,0:T(8,128)(2,1)S(1)}, bf16[2000,256]{1,0:T(8,128)(2,1)}, u32[]{:S(2)}, u32[]{:S(2)}) %collective-permute-start.25) | collective-permute-done | bytes 1024032 | tf_op jit(solution)/shard_map/ppermute | solution.py:519
  78.3 1.3 %collective-permute-start.32 = (bf16[2000,256]{1,0:T(8,128)(2,1)}, bf16[2000,256]{1,0:T(8,128)(2,1)}, u32[]{:S(2)}, u32[]{:S(2)}) collective-permute-start(bf16[2000,256]{1,0:T(8,128)(2,1)} %collective-permute-done.23.refs_5_), channel_id=1, source_target_pairs={{8,0},{12,4},{16,24},{20,28},{9,1},{13,5},{17,25},{21,29},{10,2},{... | collective-permute-start | bytes 3072008 | tf_op jit(solution)/shard_map/ppermute | solution.py:519
  79.7 34.7 %conditional.1 = (bf16[8,4,16,128]{3,2,1,0:T(8,128)(2,1)}, bf16[8,4,16,128]{3,2,1,0:T(8,128)(2,1)}, f32[64,4000]{1,0:T(8,128)}) conditional(s32[]{:T(128)} %convert_element_type.61, (s32[8]{0:T(128)S(1)}, f32[256]{0:T(256)S(1)}, bf16[4000,64]{0,1:T(8,128)(2,1)}, bf16[4000,64]{0,1:T(8,128)(2,1)}, s32[8,32]{1,0:T(8,128)S(1)}, ...), branch_computations={%region_6.14_spmd, %region_14.18_spmd} | conditional | flops 524588416 | bytes 57519072 | solution.py:656
  79.9 3.0 %project.2 = (f32[4,4,16,256]{3,2,1,0:T(8,128)S(1)}, f32[4,4,16,256]{3,2,1,0:T(8,128)S(1)}) custom-call(s32[1]{0:T(128)} %bitcast.4.core_ref, bf16[256,2048]{1,0:T(8,128)(2,1)} %get-tuple-element.347.refs_0_, bf16[256,2048]{1,0:T(8,128)(2,1)} %get-tuple-element.348.refs_1_, bf16[2000,256]{1,0:T(8,128)(2,1)} %get-tuple-element.349.refs_2_, ...), custom_call_target="tpu_custom_call" | custom-call | flops 524288000 | bytes 3596288 | tf_op jit(solution)/shard_map/cond/branch_1_fun/project/pallas_call | solution.py:291
  83.1 1.4 %collective-permute-done.refs_1_ = f32[4,4,16,256]{3,2,1,0:T(8,128)S(1)} collective-permute-done((f32[4,4,16,256]{3,2,1,0:T(8,128)S(1)}, f32[4,4,16,256]{3,2,1,0:T(8,128)S(1)}, u32[]{:S(2)}, u32[]{:S(2)}) %collective-permute-start) | collective-permute-done | bytes 262176 | tf_op jit(solution)/shard_map/cond/branch_1_fun/ppermute | solution.py:428
  84.6 1.6 %collective-permute-start.1 = (f32[4,16,256]{2,1,0:T(8,128)S(1)}, f32[4,16,256]{2,1,0:T(8,128)S(1)}, u32[]{:S(2)}, u32[]{:S(2)}) collective-permute-start(f32[4,16,256]{2,1,0:T(8,128)S(1)} %get-tuple-element.354), channel_id=1, source_target_pairs={{0,1},{1,0},{2,3},{3,2},{4,5},{5,4},{6,7},{7,6},{8,9},{9,8},{10,11... | collective-permute-start | bytes 196616 | tf_op jit(solution)/shard_map/cond/branch_1_fun/ppermute | solution.py:428
  86.2 1.5 %collective-permute-start.2 = (f32[4,16,256]{2,1,0:T(8,128)S(1)}, f32[4,16,256]{2,1,0:T(8,128)S(1)}, u32[]{:S(2)}, u32[]{:S(2)}) collective-permute-start(f32[4,16,256]{2,1,0:T(8,128)S(1)} %get-tuple-element.355), channel_id=1, source_target_pairs={{0,2},{1,3},{2,0},{3,1},{4,6},{5,7},{6,4},{7,5},{8,10},{9,11},{10,... | collective-permute-start | bytes 196616 | tf_op jit(solution)/shard_map/cond/branch_1_fun/ppermute | solution.py:428
  88.2 0.7 collective-permute-done.1
  88.9 1.5 %collective-permute-done.2 = f32[4,16,256]{2,1,0:T(8,128)S(1)} collective-permute-done((f32[4,16,256]{2,1,0:T(8,128)S(1)}, f32[4,16,256]{2,1,0:T(8,128)S(1)}, u32[]{:S(2)}, u32[]{:S(2)}) %collective-permute-start.2) | collective-permute-done | bytes 65568 | tf_op jit(solution)/shard_map/cond/branch_1_fun/ppermute | solution.py:428
  90.4 2.4 %collective-permute-done.3 = f32[4,16,256]{2,1,0:T(8,128)S(1)} collective-permute-done((f32[4,16,256]{2,1,0:T(8,128)S(1)}, f32[4,16,256]{2,1,0:T(8,128)S(1)}, u32[]{:S(2)}, u32[]{:S(2)}) %collective-permute-start.3) | collective-permute-done | bytes 65568 | tf_op jit(solution)/shard_map/cond/branch_1_fun/ppermute | solution.py:428
  93.1 4.4 %collective-permute-start.5 = (f32[4,32]{1,0:T(4,128)S(1)}, f32[4,32]{1,0:T(4,128)S(1)}, u32[]{:S(2)}, u32[]{:S(2)}) collective-permute-start(f32[4,32]{1,0:T(4,128)S(1)} %select_reduce_fusion), channel_id=1, source_target_pairs={{0,16},{4,20},{8,24},{12,28},{16,0},{20,4},{24,8},{28,12},{1,17},{... | collective-permute-start | bytes 1544 | tf_op jit(solution)/shard_map/cond/branch_1_fun/ppermute | solution.py:428
  97.5 1.8 %collective-permute-start.6 = (f32[4,32]{1,0:T(4,128)S(1)}, f32[4,32]{1,0:T(4,128)S(1)}, u32[]{:S(2)}, u32[]{:S(2)}) collective-permute-start(f32[4,32]{1,0:T(4,128)S(1)} %select_reduce_fusion), channel_id=1, source_target_pairs={{0,24},{4,28},{8,16},{12,20},{16,8},{20,12},{24,0},{28,4},{1,25},{... | collective-permute-start | bytes 1544 | tf_op jit(solution)/shard_map/cond/branch_1_fun/ppermute | solution.py:428
  99.3 3.6 %collective-permute-done.6 = f32[4,32]{1,0:T(4,128)S(1)} collective-permute-done((f32[4,32]{1,0:T(4,128)S(1)}, f32[4,32]{1,0:T(4,128)S(1)}, u32[]{:S(2)}, u32[]{:S(2)}) %collective-permute-start.6) | collective-permute-done | bytes 544 | tf_op jit(solution)/shard_map/cond/branch_1_fun/ppermute | solution.py:428
  102.9 1.0 collective-permute-done.4
  104.2 1.6 %collective-permute-start.7 = (bf16[8,1,16,128]{3,2,1,0:T(8,128)(2,1)S(1)}, bf16[8,1,16,128]{3,2,1,0:T(8,128)(2,1)S(1)}, u32[]{:S(2)}, u32[]{:S(2)}) collective-permute-start(bf16[8,1,16,128]{3,2,1,0:T(8,128)(2,1)S(1)} %bitcast.68), channel_id=1, source_target_pairs={{0,1},{1,0},{2,3},{3,2},{4,5},{5,4},{6,7},{7,6},{8,9},{9,8},{10,11... | collective-permute-start | bytes 98312 | tf_op jit(solution)/shard_map/cond/branch_1_fun/ppermute | solution.py:428
  105.7 1.5 %collective-permute-start.8 = (bf16[8,1,16,128]{3,2,1,0:T(8,128)(2,1)S(1)}, bf16[8,1,16,128]{3,2,1,0:T(8,128)(2,1)S(1)}, u32[]{:S(2)}, u32[]{:S(2)}) collective-permute-start(bf16[8,1,16,128]{3,2,1,0:T(8,128)(2,1)S(1)} %bitcast.69), channel_id=1, source_target_pairs={{0,2},{1,3},{2,0},{3,1},{4,6},{5,7},{6,4},{7,5},{8,10},{9,11},{10,... | collective-permute-start | bytes 98312 | tf_op jit(solution)/shard_map/cond/branch_1_fun/ppermute | solution.py:428
  108.2 1.5 %collective-permute-done.8.refs_2_ = bf16[8,1,16,128]{3,2,1,0:T(8,128)(2,1)S(1)} collective-permute-done((bf16[8,1,16,128]{3,2,1,0:T(8,128)(2,1)S(1)}, bf16[8,1,16,128]{3,2,1,0:T(8,128)(2,1)S(1)}, u32[]{:S(2)}, u32[]{:S(2)}) %collective-permute-start.8) | collective-permute-done | bytes 32800 | tf_op jit(solution)/shard_map/cond/branch_1_fun/ppermute | solution.py:428
  109.7 2.4 %collective-permute-done.9.refs_3_ = bf16[8,1,16,128]{3,2,1,0:T(8,128)(2,1)S(1)} collective-permute-done((bf16[8,1,16,128]{3,2,1,0:T(8,128)(2,1)S(1)}, bf16[8,1,16,128]{3,2,1,0:T(8,128)(2,1)S(1)}, u32[]{:S(2)}, u32[]{:S(2)}) %collective-permute-start.9) | collective-permute-done | bytes 32800 | tf_op jit(solution)/shard_map/cond/branch_1_fun/ppermute | solution.py:428
  112.1 0.7 in_order.1
  112.7 1.7 %collective-permute-done.10 = bf16[8,4,16,128]{3,2,1,0:T(8,128)(2,1)} collective-permute-done((bf16[8,4,16,128]{3,2,1,0:T(8,128)(2,1)}, bf16[8,4,16,128]{3,2,1,0:T(8,128)(2,1)}, u32[]{:S(2)}, u32[]{:S(2)}) %collective-permute-start.10) | collective-permute-done | bytes 131104 | tf_op jit(solution)/shard_map/cond/branch_1_fun/ppermute | solution.py:428
  114.4 3.3 %contract.1 = (f32[64,2000]{1,0:T(8,128)S(1)}, f32[64,2000]{1,0:T(8,128)S(1)}) custom-call(s32[1]{0:T(128)} %bitcast.10.core_ref, bf16[8,4,16,128]{3,2,1,0:T(8,128)(2,1)} %get-tuple-element.409.kernel_ref, bf16[8,4,16,128]{3,2,1,0:T(8,128)(2,1)} %get-tuple-element.410.got_ref, bf16[2000,256]{1,0:T(8,128)(2,1)S(1)} %straighten.1.refs_1_.refs_0_, ...), custom_call_target="tpu_custom_call" | custom-call | flops 524288000 | bytes 5120000 | tf_op jit(solution)/shard_map/contract/pallas_call | solution.py:356
  118.0 1.7 %collective-permute-done.33.back_ref = f32[64,2000]{1,0:T(8,128)S(1)} collective-permute-done((f32[64,2000]{1,0:T(8,128)S(1)}, f32[64,2000]{1,0:T(8,128)S(1)}, u32[]{:S(2)}, u32[]{:S(2)}) %collective-permute-start.33) | collective-permute-done | bytes 512032 | tf_op jit(solution)/shard_map/ppermute | solution.py:428
  119.7 1.8 %finish.1 = f32[64,4000]{1,0:T(8,128)} custom-call(s32[2]{0:T(128)S(1)} %pad_add_fusion.3.flags_ref, f32[64,2000]{1,0:T(8,128)S(1)} %get-tuple-element.412.ours_ref, f32[64,2000]{1,0:T(8,128)S(1)} %collective-permute-done.33.back_ref, f32[64,4000]{1,0:T(8,128)} %get-tuple-element.414.other_ref), custom_call_target="tpu_custom_call", output_to_operand_aliasing={{}: (3, {})} | custom-call | tf_op jit(solution)/shard_map/finish/pallas_call | solution.py:397
  (110 shorter events, 9.3 us)
Async XLA Ops:
  0.0 3.4 %copy-start.3 = (f32[256]{0:T(256)S(1)}, f32[256]{0:T(256)}, u32[]{:S(2)}) copy-start(f32[256]{0:T(256)} %param.17) | copy-start | bytes 3076
  0.0 3.3 %copy-start.4 = (s32[8]{0:T(128)S(1)}, s32[8]{0:T(128)}, u32[]{:S(2)}) copy-start(s32[8]{0:T(128)} %param.18) | copy-start | bytes 100
  0.0 3.4 %collective-permute-start.17 = (f32[1,256]{1,0:T(1,128)}, f32[1,256]{1,0:T(1,128)S(1)}, u32[]{:S(2)}, u32[]{:S(2)}) collective-permute-start(f32[1,256]{1,0:T(1,128)} %bitcast.85), channel_id=1, source_target_pairs={{0,4},{4,0},{8,12},{12,8},{16,20},{20,16},{24,28},{28,24},{1,5},{5... | collective-permute-start | bytes 3080 | tf_op jit(solution)/shard_map/ppermute | solution.py:428
  0.5 2.9 %collective-permute-start.16 = (s32[1,8]{1,0:T(1,128)}, s32[1,8]{1,0:T(1,128)S(1)}, u32[]{:S(2)}, u32[]{:S(2)}) collective-permute-start(s32[1,8]{1,0:T(1,128)} %bitcast.87), channel_id=1, source_target_pairs={{0,4},{4,0},{8,12},{12,8},{16,20},{20,16},{24,28},{28,24},{1,5},{5... | collective-permute-start | bytes 104 | tf_op jit(solution)/shard_map/ppermute | solution.py:428
  1.4 5.5 %collective-permute-start.15 = (s32[16,8]{0,1:T(8,128)S(1)}, s32[16,8]{0,1:T(8,128)S(1)}, u32[]{:S(2)}, u32[]{:S(2)}) collective-permute-start(s32[16,8]{0,1:T(8,128)S(1)} %get-tuple-element.483), channel_id=1, source_target_pairs={{0,4},{4,0},{8,12},{12,8},{16,20},{20,16},{24,28},{28,24},{1,5},{5... | collective-permute-start | bytes 1544 | tf_op jit(solution)/shard_map/ppermute | solution.py:428
  3.0 6.2 %collective-permute-start.14 = (bf16[2000,256]{1,0:T(8,128)(2,1)S(1)}, bf16[2000,256]{1,0:T(8,128)(2,1)S(1)}, u32[]{:S(2)}, u32[]{:S(2)}) collective-permute-start(bf16[2000,256]{1,0:T(8,128)(2,1)S(1)} %half_of.1), channel_id=1, source_target_pairs={{0,4},{4,0},{8,12},{12,8},{16,20},{20,16},{24,28},{28,24},{1,5},{5... | collective-permute-start | bytes 3072008 | tf_op jit(solution)/shard_map/ppermute | solution.py:428
  3.5 4.6 %collective-permute-start.18 = (f32[1,528]{1,0:T(1,128)S(1)}, f32[1,528]{1,0:T(1,128)S(1)}, u32[]{:S(2)}, u32[]{:S(2)}) collective-permute-start(f32[1,528]{1,0:T(1,128)S(1)} %pad_maximum_fusion.3), channel_id=1, source_target_pairs={{0,8},{4,12},{8,0},{12,4},{16,24},{20,28},{24,16},{28,20},{1,9},{5... | collective-permute-start | bytes 6344 | tf_op jit(solution)/shard_map/ppermute | solution.py:428
  12.7 6.8 %collective-permute-start.21 = (f32[2,528]{1,0:T(2,128)S(1)}, f32[2,528]{1,0:T(2,128)S(1)}, u32[]{:S(2)}, u32[]{:S(2)}) collective-permute-start(f32[2,528]{1,0:T(2,128)S(1)} %maximum_select_fusion.1), channel_id=1, source_target_pairs={{0,16},{4,20},{8,24},{12,28},{16,0},{20,4},{24,8},{28,12},{1,17},{... | collective-permute-start | bytes 12680 | tf_op jit(solution)/shard_map/ppermute | solution.py:428
  16.0 7.2 %collective-permute-start.19 = (bf16[2000,128]{1,0:T(8,128)(2,1)S(1)}, bf16[2000,128]{1,0:T(8,128)(2,1)S(1)}, u32[]{:S(2)}, u32[]{:S(2)}) collective-permute-start(bf16[2000,128]{1,0:T(8,128)(2,1)S(1)} %get-tuple-element.388), channel_id=1, source_target_pairs={{8,16},{12,20},{16,8},{20,12},{9,17},{13,21},{17,9},{21,13},{10,18... | collective-permute-start | bytes 1536008 | tf_op jit(solution)/shard_map/ppermute | solution.py:519
  16.7 13.3 %collective-permute-start.20 = (bf16[2000,128]{1,0:T(8,128)(2,1)S(1)}, bf16[2000,128]{1,0:T(8,128)(2,1)S(1)}, u32[]{:S(2)}, u32[]{:S(2)}) collective-permute-start(bf16[2000,128]{1,0:T(8,128)(2,1)S(1)} %get-tuple-element.389), channel_id=1, source_target_pairs={{0,8},{4,12},{8,0},{12,4},{16,24},{20,28},{24,16},{28,20},{1,9},{5... | collective-permute-start | bytes 1536008 | tf_op jit(solution)/shard_map/ppermute | solution.py:519
  23.2 9.8 %copy-start = (bf16[4000,64]{0,1:T(8,128)(2,1)S(1)}, bf16[4000,64]{0,1:T(8,128)(2,1)}, u32[]{:S(2)}) copy-start(bf16[4000,64]{0,1:T(8,128)(2,1)} %param.15) | copy-start | bytes 1536004
  23.2 9.8 %copy-start.1 = (bf16[4000,64]{0,1:T(8,128)(2,1)S(1)}, bf16[4000,64]{0,1:T(8,128)(2,1)}, u32[]{:S(2)}) copy-start(bf16[4000,64]{0,1:T(8,128)(2,1)} %param.16) | copy-start | bytes 1536004
  30.4 24.9 %collective-permute-start.22 = (bf16[2000,256]{1,0:T(8,128)(2,1)S(1)}, bf16[2000,256]{1,0:T(8,128)(2,1)S(1)}, u32[]{:S(2)}, u32[]{:S(2)}) collective-permute-start(bf16[2000,256]{1,0:T(8,128)(2,1)S(1)} %straighten.1.refs_1_.refs_0_), channel_id=1, source_target_pairs={{0,8},{4,12},{8,0},{12,4},{16,24},{20,28},{24,16},{28,20},{1,9},{5... | collective-permute-start | bytes 3072008 | tf_op jit(solution)/shard_map/ppermute | solution.py:519
  32.2 24.8 %collective-permute-start.24 = (bf16[2000,256]{1,0:T(8,128)(2,1)S(1)}, bf16[2000,256]{1,0:T(8,128)(2,1)S(1)}, u32[]{:S(2)}, u32[]{:S(2)}) collective-permute-start(bf16[2000,256]{1,0:T(8,128)(2,1)S(1)} %straighten.1.refs_1_.refs_0_), channel_id=1, source_target_pairs={{8,16},{12,20},{16,8},{20,12},{9,17},{13,21},{17,9},{21,13},{10,18... | collective-permute-start | bytes 3072008 | tf_op jit(solution)/shard_map/ppermute | solution.py:519
  33.5 2.0 %collective-permute-start.26 = (bf16[128,2048]{1,0:T(8,128)(2,1)S(1)}, bf16[128,2048]{1,0:T(8,128)(2,1)S(1)}, u32[]{:S(2)}, u32[]{:S(2)}) collective-permute-start(bf16[128,2048]{1,0:T(8,128)(2,1)S(1)} %get-tuple-element.395), channel_id=1, source_target_pairs={{0,4},{4,0},{8,12},{12,8},{16,20},{20,16},{24,28},{28,24},{1,5},{5... | collective-permute-start | bytes 1572872 | tf_op jit(solution)/shard_map/ppermute | solution.py:428
  36.5 43.2 %copy-start.2 = (s32[8,32]{1,0:T(8,128)S(1)}, s32[8,32]{1,0:T(8,128)}, u32[]{:S(2)}) copy-start(s32[8,32]{1,0:T(8,128)} %param.19) | copy-start | bytes 3076
  36.5 38.5 %collective-permute-start.31 = (bf16[256,2048]{1,0:T(8,128)(2,1)}, bf16[256,2048]{1,0:T(8,128)(2,1)}, u32[]{:S(2)}, u32[]{:S(2)}) collective-permute-start(bf16[256,2048]{1,0:T(8,128)(2,1)} %stack_panels.1.refs_0_), channel_id=1, source_target_pairs={{0,8},{4,12},{24,16},{28,20},{1,9},{5,13},{25,17},{29,21},{2,10},{... | collective-permute-start | bytes 3145736 | tf_op jit(solution)/shard_map/ppermute | solution.py:519
  55.3 19.7 %collective-permute-start.23 = (bf16[2000,256]{1,0:T(8,128)(2,1)S(1)}, bf16[2000,256]{1,0:T(8,128)(2,1)}, u32[]{:S(2)}, u32[]{:S(2)}) collective-permute-start(bf16[2000,256]{1,0:T(8,128)(2,1)S(1)} %collective-permute-done.22.refs_2_.refs_1_), channel_id=1, source_target_pairs={{8,16},{12,20},{16,8},{20,12},{9,17},{13,21},{17,9},{21,13},{10,18... | collective-permute-start | bytes 3072008 | tf_op jit(solution)/shard_map/ppermute | solution.py:519
  57.0 21.3 %collective-permute-start.25 = (bf16[2000,256]{1,0:T(8,128)(2,1)S(1)}, bf16[2000,256]{1,0:T(8,128)(2,1)}, u32[]{:S(2)}, u32[]{:S(2)}) collective-permute-start(bf16[2000,256]{1,0:T(8,128)(2,1)S(1)} %collective-permute-done.24.refs_3_.refs_2_), channel_id=1, source_target_pairs={{8,0},{12,4},{16,24},{20,28},{9,1},{13,5},{17,25},{21,29},{10,2},{... | collective-permute-start | bytes 3072008 | tf_op jit(solution)/shard_map/ppermute | solution.py:519
  61.4 2.1 %collective-permute-start.27 = (f32[6,4,16,256]{3,2,1,0:T(8,128)}, f32[6,4,16,256]{3,2,1,0:T(8,128)}, u32[]{:S(2)}, u32[]{:S(2)}) collective-permute-start(f32[6,4,16,256]{3,2,1,0:T(8,128)} %get-tuple-element.397), channel_id=1, source_target_pairs={{0,4},{4,0},{8,12},{12,8},{16,20},{20,16},{24,28},{28,24},{1,5},{5... | collective-permute-start | bytes 1179656 | tf_op jit(solution)/shard_map/ppermute | solution.py:428
  64.6 4.9 %collective-permute-start.28 = (f32[6,16,256]{2,1,0:T(8,128)S(1)}, f32[6,16,256]{2,1,0:T(8,128)S(1)}, u32[]{:S(2)}, u32[]{:S(2)}) collective-permute-start(f32[6,16,256]{2,1,0:T(8,128)S(1)} %get-tuple-element.399), channel_id=1, source_target_pairs={{0,1},{1,0},{2,3},{3,2},{4,5},{5,4},{6,7},{7,6},{8,9},{9,8},{10,11... | collective-permute-start | bytes 294920 | tf_op jit(solution)/shard_map/ppermute | solution.py:428
  66.2 5.8 %collective-permute-start.29 = (f32[6,16,256]{2,1,0:T(8,128)S(1)}, f32[6,16,256]{2,1,0:T(8,128)S(1)}, u32[]{:S(2)}, u32[]{:S(2)}) collective-permute-start(f32[6,16,256]{2,1,0:T(8,128)S(1)} %get-tuple-element.400), channel_id=1, source_target_pairs={{0,2},{1,3},{2,0},{3,1},{4,6},{5,7},{6,4},{7,5},{8,10},{9,11},{10,... | collective-permute-start | bytes 294920 | tf_op jit(solution)/shard_map/ppermute | solution.py:428
  69.5 5.5 %collective-permute-start.30 = (f32[6,16,256]{2,1,0:T(8,128)S(1)}, f32[6,16,256]{2,1,0:T(8,128)S(1)}, u32[]{:S(2)}, u32[]{:S(2)}) collective-permute-start(f32[6,16,256]{2,1,0:T(8,128)S(1)} %get-tuple-element.401), channel_id=1, source_target_pairs={{0,3},{1,2},{2,1},{3,0},{4,7},{5,6},{6,5},{7,4},{8,11},{9,10},{10,... | collective-permute-start | bytes 294920 | tf_op jit(solution)/shard_map/ppermute | solution.py:428
  78.3 36.1 %collective-permute-start.32 = (bf16[2000,256]{1,0:T(8,128)(2,1)}, bf16[2000,256]{1,0:T(8,128)(2,1)}, u32[]{:S(2)}, u32[]{:S(2)}) collective-permute-start(bf16[2000,256]{1,0:T(8,128)(2,1)} %collective-permute-done.23.refs_5_), channel_id=1, source_target_pairs={{8,0},{12,4},{16,24},{20,28},{9,1},{13,5},{17,25},{21,29},{10,2},{... | collective-permute-start | bytes 3072008 | tf_op jit(solution)/shard_map/ppermute | solution.py:519
  83.0 1.6 %collective-permute-start = (f32[4,4,16,256]{3,2,1,0:T(8,128)S(1)}, f32[4,4,16,256]{3,2,1,0:T(8,128)S(1)}, u32[]{:S(2)}, u32[]{:S(2)}) collective-permute-start(f32[4,4,16,256]{3,2,1,0:T(8,128)S(1)} %get-tuple-element.352), channel_id=1, source_target_pairs={{0,4},{4,0},{8,12},{12,8},{16,20},{20,16},{24,28},{28,24},{1,5},{5... | collective-permute-start | bytes 786440 | tf_op jit(solution)/shard_map/cond/branch_1_fun/ppermute | solution.py:428
  84.6 4.3 %collective-permute-start.1 = (f32[4,16,256]{2,1,0:T(8,128)S(1)}, f32[4,16,256]{2,1,0:T(8,128)S(1)}, u32[]{:S(2)}, u32[]{:S(2)}) collective-permute-start(f32[4,16,256]{2,1,0:T(8,128)S(1)} %get-tuple-element.354), channel_id=1, source_target_pairs={{0,1},{1,0},{2,3},{3,2},{4,5},{5,4},{6,7},{7,6},{8,9},{9,8},{10,11... | collective-permute-start | bytes 196616 | tf_op jit(solution)/shard_map/cond/branch_1_fun/ppermute | solution.py:428
  86.2 4.3 %collective-permute-start.2 = (f32[4,16,256]{2,1,0:T(8,128)S(1)}, f32[4,16,256]{2,1,0:T(8,128)S(1)}, u32[]{:S(2)}, u32[]{:S(2)}) collective-permute-start(f32[4,16,256]{2,1,0:T(8,128)S(1)} %get-tuple-element.355), channel_id=1, source_target_pairs={{0,2},{1,3},{2,0},{3,1},{4,6},{5,7},{6,4},{7,5},{8,10},{9,11},{10,... | collective-permute-start | bytes 196616 | tf_op jit(solution)/shard_map/cond/branch_1_fun/ppermute | solution.py:428
  87.7 5.2 %collective-permute-start.3 = (f32[4,16,256]{2,1,0:T(8,128)S(1)}, f32[4,16,256]{2,1,0:T(8,128)S(1)}, u32[]{:S(2)}, u32[]{:S(2)}) collective-permute-start(f32[4,16,256]{2,1,0:T(8,128)S(1)} %get-tuple-element.356), channel_id=1, source_target_pairs={{0,3},{1,2},{2,1},{3,0},{4,7},{5,6},{6,5},{7,4},{8,11},{9,10},{10,... | collective-permute-start | bytes 196616 | tf_op jit(solution)/shard_map/cond/branch_1_fun/ppermute | solution.py:428
  93.1 6.2 %collective-permute-start.5 = (f32[4,32]{1,0:T(4,128)S(1)}, f32[4,32]{1,0:T(4,128)S(1)}, u32[]{:S(2)}, u32[]{:S(2)}) collective-permute-start(f32[4,32]{1,0:T(4,128)S(1)} %select_reduce_fusion), channel_id=1, source_target_pairs={{0,16},{4,20},{8,24},{12,28},{16,0},{20,4},{24,8},{28,12},{1,17},{... | collective-permute-start | bytes 1544 | tf_op jit(solution)/shard_map/cond/branch_1_fun/ppermute | solution.py:428
  97.5 5.5 %collective-permute-start.6 = (f32[4,32]{1,0:T(4,128)S(1)}, f32[4,32]{1,0:T(4,128)S(1)}, u32[]{:S(2)}, u32[]{:S(2)}) collective-permute-start(f32[4,32]{1,0:T(4,128)S(1)} %select_reduce_fusion), channel_id=1, source_target_pairs={{0,24},{4,28},{8,16},{12,20},{16,8},{20,12},{24,0},{28,4},{1,25},{... | collective-permute-start | bytes 1544 | tf_op jit(solution)/shard_map/cond/branch_1_fun/ppermute | solution.py:428
  99.2 4.7 %collective-permute-start.4 = (f32[36,256]{1,0:T(8,128)S(1)}, f32[36,256]{1,0:T(8,128)S(1)}, u32[]{:S(2)}, u32[]{:S(2)}) collective-permute-start(f32[36,256]{1,0:T(8,128)S(1)} %select_maximum_fusion), channel_id=1, source_target_pairs={{0,8},{4,12},{8,0},{12,4},{16,24},{20,28},{24,16},{28,20},{1,9},{5... | collective-permute-start | bytes 110600 | tf_op jit(solution)/shard_map/cond/branch_1_fun/ppermute | solution.py:428
  104.2 4.0 %collective-permute-start.7 = (bf16[8,1,16,128]{3,2,1,0:T(8,128)(2,1)S(1)}, bf16[8,1,16,128]{3,2,1,0:T(8,128)(2,1)S(1)}, u32[]{:S(2)}, u32[]{:S(2)}) collective-permute-start(bf16[8,1,16,128]{3,2,1,0:T(8,128)(2,1)S(1)} %bitcast.68), channel_id=1, source_target_pairs={{0,1},{1,0},{2,3},{3,2},{4,5},{5,4},{6,7},{7,6},{8,9},{9,8},{10,11... | collective-permute-start | bytes 98312 | tf_op jit(solution)/shard_map/cond/branch_1_fun/ppermute | solution.py:428
  105.7 3.9 %collective-permute-start.8 = (bf16[8,1,16,128]{3,2,1,0:T(8,128)(2,1)S(1)}, bf16[8,1,16,128]{3,2,1,0:T(8,128)(2,1)S(1)}, u32[]{:S(2)}, u32[]{:S(2)}) collective-permute-start(bf16[8,1,16,128]{3,2,1,0:T(8,128)(2,1)S(1)} %bitcast.69), channel_id=1, source_target_pairs={{0,2},{1,3},{2,0},{3,1},{4,6},{5,7},{6,4},{7,5},{8,10},{9,11},{10,... | collective-permute-start | bytes 98312 | tf_op jit(solution)/shard_map/cond/branch_1_fun/ppermute | solution.py:428
  107.3 4.8 %collective-permute-start.9 = (bf16[8,1,16,128]{3,2,1,0:T(8,128)(2,1)S(1)}, bf16[8,1,16,128]{3,2,1,0:T(8,128)(2,1)S(1)}, u32[]{:S(2)}, u32[]{:S(2)}) collective-permute-start(bf16[8,1,16,128]{3,2,1,0:T(8,128)(2,1)S(1)} %bitcast.70), channel_id=1, source_target_pairs={{0,3},{1,2},{2,1},{3,0},{4,7},{5,6},{6,5},{7,4},{8,11},{9,10},{10,... | collective-permute-start | bytes 98312 | tf_op jit(solution)/shard_map/cond/branch_1_fun/ppermute | solution.py:428
  112.7 1.7 %collective-permute-start.10 = (bf16[8,4,16,128]{3,2,1,0:T(8,128)(2,1)}, bf16[8,4,16,128]{3,2,1,0:T(8,128)(2,1)}, u32[]{:S(2)}, u32[]{:S(2)}) collective-permute-start(bf16[8,4,16,128]{3,2,1,0:T(8,128)(2,1)} %in_order.1), channel_id=1, source_target_pairs={{0,4},{4,0},{8,12},{12,8},{16,20},{20,16},{24,28},{28,24},{1,5},{5... | collective-permute-start | bytes 393224 | tf_op jit(solution)/shard_map/cond/branch_1_fun/ppermute | solution.py:428
  117.7 2.0 %collective-permute-start.33 = (f32[64,2000]{1,0:T(8,128)S(1)}, f32[64,2000]{1,0:T(8,128)S(1)}, u32[]{:S(2)}, u32[]{:S(2)}) collective-permute-start(f32[64,2000]{1,0:T(8,128)S(1)} %get-tuple-element.413), channel_id=1, source_target_pairs={{0,4},{4,0},{8,12},{12,8},{16,20},{20,16},{24,28},{28,24},{1,5},{5... | collective-permute-start | bytes 1536008 | tf_op jit(solution)/shard_map/ppermute | solution.py:428

commit v11 on v10

--- a/solution.py
+++ b/solution.py
@@ -321,7 +321,7 @@
     )(occ[None], *parts)
 
 
-def contract(kernel, got, windows, core):
+def contract(kernel, got, windows, core, fetched):
     tiles, shares, piece, columns = kernel.shape
     parts = [x.shape[0] for x in windows[0][0]]
     rows = windows[0][0][0].shape[1]
@@ -329,10 +329,16 @@
     own = columns // 2
     arrays = distinct([x for window in windows for addend in window for x in addend])
     per_window = tiles // len(windows)
+    coming = [i for i, x in enumerate(arrays) if any(x is y for y in fetched)]
 
     def body(core_ref, kernel_ref, got_ref, *refs):
-        array_refs = refs[:-3]
-        mine_ref, other_ref, order_ref = refs[-3:]
+        array_refs = list(refs[: len(arrays)])
+        mine_ref, other_ref, order_ref, *held, sems = refs[len(arrays) :]
+        copies = {}
+        for n, i in enumerate(coming):
+            copies[i] = pltpu.make_async_copy(array_refs[i], held[n], sems.at[n])
+            copies[i].start()
+            array_refs[i] = held[n]
         first = core_ref[0] == 0
         order_ref[:, core_ref[0]] = kernel_ref[...].astype(F32)
         order_ref[:, 1 - core_ref[0]] = got_ref[...].astype(F32)
@@ -344,6 +350,8 @@
         for p, size in enumerate(parts):
             total = None
             for window, part in zip(windows, kernels):
+                for i in [i for i in copies if any(arrays[i] is x[p] for x in window)]:
+                    copies.pop(i).wait()
                 value = read_window(window, p, arrays, array_refs)
                 term = jnp.dot(value, part, preferred_element_type=F32)
                 total = term if total is None else total + term
@@ -356,9 +364,14 @@
     return pl.pallas_call(
         body,
         out_shape=(shape, shape),
-        in_specs=[SCALARS] + [WHOLE] * (2 + len(arrays)),
+        in_specs=[SCALARS, WHOLE, WHOLE]
+        + [
+            pl.BlockSpec(memory_space=pl.ANY) if i in coming else WHOLE for i in range(len(arrays))
+        ],
         out_specs=(WHOLE, WHOLE),
-        scratch_shapes=[pltpu.VMEM((tiles, 2, shares, piece, columns), F32)],
+        scratch_shapes=[pltpu.VMEM((tiles, 2, shares, piece, columns), F32)]
+        + [pltpu.VMEM(arrays[i].shape, BF16) for i in coming]
+        + [pltpu.SemaphoreType.DMA((len(coming),))],
         compiler_params=pltpu.CompilerParams(vmem_limit_bytes=20 * MIB),
         name="contract",
         cost_estimate=pl.CostEstimate(
@@ -657,7 +670,7 @@
     early_windows = [w for w, _ in early_jobs]
     early_windows[2] = early_windows[2] + [late]
     windows = early_windows + [late_window]
-    ours, theirs = contract(kernel, got_kernel, windows, core)
+    ours, theirs = contract(kernel, got_kernel, windows, core, late + by_a + by_b)
     back = flip(theirs, "grid", 1)
     return finish(core, fits, ours, back, other, scale).T
 

time: 122 us -> 124 us (1.016)
  Pallas kernels: 19.7 us -> 21.1 us
    pallas_call x1, Pallas kernels: 3.3 us -> 4.73 us  [contract(): pl.pallas_call(body, out_shape=(shape, shape), in_specs=[SCALARS, WHOLE,...]
where the time goes in v11:
time: 124 us; the launch traced here: 123 us
  waiting for transfers between devices  50.7 us (41%)
  starting transfers between devices  42.9 us (35%)
  Pallas kernels  21.1 us (17%)
  other arithmetic  4.2 us (3%)
  local copies, waits for them, and re-layouts  2.15 us (2%)
  between operations  1.75 us (1%)
    ppermute x23, waiting for transfers between devices, flip(): return lax.ppermute(x, axis, [(i, i ^ bit) for i in range(count)])  28 us
    ppermute x23, starting transfers between devices, flip(): return lax.ppermute(x, axis, [(i, i ^ bit) for i in range(count)])  26.3 us
    ppermute x8, waiting for transfers between devices, sent(): return lax.ppermute(x, 'grid', along(pairs))  22.7 us
    ppermute x8, starting transfers between devices, sent(): return lax.ppermute(x, 'grid', along(pairs))  16.6 us
    pallas_call x2, Pallas kernels, project(): pl.pallas_call(body, out_shape=(shape, shape), in_specs=[SCALARS] + [WHOL...  6.2 us
    pallas_call x1, Pallas kernels, contract(): pl.pallas_call(body, out_shape=(shape, shape), in_specs=[SCALARS, WHOLE,...  4.73 us
    pallas_call x1, Pallas kernels, compact(): pl.pallas_call(body, out_shape=shapes, in_specs=[SCALARS, pl.BlockSpec(me...  3.5 us
  transfers between devices with their start and end apart: 31, of which 19 were waited for; matrix products, arithmetic and copies ran while one was open for 5% of the time, Pallas kernels for 9%

profile of v11, /device:TPU:0, one launch (start us, length us, event | category | flops | bytes accessed | tf_op | source)
XLA Modules:
  0.0 123.1 jit_solution(13398634759312252235)
XLA Ops:
  0.5 0.8 dynamic-slice_bitcast_fusion
  1.8 1.2 half_of.1
  3.5 3.0 %collective-permute-start.18 = (f32[1,528]{1,0:T(1,128)S(1)}, f32[1,528]{1,0:T(1,128)S(1)}, u32[]{:S(2)}, u32[]{:S(2)}) collective-permute-start(f32[1,528]{1,0:T(1,128)S(1)} %pad_maximum_fusion.3), channel_id=1, source_target_pairs={{0,8},{4,12},{8,0},{12,4},{16,24},{20,28},{24,16},{28,20},{1,9},{5... | collective-permute-start | bytes 6344 | tf_op jit(solution)/shard_map/ppermute | solution.py:441
  7.2 0.9 collective-permute-done.18
  9.2 3.5 %compact.1 = (bf16[2000,128]{1,0:T(8,128)(2,1)S(1)}, bf16[2000,128]{1,0:T(8,128)(2,1)S(1)}, bf16[2000,128]{1,0:T(8,128)(2,1)S(1)}, bf16[2000,128]{1,0:T(8,128)(2,1)S(1)}) custom-call(s32[2]{0:T(128)S(1)} %pad_add_fusion.1.flags_ref, bf16[4000,256]{1,0:T(8,128)(2,1)} %bitcast.73, bf16[2000,256]{1,0:T(8,128)(2,1)S(1)} %collective-permute-done.14.got_ref, ...), custom_call_target="tpu_custom_call" | custom-call | flops 1048576000 | bytes 4096000 | tf_op jit(solution)/shard_map/compact/pallas_call | solution.py:133
  12.7 3.1 %collective-permute-start.21 = (f32[2,528]{1,0:T(2,128)S(1)}, f32[2,528]{1,0:T(2,128)S(1)}, u32[]{:S(2)}, u32[]{:S(2)}) collective-permute-start(f32[2,528]{1,0:T(2,128)S(1)} %maximum_select_fusion.1), channel_id=1, source_target_pairs={{0,16},{4,20},{8,24},{12,28},{16,0},{20,4},{24,8},{28,12},{1,17},{... | collective-permute-start | bytes 12680 | tf_op jit(solution)/shard_map/ppermute | solution.py:441
  16.0 0.7 collective-permute-start.19
  16.7 2.9 %collective-permute-start.20 = (bf16[2000,128]{1,0:T(8,128)(2,1)S(1)}, bf16[2000,128]{1,0:T(8,128)(2,1)S(1)}, u32[]{:S(2)}, u32[]{:S(2)}) collective-permute-start(bf16[2000,128]{1,0:T(8,128)(2,1)S(1)} %get-tuple-element.389), channel_id=1, source_target_pairs={{0,8},{4,12},{8,0},{12,4},{16,24},{20,28},{24,16},{28,20},{1,9},{5... | collective-permute-start | bytes 1536008 | tf_op jit(solution)/shard_map/ppermute | solution.py:532
  23.2 6.8 %collective-permute-done.20.refs_3_ = bf16[2000,128]{1,0:T(8,128)(2,1)S(1)} collective-permute-done((bf16[2000,128]{1,0:T(8,128)(2,1)S(1)}, bf16[2000,128]{1,0:T(8,128)(2,1)S(1)}, u32[]{:S(2)}, u32[]{:S(2)}) %collective-permute-start.20) | collective-permute-done | bytes 512032 | tf_op jit(solution)/shard_map/ppermute | solution.py:532
  30.4 1.8 %collective-permute-start.22 = (bf16[2000,256]{1,0:T(8,128)(2,1)S(1)}, bf16[2000,256]{1,0:T(8,128)(2,1)S(1)}, u32[]{:S(2)}, u32[]{:S(2)}) collective-permute-start(bf16[2000,256]{1,0:T(8,128)(2,1)S(1)} %straighten.1.refs_1_.refs_0_), channel_id=1, source_target_pairs={{0,8},{4,12},{8,0},{12,4},{16,24},{20,28},{24,16},{28,20},{1,9},{5... | collective-permute-start | bytes 3072008 | tf_op jit(solution)/shard_map/ppermute | solution.py:532
  32.2 0.7 collective-permute-start.24
  33.5 1.9 %collective-permute-done.26.got_ref = bf16[128,2048]{1,0:T(8,128)(2,1)S(1)} collective-permute-done((bf16[128,2048]{1,0:T(8,128)(2,1)S(1)}, bf16[128,2048]{1,0:T(8,128)(2,1)S(1)}, u32[]{:S(2)}, u32[]{:S(2)}) %collective-permute-start.26) | collective-permute-done | bytes 524320 | tf_op jit(solution)/shard_map/ppermute | solution.py:441
  35.4 1.1 stack_panels.1.refs_0_
  36.5 6.2 %collective-permute-start.31 = (bf16[256,2048]{1,0:T(8,128)(2,1)}, bf16[256,2048]{1,0:T(8,128)(2,1)}, u32[]{:S(2)}, u32[]{:S(2)}) collective-permute-start(bf16[256,2048]{1,0:T(8,128)(2,1)} %stack_panels.1.refs_0_), channel_id=1, source_target_pairs={{0,8},{4,12},{24,16},{28,20},{1,9},{5,13},{25,17},{29,21},{2,10},{... | collective-permute-start | bytes 3145736 | tf_op jit(solution)/shard_map/ppermute | solution.py:532
  42.7 12.6 %collective-permute-done.22.refs_2_.refs_1_ = bf16[2000,256]{1,0:T(8,128)(2,1)S(1)} collective-permute-done((bf16[2000,256]{1,0:T(8,128)(2,1)S(1)}, bf16[2000,256]{1,0:T(8,128)(2,1)S(1)}, u32[]{:S(2)}, u32[]{:S(2)}) %collective-permute-start.22) | collective-permute-done | bytes 1024032 | tf_op jit(solution)/shard_map/ppermute | solution.py:532
  55.3 1.7 %collective-permute-start.23 = (bf16[2000,256]{1,0:T(8,128)(2,1)S(1)}, bf16[2000,256]{1,0:T(8,128)(2,1)}, u32[]{:S(2)}, u32[]{:S(2)}) collective-permute-start(bf16[2000,256]{1,0:T(8,128)(2,1)S(1)} %collective-permute-done.22.refs_2_.refs_1_), channel_id=1, source_target_pairs={{8,16},{12,20},{16,8},{20,12},{9,17},{13,21},{17,9},{21,13},{10,18... | collective-permute-start | bytes 3072008 | tf_op jit(solution)/shard_map/ppermute | solution.py:532
  57.0 1.3 %collective-permute-start.25 = (bf16[2000,256]{1,0:T(8,128)(2,1)S(1)}, bf16[2000,256]{1,0:T(8,128)(2,1)}, u32[]{:S(2)}, u32[]{:S(2)}) collective-permute-start(bf16[2000,256]{1,0:T(8,128)(2,1)S(1)} %collective-permute-done.24.refs_3_.refs_2_), channel_id=1, source_target_pairs={{8,0},{12,4},{16,24},{20,28},{9,1},{13,5},{17,25},{21,29},{10,2},{... | collective-permute-start | bytes 3072008 | tf_op jit(solution)/shard_map/ppermute | solution.py:532
  58.3 3.2 %project.3 = (f32[6,4,16,256]{3,2,1,0:T(8,128)S(1)}, f32[6,4,16,256]{3,2,1,0:T(8,128)}) custom-call(s32[1]{0:T(128)} %bitcast.10.core_ref, bf16[256,2048]{1,0:T(8,128)(2,1)} %stack_panels.1.refs_0_, bf16[2000,256]{1,0:T(8,128)(2,1)S(1)} %straighten.1.refs_1_.refs_0_, bf16[2000,256]{1,0:T(8,128)(2,1)S(1)} %collective-permute-done.22.refs_2_.refs_1_, ...), custom_call_target="tpu_custom_call" | custom-call | flops 786432000 | bytes 4882432 | tf_op jit(solution)/shard_map/project/pallas_call | solution.py:291
  61.5 2.0 %collective-permute-done.27.refs_1_ = f32[6,4,16,256]{3,2,1,0:T(8,128)} collective-permute-done((f32[6,4,16,256]{3,2,1,0:T(8,128)}, f32[6,4,16,256]{3,2,1,0:T(8,128)}, u32[]{:S(2)}, u32[]{:S(2)}) %collective-permute-start.27) | collective-permute-done | bytes 393248 | tf_op jit(solution)/shard_map/ppermute | solution.py:441
  63.5 1.0 split_sum.3
  64.6 1.6 %collective-permute-start.28 = (f32[6,16,256]{2,1,0:T(8,128)S(1)}, f32[6,16,256]{2,1,0:T(8,128)S(1)}, u32[]{:S(2)}, u32[]{:S(2)}) collective-permute-start(f32[6,16,256]{2,1,0:T(8,128)S(1)} %get-tuple-element.399), channel_id=1, source_target_pairs={{0,1},{1,0},{2,3},{3,2},{4,5},{5,4},{6,7},{7,6},{8,9},{9,8},{10,11... | collective-permute-start | bytes 294920 | tf_op jit(solution)/shard_map/ppermute | solution.py:441
  66.2 1.5 %collective-permute-start.29 = (f32[6,16,256]{2,1,0:T(8,128)S(1)}, f32[6,16,256]{2,1,0:T(8,128)S(1)}, u32[]{:S(2)}, u32[]{:S(2)}) collective-permute-start(f32[6,16,256]{2,1,0:T(8,128)S(1)} %get-tuple-element.400), channel_id=1, source_target_pairs={{0,2},{1,3},{2,0},{3,1},{4,6},{5,7},{6,4},{7,5},{8,10},{9,11},{10,... | collective-permute-start | bytes 294920 | tf_op jit(solution)/shard_map/ppermute | solution.py:441
  67.7 1.7 %collective-permute-done.28 = f32[6,16,256]{2,1,0:T(8,128)S(1)} collective-permute-done((f32[6,16,256]{2,1,0:T(8,128)S(1)}, f32[6,16,256]{2,1,0:T(8,128)S(1)}, u32[]{:S(2)}, u32[]{:S(2)}) %collective-permute-start.28) | collective-permute-done | bytes 98336 | tf_op jit(solution)/shard_map/ppermute | solution.py:441
  69.5 2.4 %collective-permute-start.30 = (f32[6,16,256]{2,1,0:T(8,128)S(1)}, f32[6,16,256]{2,1,0:T(8,128)S(1)}, u32[]{:S(2)}, u32[]{:S(2)}) collective-permute-start(f32[6,16,256]{2,1,0:T(8,128)S(1)} %get-tuple-element.401), channel_id=1, source_target_pairs={{0,3},{1,2},{2,1},{3,0},{4,7},{5,6},{6,5},{7,4},{8,11},{9,10},{10,... | collective-permute-start | bytes 294920 | tf_op jit(solution)/shard_map/ppermute | solution.py:441
  72.0 3.0 %collective-permute-done.30 = f32[6,16,256]{2,1,0:T(8,128)S(1)} collective-permute-done((f32[6,16,256]{2,1,0:T(8,128)S(1)}, f32[6,16,256]{2,1,0:T(8,128)S(1)}, u32[]{:S(2)}, u32[]{:S(2)}) %collective-permute-start.30) | collective-permute-done | bytes 98336 | tf_op jit(solution)/shard_map/ppermute | solution.py:441
  75.0 3.3 %collective-permute-done.25.refs_4_ = bf16[2000,256]{1,0:T(8,128)(2,1)} collective-permute-done((bf16[2000,256]{1,0:T(8,128)(2,1)S(1)}, bf16[2000,256]{1,0:T(8,128)(2,1)}, u32[]{:S(2)}, u32[]{:S(2)}) %collective-permute-start.25) | collective-permute-done | bytes 1024032 | tf_op jit(solution)/shard_map/ppermute | solution.py:532
  78.3 1.3 %collective-permute-start.32 = (bf16[2000,256]{1,0:T(8,128)(2,1)}, bf16[2000,256]{1,0:T(8,128)(2,1)}, u32[]{:S(2)}, u32[]{:S(2)}) collective-permute-start(bf16[2000,256]{1,0:T(8,128)(2,1)} %collective-permute-done.23.refs_5_), channel_id=1, source_target_pairs={{8,0},{12,4},{16,24},{20,28},{9,1},{13,5},{17,25},{21,29},{10,2},{... | collective-permute-start | bytes 3072008 | tf_op jit(solution)/shard_map/ppermute | solution.py:532
  79.7 34.7 %conditional.1 = (bf16[8,4,16,128]{3,2,1,0:T(8,128)(2,1)}, bf16[8,4,16,128]{3,2,1,0:T(8,128)(2,1)}, f32[64,4000]{1,0:T(8,128)}) conditional(s32[]{:T(128)} %convert_element_type.61, (s32[8]{0:T(128)S(1)}, f32[256]{0:T(256)S(1)}, bf16[4000,64]{0,1:T(8,128)(2,1)}, bf16[4000,64]{0,1:T(8,128)(2,1)}, s32[8,32]{1,0:T(8,128)S(1)}, ...), branch_computations={%region_6.14_spmd, %region_14.18_spmd} | conditional | flops 524588416 | bytes 57519072 | solution.py:669
  79.9 3.0 %project.2 = (f32[4,4,16,256]{3,2,1,0:T(8,128)S(1)}, f32[4,4,16,256]{3,2,1,0:T(8,128)S(1)}) custom-call(s32[1]{0:T(128)} %bitcast.4.core_ref, bf16[256,2048]{1,0:T(8,128)(2,1)} %get-tuple-element.347.refs_0_, bf16[256,2048]{1,0:T(8,128)(2,1)} %get-tuple-element.348.refs_1_, bf16[2000,256]{1,0:T(8,128)(2,1)} %get-tuple-element.349.refs_2_, ...), custom_call_target="tpu_custom_call" | custom-call | flops 524288000 | bytes 3596288 | tf_op jit(solution)/shard_map/cond/branch_1_fun/project/pallas_call | solution.py:291
  83.1 1.4 %collective-permute-done.refs_1_ = f32[4,4,16,256]{3,2,1,0:T(8,128)S(1)} collective-permute-done((f32[4,4,16,256]{3,2,1,0:T(8,128)S(1)}, f32[4,4,16,256]{3,2,1,0:T(8,128)S(1)}, u32[]{:S(2)}, u32[]{:S(2)}) %collective-permute-start) | collective-permute-done | bytes 262176 | tf_op jit(solution)/shard_map/cond/branch_1_fun/ppermute | solution.py:441
  84.6 1.6 %collective-permute-start.1 = (f32[4,16,256]{2,1,0:T(8,128)S(1)}, f32[4,16,256]{2,1,0:T(8,128)S(1)}, u32[]{:S(2)}, u32[]{:S(2)}) collective-permute-start(f32[4,16,256]{2,1,0:T(8,128)S(1)} %get-tuple-element.354), channel_id=1, source_target_pairs={{0,1},{1,0},{2,3},{3,2},{4,5},{5,4},{6,7},{7,6},{8,9},{9,8},{10,11... | collective-permute-start | bytes 196616 | tf_op jit(solution)/shard_map/cond/branch_1_fun/ppermute | solution.py:441
  86.2 1.5 %collective-permute-start.2 = (f32[4,16,256]{2,1,0:T(8,128)S(1)}, f32[4,16,256]{2,1,0:T(8,128)S(1)}, u32[]{:S(2)}, u32[]{:S(2)}) collective-permute-start(f32[4,16,256]{2,1,0:T(8,128)S(1)} %get-tuple-element.355), channel_id=1, source_target_pairs={{0,2},{1,3},{2,0},{3,1},{4,6},{5,7},{6,4},{7,5},{8,10},{9,11},{10,... | collective-permute-start | bytes 196616 | tf_op jit(solution)/shard_map/cond/branch_1_fun/ppermute | solution.py:441
  88.2 0.7 collective-permute-done.1
  88.9 1.5 %collective-permute-done.2 = f32[4,16,256]{2,1,0:T(8,128)S(1)} collective-permute-done((f32[4,16,256]{2,1,0:T(8,128)S(1)}, f32[4,16,256]{2,1,0:T(8,128)S(1)}, u32[]{:S(2)}, u32[]{:S(2)}) %collective-permute-start.2) | collective-permute-done | bytes 65568 | tf_op jit(solution)/shard_map/cond/branch_1_fun/ppermute | solution.py:441
  90.4 2.4 %collective-permute-done.3 = f32[4,16,256]{2,1,0:T(8,128)S(1)} collective-permute-done((f32[4,16,256]{2,1,0:T(8,128)S(1)}, f32[4,16,256]{2,1,0:T(8,128)S(1)}, u32[]{:S(2)}, u32[]{:S(2)}) %collective-permute-start.3) | collective-permute-done | bytes 65568 | tf_op jit(solution)/shard_map/cond/branch_1_fun/ppermute | solution.py:441
  93.1 4.4 %collective-permute-start.5 = (f32[4,32]{1,0:T(4,128)S(1)}, f32[4,32]{1,0:T(4,128)S(1)}, u32[]{:S(2)}, u32[]{:S(2)}) collective-permute-start(f32[4,32]{1,0:T(4,128)S(1)} %select_reduce_fusion), channel_id=1, source_target_pairs={{0,16},{4,20},{8,24},{12,28},{16,0},{20,4},{24,8},{28,12},{1,17},{... | collective-permute-start | bytes 1544 | tf_op jit(solution)/shard_map/cond/branch_1_fun/ppermute | solution.py:441
  97.5 1.8 %collective-permute-start.6 = (f32[4,32]{1,0:T(4,128)S(1)}, f32[4,32]{1,0:T(4,128)S(1)}, u32[]{:S(2)}, u32[]{:S(2)}) collective-permute-start(f32[4,32]{1,0:T(4,128)S(1)} %select_reduce_fusion), channel_id=1, source_target_pairs={{0,24},{4,28},{8,16},{12,20},{16,8},{20,12},{24,0},{28,4},{1,25},{... | collective-permute-start | bytes 1544 | tf_op jit(solution)/shard_map/cond/branch_1_fun/ppermute | solution.py:441
  99.3 3.6 %collective-permute-done.6 = f32[4,32]{1,0:T(4,128)S(1)} collective-permute-done((f32[4,32]{1,0:T(4,128)S(1)}, f32[4,32]{1,0:T(4,128)S(1)}, u32[]{:S(2)}, u32[]{:S(2)}) %collective-permute-start.6) | collective-permute-done | bytes 544 | tf_op jit(solution)/shard_map/cond/branch_1_fun/ppermute | solution.py:441
  102.9 1.0 collective-permute-done.4
  104.2 1.6 %collective-permute-start.7 = (bf16[8,1,16,128]{3,2,1,0:T(8,128)(2,1)S(1)}, bf16[8,1,16,128]{3,2,1,0:T(8,128)(2,1)S(1)}, u32[]{:S(2)}, u32[]{:S(2)}) collective-permute-start(bf16[8,1,16,128]{3,2,1,0:T(8,128)(2,1)S(1)} %bitcast.68), channel_id=1, source_target_pairs={{0,1},{1,0},{2,3},{3,2},{4,5},{5,4},{6,7},{7,6},{8,9},{9,8},{10,11... | collective-permute-start | bytes 98312 | tf_op jit(solution)/shard_map/cond/branch_1_fun/ppermute | solution.py:441
  105.7 1.5 %collective-permute-start.8 = (bf16[8,1,16,128]{3,2,1,0:T(8,128)(2,1)S(1)}, bf16[8,1,16,128]{3,2,1,0:T(8,128)(2,1)S(1)}, u32[]{:S(2)}, u32[]{:S(2)}) collective-permute-start(bf16[8,1,16,128]{3,2,1,0:T(8,128)(2,1)S(1)} %bitcast.69), channel_id=1, source_target_pairs={{0,2},{1,3},{2,0},{3,1},{4,6},{5,7},{6,4},{7,5},{8,10},{9,11},{10,... | collective-permute-start | bytes 98312 | tf_op jit(solution)/shard_map/cond/branch_1_fun/ppermute | solution.py:441
  108.2 1.5 %collective-permute-done.8.refs_2_ = bf16[8,1,16,128]{3,2,1,0:T(8,128)(2,1)S(1)} collective-permute-done((bf16[8,1,16,128]{3,2,1,0:T(8,128)(2,1)S(1)}, bf16[8,1,16,128]{3,2,1,0:T(8,128)(2,1)S(1)}, u32[]{:S(2)}, u32[]{:S(2)}) %collective-permute-start.8) | collective-permute-done | bytes 32800 | tf_op jit(solution)/shard_map/cond/branch_1_fun/ppermute | solution.py:441
  109.7 2.4 %collective-permute-done.9.refs_3_ = bf16[8,1,16,128]{3,2,1,0:T(8,128)(2,1)S(1)} collective-permute-done((bf16[8,1,16,128]{3,2,1,0:T(8,128)(2,1)S(1)}, bf16[8,1,16,128]{3,2,1,0:T(8,128)(2,1)S(1)}, u32[]{:S(2)}, u32[]{:S(2)}) %collective-permute-start.9) | collective-permute-done | bytes 32800 | tf_op jit(solution)/shard_map/cond/branch_1_fun/ppermute | solution.py:441
  112.1 0.7 in_order.1
  112.7 1.7 %collective-permute-done.10 = bf16[8,4,16,128]{3,2,1,0:T(8,128)(2,1)} collective-permute-done((bf16[8,4,16,128]{3,2,1,0:T(8,128)(2,1)}, bf16[8,4,16,128]{3,2,1,0:T(8,128)(2,1)}, u32[]{:S(2)}, u32[]{:S(2)}) %collective-permute-start.10) | collective-permute-done | bytes 131104 | tf_op jit(solution)/shard_map/cond/branch_1_fun/ppermute | solution.py:441
  114.4 4.7 %contract.1 = (f32[64,2000]{1,0:T(8,128)S(1)}, f32[64,2000]{1,0:T(8,128)S(1)}) custom-call(s32[1]{0:T(128)} %bitcast.10.core_ref, bf16[8,4,16,128]{3,2,1,0:T(8,128)(2,1)} %get-tuple-element.409.kernel_ref, bf16[8,4,16,128]{3,2,1,0:T(8,128)(2,1)} %get-tuple-element.410.got_ref, bf16[2000,256]{1,0:T(8,128)(2,1)S(1)} %straighten.1.refs_1_.refs_0_, ...), custom_call_target="tpu_custom_call" | custom-call | flops 524288000 | bytes 5120000 | tf_op jit(solution)/shard_map/contract/pallas_call | solution.py:364
  119.5 1.7 %collective-permute-done.33.back_ref = f32[64,2000]{1,0:T(8,128)S(1)} collective-permute-done((f32[64,2000]{1,0:T(8,128)S(1)}, f32[64,2000]{1,0:T(8,128)S(1)}, u32[]{:S(2)}, u32[]{:S(2)}) %collective-permute-start.33) | collective-permute-done | bytes 512032 | tf_op jit(solution)/shard_map/ppermute | solution.py:441
  121.1 1.8 %finish.1 = f32[64,4000]{1,0:T(8,128)} custom-call(s32[2]{0:T(128)S(1)} %pad_add_fusion.3.flags_ref, f32[64,2000]{1,0:T(8,128)S(1)} %get-tuple-element.412.ours_ref, f32[64,2000]{1,0:T(8,128)S(1)} %collective-permute-done.33.back_ref, f32[64,4000]{1,0:T(8,128)} %get-tuple-element.414.other_ref), custom_call_target="tpu_custom_call", output_to_operand_aliasing={{}: (3, {})} | custom-call | tf_op jit(solution)/shard_map/finish/pallas_call | solution.py:410
  (110 shorter events, 9.3 us)
Async XLA Ops:
  0.0 3.4 %copy-start.3 = (f32[256]{0:T(256)S(1)}, f32[256]{0:T(256)}, u32[]{:S(2)}) copy-start(f32[256]{0:T(256)} %param.17) | copy-start | bytes 3076
  0.0 3.3 %copy-start.4 = (s32[8]{0:T(128)S(1)}, s32[8]{0:T(128)}, u32[]{:S(2)}) copy-start(s32[8]{0:T(128)} %param.18) | copy-start | bytes 100
  0.0 3.4 %collective-permute-start.17 = (f32[1,256]{1,0:T(1,128)}, f32[1,256]{1,0:T(1,128)S(1)}, u32[]{:S(2)}, u32[]{:S(2)}) collective-permute-start(f32[1,256]{1,0:T(1,128)} %bitcast.85), channel_id=1, source_target_pairs={{0,4},{4,0},{8,12},{12,8},{16,20},{20,16},{24,28},{28,24},{1,5},{5... | collective-permute-start | bytes 3080 | tf_op jit(solution)/shard_map/ppermute | solution.py:441
  0.5 2.9 %collective-permute-start.16 = (s32[1,8]{1,0:T(1,128)}, s32[1,8]{1,0:T(1,128)S(1)}, u32[]{:S(2)}, u32[]{:S(2)}) collective-permute-start(s32[1,8]{1,0:T(1,128)} %bitcast.87), channel_id=1, source_target_pairs={{0,4},{4,0},{8,12},{12,8},{16,20},{20,16},{24,28},{28,24},{1,5},{5... | collective-permute-start | bytes 104 | tf_op jit(solution)/shard_map/ppermute | solution.py:441
  1.4 5.5 %collective-permute-start.15 = (s32[16,8]{0,1:T(8,128)S(1)}, s32[16,8]{0,1:T(8,128)S(1)}, u32[]{:S(2)}, u32[]{:S(2)}) collective-permute-start(s32[16,8]{0,1:T(8,128)S(1)} %get-tuple-element.483), channel_id=1, source_target_pairs={{0,4},{4,0},{8,12},{12,8},{16,20},{20,16},{24,28},{28,24},{1,5},{5... | collective-permute-start | bytes 1544 | tf_op jit(solution)/shard_map/ppermute | solution.py:441
  3.0 6.2 %collective-permute-start.14 = (bf16[2000,256]{1,0:T(8,128)(2,1)S(1)}, bf16[2000,256]{1,0:T(8,128)(2,1)S(1)}, u32[]{:S(2)}, u32[]{:S(2)}) collective-permute-start(bf16[2000,256]{1,0:T(8,128)(2,1)S(1)} %half_of.1), channel_id=1, source_target_pairs={{0,4},{4,0},{8,12},{12,8},{16,20},{20,16},{24,28},{28,24},{1,5},{5... | collective-permute-start | bytes 3072008 | tf_op jit(solution)/shard_map/ppermute | solution.py:441
  3.5 4.6 %collective-permute-start.18 = (f32[1,528]{1,0:T(1,128)S(1)}, f32[1,528]{1,0:T(1,128)S(1)}, u32[]{:S(2)}, u32[]{:S(2)}) collective-permute-start(f32[1,528]{1,0:T(1,128)S(1)} %pad_maximum_fusion.3), channel_id=1, source_target_pairs={{0,8},{4,12},{8,0},{12,4},{16,24},{20,28},{24,16},{28,20},{1,9},{5... | collective-permute-start | bytes 6344 | tf_op jit(solution)/shard_map/ppermute | solution.py:441
  12.7 6.8 %collective-permute-start.21 = (f32[2,528]{1,0:T(2,128)S(1)}, f32[2,528]{1,0:T(2,128)S(1)}, u32[]{:S(2)}, u32[]{:S(2)}) collective-permute-start(f32[2,528]{1,0:T(2,128)S(1)} %maximum_select_fusion.1), channel_id=1, source_target_pairs={{0,16},{4,20},{8,24},{12,28},{16,0},{20,4},{24,8},{28,12},{1,17},{... | collective-permute-start | bytes 12680 | tf_op jit(solution)/shard_map/ppermute | solution.py:441
  16.0 7.2 %collective-permute-start.19 = (bf16[2000,128]{1,0:T(8,128)(2,1)S(1)}, bf16[2000,128]{1,0:T(8,128)(2,1)S(1)}, u32[]{:S(2)}, u32[]{:S(2)}) collective-permute-start(bf16[2000,128]{1,0:T(8,128)(2,1)S(1)} %get-tuple-element.388), channel_id=1, source_target_pairs={{8,16},{12,20},{16,8},{20,12},{9,17},{13,21},{17,9},{21,13},{10,18... | collective-permute-start | bytes 1536008 | tf_op jit(solution)/shard_map/ppermute | solution.py:532
  16.7 13.3 %collective-permute-start.20 = (bf16[2000,128]{1,0:T(8,128)(2,1)S(1)}, bf16[2000,128]{1,0:T(8,128)(2,1)S(1)}, u32[]{:S(2)}, u32[]{:S(2)}) collective-permute-start(bf16[2000,128]{1,0:T(8,128)(2,1)S(1)} %get-tuple-element.389), channel_id=1, source_target_pairs={{0,8},{4,12},{8,0},{12,4},{16,24},{20,28},{24,16},{28,20},{1,9},{5... | collective-permute-start | bytes 1536008 | tf_op jit(solution)/shard_map/ppermute | solution.py:532
  23.2 9.8 %copy-start = (bf16[4000,64]{0,1:T(8,128)(2,1)S(1)}, bf16[4000,64]{0,1:T(8,128)(2,1)}, u32[]{:S(2)}) copy-start(bf16[4000,64]{0,1:T(8,128)(2,1)} %param.15) | copy-start | bytes 1536004
  23.2 9.8 %copy-start.1 = (bf16[4000,64]{0,1:T(8,128)(2,1)S(1)}, bf16[4000,64]{0,1:T(8,128)(2,1)}, u32[]{:S(2)}) copy-start(bf16[4000,64]{0,1:T(8,128)(2,1)} %param.16) | copy-start | bytes 1536004
  30.4 24.9 %collective-permute-start.22 = (bf16[2000,256]{1,0:T(8,128)(2,1)S(1)}, bf16[2000,256]{1,0:T(8,128)(2,1)S(1)}, u32[]{:S(2)}, u32[]{:S(2)}) collective-permute-start(bf16[2000,256]{1,0:T(8,128)(2,1)S(1)} %straighten.1.refs_1_.refs_0_), channel_id=1, source_target_pairs={{0,8},{4,12},{8,0},{12,4},{16,24},{20,28},{24,16},{28,20},{1,9},{5... | collective-permute-start | bytes 3072008 | tf_op jit(solution)/shard_map/ppermute | solution.py:532
  32.2 24.8 %collective-permute-start.24 = (bf16[2000,256]{1,0:T(8,128)(2,1)S(1)}, bf16[2000,256]{1,0:T(8,128)(2,1)S(1)}, u32[]{:S(2)}, u32[]{:S(2)}) collective-permute-start(bf16[2000,256]{1,0:T(8,128)(2,1)S(1)} %straighten.1.refs_1_.refs_0_), channel_id=1, source_target_pairs={{8,16},{12,20},{16,8},{20,12},{9,17},{13,21},{17,9},{21,13},{10,18... | collective-permute-start | bytes 3072008 | tf_op jit(solution)/shard_map/ppermute | solution.py:532
  33.5 2.0 %collective-permute-start.26 = (bf16[128,2048]{1,0:T(8,128)(2,1)S(1)}, bf16[128,2048]{1,0:T(8,128)(2,1)S(1)}, u32[]{:S(2)}, u32[]{:S(2)}) collective-permute-start(bf16[128,2048]{1,0:T(8,128)(2,1)S(1)} %get-tuple-element.395), channel_id=1, source_target_pairs={{0,4},{4,0},{8,12},{12,8},{16,20},{20,16},{24,28},{28,24},{1,5},{5... | collective-permute-start | bytes 1572872 | tf_op jit(solution)/shard_map/ppermute | solution.py:441
  36.5 43.2 %copy-start.2 = (s32[8,32]{1,0:T(8,128)S(1)}, s32[8,32]{1,0:T(8,128)}, u32[]{:S(2)}) copy-start(s32[8,32]{1,0:T(8,128)} %param.19) | copy-start | bytes 3076
  36.5 38.5 %collective-permute-start.31 = (bf16[256,2048]{1,0:T(8,128)(2,1)}, bf16[256,2048]{1,0:T(8,128)(2,1)}, u32[]{:S(2)}, u32[]{:S(2)}) collective-permute-start(bf16[256,2048]{1,0:T(8,128)(2,1)} %stack_panels.1.refs_0_), channel_id=1, source_target_pairs={{0,8},{4,12},{24,16},{28,20},{1,9},{5,13},{25,17},{29,21},{2,10},{... | collective-permute-start | bytes 3145736 | tf_op jit(solution)/shard_map/ppermute | solution.py:532
  55.3 19.7 %collective-permute-start.23 = (bf16[2000,256]{1,0:T(8,128)(2,1)S(1)}, bf16[2000,256]{1,0:T(8,128)(2,1)}, u32[]{:S(2)}, u32[]{:S(2)}) collective-permute-start(bf16[2000,256]{1,0:T(8,128)(2,1)S(1)} %collective-permute-done.22.refs_2_.refs_1_), channel_id=1, source_target_pairs={{8,16},{12,20},{16,8},{20,12},{9,17},{13,21},{17,9},{21,13},{10,18... | collective-permute-start | bytes 3072008 | tf_op jit(solution)/shard_map/ppermute | solution.py:532
  57.0 21.3 %collective-permute-start.25 = (bf16[2000,256]{1,0:T(8,128)(2,1)S(1)}, bf16[2000,256]{1,0:T(8,128)(2,1)}, u32[]{:S(2)}, u32[]{:S(2)}) collective-permute-start(bf16[2000,256]{1,0:T(8,128)(2,1)S(1)} %collective-permute-done.24.refs_3_.refs_2_), channel_id=1, source_target_pairs={{8,0},{12,4},{16,24},{20,28},{9,1},{13,5},{17,25},{21,29},{10,2},{... | collective-permute-start | bytes 3072008 | tf_op jit(solution)/shard_map/ppermute | solution.py:532
  61.4 2.1 %collective-permute-start.27 = (f32[6,4,16,256]{3,2,1,0:T(8,128)}, f32[6,4,16,256]{3,2,1,0:T(8,128)}, u32[]{:S(2)}, u32[]{:S(2)}) collective-permute-start(f32[6,4,16,256]{3,2,1,0:T(8,128)} %get-tuple-element.397), channel_id=1, source_target_pairs={{0,4},{4,0},{8,12},{12,8},{16,20},{20,16},{24,28},{28,24},{1,5},{5... | collective-permute-start | bytes 1179656 | tf_op jit(solution)/shard_map/ppermute | solution.py:441
  64.6 4.9 %collective-permute-start.28 = (f32[6,16,256]{2,1,0:T(8,128)S(1)}, f32[6,16,256]{2,1,0:T(8,128)S(1)}, u32[]{:S(2)}, u32[]{:S(2)}) collective-permute-start(f32[6,16,256]{2,1,0:T(8,128)S(1)} %get-tuple-element.399), channel_id=1, source_target_pairs={{0,1},{1,0},{2,3},{3,2},{4,5},{5,4},{6,7},{7,6},{8,9},{9,8},{10,11... | collective-permute-start | bytes 294920 | tf_op jit(solution)/shard_map/ppermute | solution.py:441
  66.2 5.8 %collective-permute-start.29 = (f32[6,16,256]{2,1,0:T(8,128)S(1)}, f32[6,16,256]{2,1,0:T(8,128)S(1)}, u32[]{:S(2)}, u32[]{:S(2)}) collective-permute-start(f32[6,16,256]{2,1,0:T(8,128)S(1)} %get-tuple-element.400), channel_id=1, source_target_pairs={{0,2},{1,3},{2,0},{3,1},{4,6},{5,7},{6,4},{7,5},{8,10},{9,11},{10,... | collective-permute-start | bytes 294920 | tf_op jit(solution)/shard_map/ppermute | solution.py:441
  69.5 5.5 %collective-permute-start.30 = (f32[6,16,256]{2,1,0:T(8,128)S(1)}, f32[6,16,256]{2,1,0:T(8,128)S(1)}, u32[]{:S(2)}, u32[]{:S(2)}) collective-permute-start(f32[6,16,256]{2,1,0:T(8,128)S(1)} %get-tuple-element.401), channel_id=1, source_target_pairs={{0,3},{1,2},{2,1},{3,0},{4,7},{5,6},{6,5},{7,4},{8,11},{9,10},{10,... | collective-permute-start | bytes 294920 | tf_op jit(solution)/shard_map/ppermute | solution.py:441
  78.3 36.1 %collective-permute-start.32 = (bf16[2000,256]{1,0:T(8,128)(2,1)}, bf16[2000,256]{1,0:T(8,128)(2,1)}, u32[]{:S(2)}, u32[]{:S(2)}) collective-permute-start(bf16[2000,256]{1,0:T(8,128)(2,1)} %collective-permute-done.23.refs_5_), channel_id=1, source_target_pairs={{8,0},{12,4},{16,24},{20,28},{9,1},{13,5},{17,25},{21,29},{10,2},{... | collective-permute-start | bytes 3072008 | tf_op jit(solution)/shard_map/ppermute | solution.py:532
  83.0 1.6 %collective-permute-start = (f32[4,4,16,256]{3,2,1,0:T(8,128)S(1)}, f32[4,4,16,256]{3,2,1,0:T(8,128)S(1)}, u32[]{:S(2)}, u32[]{:S(2)}) collective-permute-start(f32[4,4,16,256]{3,2,1,0:T(8,128)S(1)} %get-tuple-element.352), channel_id=1, source_target_pairs={{0,4},{4,0},{8,12},{12,8},{16,20},{20,16},{24,28},{28,24},{1,5},{5... | collective-permute-start | bytes 786440 | tf_op jit(solution)/shard_map/cond/branch_1_fun/ppermute | solution.py:441
  84.6 4.3 %collective-permute-start.1 = (f32[4,16,256]{2,1,0:T(8,128)S(1)}, f32[4,16,256]{2,1,0:T(8,128)S(1)}, u32[]{:S(2)}, u32[]{:S(2)}) collective-permute-start(f32[4,16,256]{2,1,0:T(8,128)S(1)} %get-tuple-element.354), channel_id=1, source_target_pairs={{0,1},{1,0},{2,3},{3,2},{4,5},{5,4},{6,7},{7,6},{8,9},{9,8},{10,11... | collective-permute-start | bytes 196616 | tf_op jit(solution)/shard_map/cond/branch_1_fun/ppermute | solution.py:441
  86.2 4.3 %collective-permute-start.2 = (f32[4,16,256]{2,1,0:T(8,128)S(1)}, f32[4,16,256]{2,1,0:T(8,128)S(1)}, u32[]{:S(2)}, u32[]{:S(2)}) collective-permute-start(f32[4,16,256]{2,1,0:T(8,128)S(1)} %get-tuple-element.355), channel_id=1, source_target_pairs={{0,2},{1,3},{2,0},{3,1},{4,6},{5,7},{6,4},{7,5},{8,10},{9,11},{10,... | collective-permute-start | bytes 196616 | tf_op jit(solution)/shard_map/cond/branch_1_fun/ppermute | solution.py:441
  87.7 5.2 %collective-permute-start.3 = (f32[4,16,256]{2,1,0:T(8,128)S(1)}, f32[4,16,256]{2,1,0:T(8,128)S(1)}, u32[]{:S(2)}, u32[]{:S(2)}) collective-permute-start(f32[4,16,256]{2,1,0:T(8,128)S(1)} %get-tuple-element.356), channel_id=1, source_target_pairs={{0,3},{1,2},{2,1},{3,0},{4,7},{5,6},{6,5},{7,4},{8,11},{9,10},{10,... | collective-permute-start | bytes 196616 | tf_op jit(solution)/shard_map/cond/branch_1_fun/ppermute | solution.py:441
  93.1 6.2 %collective-permute-start.5 = (f32[4,32]{1,0:T(4,128)S(1)}, f32[4,32]{1,0:T(4,128)S(1)}, u32[]{:S(2)}, u32[]{:S(2)}) collective-permute-start(f32[4,32]{1,0:T(4,128)S(1)} %select_reduce_fusion), channel_id=1, source_target_pairs={{0,16},{4,20},{8,24},{12,28},{16,0},{20,4},{24,8},{28,12},{1,17},{... | collective-permute-start | bytes 1544 | tf_op jit(solution)/shard_map/cond/branch_1_fun/ppermute | solution.py:441
  97.5 5.5 %collective-permute-start.6 = (f32[4,32]{1,0:T(4,128)S(1)}, f32[4,32]{1,0:T(4,128)S(1)}, u32[]{:S(2)}, u32[]{:S(2)}) collective-permute-start(f32[4,32]{1,0:T(4,128)S(1)} %select_reduce_fusion), channel_id=1, source_target_pairs={{0,24},{4,28},{8,16},{12,20},{16,8},{20,12},{24,0},{28,4},{1,25},{... | collective-permute-start | bytes 1544 | tf_op jit(solution)/shard_map/cond/branch_1_fun/ppermute | solution.py:441
  99.2 4.7 %collective-permute-start.4 = (f32[36,256]{1,0:T(8,128)S(1)}, f32[36,256]{1,0:T(8,128)S(1)}, u32[]{:S(2)}, u32[]{:S(2)}) collective-permute-start(f32[36,256]{1,0:T(8,128)S(1)} %select_maximum_fusion), channel_id=1, source_target_pairs={{0,8},{4,12},{8,0},{12,4},{16,24},{20,28},{24,16},{28,20},{1,9},{5... | collective-permute-start | bytes 110600 | tf_op jit(solution)/shard_map/cond/branch_1_fun/ppermute | solution.py:441
  104.2 4.0 %collective-permute-start.7 = (bf16[8,1,16,128]{3,2,1,0:T(8,128)(2,1)S(1)}, bf16[8,1,16,128]{3,2,1,0:T(8,128)(2,1)S(1)}, u32[]{:S(2)}, u32[]{:S(2)}) collective-permute-start(bf16[8,1,16,128]{3,2,1,0:T(8,128)(2,1)S(1)} %bitcast.68), channel_id=1, source_target_pairs={{0,1},{1,0},{2,3},{3,2},{4,5},{5,4},{6,7},{7,6},{8,9},{9,8},{10,11... | collective-permute-start | bytes 98312 | tf_op jit(solution)/shard_map/cond/branch_1_fun/ppermute | solution.py:441
  105.7 3.9 %collective-permute-start.8 = (bf16[8,1,16,128]{3,2,1,0:T(8,128)(2,1)S(1)}, bf16[8,1,16,128]{3,2,1,0:T(8,128)(2,1)S(1)}, u32[]{:S(2)}, u32[]{:S(2)}) collective-permute-start(bf16[8,1,16,128]{3,2,1,0:T(8,128)(2,1)S(1)} %bitcast.69), channel_id=1, source_target_pairs={{0,2},{1,3},{2,0},{3,1},{4,6},{5,7},{6,4},{7,5},{8,10},{9,11},{10,... | collective-permute-start | bytes 98312 | tf_op jit(solution)/shard_map/cond/branch_1_fun/ppermute | solution.py:441
  107.3 4.8 %collective-permute-start.9 = (bf16[8,1,16,128]{3,2,1,0:T(8,128)(2,1)S(1)}, bf16[8,1,16,128]{3,2,1,0:T(8,128)(2,1)S(1)}, u32[]{:S(2)}, u32[]{:S(2)}) collective-permute-start(bf16[8,1,16,128]{3,2,1,0:T(8,128)(2,1)S(1)} %bitcast.70), channel_id=1, source_target_pairs={{0,3},{1,2},{2,1},{3,0},{4,7},{5,6},{6,5},{7,4},{8,11},{9,10},{10,... | collective-permute-start | bytes 98312 | tf_op jit(solution)/shard_map/cond/branch_1_fun/ppermute | solution.py:441
  112.7 1.7 %collective-permute-start.10 = (bf16[8,4,16,128]{3,2,1,0:T(8,128)(2,1)}, bf16[8,4,16,128]{3,2,1,0:T(8,128)(2,1)}, u32[]{:S(2)}, u32[]{:S(2)}) collective-permute-start(bf16[8,4,16,128]{3,2,1,0:T(8,128)(2,1)} %in_order.1), channel_id=1, source_target_pairs={{0,4},{4,0},{8,12},{12,8},{16,20},{20,16},{24,28},{28,24},{1,5},{5... | collective-permute-start | bytes 393224 | tf_op jit(solution)/shard_map/cond/branch_1_fun/ppermute | solution.py:441
  119.2 2.0 %collective-permute-start.33 = (f32[64,2000]{1,0:T(8,128)S(1)}, f32[64,2000]{1,0:T(8,128)S(1)}, u32[]{:S(2)}, u32[]{:S(2)}) collective-permute-start(f32[64,2000]{1,0:T(8,128)S(1)} %get-tuple-element.413), channel_id=1, source_target_pairs={{0,4},{4,0},{8,12},{12,8},{16,20},{20,16},{24,28},{28,24},{1,5},{5... | collective-permute-start | bytes 1536008 | tf_op jit(solution)/shard_map/ppermute | solution.py:441
